TPU v7x, 32 devices: a whole 2x2x4 slice. The times are simulated.
32 devices in a mesh: dp: 8 (over z, core), proto: 4 (over y, x).
Axes of the slice: x: 2, y: 2, z: 4, core: 2. Of those that a mesh axis runs over, the one named last changes fastest.
Arguments:
- codes_view: bfloat16 [4096, 256], P('dp'), may hold values from -16 to 16
- pred_view: bfloat16 [4096, 256], P('dp'), may hold values from -32 to 32
- prototypes: bfloat16 [65536, 256], P(('proto', 'dp')), may hold values from -1.5 to 1.5
Outputs:
- swap_loss: float32 [4096], P('dp')
- pull: float32 [4096, 256], P('dp', 'proto')
All inputs are finite; a program needn't handle non-finite values.
Results may differ from a plain program's by a relative error of at most 0.0025.
Values may be sent and summed in bfloat16 or wider, within the bound.
No kernel may reach another device: no remote copies, remote signals or barrier semaphores. Data moves between devices by JAX's collectives and lax.ppermute only.
A program may use at most 64 MiB of HBM per device.

v0:
```python
import jax
import jax.numpy as jnp
from jax import lax
from jax.sharding import PartitionSpec as P

code_temp = 0.05
pred_temp = 0.1


def joined(part, axis, combine):
    gathered = jax.tree.map(lambda a: lax.all_gather(a, axis), part)

    def take(source):
        return jax.tree.map(lambda a: lax.dynamic_index_in_dim(a, source, 0, False), gathered)

    return lax.fori_loop(
        1, lax.axis_size(axis), lambda source, state: combine(state, take(source)), take(0)
    )


def scores(embeds, protos, temp):
    return (
        lax.dot_general(
            embeds, protos, (((1,), (1,)), ((), ())), preferred_element_type=jnp.float32
        )
        / temp
    )


def join_rows(first, second):
    peak = jnp.maximum(first[1], second[1])
    total = first[2] * jnp.exp(first[1] - peak) + second[2] * jnp.exp(second[1] - peak)
    return (first[0] + second[0], peak, total)


def local_map(func, whole, width):
    shaped = whole.reshape(whole.shape[0] // width, width, whole.shape[1])
    result = lax.map(lambda piece: func(piece, 0), shaped)
    return jax.tree.map(lambda part_out: part_out.reshape(-1), result)


def local_fold(func, whole, width, start_carry):

    def step(index, carry):
        piece = lax.dynamic_slice_in_dim(whole, index * width, width, 0)
        return func(carry, piece, index * width)

    return lax.fori_loop(0, whole.shape[0] // width, step, start_carry)


def body(codes_view, pred_view, prototypes):
    local_rows = codes_view.shape[0]
    proto_count = prototypes.shape[0] * lax.axis_size("dp")
    width = min(512, proto_count)

    def column_stats(piece, start):
        logits = scores(codes_view, piece, code_temp)
        peak = jnp.max(logits, axis=0)
        return (peak, jnp.sum(jnp.exp(logits - peak[None, :]), axis=0))

    gathered = lax.all_gather(prototypes, "dp", axis=0, tiled=True)
    local_peak, local_total = local_map(column_stats, gathered, width)
    col_peak = lax.pmax(local_peak, "dp")
    col_total = lax.psum(local_total * jnp.exp(local_peak - col_peak), "dp")
    col_offset = col_peak + jnp.log(col_total)

    def row_step(carry, piece, start):
        mass, peak, total = carry
        offset = lax.dynamic_slice_in_dim(col_offset, start, piece.shape[0], 0)
        logits = scores(codes_view, piece, code_temp)
        mass = mass + jnp.sum(jnp.exp(logits - offset[None, :]), axis=1)
        pred = scores(pred_view, piece, pred_temp)
        new_peak = jnp.maximum(peak, jnp.max(pred, axis=1))
        total = total * jnp.exp(peak - new_peak) + jnp.sum(
            jnp.exp(pred - new_peak[:, None]), axis=1
        )
        return (mass, new_peak, total)

    row_start = (
        jnp.zeros((local_rows,), jnp.float32),
        jnp.full((local_rows,), -1e30, jnp.float32),
        jnp.zeros((local_rows,), jnp.float32),
    )
    row_local = local_fold(row_step, gathered, width, row_start)
    mass, peak, total = joined(row_local, "proto", join_rows)
    log_norm = peak + jnp.log(total)

    def target_step(carry, piece, start):
        cross, pull = carry
        offset = lax.dynamic_slice_in_dim(col_offset, start, piece.shape[0], 0)
        logits = scores(codes_view, piece, code_temp)
        targets = jnp.exp(logits - offset[None, :]) / mass[:, None]
        pred = scores(pred_view, piece, pred_temp)
        probs = jnp.exp(pred - log_norm[:, None])
        cross = cross + jnp.sum(targets * pred, axis=1)
        diff = (targets - probs).astype(jnp.bfloat16)
        pull = pull + jnp.dot(diff, piece, preferred_element_type=jnp.float32)
        return (cross, pull)

    target_start = (
        jnp.zeros((local_rows,), jnp.float32),
        jnp.zeros((local_rows, prototypes.shape[1]), jnp.float32),
    )
    cross, pull = local_fold(target_step, gathered, width, target_start)
    cross = lax.psum(cross, "proto")
    pull_part = lax.psum_scatter(pull, "proto", scatter_dimension=1, tiled=True)
    return (log_norm - cross, pull_part)


def solution(mesh):
    placed = (P("dp", None), P("dp", None), P(("proto", "dp"), None))
    return jax.shard_map(
        body, mesh=mesh, in_specs=placed, out_specs=(P("dp"), P("dp", "proto")), check_vma=False
    )
```

profile of v0, /device:TPU:0, one launch (start us, length us, event | category | flops | bytes accessed | tf_op | source)
XLA Modules:
  0.0 553.3 jit_solution(11226916531319293168)
XLA Ops:
  8.0 86.4 %all-gather.8.cloned.1.call-done = bf16[16384,256]{1,0:T(8,128)(2,1)} async-done(((bf16[2048,256]{1,0:T(8,128)(2,1)}), bf16[16384,256]{1,0:T(8,128)(2,1)}) %all-gather.8.cloned.1.call-update) | async-done | bytes 8388624 | tf_op jit(solution)/shard_map/all_gather | solution.py:61
  94.4 55.1 %while.65 = (s32[]{:T(128)}, f32[32,512]{1,0:T(8,128)S(1)}, f32[32,512]{1,0:T(8,128)S(1)}, bf16[32,512,256]{2,1,0:T(8,128)(2,1)}, bf16[512,256]{1,0:T(8,128)(2,1)}, /*index=5*/s32[]{:T(128)}, s32[]{:T(128)}) while((s32[]{:T(128)}, f32[32,512]{1,0:T(8,128)S(1)}, f32[32,512]{1,0:T(8,128)S(1)}, bf16[32,512,256]{2,1,0:T(8,128)(2,1)}, ...), condition=%wide.region_3.4_spmd, body=%wide.region_0.3_spmd.sunk | while | flops 135265280 | bytes 2635873 | solution.py:38
  150.3 52.3 %all-reduce.3.cloned.1.call-done = f32[16384]{0:T(1024)} async-done(((f32[16384]{0:T(1024)}), f32[16384]{0:T(1024)}) %all-reduce.3.cloned.1.call-update) | async-done | bytes 65552 | tf_op jit(solution)/shard_map/pmax | solution.py:63
  202.6 1.5 exponential_multiply_fusion
  204.2 54.0 %all-reduce.5.cloned.1.call-done = f32[16384]{0:T(1024)} async-done(((f32[16384]{0:T(1024)}), f32[16384]{0:T(1024)}) %all-reduce.5.cloned.1.call-update) | async-done | bytes 65552 | tf_op jit(solution)/shard_map/psum | solution.py:64
  259.2 97.8 %while.67 = (s32[]{:T(128)}, f32[512]{0:T(512)S(1)}, f32[512]{0:T(512)S(1)}, f32[512]{0:T(512)S(1)}, bf16[16384,256]{1,0:T(8,128)(2,1)}, /*index=5*/bf16[512,256...) while((s32[]{:T(128)}, f32[512]{0:T(512)S(1)}, ...), condition=%wide.region_10.11_spmd.clone, body=%wide.region_6.10_spmd.clone.sunk | while | flops 270273536 | bytes 3186882 | solution.py:48
  357.0 8.0 %all-gather.3 = f32[4,1,512]{2,1,0:T(1,128)S(1)} all-gather(f32[1,1,512]{2,1,0:T(1,128)S(1)} %bitcast.77), channel_id=2, replica_groups=mesh['dp'=8,'proto'=4] {'proto'}, dimensions={0}, use_global_device_ids=true | all-gather | bytes 10240 | tf_op jit(solution)/shard_map/all_gather | solution.py:11
  365.0 8.0 %all-gather.4 = f32[4,1,512]{2,1,0:T(1,128)S(1)} all-gather(f32[1,1,512]{2,1,0:T(1,128)S(1)} %bitcast.69), channel_id=3, replica_groups=mesh['dp'=8,'proto'=4] {'proto'}, dimensions={0}, use_global_device_ids=true | all-gather | bytes 10240 | tf_op jit(solution)/shard_map/all_gather | solution.py:11
  373.0 7.1 %all-gather.5 = f32[4,1,512]{2,1,0:T(1,128)S(1)} all-gather(f32[1,1,512]{2,1,0:T(1,128)S(1)} %bitcast.78), channel_id=4, replica_groups=mesh['dp'=8,'proto'=4] {'proto'}, dimensions={0}, use_global_device_ids=true | all-gather | bytes 10240 | tf_op jit(solution)/shard_map/all_gather | solution.py:11
  380.4 142.6 %while.68 = (s32[]{:T(128)}, f32[512]{0:T(512)S(1)}, f32[512,256]{1,0:T(8,128)S(1)}, bf16[16384,256]{1,0:T(8,128)(2,1)}, bf16[512,256]{1,0:T(8,128)(2,1)}, /*ind...) while((s32[]{:T(128)}, f32[512]{0:T(512)S(1)}, ...), condition=%wide.region_15.16_spmd.clone, body=%wide.region_13.15_spmd.clone.sunk | while | flops 405275136 | bytes 7620814 | solution.py:48
  383.3 1.6 convolution_add_fusion.2
  387.8 1.6 convolution_add_fusion.2
  390.7 1.5 multiply_reduce_fusion.2
  392.3 1.6 convolution_add_fusion.2
  395.2 1.5 multiply_reduce_fusion.2
  396.7 1.6 convolution_add_fusion.2
  399.7 1.5 multiply_reduce_fusion.2
  401.2 1.6 convolution_add_fusion.2
  404.1 1.5 multiply_reduce_fusion.2
  405.6 1.6 convolution_add_fusion.2
  410.1 1.6 convolution_add_fusion.2
  414.5 1.6 convolution_add_fusion.2
  419.0 1.6 convolution_add_fusion.2
  423.4 1.6 convolution_add_fusion.2
  427.9 1.6 convolution_add_fusion.2
  432.3 1.6 convolution_add_fusion.2
  436.8 1.6 convolution_add_fusion.2
  441.3 1.6 convolution_add_fusion.2
  445.7 1.6 convolution_add_fusion.2
  450.2 1.6 convolution_add_fusion.2
  454.6 1.6 convolution_add_fusion.2
  459.1 1.6 convolution_add_fusion.2
  463.5 1.6 convolution_add_fusion.2
  468.0 1.6 convolution_add_fusion.2
  472.4 1.6 convolution_add_fusion.2
  476.9 1.6 convolution_add_fusion.2
  481.3 1.6 convolution_add_fusion.2
  485.8 1.6 convolution_add_fusion.2
  490.3 1.6 convolution_add_fusion.2
  494.7 1.6 convolution_add_fusion.2
  499.2 1.6 convolution_add_fusion.2
  503.6 1.6 convolution_add_fusion.2
  508.1 1.6 convolution_add_fusion.2
  512.5 1.6 convolution_add_fusion.2
  517.0 1.6 convolution_add_fusion.2
  521.4 1.6 convolution_add_fusion.2
  524.0 8.9 %psum.15 = f32[512]{0:T(512)S(1)} all-reduce(f32[512]{0:T(512)S(1)} %get-tuple-element.512), channel_id=1, replica_groups=mesh['dp'=8,'proto'=4] {'proto'}, use_global_device_ids=true, to_apply=%region_16.17 | all-reduce | flops 512 | bytes 4096 | tf_op jit(solution)/shard_map/psum | solution.py:105
  533.6 13.2 %reduce-scatter.2.cloned.1.call-done = f32[512,64]{0,1:T(8,128)} async-done(((f32[512,256]{0,1:T(8,128)}), f32[512,64]{0,1:T(8,128)}) %reduce-scatter.2.cloned.1.call-update) | async-done | bytes 131088 | tf_op jit(solution)/shard_map/reduce_scatter | solution.py:106
  (518 shorter events, 240.2 us)
Async XLA Ops:
  7.2 252.0 %copy-start = (bf16[512,256]{1,0:T(8,128)(2,1)S(1)}, bf16[512,256]{1,0:T(8,128)(2,1)}, u32[]{:S(2)}) copy-start(bf16[512,256]{1,0:T(8,128)(2,1)} %param.12) | copy-start | bytes 786436
  7.2 87.2 %all-gather.8.cloned.1.call-start = ((), (), s32[]{:S(2)}) async-start(), calls=%async_computation.1 | async-start | bytes 9437184 | tf_op jit(solution)/shard_map/all_gather | solution.py:61
  7.9 194.7 %all-reduce.3.cloned.1.call-start = ((), (), s32[]{:S(2)}) async-start(), calls=%async_computation.2 | async-start | bytes 131072 | tf_op jit(solution)/shard_map/pmax | solution.py:63
  150.2 108.0 %all-reduce.5.cloned.1.call-start = ((), (), s32[]{:S(2)}) async-start(), calls=%async_computation.3 | async-start | bytes 131072 | tf_op jit(solution)/shard_map/psum | solution.py:64
  204.1 342.7 %reduce-scatter.2.cloned.1.call-start = ((), (), s32[]{:S(2)}) async-start(), calls=%async_computation.4 | async-start | bytes 655360 | tf_op jit(solution)/shard_map/reduce_scatter | solution.py:106
Sparse Core Ops, SparseCore 0:
  9.6 84.7 all-gather.7
  150.3 52.1 all-reduce.2
  205.6 52.6 all-reduce.4
  524.1 22.6 reduce-scatter.1
where the time goes:
time: 559 us; the launch traced here: 553 us
  matrix products  269 us (48%)
  waiting for transfers between devices  207 us (37%)
  blocking collectives  32.1 us (6%)
  other arithmetic  17.1 us (3%)
  between operations  13.9 us (2%)
  local copies, waits for them, and re-layouts  10.4 us (2%)
    dot_general x160, matrix products, scores(): lax.dot_general(embeds, protos, (((1,), (1,)), ((), ())), preferred_eleme...  219 us
    all_gather x1, waiting for transfers between devices, body(): gathered = lax.all_gather(prototypes, 'dp', axis=0, tiled=True)  86.4 us
    psum x1, waiting for transfers between devices, body(): col_total = lax.psum(local_total * jnp.exp(local_peak - col_peak), 'dp')  54 us
    pmax x1, waiting for transfers between devices, body(): col_peak = lax.pmax(local_peak, 'dp')  52.3 us
    dot_general x32, matrix products, target_step(): pull = pull + jnp.dot(diff, piece, preferred_element_type=jnp.float32)  49.6 us
    all_gather x3, blocking collectives, joined(): gathered = jax.tree.map(lambda a: lax.all_gather(a, axis), part)  23.2 us
    reduce_scatter x1, waiting for transfers between devices, body(): pull_part = lax.psum_scatter(pull, 'proto', scatter_dimension=1, tiled=True)  13.2 us
  transfers between devices with their start and end apart: 4, of which 4 were waited for; matrix products, arithmetic and copies ran while one was open for 0% of the time, Pallas kernels for 0%

commit v1 on v0

v1 whole, which is shorter than its diff:
```python
import functools
import math

import jax
import jax.numpy as jnp
from jax import lax
from jax.experimental import pallas as pl
from jax.experimental.pallas import tpu as pltpu
from jax.sharding import PartitionSpec as P

code_temp = 0.05
pred_temp = 0.1
code_scale = math.log2(math.e) / code_temp
pred_scale = math.log2(math.e) / pred_temp
log2 = math.log(2.0)
stat_rows = 8
sent_rows = 16
low = -1e30
chunk = 512
kernel_bytes = 24 * 1024 * 1024


def scores(embeds, protos):
    return lax.dot_general(
        embeds, protos, (((1,), (1,)), ((), ())), preferred_element_type=jnp.float32
    )


def bare(value):
    return value.astype(jnp.bfloat16)


def add(parts):
    return functools.reduce(jnp.add, parts)


def lane_fold(combine, value):
    parts = [value[:, i : i + 128] for i in range(0, value.shape[1], 128)]
    return functools.reduce(combine, parts)


def padded(rows, width):
    filler = jnp.zeros((stat_rows - len(rows), width), jnp.float32)
    return jnp.concatenate([*rows, filler], axis=0)


def split_stats(stats):
    terms = []
    for row in stats:
        for _ in range(3):
            term = bare(row)
            row = row - term.astype(jnp.float32)
            terms.append(term)
    filler = jnp.zeros((sent_rows - len(terms), stats[0].shape[1]), jnp.bfloat16)
    return jnp.concatenate([*terms, filler], axis=0)


def join_stats(terms, count):
    wide = terms.astype(jnp.float32)
    return [add([wide[3 * i + j : 3 * i + j + 1] for j in range(3)]) for i in range(count)]


def parted(value):
    share = value.shape[0] - stat_rows
    return value[:share, :], [value[share + i : share + i + 1, :] for i in range(2)]


def parted_sent(value):
    share = value.shape[0] - sent_rows
    return value[:share, :].astype(jnp.float32), join_stats(value[share:, :], 2)


def packed(part):
    pull, stats = part
    return jnp.concatenate([pull, padded(stats, pull.shape[1])], axis=0)


def join_preds(parts):
    peak = functools.reduce(jnp.maximum, [stats[0] for _, stats in parts])
    factors = [jnp.exp2(stats[0] - peak) for _, stats in parts]
    pull = add([part * factor for (part, _), factor in zip(parts, factors)])
    total = add([stats[1] * factor for (_, stats), factor in zip(parts, factors)])
    return pull, [peak, total]


def join_targets(parts):
    stats = [add([stats[i] for _, stats in parts]) for i in range(2)]
    return add([part for part, _ in parts]), stats


joins = {"pred": join_preds, "target": join_targets}


def send(info, place, pull, stats, kept, *sent):
    *sent, flipped = sent
    whole = len(sent) == 1
    count = sent[0].shape[0] if whole else len(sent) + 1
    share = pull.shape[1] // count
    high, tall = share + stat_rows, share + sent_rows
    flipped[...] = pull.T
    mine = pl.multiple_of(info[1] * share, share)
    kept[place * high : place * high + share, :] = flipped[pl.ds(mine, share), :]
    kept[place * high + share : (place + 1) * high, :] = padded(stats, pull.shape[0])
    terms = split_stats(stats)
    for s in range(count) if whole else range(1, count):
        out, start = sent[0].at[s] if whole else sent[s - 1], s * share
        if not whole:
            start = pl.multiple_of((info[1] ^ s) * share, share)
        out[place * tall : place * tall + share, :] = bare(flipped[pl.ds(start, share), :])
        out[place * tall + share : (place + 1) * tall, :] = terms


def whole(value):
    return pl.BlockSpec(value.shape, lambda *_: (0,) * len(value.shape))


def call(kernel, name, info, grid, ins, in_specs, outs, out_specs, scratch, flops, exps):
    values = pl.pallas_call(
        kernel,
        grid_spec=pltpu.PrefetchScalarGridSpec(
            num_scalar_prefetch=1,
            grid=grid,
            in_specs=in_specs,
            out_specs=out_specs,
            scratch_shapes=scratch,
        ),
        out_shape=outs,
        compiler_params=pltpu.CompilerParams(
            vmem_limit_bytes=kernel_bytes if exps else kernel_bytes // 2
        ),
        cost_estimate=pl.CostEstimate(flops=flops, bytes_accessed=flops // 128, transcendentals=exps),
        name=name,
    )(info, *ins)
    info, first = lax.optimization_barrier((info, values[0]))
    return info, first, *values[1:]


def placed_rows(info, quarters, block):
    part = quarters[0].shape[1]
    for s, quarter in enumerate(quarters):
        place = pl.multiple_of((info[1] ^ s) * part, part)
        block[pl.ds(place, part), :] = quarter[0]


def over_chunks(protos, width, step, unrolled=False):
    count = protos[0].shape[0] // width
    if unrolled:
        for i in range(count):
            for half, part in enumerate(protos):
                step(half * count + i, part[i * width : (i + 1) * width, :])
        return

    def both(i, carry):
        at = pl.ds(pl.multiple_of(i * width, width), width)
        for half, part in enumerate(protos):
            step(half * count + i, part[at, :])
        return carry

    lax.fori_loop(0, count, both, 0)


def stats_kernel(fresh, info, *refs):
    if fresh:
        block, *protos, stats = refs
    else:
        *codes, near, across, before, stats, block = refs
        protos = near, across
        placed_rows(info, codes, block)

    @pl.when(pl.program_id(0) == 0)
    def _():
        if fresh:
            stats[:, 0:1, :] = jnp.full((stats.shape[0], 1, stats.shape[2]), low, jnp.float32)
            stats[:, 1:, :] = jnp.zeros((stats.shape[0], stat_rows - 1, stats.shape[2]), jnp.float32)
        else:
            stats[...] = before[...]

    def step(j, protos):
        raw = scores(block[...], protos)
        old, total = stats[j, 0:1, :], stats[j, 1:2, :]
        new = jnp.maximum(old, jnp.max(raw, axis=0, keepdims=True))
        value = jnp.exp2((raw - new) * code_scale)
        stats[j, 1:2, :] = total * jnp.exp2((old - new) * code_scale) + jnp.sum(
            value, axis=0, keepdims=True
        )
        stats[j, 0:1, :] = new

    over_chunks(protos, stats.shape[2], step, True)


def stats_part(info, codes, protos, before, rows):
    count, dim = protos[0].shape
    width = min(chunk, count)
    fresh = before is None
    ins = [*codes, *protos]
    if fresh:
        blocks, scratch = 1, []
        specs = [whole(value) for value in ins]
    else:
        blocks, scratch = codes[0].shape[0], [pltpu.VMEM((rows, dim), jnp.bfloat16)]
        ins = [*ins, before]
        specs = [pl.BlockSpec((1, *part.shape[1:]), lambda i, info: (i, 0, 0)) for part in codes]
        specs += [whole(value) for value in ins[-3:]]
    out = jax.ShapeDtypeStruct((2 * count // width, stat_rows, width), jnp.float32)
    return call(
        functools.partial(stats_kernel, fresh), "stats_part", info, (blocks,), ins, specs, [out],
        [whole(out)], scratch, 4 * blocks * rows * count * dim, 2 * blocks * rows * count,
    )


def weighted(value, protos):
    return jnp.dot(bare(value), protos, preferred_element_type=jnp.float32)


def row_of(combine, value):
    return combine(value.T, axis=0, keepdims=True)


def pred_logits(preds, protos, raws, top, j):
    raw = scores(preds[...], protos)
    raws[j] = raw
    top[...] = jnp.maximum(top[...], lane_fold(jnp.maximum, raw))


def pred_pull(protos, raws, top, total, pull):
    width = raws.shape[2]
    stats = [row_of(jnp.max, top[...]) * pred_scale]
    peak = jnp.max(top[...], axis=1, keepdims=True)
    top[...] = jnp.broadcast_to(peak, top.shape)
    total[...] = jnp.zeros(total.shape, jnp.float32)
    pull[...] = jnp.zeros(pull.shape, jnp.float32)

    def step(j, protos):
        peak = jnp.concatenate([top[...]] * (width // 128), axis=1)
        value = jnp.exp2((raws[j] - peak) * pred_scale)
        total[...] += lane_fold(jnp.add, value)
        pull[...] += weighted(value, protos)

    over_chunks(protos, width, step)
    return pull[...], [*stats, row_of(jnp.sum, total[...])]


def target_step(codes, protos, stats, other, total, pull, j):
    count = stats.shape[0] // 2
    here, there = stats[j], other[(j + count) % (2 * count)]
    peak = jnp.maximum(here[0:1], there[0:1])
    mass = here[1:2] * jnp.exp2((here[0:1] - peak) * code_scale) + there[1:2] * jnp.exp2(
        (there[0:1] - peak) * code_scale
    )
    offset = peak * code_scale + jnp.log2(mass)
    value = jnp.exp2(scores(codes[...], protos) * code_scale - offset)
    total[...] += lane_fold(jnp.add, value)
    pull[...] += weighted(value, protos)


def target_stats(preds, total, pull):
    cross = lane_fold(jnp.add, pull[...] * preds[...].astype(jnp.float32))
    return [row_of(jnp.sum, total[...]), row_of(jnp.sum, cross)]


def pred_kernel(info, preds, near, across, *refs):
    *outs, raws, top, total, pull, flipped = refs
    protos = near, across
    top[...] = jnp.full(top.shape, low, jnp.float32)
    over_chunks(protos, raws.shape[2], lambda j, part: pred_logits(preds, part, raws, top, j))
    send(info, 0, *pred_pull(protos, raws, top, total, pull), *outs, flipped)


def target_kernel(info, codes, preds, near, across, stats, other, *refs):
    *refs, total, pull, flipped = refs
    earlier, outs = refs[: len(refs) // 2], refs[len(refs) // 2 :]
    total[...] = jnp.zeros(total.shape, jnp.float32)
    pull[...] = jnp.zeros(pull.shape, jnp.float32)
    over_chunks(
        (near, across),
        stats.shape[2],
        lambda j, part: target_step(codes, part, stats, other, total, pull, j),
        True,
    )
    send(info, 0, pull[...], target_stats(preds, total, pull), *outs, flipped)
    for part, out in zip(earlier, outs):
        out[part.shape[0] :, :] = part[...]


def both_kernel(info, *refs):
    *quarters, preds, near, across, stats, other, kept, sent = refs[:-6]
    raws, top, total, pull, flipped, codes = refs[-6:]
    protos = near, across
    placed_rows(info, quarters, codes)
    top[...] = jnp.full(top.shape, low, jnp.float32)
    total[...] = jnp.zeros(total.shape, jnp.float32)
    pull[...] = jnp.zeros(pull.shape, jnp.float32)

    def step(j, part):
        pred_logits(preds, part, raws, top, j)
        target_step(codes, part, stats, other, total, pull, j)

    over_chunks(protos, stats.shape[2], step)
    send(info, 0, pull[...], target_stats(preds, total, pull), kept, sent, flipped)
    send(info, 1, *pred_pull(protos, raws, top, total, pull), kept, sent, flipped)


def rows_part(info, codes, preds, protos, stats, other, rows, proto_count, aways, earlier):
    count, dim = protos[0].shape
    share = dim // proto_count
    width, blocks = min(chunk, count), max(len(aways), 1)
    shapes = [(2 * count // width, rows, width), (rows, 128), (rows, 128), (rows, dim), (dim, rows)]
    scratch = [pltpu.VMEM(shape, jnp.float32) for shape in shapes]
    away = lambda i: aways[0] + i * (aways[1] - aways[0] if len(aways) > 1 else 0)
    if codes is None:
        kernel, ins = pred_kernel, [preds, *protos]
        specs = [whole(value) for value in ins]
    elif not aways:
        kernel, ins = target_kernel, [codes, preds, *protos, stats, other, *earlier]
        specs, scratch = [whole(value) for value in ins], scratch[2:]
    else:
        kernel, ins = both_kernel, [*codes, preds, *protos, stats, other]
        quarter = pl.BlockSpec((1, *codes[0].shape[1:]), lambda i, info: (away(i) - 1, 0, 0))
        block = pl.BlockSpec((rows, dim), lambda i, info: (info[0] ^ away(i), 0))
        specs = [quarter] * len(codes) + [block] + [whole(value) for value in ins[-4:]]
        scratch = [*scratch, pltpu.VMEM((rows, dim), jnp.bfloat16)]
    parts, work = 2 if codes is not None else 1, 2 if aways else 1
    high, tall = parts * (share + stat_rows), parts * (share + sent_rows)
    outs = [jax.ShapeDtypeStruct((high, blocks * rows), jnp.float32)]
    out_specs = [pl.BlockSpec((high, rows), lambda i, info: (0, i))]
    if aways:
        outs.append(jax.ShapeDtypeStruct((proto_count, tall, blocks * rows), jnp.bfloat16))
        out_specs.append(pl.BlockSpec((proto_count, tall, rows), lambda i, info: (0, 0, i)))
    else:
        outs += [jax.ShapeDtypeStruct((tall, rows), jnp.bfloat16)] * (proto_count - 1)
        out_specs += [whole(out) for out in outs[1:]]
    return call(
        kernel, "rows_part", info, (blocks,), ins, specs, outs, out_specs, scratch,
        blocks * work * 8 * rows * count * dim, blocks * work * 2 * rows * count,
    )


def chosen(here, kept, other):
    pull, stats = kept
    far_pull, far_stats = other
    return jnp.where(here, pull, far_pull), [
        jnp.where(here, mine, theirs) for mine, theirs in zip(stats, far_stats)
    ]


names = ["target", "pred"]


def packed_far(target, pred):
    pull, stats = pred
    high = bare(pull)
    rest = bare(pull - high.astype(jnp.float32))
    return jnp.concatenate([bare(target[0]), high, rest, split_stats([*target[1], *stats])], axis=0)


def parted_far(value):
    share = (value.shape[0] - sent_rows) // 3
    target, high, rest = [
        value[i * share : (i + 1) * share, :].astype(jnp.float32) for i in range(3)
    ]
    stats = join_stats(value[3 * share :, :], 4)
    return {"target": (target, stats[:2]), "pred": (high + rest, stats[2:])}


def spread_kernel(info, kept, arrived, *outs):
    high, tall = kept.shape[0] // len(names), arrived.shape[1] // len(names)
    rows = outs[0].shape[1]
    for block, out in enumerate(outs):
        at = slice(block * rows, (block + 1) * rows)
        results = []
        for i, name in enumerate(names):
            mine = parted(kept[i * high : (i + 1) * high, at])
            parts = [
                chosen(info[1] == s, mine, parted_sent(arrived[s, i * tall : (i + 1) * tall, at]))
                for s in range(arrived.shape[0])
            ]
            results.append(joins[name](parts))
        out[...] = packed_far(*results)


def join_spread(info, kept, arrived, rows):
    share = kept.shape[0] // len(names) - stat_rows
    outs = [
        jax.ShapeDtypeStruct((3 * share + sent_rows, rows), jnp.bfloat16)
        for _ in range(kept.shape[1] // rows)
    ]
    return call(
        spread_kernel, "join_spread", info, (1,), [kept, arrived], [whole(kept), whole(arrived)],
        outs, [whole(out) for out in outs], [], 1 << 20, 0,
    )


def final_kernel(count, info, *refs):
    kept, sent, (loss, pull) = refs[0], refs[1:count], refs[-2:]
    far = [parted_far(part[...]) for part in refs[count:-2]]
    high, tall = kept.shape[0] // len(names), sent[0].shape[0] // len(names)
    target, pred = [
        joins[name](
            [parted(kept[i * high : (i + 1) * high, :])]
            + [parted_sent(part[i * tall : (i + 1) * tall, :]) for part in sent]
            + [part[name] for part in far]
        )
        for i, name in enumerate(names)
    ]
    (target, (mass, cross)), (pred, (peak, total)) = target, pred
    pull[...] = target / mass - pred / total
    loss[...] = peak * log2 + jnp.log(total) - cross / mass / pred_temp


def finish(info, own, others):
    high, length = own[0].shape
    outs = [
        jax.ShapeDtypeStruct((1, length), jnp.float32),
        jax.ShapeDtypeStruct((high // len(names) - stat_rows, length), jnp.float32),
    ]
    ins = [*own, *others]
    return call(
        functools.partial(final_kernel, len(own)), "finish", info, (1,), ins,
        [whole(value) for value in ins], outs, [whole(out) for out in outs], [], 1 << 20, 0,
    )[1:]


def swap(value, axis, bits):
    count = lax.axis_size(axis)
    return lax.ppermute(value, axis, [(i, i ^ bits) for i in range(count)])


def body(codes_view, pred_view, prototypes):
    rows = codes_view.shape[0]
    dp_count, proto_count = lax.axis_size("dp"), lax.axis_size("proto")
    z_count = dp_count // 2
    me, proto = lax.axis_index("dp"), lax.axis_index("proto")
    info = jnp.stack([me // 2, proto]).astype(jnp.int32)
    same_core = [[2 * z + core for z in range(z_count)] for core in range(2)]

    def rows_of(info, codes, preds, aways, earlier):
        return rows_part(
            info, codes, preds, protos, stats, other, rows, proto_count, aways, earlier
        )

    def far_rows(info, aways):
        info, kept, out = rows_of(info, codes, preds, aways, None)
        return info, kept, lax.all_to_all(out, "proto", 0, 0)

    protos = prototypes, swap(prototypes, "dp", 1)
    part = rows // proto_count
    piece = lax.dynamic_slice_in_dim(codes_view, proto * part, part, 0)
    quarters = [swap(piece, "dp", 2 * t) for t in range(1, z_count)]
    preds = lax.all_gather(pred_view, "dp", axis=0, tiled=True, axis_index_groups=same_core)

    stats = other = None
    info, stats = stats_part(info, [codes_view], protos, None, rows)
    quarters, info = lax.optimization_barrier((quarters, info))
    quarters = jnp.stack(quarters)
    codes = [quarters] + [swap(quarters, "proto", s) for s in range(1, proto_count)]
    info, *earlier = rows_of(info, None, pred_view, (), None)
    info, stats = stats_part(info, codes, protos, stats, rows)
    other = swap(stats, "dp", 1)

    aways = range(z_count - 1, 1, -1)
    info, far_kept, far_arrived = far_rows(info, aways)
    info, next_kept, next_arrived = far_rows(info, (1,))
    info, *far = join_spread(info, far_kept, far_arrived, rows)
    far = [swap(part, "dp", 2 * away) for away, part in zip(aways, far)]
    info, kept, *out = rows_of(info, codes_view, pred_view, (), earlier)
    own = [kept] + [swap(value, "proto", s) for s, value in enumerate(out, 1)]
    far[:1], next_arrived = lax.optimization_barrier((far[:1], next_arrived))
    info, part = join_spread(info, next_kept, next_arrived, rows)
    loss, pull = finish(info, own, [*far, swap(part, "dp", 2)])
    return (loss.reshape(rows), pull.T)


def solution(mesh):
    placed = (P("dp", None), P("dp", None), P(("proto", "dp"), None))
    return jax.shard_map(
        body, mesh=mesh, in_specs=placed, out_specs=(P("dp"), P("dp", "proto")), check_vma=False
    )
```

time: 559 us -> 124 us (0.22)
  matrix products: 269 us -> 0 us
  waiting for transfers between devices: 207 us -> 14.3 us
  Pallas kernels: 0 us -> 48.9 us
  starting transfers between devices: 0.16 us -> 34.2 us
  blocking collectives: 32.1 us -> 0 us
  other arithmetic: 17.1 us -> 0.1 us
    dot_general x192 -> x0, matrix products: 269 us -> none  [the longest x160 219 us: scores(): lax.dot_general(embeds, protos, (((1,), (1,)), ((), ())), preferred_eleme...]
    all_gather x1, waiting for transfers between devices: 86.4 us -> 0.01 us  [body(): lax.all_gather(pred_view, 'dp', axis=0, tiled=True, axis_index_groups=sam...]
    psum x1 -> x0, waiting for transfers between devices: 54 us -> none  [body(): col_total = lax.psum(local_total * jnp.exp(local_peak - col_peak), 'dp')]
    pmax x1 -> x0, waiting for transfers between devices: 52.3 us -> none  [body(): col_peak = lax.pmax(local_peak, 'dp')]
    pallas_call x0 -> x9, Pallas kernels: none -> 48.9 us  [call(): pl.pallas_call(kernel, grid_spec=pltpu.PrefetchScalarGridSpec(num_scalar_...]
    ppermute x0 -> x14, starting transfers between devices: none -> 26.7 us  [swap(): return lax.ppermute(value, axis, [(i, i ^ bits) for i in range(count)])]
    all_gather x3 -> x0, blocking collectives: 23.2 us -> none  [joined(): gathered = jax.tree.map(lambda a: lax.all_gather(a, axis), part)]
    reduce_scatter x1 -> x0, waiting for transfers between devices: 13.2 us -> none  [body(): pull_part = lax.psum_scatter(pull, 'proto', scatter_dimension=1, tiled=True)]
  transfers between devices with their start and end apart: 4 -> 17, of which waited for: 4 -> 9; matrix products, arithmetic and copies ran while one was open for 0% -> 1% of each run, Pallas kernels for 0% -> 25%
where the time goes in v1:
time: 124 us; the launch traced here: 123 us
  Pallas kernels  48.9 us (39%)
  starting transfers between devices  34.2 us (28%)
  waiting for transfers between devices  14.3 us (12%)
  between operations  14.3 us (12%)
  local copies, waits for them, and re-layouts  11.4 us (9%)
    pallas_call x9, Pallas kernels, call(): pl.pallas_call(kernel, grid_spec=pltpu.PrefetchScalarGridSpec(num_scalar_...  48.9 us
    ppermute x14, starting transfers between devices, swap(): return lax.ppermute(value, axis, [(i, i ^ bits) for i in range(count)])  26.7 us
    ppermute x14, waiting for transfers between devices, swap(): return lax.ppermute(value, axis, [(i, i ^ bits) for i in range(count)])  10.7 us
    unnamed x56, local copies, waits for them, and re-layouts  10.6 us
    all_to_all x2, starting transfers between devices, far_rows(): return (info, kept, lax.all_to_all(out, 'proto', 0, 0))  7.46 us
    all_to_all x2, waiting for transfers between devices, far_rows(): return (info, kept, lax.all_to_all(out, 'proto', 0, 0))  3.47 us
  transfers between devices with their start and end apart: 17, of which 9 were waited for; matrix products, arithmetic and copies ran while one was open for 1% of the time, Pallas kernels for 25%

profile of v1, /device:TPU:0, one launch (start us, length us, event | category | flops | bytes accessed | tf_op | source)
XLA Modules:
  0.0 123.2 jit_solution(9554657808884145937)
XLA Ops:
  7.2 0.0 all-gather.2.cloned.1.call-start
  7.2 0.5 collective-permute-start.3
  7.7 0.2 all-gather.2.cloned.1.call-update
  7.9 0.8 constant_dynamic-slice_fusion
  8.8 5.0 %collective-permute-start.2 = (bf16[128,256]{1,0:T(8,128)(2,1)S(1)}, bf16[128,256]{1,0:T(8,128)(2,1)S(1)}, u32[]{:S(2)}, u32[]{:S(2)}) collective-permute-start(bf16[128,256]{1,0:T(8,128)(2,1)S(1)} %constant_dynamic-slice_fusion), channel_id=1, source_target_pairs={{0,24},{4,28},{8,16},{12,20},{16,8},{20,12},{24,0},{28,4},{1,25},{... | collective-permute-start | bytes 196616 | tf_op jit(solution)/shard_map/ppermute | solution.py:425
  13.8 0.6 collective-permute-start
  14.4 0.1 pad_add_fusion.info
  14.5 1.0 copy-done.1
  15.4 1.2 copy-done.3
  16.7 3.3 %stats_part.2.refs_6_ = f32[8,8,512]{2,1,0:T(8,128)S(1)} custom-call(s32[2]{0:T(128)S(1)} %pad_add_fusion.info, bf16[512,256]{1,0:T(8,128)(2,1)S(1)} %copy-done.1, bf16[2048,256]{1,0:T(8,128)(2,1)S(1)} %copy-done.3, bf16[2048,256]{1,0:T(8,128)(2,1)S(1)} %collective-permute-done.3.refs_2_.across.refs_5_.refs_6_), custom_call_target="tpu_custom_call" | custom-call | flops 1073741824 | bytes 8388608 | tf_op jit(solution)/shard_map/stats_part/pallas_call | solution.py:118
  20.1 2.7 %collective-permute-start.6 = (bf16[3,128,256]{2,1,0:T(8,128)(2,1)S(1)}, bf16[3,128,256]{2,1,0:T(8,128)(2,1)S(1)}, u32[]{:S(2)}, u32[]{:S(2)}) collective-permute-start(bf16[3,128,256]{2,1,0:T(8,128)(2,1)S(1)} %pad_maximum_fusion.refs_0_), channel_id=1, source_target_pairs={{0,3},{1,2},{2,1},{3,0},{4,7},{5,6},{6,5},{7,4},{8,11},{9,10},{10,... | collective-permute-start | bytes 589832 | tf_op jit(solution)/shard_map/ppermute | solution.py:425
  22.8 0.5 collective-permute-start.5
  23.3 0.3 collective-permute-start.4
  23.6 4.9 %rows_part.4 = (f32[72,512]{1,0:T(8,128)S(1)}, bf16[80,512]{1,0:T(8,128)(2,1)S(1)}, bf16[80,512]{1,0:T(8,128)(2,1)S(1)}, bf16[80,512]{1,0:T(8,128)(2,1)S(1)}) custom-call(s32[2]{0:T(128)S(1)} %pad_add_fusion.info, bf16[512,256]{1,0:T(8,128)(2,1)S(1)} %copy-done, bf16[2048,256]{1,0:T(8,128)(2,1)S(1)} %copy-done.4, ...), custom_call_target="tpu_custom_call" | custom-call | flops 2147483648 | bytes 16777216 | tf_op jit(solution)/shard_map/rows_part/pallas_call | solution.py:118
  28.6 0.3 collective-permute-done.6.refs_3_
  28.9 2.5 %collective-permute-done.5.refs_2_ = bf16[3,128,256]{2,1,0:T(8,128)(2,1)S(1)} collective-permute-done((bf16[3,128,256]{2,1,0:T(8,128)(2,1)S(1)}, bf16[3,128,256]{2,1,0:T(8,128)(2,1)S(1)}, u32[]{:S(2)}, u32[]{:S(2)}) %collective-permute-start.5) | collective-permute-done | bytes 196640 | tf_op jit(solution)/shard_map/ppermute | solution.py:425
  31.4 0.1 collective-permute-done.4.refs_1_
  31.5 8.6 %stats_part.3.refs_7_.stats = f32[8,8,512]{2,1,0:T(8,128)S(1)} custom-call(s32[2]{0:T(128)S(1)} %pad_add_fusion.info, bf16[3,128,256]{2,1,0:T(8,128)(2,1)S(1)} %pad_maximum_fusion.refs_0_, bf16[3,128,256]{2,1,0:T(8,128)(2,1)S(1)} %collective-permute-done.4.refs_1_, bf16[3,128,256]{2,1,0:T(8,128)(2,1)S(1)} %collective-permute-done.5.refs_2_, ...), custom_call_target="tpu_custom_call" | custom-call | flops 3221225472 | bytes 25165824 | tf_op jit(solution)/shard_map/stats_part/pallas_call | solution.py:118
  40.2 0.1 collective-permute-start.7
  40.3 1.3 %collective-permute-done.7.refs_8_.other = f32[8,8,512]{2,1,0:T(8,128)S(1)} collective-permute-done((f32[8,8,512]{2,1,0:T(8,128)S(1)}, f32[8,8,512]{2,1,0:T(8,128)S(1)}, u32[]{:S(2)}, u32[]{:S(2)}) %collective-permute-start.7) | collective-permute-done | bytes 131104 | tf_op jit(solution)/shard_map/ppermute | solution.py:425
  41.7 1.3 %copy-done.8 = bf16[2048,256]{1,0:T(8,128)(2,1)S(1)} copy-done((bf16[2048,256]{1,0:T(8,128)(2,1)S(1)}, bf16[2048,256]{1,0:T(8,128)(2,1)}, u32[]{:S(2)}) %copy-start.8) | copy-done | bytes 1048600
  42.9 1.2 copy-done.11
  44.1 16.2 %rows_part.5 = (f32[144,1024]{1,0:T(8,128)S(1)}, bf16[4,160,1024]{2,1,0:T(8,128)(2,1)}) custom-call(s32[2]{0:T(128)S(1)} %pad_add_fusion.info, bf16[3,128,256]{2,1,0:T(8,128)(2,1)S(1)} %pad_maximum_fusion.refs_0_, bf16[3,128,256]{2,1,0:T(8,128)(2,1)S(1)} %collective-permute-done.4.refs_1_, bf16[3,128,256]{2,1,0:T(8,128)(2,1)S(1)} %collective-permute-done.5.refs_2_, ...), custom_call_target="tpu_custom_call" | custom-call | flops 8589934592 | bytes 67108864 | tf_op jit(solution)/shard_map/rows_part/pallas_call | solution.py:118
  60.4 3.9 %all-to-all-start = ((bf16[4,160,1024]{2,1,0:T(8,128)(2,1)}), bf16[4,160,1024]{2,1,0:T(8,128)(2,1)S(1)}, u32[]{:S(2)}, u32[]{:S(2)}) async-start(bf16[4,160,1024]{2,1,0:T(8,128)(2,1)} %get-tuple-element.56), calls=%async_computation | async-start | bytes 2621440 | tf_op jit(solution)/shard_map/all_to_all | solution.py:443
  64.2 0.0 copy-start.5
  64.3 1.2 copy-done.5
  65.5 1.2 copy-done.9
  66.7 1.2 copy-done.12
  67.9 0.9 copy-done.18
  68.8 8.7 %rows_part.6 = (f32[144,512]{1,0:T(8,128)S(1)}, bf16[4,160,512]{2,1,0:T(8,128)(2,1)}) custom-call(s32[2]{0:T(128)S(1)} %pad_add_fusion.info, bf16[3,128,256]{2,1,0:T(8,128)(2,1)S(1)} %pad_maximum_fusion.refs_0_, bf16[3,128,256]{2,1,0:T(8,128)(2,1)S(1)} %copy-done.16, bf16[3,128,256]{2,1,0:T(8,128)(2,1)S(1)} %copy-done.14, ...), custom_call_target="tpu_custom_call" | custom-call | flops 4294967296 | bytes 33554432 | tf_op jit(solution)/shard_map/rows_part/pallas_call | solution.py:118
  77.6 3.5 %all-to-all-done.arrived = bf16[4,160,1024]{2,1,0:T(8,128)(2,1)S(1)} async-done(((bf16[4,160,1024]{2,1,0:T(8,128)(2,1)}), bf16[4,160,1024]{2,1,0:T(8,128)(2,1)S(1)}, u32[]{:S(2)}, u32[]{:S(2)}) %all-to-all-start) | async-done | bytes 1310752 | tf_op jit(solution)/shard_map/all_to_all | solution.py:443
  81.0 3.6 %all-to-all-start.1 = ((bf16[4,160,512]{2,1,0:T(8,128)(2,1)}), bf16[4,160,512]{2,1,0:T(8,128)(2,1)S(1)}, u32[]{:S(2)}, u32[]{:S(2)}) async-start(bf16[4,160,512]{2,1,0:T(8,128)(2,1)} %get-tuple-element.67), calls=%async_computation.1 | async-start | bytes 1310720 | tf_op jit(solution)/shard_map/all_to_all | solution.py:443
  84.7 0.0 copy-start.19
  84.7 1.6 %join_spread.2 = (bf16[208,512]{1,0:T(8,128)(2,1)}, bf16[208,512]{1,0:T(8,128)(2,1)}) custom-call(s32[2]{0:T(128)S(1)} %pad_add_fusion.info, f32[144,1024]{1,0:T(8,128)S(1)} %get-tuple-element.55.kept, bf16[4,160,1024]{2,1,0:T(8,128)(2,1)S(1)} %all-to-all-done.arrived), custom_call_target="tpu_custom_call" | custom-call | flops 1048576 | bytes 8192 | tf_op jit(solution)/shard_map/join_spread/pallas_call | solution.py:118
  86.4 3.5 %collective-permute-start.8 = (bf16[208,512]{1,0:T(8,128)(2,1)}, bf16[208,512]{1,0:T(8,128)(2,1)S(1)}, u32[]{:S(2)}, u32[]{:S(2)}) collective-permute-start(bf16[208,512]{1,0:T(8,128)(2,1)} %get-tuple-element.66), channel_id=1, source_target_pairs={{0,24},{4,28},{8,16},{12,20},{16,8},{20,12},{24,0},{28,4},{1,25},{... | collective-permute-start | bytes 638984 | tf_op jit(solution)/shard_map/ppermute | solution.py:425
  90.0 1.2 copy-done.10
  91.2 3.2 %rows_part.7 = (f32[144,512]{1,0:T(8,128)S(1)}, bf16[160,512]{1,0:T(8,128)(2,1)S(1)}, bf16[160,512]{1,0:T(8,128)(2,1)S(1)}, bf16[160,512]{1,0:T(8,128)(2,1)S(1)}) custom-call(s32[2]{0:T(128)S(1)} %pad_add_fusion.info, bf16[512,256]{1,0:T(8,128)(2,1)S(1)} %copy-done.2, bf16[512,256]{1,0:T(8,128)(2,1)S(1)} %copy-done, bf16[2048,256]{1,0:T(8,128)(2,1)S(1)} %copy-done.6, ...), custom_call_target="tpu_custom_call" | custom-call | flops 2147483648 | bytes 16777216 | tf_op jit(solution)/shard_map/rows_part/pallas_call | solution.py:118
  94.4 0.1 collective-permute-start.12
  94.5 0.5 collective-permute-done.8.refs_4_
  95.0 0.8 join_spread.3
  95.7 9.8 %collective-permute-start.13 = (bf16[208,512]{1,0:T(8,128)(2,1)S(1)}, bf16[208,512]{1,0:T(8,128)(2,1)S(1)}, u32[]{:S(2)}, u32[]{:S(2)}) collective-permute-start(bf16[208,512]{1,0:T(8,128)(2,1)S(1)} %join_spread.3), channel_id=1, source_target_pairs={{0,8},{4,12},{8,0},{12,4},{16,24},{20,28},{24,16},{28,20},{1,9},{5... | collective-permute-start | bytes 638984 | tf_op jit(solution)/shard_map/ppermute | solution.py:425
  105.5 1.7 %collective-permute-start.9 = (bf16[160,512]{1,0:T(8,128)(2,1)S(1)}, bf16[160,512]{1,0:T(8,128)(2,1)S(1)}, u32[]{:S(2)}, u32[]{:S(2)}) collective-permute-start(bf16[160,512]{1,0:T(8,128)(2,1)S(1)} %get-tuple-element.71), channel_id=1, source_target_pairs={{0,1},{1,0},{2,3},{3,2},{4,5},{5,4},{6,7},{7,6},{8,9},{9,8},{10,11... | collective-permute-start | bytes 491528 | tf_op jit(solution)/shard_map/ppermute | solution.py:425
  107.2 1.5 %collective-permute-start.10 = (bf16[160,512]{1,0:T(8,128)(2,1)S(1)}, bf16[160,512]{1,0:T(8,128)(2,1)S(1)}, u32[]{:S(2)}, u32[]{:S(2)}) collective-permute-start(bf16[160,512]{1,0:T(8,128)(2,1)S(1)} %get-tuple-element.72), channel_id=1, source_target_pairs={{0,2},{1,3},{2,0},{3,1},{4,6},{5,7},{6,4},{7,5},{8,10},{9,11},{10,... | collective-permute-start | bytes 491528 | tf_op jit(solution)/shard_map/ppermute | solution.py:425
  108.7 0.3 collective-permute-start.11
  109.0 2.9 %collective-permute-done.9.refs_1_ = bf16[160,512]{1,0:T(8,128)(2,1)S(1)} collective-permute-done((bf16[160,512]{1,0:T(8,128)(2,1)S(1)}, bf16[160,512]{1,0:T(8,128)(2,1)S(1)}, u32[]{:S(2)}, u32[]{:S(2)}) %collective-permute-start.9) | collective-permute-done | bytes 163872 | tf_op jit(solution)/shard_map/ppermute | solution.py:425
  111.9 1.6 %collective-permute-done.10.refs_2_ = bf16[160,512]{1,0:T(8,128)(2,1)S(1)} collective-permute-done((bf16[160,512]{1,0:T(8,128)(2,1)S(1)}, bf16[160,512]{1,0:T(8,128)(2,1)S(1)}, u32[]{:S(2)}, u32[]{:S(2)}) %collective-permute-start.10) | collective-permute-done | bytes 163872 | tf_op jit(solution)/shard_map/ppermute | solution.py:425
  113.6 1.4 %collective-permute-done.11.refs_3_ = bf16[160,512]{1,0:T(8,128)(2,1)S(1)} collective-permute-done((bf16[160,512]{1,0:T(8,128)(2,1)S(1)}, bf16[160,512]{1,0:T(8,128)(2,1)S(1)}, u32[]{:S(2)}, u32[]{:S(2)}) %collective-permute-start.11) | collective-permute-done | bytes 163872 | tf_op jit(solution)/shard_map/ppermute | solution.py:425
  114.9 1.5 %finish.1 = (f32[1,512]{1,0:T(1,128)}, f32[64,512]{1,0:T(8,128)}) custom-call(s32[2]{0:T(128)S(1)} %pad_add_fusion.info, f32[144,512]{1,0:T(8,128)S(1)} %get-tuple-element.70.refs_0_, bf16[160,512]{1,0:T(8,128)(2,1)S(1)} %collective-permute-done.9.refs_1_, bf16[160,512]{1,0:T(8,128)(2,1)S(1)} %collective-permute-done.10.refs_2_, ...), custom_call_target="tpu_custom_call" | custom-call | flops 1048576 | bytes 8192 | tf_op jit(solution)/shard_map/finish/pallas_call | solution.py:118
  (55 shorter events, 0.1 us)
Async XLA Ops:
  7.2 34.5 %all-gather.2.cloned.1.call-start = ((), (), s32[]{:S(2)}) async-start(), calls=%async_computation.2 | async-start | bytes 1310720 | tf_op jit(solution)/shard_map/all_gather | solution.py:449
  7.2 7.2 %collective-permute-start.3 = (bf16[2048,256]{1,0:T(8,128)(2,1)}, bf16[2048,256]{1,0:T(8,128)(2,1)S(1)}, u32[]{:S(2)}, u32[]{:S(2)}) collective-permute-start(bf16[2048,256]{1,0:T(8,128)(2,1)} %near.3), channel_id=1, source_target_pairs={{0,4},{4,0},{8,12},{12,8},{16,20},{20,16},{24,28},{28,24},{1,5},{5... | collective-permute-start | bytes 3145736 | tf_op jit(solution)/shard_map/ppermute | solution.py:425
  8.8 11.3 %collective-permute-start.2 = (bf16[128,256]{1,0:T(8,128)(2,1)S(1)}, bf16[128,256]{1,0:T(8,128)(2,1)S(1)}, u32[]{:S(2)}, u32[]{:S(2)}) collective-permute-start(bf16[128,256]{1,0:T(8,128)(2,1)S(1)} %constant_dynamic-slice_fusion), channel_id=1, source_target_pairs={{0,24},{4,28},{8,16},{12,20},{16,8},{20,12},{24,0},{28,4},{1,25},{... | collective-permute-start | bytes 196616 | tf_op jit(solution)/shard_map/ppermute | solution.py:425
  13.8 6.2 %collective-permute-start.1 = (bf16[128,256]{1,0:T(8,128)(2,1)S(1)}, bf16[128,256]{1,0:T(8,128)(2,1)S(1)}, u32[]{:S(2)}, u32[]{:S(2)}) collective-permute-start(bf16[128,256]{1,0:T(8,128)(2,1)S(1)} %constant_dynamic-slice_fusion), channel_id=1, source_target_pairs={{0,16},{4,20},{8,24},{12,28},{16,0},{20,4},{24,8},{28,12},{1,17},{... | collective-permute-start | bytes 196616 | tf_op jit(solution)/shard_map/ppermute | solution.py:425
  13.8 6.2 %collective-permute-start = (bf16[128,256]{1,0:T(8,128)(2,1)S(1)}, bf16[128,256]{1,0:T(8,128)(2,1)S(1)}, u32[]{:S(2)}, u32[]{:S(2)}) collective-permute-start(bf16[128,256]{1,0:T(8,128)(2,1)S(1)} %constant_dynamic-slice_fusion), channel_id=1, source_target_pairs={{0,8},{4,12},{8,0},{12,4},{16,24},{20,28},{24,16},{28,20},{1,9},{5... | collective-permute-start | bytes 196616 | tf_op jit(solution)/shard_map/ppermute | solution.py:425
  14.4 9.2 %copy-start = (bf16[512,256]{1,0:T(8,128)(2,1)S(1)}, bf16[512,256]{1,0:T(8,128)(2,1)}, u32[]{:S(2)}) copy-start(bf16[512,256]{1,0:T(8,128)(2,1)} %preds.3) | copy-start | bytes 786436
  14.4 1.0 copy-start.1
  15.4 1.2 copy-start.3
  16.7 14.9 %copy-start.7 = (bf16[2048,256]{1,0:T(8,128)(2,1)}, bf16[2048,256]{1,0:T(8,128)(2,1)S(1)}, u32[]{:S(2)}) copy-start(bf16[2048,256]{1,0:T(8,128)(2,1)S(1)} %collective-permute-done.3.refs_2_.across.refs_5_.refs_6_) | copy-start | bytes 3145732
  16.7 7.0 %copy-start.4 = (bf16[2048,256]{1,0:T(8,128)(2,1)S(1)}, bf16[2048,256]{1,0:T(8,128)(2,1)}, u32[]{:S(2)}) copy-start(bf16[2048,256]{1,0:T(8,128)(2,1)} %near.3) | copy-start | bytes 3145732
  20.1 8.8 %collective-permute-start.6 = (bf16[3,128,256]{2,1,0:T(8,128)(2,1)S(1)}, bf16[3,128,256]{2,1,0:T(8,128)(2,1)S(1)}, u32[]{:S(2)}, u32[]{:S(2)}) collective-permute-start(bf16[3,128,256]{2,1,0:T(8,128)(2,1)S(1)} %pad_maximum_fusion.refs_0_), channel_id=1, source_target_pairs={{0,3},{1,2},{2,1},{3,0},{4,7},{5,6},{6,5},{7,4},{8,11},{9,10},{10,... | collective-permute-start | bytes 589832 | tf_op jit(solution)/shard_map/ppermute | solution.py:425
  22.8 8.6 %collective-permute-start.5 = (bf16[3,128,256]{2,1,0:T(8,128)(2,1)S(1)}, bf16[3,128,256]{2,1,0:T(8,128)(2,1)S(1)}, u32[]{:S(2)}, u32[]{:S(2)}) collective-permute-start(bf16[3,128,256]{2,1,0:T(8,128)(2,1)S(1)} %pad_maximum_fusion.refs_0_), channel_id=1, source_target_pairs={{0,2},{1,3},{2,0},{3,1},{4,6},{5,7},{6,4},{7,5},{8,10},{9,11},{10,... | collective-permute-start | bytes 589832 | tf_op jit(solution)/shard_map/ppermute | solution.py:425
  23.3 8.2 %collective-permute-start.4 = (bf16[3,128,256]{2,1,0:T(8,128)(2,1)S(1)}, bf16[3,128,256]{2,1,0:T(8,128)(2,1)S(1)}, u32[]{:S(2)}, u32[]{:S(2)}) collective-permute-start(bf16[3,128,256]{2,1,0:T(8,128)(2,1)S(1)} %pad_maximum_fusion.refs_0_), channel_id=1, source_target_pairs={{0,1},{1,0},{2,3},{3,2},{4,5},{5,4},{6,7},{7,6},{8,9},{9,8},{10,11... | collective-permute-start | bytes 589832 | tf_op jit(solution)/shard_map/ppermute | solution.py:425
  28.5 11.7 %copy-start.20 = (f32[72,512]{1,0:T(8,128)}, f32[72,512]{1,0:T(8,128)S(1)}, u32[]{:S(2)}) copy-start(f32[72,512]{1,0:T(8,128)S(1)} %get-tuple-element.59.refs_0_) | copy-start | bytes 442372
  28.5 11.7 %copy-start.22 = (bf16[80,512]{1,0:T(8,128)(2,1)}, bf16[80,512]{1,0:T(8,128)(2,1)S(1)}, u32[]{:S(2)}) copy-start(bf16[80,512]{1,0:T(8,128)(2,1)S(1)} %get-tuple-element.60.refs_1_) | copy-start | bytes 245764
  28.5 11.7 %copy-start.24 = (bf16[80,512]{1,0:T(8,128)(2,1)}, bf16[80,512]{1,0:T(8,128)(2,1)S(1)}, u32[]{:S(2)}) copy-start(bf16[80,512]{1,0:T(8,128)(2,1)S(1)} %get-tuple-element.61.refs_2_) | copy-start | bytes 245764
  28.6 11.7 %copy-start.26 = (bf16[80,512]{1,0:T(8,128)(2,1)}, bf16[80,512]{1,0:T(8,128)(2,1)S(1)}, u32[]{:S(2)}) copy-start(bf16[80,512]{1,0:T(8,128)(2,1)S(1)} %get-tuple-element.62.refs_3_) | copy-start | bytes 245764
  31.4 10.2 %copy-start.13 = (bf16[3,128,256]{2,1,0:T(8,128)(2,1)}, bf16[3,128,256]{2,1,0:T(8,128)(2,1)S(1)}, u32[]{:S(2)}) copy-start(bf16[3,128,256]{2,1,0:T(8,128)(2,1)S(1)} %collective-permute-done.5.refs_2_) | copy-start | bytes 589828
  31.5 10.1 %copy-start.15 = (bf16[3,128,256]{2,1,0:T(8,128)(2,1)}, bf16[3,128,256]{2,1,0:T(8,128)(2,1)S(1)}, u32[]{:S(2)}) copy-start(bf16[3,128,256]{2,1,0:T(8,128)(2,1)S(1)} %collective-permute-done.4.refs_1_) | copy-start | bytes 589828
  40.2 1.4 %collective-permute-start.7 = (f32[8,8,512]{2,1,0:T(8,128)S(1)}, f32[8,8,512]{2,1,0:T(8,128)S(1)}, u32[]{:S(2)}, u32[]{:S(2)}) collective-permute-start(f32[8,8,512]{2,1,0:T(8,128)S(1)} %stats_part.3.refs_7_.stats), channel_id=1, source_target_pairs={{0,4},{4,0},{8,12},{12,8},{16,20},{20,16},{24,28},{28,24},{1,5},{5... | collective-permute-start | bytes 393224 | tf_op jit(solution)/shard_map/ppermute | solution.py:425
  41.6 18.7 %copy-start.17 = (f32[8,8,512]{2,1,0:T(8,128)}, f32[8,8,512]{2,1,0:T(8,128)S(1)}, u32[]{:S(2)}) copy-start(f32[8,8,512]{2,1,0:T(8,128)S(1)} %collective-permute-done.7.refs_8_.other) | copy-start | bytes 393220
  41.6 1.3 %copy-start.8 = (bf16[2048,256]{1,0:T(8,128)(2,1)S(1)}, bf16[2048,256]{1,0:T(8,128)(2,1)}, u32[]{:S(2)}) copy-start(bf16[2048,256]{1,0:T(8,128)(2,1)} %copy-done.7) | copy-start | bytes 3145732
  42.9 1.2 copy-start.11
  60.4 3.9 %copy-start.14 = (bf16[3,128,256]{2,1,0:T(8,128)(2,1)S(1)}, bf16[3,128,256]{2,1,0:T(8,128)(2,1)}, u32[]{:S(2)}) copy-start(bf16[3,128,256]{2,1,0:T(8,128)(2,1)} %copy-done.13) | copy-start | bytes 589828
  60.4 3.9 %copy-start.16 = (bf16[3,128,256]{2,1,0:T(8,128)(2,1)S(1)}, bf16[3,128,256]{2,1,0:T(8,128)(2,1)}, u32[]{:S(2)}) copy-start(bf16[3,128,256]{2,1,0:T(8,128)(2,1)} %copy-done.15) | copy-start | bytes 589828
  60.4 20.7 %all-to-all-start = ((bf16[4,160,1024]{2,1,0:T(8,128)(2,1)}), bf16[4,160,1024]{2,1,0:T(8,128)(2,1)S(1)}, u32[]{:S(2)}, u32[]{:S(2)}) async-start(bf16[4,160,1024]{2,1,0:T(8,128)(2,1)} %get-tuple-element.56), calls=%async_computation | async-start | bytes 2621440 | tf_op jit(solution)/shard_map/all_to_all | solution.py:443
  64.2 1.2 copy-start.5
  65.5 1.2 copy-start.9
  66.7 1.2 copy-start.12
  67.9 0.9 copy-start.18
  81.0 8.9 %copy-start.2 = (bf16[512,256]{1,0:T(8,128)(2,1)S(1)}, bf16[512,256]{1,0:T(8,128)(2,1)}, u32[]{:S(2)}) copy-start(bf16[512,256]{1,0:T(8,128)(2,1)} %codes.1) | copy-start | bytes 786436
  81.0 13.4 %all-to-all-start.1 = ((bf16[4,160,512]{2,1,0:T(8,128)(2,1)}), bf16[4,160,512]{2,1,0:T(8,128)(2,1)S(1)}, u32[]{:S(2)}, u32[]{:S(2)}) async-start(bf16[4,160,512]{2,1,0:T(8,128)(2,1)} %get-tuple-element.67), calls=%async_computation.1 | async-start | bytes 1310720 | tf_op jit(solution)/shard_map/all_to_all | solution.py:443
  84.7 5.3 %copy-start.6 = (bf16[2048,256]{1,0:T(8,128)(2,1)S(1)}, bf16[2048,256]{1,0:T(8,128)(2,1)}, u32[]{:S(2)}) copy-start(bf16[2048,256]{1,0:T(8,128)(2,1)} %near.3) | copy-start | bytes 3145732
  84.7 5.2 %copy-start.19 = (f32[8,8,512]{2,1,0:T(8,128)S(1)}, f32[8,8,512]{2,1,0:T(8,128)}, u32[]{:S(2)}) copy-start(f32[8,8,512]{2,1,0:T(8,128)} %copy-done.17) | copy-start | bytes 393220
  84.7 5.2 %copy-start.21 = (f32[72,512]{1,0:T(8,128)S(1)}, f32[72,512]{1,0:T(8,128)}, u32[]{:S(2)}) copy-start(f32[72,512]{1,0:T(8,128)} %copy-done.20) | copy-start | bytes 442372
  84.7 5.2 %copy-start.23 = (bf16[80,512]{1,0:T(8,128)(2,1)S(1)}, bf16[80,512]{1,0:T(8,128)(2,1)}, u32[]{:S(2)}) copy-start(bf16[80,512]{1,0:T(8,128)(2,1)} %copy-done.22) | copy-start | bytes 245764
  84.7 5.2 %copy-start.25 = (bf16[80,512]{1,0:T(8,128)(2,1)S(1)}, bf16[80,512]{1,0:T(8,128)(2,1)}, u32[]{:S(2)}) copy-start(bf16[80,512]{1,0:T(8,128)(2,1)} %copy-done.24) | copy-start | bytes 245764
  84.7 5.2 %copy-start.27 = (bf16[80,512]{1,0:T(8,128)(2,1)S(1)}, bf16[80,512]{1,0:T(8,128)(2,1)}, u32[]{:S(2)}) copy-start(bf16[80,512]{1,0:T(8,128)(2,1)} %copy-done.26) | copy-start | bytes 245764
  86.4 8.6 %collective-permute-start.8 = (bf16[208,512]{1,0:T(8,128)(2,1)}, bf16[208,512]{1,0:T(8,128)(2,1)S(1)}, u32[]{:S(2)}, u32[]{:S(2)}) collective-permute-start(bf16[208,512]{1,0:T(8,128)(2,1)} %get-tuple-element.66), channel_id=1, source_target_pairs={{0,24},{4,28},{8,16},{12,20},{16,8},{20,12},{24,0},{28,4},{1,25},{... | collective-permute-start | bytes 638984 | tf_op jit(solution)/shard_map/ppermute | solution.py:425
  90.0 1.2 copy-start.10
  94.4 20.5 %collective-permute-start.12 = (bf16[208,512]{1,0:T(8,128)(2,1)}, bf16[208,512]{1,0:T(8,128)(2,1)S(1)}, u32[]{:S(2)}, u32[]{:S(2)}) collective-permute-start(bf16[208,512]{1,0:T(8,128)(2,1)} %get-tuple-element.75), channel_id=1, source_target_pairs={{0,16},{4,20},{8,24},{12,28},{16,0},{20,4},{24,8},{28,12},{1,17},{... | collective-permute-start | bytes 638984 | tf_op jit(solution)/shard_map/ppermute | solution.py:425
  95.7 19.2 %collective-permute-start.13 = (bf16[208,512]{1,0:T(8,128)(2,1)S(1)}, bf16[208,512]{1,0:T(8,128)(2,1)S(1)}, u32[]{:S(2)}, u32[]{:S(2)}) collective-permute-start(bf16[208,512]{1,0:T(8,128)(2,1)S(1)} %join_spread.3), channel_id=1, source_target_pairs={{0,8},{4,12},{8,0},{12,4},{16,24},{20,28},{24,16},{28,20},{1,9},{5... | collective-permute-start | bytes 638984 | tf_op jit(solution)/shard_map/ppermute | solution.py:425
  105.5 6.4 %collective-permute-start.9 = (bf16[160,512]{1,0:T(8,128)(2,1)S(1)}, bf16[160,512]{1,0:T(8,128)(2,1)S(1)}, u32[]{:S(2)}, u32[]{:S(2)}) collective-permute-start(bf16[160,512]{1,0:T(8,128)(2,1)S(1)} %get-tuple-element.71), channel_id=1, source_target_pairs={{0,1},{1,0},{2,3},{3,2},{4,5},{5,4},{6,7},{7,6},{8,9},{9,8},{10,11... | collective-permute-start | bytes 491528 | tf_op jit(solution)/shard_map/ppermute | solution.py:425
  107.2 6.3 %collective-permute-start.10 = (bf16[160,512]{1,0:T(8,128)(2,1)S(1)}, bf16[160,512]{1,0:T(8,128)(2,1)S(1)}, u32[]{:S(2)}, u32[]{:S(2)}) collective-permute-start(bf16[160,512]{1,0:T(8,128)(2,1)S(1)} %get-tuple-element.72), channel_id=1, source_target_pairs={{0,2},{1,3},{2,0},{3,1},{4,6},{5,7},{6,4},{7,5},{8,10},{9,11},{10,... | collective-permute-start | bytes 491528 | tf_op jit(solution)/shard_map/ppermute | solution.py:425
  108.7 6.2 %collective-permute-start.11 = (bf16[160,512]{1,0:T(8,128)(2,1)S(1)}, bf16[160,512]{1,0:T(8,128)(2,1)S(1)}, u32[]{:S(2)}, u32[]{:S(2)}) collective-permute-start(bf16[160,512]{1,0:T(8,128)(2,1)S(1)} %get-tuple-element.73), channel_id=1, source_target_pairs={{0,3},{1,2},{2,1},{3,0},{4,7},{5,6},{6,5},{7,4},{8,11},{9,10},{10,... | collective-permute-start | bytes 491528 | tf_op jit(solution)/shard_map/ppermute | solution.py:425
Sparse Core Ops, SparseCore 0:
  9.6 30.6 all-gather.1

commit v2 on v1

--- a/solution.py
+++ b/solution.py
@@ -17,7 +17,7 @@
 sent_rows = 16
 low = -1e30
 chunk = 512
-kernel_bytes = 24 * 1024 * 1024
+mebi = 1024 * 1024
 
 
 def scores(embeds, protos):
@@ -114,7 +114,7 @@
     return pl.BlockSpec(value.shape, lambda *_: (0,) * len(value.shape))
 
 
-def call(kernel, name, info, grid, ins, in_specs, outs, out_specs, scratch, flops, exps):
+def call(kernel, name, info, grid, ins, in_specs, outs, out_specs, scratch, flops, exps, room):
     values = pl.pallas_call(
         kernel,
         grid_spec=pltpu.PrefetchScalarGridSpec(
@@ -125,9 +125,7 @@
             scratch_shapes=scratch,
         ),
         out_shape=outs,
-        compiler_params=pltpu.CompilerParams(
-            vmem_limit_bytes=kernel_bytes if exps else kernel_bytes // 2
-        ),
+        compiler_params=pltpu.CompilerParams(vmem_limit_bytes=room * mebi),
         cost_estimate=pl.CostEstimate(flops=flops, bytes_accessed=flops // 128, transcendentals=exps),
         name=name,
     )(info, *ins)
@@ -204,7 +202,7 @@
     out = jax.ShapeDtypeStruct((2 * count // width, stat_rows, width), jnp.float32)
     return call(
         functools.partial(stats_kernel, fresh), "stats_part", info, (blocks,), ins, specs, [out],
-        [whole(out)], scratch, 4 * blocks * rows * count * dim, 2 * blocks * rows * count,
+        [whole(out)], scratch, 4 * blocks * rows * count * dim, 2 * blocks * rows * count, 6,
     )
 
 
@@ -332,6 +330,7 @@
     return call(
         kernel, "rows_part", info, (blocks,), ins, specs, outs, out_specs, scratch,
         blocks * work * 8 * rows * count * dim, blocks * work * 2 * rows * count,
+        6 if kernel is target_kernel else 14,
     )
 
 
@@ -386,7 +385,7 @@
     ]
     return call(
         spread_kernel, "join_spread", info, (1,), [kept, arrived], [whole(kept), whole(arrived)],
-        outs, [whole(out) for out in outs], [], 1 << 20, 0,
+        outs, [whole(out) for out in outs], [], 1 << 20, 0, 5,
     )
 
 
@@ -416,7 +415,7 @@
     ins = [*own, *others]
     return call(
         functools.partial(final_kernel, len(own)), "finish", info, (1,), ins,
-        [whole(value) for value in ins], outs, [whole(out) for out in outs], [], 1 << 20, 0,
+        [whole(value) for value in ins], outs, [whole(out) for out in outs], [], 1 << 20, 0, 5,
     )[1:]
 
 
@@ -466,6 +465,7 @@
     own = [kept] + [swap(value, "proto", s) for s, value in enumerate(out, 1)]
     far[:1], next_arrived = lax.optimization_barrier((far[:1], next_arrived))
     info, part = join_spread(info, next_kept, next_arrived, rows)
+    own, part = lax.optimization_barrier((own, part))
     loss, pull = finish(info, own, [*far, swap(part, "dp", 2)])
     return (loss.reshape(rows), pull.T)
 

time: 124 us -> 121 us (0.976)
  starting transfers between devices: 34.2 us -> 24.4 us
  waiting for transfers between devices: 14.3 us -> 21.6 us
    ppermute x14, starting transfers between devices: 26.7 us -> 16.9 us  [swap(): return lax.ppermute(value, axis, [(i, i ^ bits) for i in range(count)])]
    ppermute x14, waiting for transfers between devices: 10.7 us -> 17.9 us  [swap(): return lax.ppermute(value, axis, [(i, i ^ bits) for i in range(count)])]
    unnamed x56 -> x60, local copies, waits for them, and re-layouts: 10.6 us -> 10.6 us
  transfers between devices with their start and end apart: 17 -> 17, of which waited for: 9 -> 9; matrix products, arithmetic and copies ran while one was open for 1% -> 1% of each run, Pallas kernels for 25% -> 26%
where the time goes in v2:
time: 121 us
  Pallas kernels  48.9 us (40%)
  starting transfers between devices  24.4 us (20%)
  waiting for transfers between devices  21.6 us (18%)
  between operations  14.4 us (12%)
  local copies, waits for them, and re-layouts  11.4 us (9%)
    pallas_call x9, Pallas kernels, call(): pl.pallas_call(kernel, grid_spec=pltpu.PrefetchScalarGridSpec(num_scalar_...  48.9 us
    ppermute x14, waiting for transfers between devices, swap(): return lax.ppermute(value, axis, [(i, i ^ bits) for i in range(count)])  17.9 us
    ppermute x14, starting transfers between devices, swap(): return lax.ppermute(value, axis, [(i, i ^ bits) for i in range(count)])  16.9 us
    unnamed x60, local copies, waits for them, and re-layouts  10.6 us
    all_to_all x2, starting transfers between devices, far_rows(): return (info, kept, lax.all_to_all(out, 'proto', 0, 0))  7.46 us
    all_to_all x2, waiting for transfers between devices, far_rows(): return (info, kept, lax.all_to_all(out, 'proto', 0, 0))  3.47 us
  transfers between devices with their start and end apart: 17, of which 9 were waited for; matrix products, arithmetic and copies ran while one was open for 1% of the time, Pallas kernels for 26%

profile of v2, /device:TPU:0, one launch (start us, length us, event | category | flops | bytes accessed | tf_op | source)
XLA Modules:
  0.0 120.7 jit_solution(4326455117504278852)
XLA Ops:
  7.2 0.0 all-gather.2.cloned.1.call-start
  7.2 0.5 collective-permute-start.3
  7.7 0.2 all-gather.2.cloned.1.call-update
  7.9 0.8 constant_dynamic-slice_fusion
  8.8 5.0 %collective-permute-start.2 = (bf16[128,256]{1,0:T(8,128)(2,1)S(1)}, bf16[128,256]{1,0:T(8,128)(2,1)S(1)}, u32[]{:S(2)}, u32[]{:S(2)}) collective-permute-start(bf16[128,256]{1,0:T(8,128)(2,1)S(1)} %constant_dynamic-slice_fusion), channel_id=1, source_target_pairs={{0,24},{4,28},{8,16},{12,20},{16,8},{20,12},{24,0},{28,4},{1,25},{... | collective-permute-start | bytes 196616 | tf_op jit(solution)/shard_map/ppermute | solution.py:424
  13.8 0.6 collective-permute-start
  14.4 0.1 pad_add_fusion.info
  14.5 1.0 copy-done.1
  15.4 1.2 %copy-done.3 = bf16[2048,256]{1,0:T(8,128)(2,1)S(1)} copy-done((bf16[2048,256]{1,0:T(8,128)(2,1)S(1)}, bf16[2048,256]{1,0:T(8,128)(2,1)}, u32[]{:S(2)}) %copy-start.3) | copy-done | bytes 1048600
  16.7 3.3 %stats_part.2.refs_6_ = f32[8,8,512]{2,1,0:T(8,128)S(1)} custom-call(s32[2]{0:T(128)S(1)} %pad_add_fusion.info, bf16[512,256]{1,0:T(8,128)(2,1)S(1)} %copy-done.1, bf16[2048,256]{1,0:T(8,128)(2,1)S(1)} %copy-done.3, bf16[2048,256]{1,0:T(8,128)(2,1)S(1)} %collective-permute-done.3.refs_2_.across.refs_5_.refs_6_), custom_call_target="tpu_custom_call" | custom-call | flops 1073741824 | bytes 8388608 | tf_op jit(solution)/shard_map/stats_part/pallas_call | solution.py:118
  20.1 2.7 %collective-permute-start.6 = (bf16[3,128,256]{2,1,0:T(8,128)(2,1)S(1)}, bf16[3,128,256]{2,1,0:T(8,128)(2,1)S(1)}, u32[]{:S(2)}, u32[]{:S(2)}) collective-permute-start(bf16[3,128,256]{2,1,0:T(8,128)(2,1)S(1)} %pad_maximum_fusion.refs_0_), channel_id=1, source_target_pairs={{0,3},{1,2},{2,1},{3,0},{4,7},{5,6},{6,5},{7,4},{8,11},{9,10},{10,... | collective-permute-start | bytes 589832 | tf_op jit(solution)/shard_map/ppermute | solution.py:424
  22.8 0.5 collective-permute-start.5
  23.3 0.3 collective-permute-start.4
  23.6 4.9 %rows_part.4 = (f32[72,512]{1,0:T(8,128)S(1)}, bf16[80,512]{1,0:T(8,128)(2,1)S(1)}, bf16[80,512]{1,0:T(8,128)(2,1)S(1)}, bf16[80,512]{1,0:T(8,128)(2,1)S(1)}) custom-call(s32[2]{0:T(128)S(1)} %pad_add_fusion.info, bf16[512,256]{1,0:T(8,128)(2,1)S(1)} %copy-done, bf16[2048,256]{1,0:T(8,128)(2,1)S(1)} %copy-done.4, ...), custom_call_target="tpu_custom_call" | custom-call | flops 2147483648 | bytes 16777216 | tf_op jit(solution)/shard_map/rows_part/pallas_call | solution.py:118
  28.6 0.3 collective-permute-done.6.refs_3_
  28.9 2.5 %collective-permute-done.5.refs_2_ = bf16[3,128,256]{2,1,0:T(8,128)(2,1)S(1)} collective-permute-done((bf16[3,128,256]{2,1,0:T(8,128)(2,1)S(1)}, bf16[3,128,256]{2,1,0:T(8,128)(2,1)S(1)}, u32[]{:S(2)}, u32[]{:S(2)}) %collective-permute-start.5) | collective-permute-done | bytes 196640 | tf_op jit(solution)/shard_map/ppermute | solution.py:424
  31.4 0.1 collective-permute-done.4.refs_1_
  31.5 8.6 %stats_part.3.refs_7_.stats = f32[8,8,512]{2,1,0:T(8,128)S(1)} custom-call(s32[2]{0:T(128)S(1)} %pad_add_fusion.info, bf16[3,128,256]{2,1,0:T(8,128)(2,1)S(1)} %pad_maximum_fusion.refs_0_, bf16[3,128,256]{2,1,0:T(8,128)(2,1)S(1)} %collective-permute-done.4.refs_1_, bf16[3,128,256]{2,1,0:T(8,128)(2,1)S(1)} %collective-permute-done.5.refs_2_, ...), custom_call_target="tpu_custom_call" | custom-call | flops 3221225472 | bytes 25165824 | tf_op jit(solution)/shard_map/stats_part/pallas_call | solution.py:118
  40.2 0.0 copy-start.17
  40.2 0.1 collective-permute-start.7
  40.3 1.3 %collective-permute-done.7.refs_8_.other = f32[8,8,512]{2,1,0:T(8,128)S(1)} collective-permute-done((f32[8,8,512]{2,1,0:T(8,128)S(1)}, f32[8,8,512]{2,1,0:T(8,128)S(1)}, u32[]{:S(2)}, u32[]{:S(2)}) %collective-permute-start.7) | collective-permute-done | bytes 131104 | tf_op jit(solution)/shard_map/ppermute | solution.py:424
  41.7 1.3 %copy-done.8 = bf16[2048,256]{1,0:T(8,128)(2,1)S(1)} copy-done((bf16[2048,256]{1,0:T(8,128)(2,1)S(1)}, bf16[2048,256]{1,0:T(8,128)(2,1)}, u32[]{:S(2)}) %copy-start.8) | copy-done | bytes 1048600
  42.9 1.2 %copy-done.11 = bf16[2048,256]{1,0:T(8,128)(2,1)S(1)} copy-done((bf16[2048,256]{1,0:T(8,128)(2,1)S(1)}, bf16[2048,256]{1,0:T(8,128)(2,1)}, u32[]{:S(2)}) %copy-start.11) | copy-done | bytes 1048600
  44.2 16.2 %rows_part.5 = (f32[144,1024]{1,0:T(8,128)S(1)}, bf16[4,160,1024]{2,1,0:T(8,128)(2,1)}) custom-call(s32[2]{0:T(128)S(1)} %pad_add_fusion.info, bf16[3,128,256]{2,1,0:T(8,128)(2,1)S(1)} %pad_maximum_fusion.refs_0_, bf16[3,128,256]{2,1,0:T(8,128)(2,1)S(1)} %collective-permute-done.4.refs_1_, bf16[3,128,256]{2,1,0:T(8,128)(2,1)S(1)} %collective-permute-done.5.refs_2_, ...), custom_call_target="tpu_custom_call" | custom-call | flops 8589934592 | bytes 67108864 | tf_op jit(solution)/shard_map/rows_part/pallas_call | solution.py:118
  60.4 3.9 %all-to-all-start = ((bf16[4,160,1024]{2,1,0:T(8,128)(2,1)}), bf16[4,160,1024]{2,1,0:T(8,128)(2,1)S(1)}, u32[]{:S(2)}, u32[]{:S(2)}) async-start(bf16[4,160,1024]{2,1,0:T(8,128)(2,1)} %get-tuple-element.61), calls=%async_computation | async-start | bytes 2621440 | tf_op jit(solution)/shard_map/all_to_all | solution.py:442
  64.3 0.0 copy-start.5
  64.3 1.2 %copy-done.5 = bf16[2048,256]{1,0:T(8,128)(2,1)S(1)} copy-done((bf16[2048,256]{1,0:T(8,128)(2,1)S(1)}, bf16[2048,256]{1,0:T(8,128)(2,1)}, u32[]{:S(2)}) %copy-start.5) | copy-done | bytes 1048600
  65.5 1.2 %copy-done.9 = bf16[2048,256]{1,0:T(8,128)(2,1)S(1)} copy-done((bf16[2048,256]{1,0:T(8,128)(2,1)S(1)}, bf16[2048,256]{1,0:T(8,128)(2,1)}, u32[]{:S(2)}) %copy-start.9) | copy-done | bytes 1048600
  66.7 1.2 %copy-done.12 = bf16[2048,256]{1,0:T(8,128)(2,1)S(1)} copy-done((bf16[2048,256]{1,0:T(8,128)(2,1)S(1)}, bf16[2048,256]{1,0:T(8,128)(2,1)}, u32[]{:S(2)}) %copy-start.12) | copy-done | bytes 1048600
  68.0 0.9 copy-done.20
  68.9 8.7 %rows_part.6 = (f32[144,512]{1,0:T(8,128)S(1)}, bf16[4,160,512]{2,1,0:T(8,128)(2,1)}) custom-call(s32[2]{0:T(128)S(1)} %pad_add_fusion.info, bf16[3,128,256]{2,1,0:T(8,128)(2,1)S(1)} %pad_maximum_fusion.refs_0_, bf16[3,128,256]{2,1,0:T(8,128)(2,1)S(1)} %copy-done.16, bf16[3,128,256]{2,1,0:T(8,128)(2,1)S(1)} %copy-done.14, ...), custom_call_target="tpu_custom_call" | custom-call | flops 4294967296 | bytes 33554432 | tf_op jit(solution)/shard_map/rows_part/pallas_call | solution.py:118
  77.6 3.5 %all-to-all-done.arrived = bf16[4,160,1024]{2,1,0:T(8,128)(2,1)S(1)} async-done(((bf16[4,160,1024]{2,1,0:T(8,128)(2,1)}), bf16[4,160,1024]{2,1,0:T(8,128)(2,1)S(1)}, u32[]{:S(2)}, u32[]{:S(2)}) %all-to-all-start) | async-done | bytes 1310752 | tf_op jit(solution)/shard_map/all_to_all | solution.py:442
  81.1 3.6 %all-to-all-start.1 = ((bf16[4,160,512]{2,1,0:T(8,128)(2,1)}), bf16[4,160,512]{2,1,0:T(8,128)(2,1)S(1)}, u32[]{:S(2)}, u32[]{:S(2)}) async-start(bf16[4,160,512]{2,1,0:T(8,128)(2,1)} %get-tuple-element.72), calls=%async_computation.1 | async-start | bytes 1310720 | tf_op jit(solution)/shard_map/all_to_all | solution.py:442
  84.7 0.0 copy-start.6
  84.7 0.0 copy-start.18
  84.8 1.6 %join_spread.2 = (bf16[208,512]{1,0:T(8,128)(2,1)}, bf16[208,512]{1,0:T(8,128)(2,1)}) custom-call(s32[2]{0:T(128)S(1)} %pad_add_fusion.info, f32[144,1024]{1,0:T(8,128)S(1)} %get-tuple-element.60.kept, bf16[4,160,1024]{2,1,0:T(8,128)(2,1)S(1)} %all-to-all-done.arrived), custom_call_target="tpu_custom_call" | custom-call | flops 1048576 | bytes 8192 | tf_op jit(solution)/shard_map/join_spread/pallas_call | solution.py:118
  86.4 3.5 %collective-permute-start.8 = (bf16[208,512]{1,0:T(8,128)(2,1)}, bf16[208,512]{1,0:T(8,128)(2,1)S(1)}, u32[]{:S(2)}, u32[]{:S(2)}) collective-permute-start(bf16[208,512]{1,0:T(8,128)(2,1)} %get-tuple-element.71), channel_id=1, source_target_pairs={{0,24},{4,28},{8,16},{12,20},{16,8},{20,12},{24,0},{28,4},{1,25},{... | collective-permute-start | bytes 638984 | tf_op jit(solution)/shard_map/ppermute | solution.py:424
  90.0 1.2 %copy-done.10 = bf16[2048,256]{1,0:T(8,128)(2,1)S(1)} copy-done((bf16[2048,256]{1,0:T(8,128)(2,1)S(1)}, bf16[2048,256]{1,0:T(8,128)(2,1)}, u32[]{:S(2)}) %copy-start.10) | copy-done | bytes 1048600
  91.2 3.2 %rows_part.7 = (f32[144,512]{1,0:T(8,128)S(1)}, bf16[160,512]{1,0:T(8,128)(2,1)S(1)}, bf16[160,512]{1,0:T(8,128)(2,1)S(1)}, bf16[160,512]{1,0:T(8,128)(2,1)S(1)}) custom-call(s32[2]{0:T(128)S(1)} %pad_add_fusion.info, bf16[512,256]{1,0:T(8,128)(2,1)S(1)} %copy-done.2, bf16[512,256]{1,0:T(8,128)(2,1)S(1)} %copy-done, bf16[2048,256]{1,0:T(8,128)(2,1)S(1)} %copy-done.6, ...), custom_call_target="tpu_custom_call" | custom-call | flops 2147483648 | bytes 16777216 | tf_op jit(solution)/shard_map/rows_part/pallas_call | solution.py:118
  94.5 2.0 %collective-permute-start.9 = (bf16[160,512]{1,0:T(8,128)(2,1)S(1)}, bf16[160,512]{1,0:T(8,128)(2,1)S(1)}, u32[]{:S(2)}, u32[]{:S(2)}) collective-permute-start(bf16[160,512]{1,0:T(8,128)(2,1)S(1)} %get-tuple-element.76), channel_id=1, source_target_pairs={{0,1},{1,0},{2,3},{3,2},{4,5},{5,4},{6,7},{7,6},{8,9},{9,8},{10,11... | collective-permute-start | bytes 491528 | tf_op jit(solution)/shard_map/ppermute | solution.py:424
  96.5 1.5 %collective-permute-start.10 = (bf16[160,512]{1,0:T(8,128)(2,1)S(1)}, bf16[160,512]{1,0:T(8,128)(2,1)S(1)}, u32[]{:S(2)}, u32[]{:S(2)}) collective-permute-start(bf16[160,512]{1,0:T(8,128)(2,1)S(1)} %get-tuple-element.77), channel_id=1, source_target_pairs={{0,2},{1,3},{2,0},{3,1},{4,6},{5,7},{6,4},{7,5},{8,10},{9,11},{10,... | collective-permute-start | bytes 491528 | tf_op jit(solution)/shard_map/ppermute | solution.py:424
  97.9 0.1 collective-permute-start.11
  98.0 0.8 join_spread.3
  98.8 2.2 %collective-permute-done.9.refs_1_ = bf16[160,512]{1,0:T(8,128)(2,1)S(1)} collective-permute-done((bf16[160,512]{1,0:T(8,128)(2,1)S(1)}, bf16[160,512]{1,0:T(8,128)(2,1)S(1)}, u32[]{:S(2)}, u32[]{:S(2)}) %collective-permute-start.9) | collective-permute-done | bytes 163872 | tf_op jit(solution)/shard_map/ppermute | solution.py:424
  101.0 4.1 %collective-permute-done.10.refs_2_ = bf16[160,512]{1,0:T(8,128)(2,1)S(1)} collective-permute-done((bf16[160,512]{1,0:T(8,128)(2,1)S(1)}, bf16[160,512]{1,0:T(8,128)(2,1)S(1)}, u32[]{:S(2)}, u32[]{:S(2)}) %collective-permute-start.10) | collective-permute-done | bytes 163872 | tf_op jit(solution)/shard_map/ppermute | solution.py:424
  105.1 2.9 %collective-permute-done.12.refs_5_ = bf16[208,512]{1,0:T(8,128)(2,1)S(1)} collective-permute-done((bf16[208,512]{1,0:T(8,128)(2,1)}, bf16[208,512]{1,0:T(8,128)(2,1)S(1)}, u32[]{:S(2)}, u32[]{:S(2)}) %collective-permute-start.12) | collective-permute-done | bytes 213024 | tf_op jit(solution)/shard_map/ppermute | solution.py:424
  108.0 4.5 %collective-permute-done.13.refs_6_ = bf16[208,512]{1,0:T(8,128)(2,1)S(1)} collective-permute-done((bf16[208,512]{1,0:T(8,128)(2,1)S(1)}, bf16[208,512]{1,0:T(8,128)(2,1)S(1)}, u32[]{:S(2)}, u32[]{:S(2)}) %collective-permute-start.13) | collective-permute-done | bytes 213024 | tf_op jit(solution)/shard_map/ppermute | solution.py:424
  112.4 1.4 %finish.1 = (f32[1,512]{1,0:T(1,128)}, f32[64,512]{1,0:T(8,128)}) custom-call(s32[2]{0:T(128)S(1)} %pad_add_fusion.info, f32[144,512]{1,0:T(8,128)S(1)} %get-tuple-element.80.refs_0_, bf16[160,512]{1,0:T(8,128)(2,1)S(1)} %collective-permute-done.9.refs_1_, bf16[160,512]{1,0:T(8,128)(2,1)S(1)} %collective-permute-done.10.refs_2_, ...), custom_call_target="tpu_custom_call" | custom-call | flops 1048576 | bytes 8192 | tf_op jit(solution)/shard_map/finish/pallas_call | solution.py:118
  (59 shorter events, 0.1 us)
Async XLA Ops:
  7.2 34.5 %all-gather.2.cloned.1.call-start = ((), (), s32[]{:S(2)}) async-start(), calls=%async_computation.2 | async-start | bytes 1310720 | tf_op jit(solution)/shard_map/all_gather | solution.py:448
  7.2 7.2 %collective-permute-start.3 = (bf16[2048,256]{1,0:T(8,128)(2,1)}, bf16[2048,256]{1,0:T(8,128)(2,1)S(1)}, u32[]{:S(2)}, u32[]{:S(2)}) collective-permute-start(bf16[2048,256]{1,0:T(8,128)(2,1)} %near.3), channel_id=1, source_target_pairs={{0,4},{4,0},{8,12},{12,8},{16,20},{20,16},{24,28},{28,24},{1,5},{5... | collective-permute-start | bytes 3145736 | tf_op jit(solution)/shard_map/ppermute | solution.py:424
  8.8 11.3 %collective-permute-start.2 = (bf16[128,256]{1,0:T(8,128)(2,1)S(1)}, bf16[128,256]{1,0:T(8,128)(2,1)S(1)}, u32[]{:S(2)}, u32[]{:S(2)}) collective-permute-start(bf16[128,256]{1,0:T(8,128)(2,1)S(1)} %constant_dynamic-slice_fusion), channel_id=1, source_target_pairs={{0,24},{4,28},{8,16},{12,20},{16,8},{20,12},{24,0},{28,4},{1,25},{... | collective-permute-start | bytes 196616 | tf_op jit(solution)/shard_map/ppermute | solution.py:424
  13.8 6.2 %collective-permute-start.1 = (bf16[128,256]{1,0:T(8,128)(2,1)S(1)}, bf16[128,256]{1,0:T(8,128)(2,1)S(1)}, u32[]{:S(2)}, u32[]{:S(2)}) collective-permute-start(bf16[128,256]{1,0:T(8,128)(2,1)S(1)} %constant_dynamic-slice_fusion), channel_id=1, source_target_pairs={{0,16},{4,20},{8,24},{12,28},{16,0},{20,4},{24,8},{28,12},{1,17},{... | collective-permute-start | bytes 196616 | tf_op jit(solution)/shard_map/ppermute | solution.py:424
  13.8 6.2 %collective-permute-start = (bf16[128,256]{1,0:T(8,128)(2,1)S(1)}, bf16[128,256]{1,0:T(8,128)(2,1)S(1)}, u32[]{:S(2)}, u32[]{:S(2)}) collective-permute-start(bf16[128,256]{1,0:T(8,128)(2,1)S(1)} %constant_dynamic-slice_fusion), channel_id=1, source_target_pairs={{0,8},{4,12},{8,0},{12,4},{16,24},{20,28},{24,16},{28,20},{1,9},{5... | collective-permute-start | bytes 196616 | tf_op jit(solution)/shard_map/ppermute | solution.py:424
  14.4 9.2 %copy-start = (bf16[512,256]{1,0:T(8,128)(2,1)S(1)}, bf16[512,256]{1,0:T(8,128)(2,1)}, u32[]{:S(2)}) copy-start(bf16[512,256]{1,0:T(8,128)(2,1)} %preds.3) | copy-start | bytes 786436
  14.4 1.0 copy-start.1
  15.4 1.2 %copy-start.3 = (bf16[2048,256]{1,0:T(8,128)(2,1)S(1)}, bf16[2048,256]{1,0:T(8,128)(2,1)}, u32[]{:S(2)}) copy-start(bf16[2048,256]{1,0:T(8,128)(2,1)} %near.3) | copy-start | bytes 3145732
  16.7 14.9 %copy-start.7 = (bf16[2048,256]{1,0:T(8,128)(2,1)}, bf16[2048,256]{1,0:T(8,128)(2,1)S(1)}, u32[]{:S(2)}) copy-start(bf16[2048,256]{1,0:T(8,128)(2,1)S(1)} %collective-permute-done.3.refs_2_.across.refs_5_.refs_6_) | copy-start | bytes 3145732
  16.7 7.0 %copy-start.4 = (bf16[2048,256]{1,0:T(8,128)(2,1)S(1)}, bf16[2048,256]{1,0:T(8,128)(2,1)}, u32[]{:S(2)}) copy-start(bf16[2048,256]{1,0:T(8,128)(2,1)} %near.3) | copy-start | bytes 3145732
  20.1 8.8 %collective-permute-start.6 = (bf16[3,128,256]{2,1,0:T(8,128)(2,1)S(1)}, bf16[3,128,256]{2,1,0:T(8,128)(2,1)S(1)}, u32[]{:S(2)}, u32[]{:S(2)}) collective-permute-start(bf16[3,128,256]{2,1,0:T(8,128)(2,1)S(1)} %pad_maximum_fusion.refs_0_), channel_id=1, source_target_pairs={{0,3},{1,2},{2,1},{3,0},{4,7},{5,6},{6,5},{7,4},{8,11},{9,10},{10,... | collective-permute-start | bytes 589832 | tf_op jit(solution)/shard_map/ppermute | solution.py:424
  22.8 8.6 %collective-permute-start.5 = (bf16[3,128,256]{2,1,0:T(8,128)(2,1)S(1)}, bf16[3,128,256]{2,1,0:T(8,128)(2,1)S(1)}, u32[]{:S(2)}, u32[]{:S(2)}) collective-permute-start(bf16[3,128,256]{2,1,0:T(8,128)(2,1)S(1)} %pad_maximum_fusion.refs_0_), channel_id=1, source_target_pairs={{0,2},{1,3},{2,0},{3,1},{4,6},{5,7},{6,4},{7,5},{8,10},{9,11},{10,... | collective-permute-start | bytes 589832 | tf_op jit(solution)/shard_map/ppermute | solution.py:424
  23.3 8.2 %collective-permute-start.4 = (bf16[3,128,256]{2,1,0:T(8,128)(2,1)S(1)}, bf16[3,128,256]{2,1,0:T(8,128)(2,1)S(1)}, u32[]{:S(2)}, u32[]{:S(2)}) collective-permute-start(bf16[3,128,256]{2,1,0:T(8,128)(2,1)S(1)} %pad_maximum_fusion.refs_0_), channel_id=1, source_target_pairs={{0,1},{1,0},{2,3},{3,2},{4,5},{5,4},{6,7},{7,6},{8,9},{9,8},{10,11... | collective-permute-start | bytes 589832 | tf_op jit(solution)/shard_map/ppermute | solution.py:424
  28.5 11.7 %copy-start.22 = (f32[72,512]{1,0:T(8,128)}, f32[72,512]{1,0:T(8,128)S(1)}, u32[]{:S(2)}) copy-start(f32[72,512]{1,0:T(8,128)S(1)} %get-tuple-element.64.refs_0_) | copy-start | bytes 442372
  28.5 11.7 %copy-start.24 = (bf16[80,512]{1,0:T(8,128)(2,1)}, bf16[80,512]{1,0:T(8,128)(2,1)S(1)}, u32[]{:S(2)}) copy-start(bf16[80,512]{1,0:T(8,128)(2,1)S(1)} %get-tuple-element.65.refs_1_) | copy-start | bytes 245764
  28.5 11.7 %copy-start.26 = (bf16[80,512]{1,0:T(8,128)(2,1)}, bf16[80,512]{1,0:T(8,128)(2,1)S(1)}, u32[]{:S(2)}) copy-start(bf16[80,512]{1,0:T(8,128)(2,1)S(1)} %get-tuple-element.66.refs_2_) | copy-start | bytes 245764
  28.6 11.7 %copy-start.28 = (bf16[80,512]{1,0:T(8,128)(2,1)}, bf16[80,512]{1,0:T(8,128)(2,1)S(1)}, u32[]{:S(2)}) copy-start(bf16[80,512]{1,0:T(8,128)(2,1)S(1)} %get-tuple-element.67.refs_3_) | copy-start | bytes 245764
  31.4 10.2 %copy-start.13 = (bf16[3,128,256]{2,1,0:T(8,128)(2,1)}, bf16[3,128,256]{2,1,0:T(8,128)(2,1)S(1)}, u32[]{:S(2)}) copy-start(bf16[3,128,256]{2,1,0:T(8,128)(2,1)S(1)} %collective-permute-done.5.refs_2_) | copy-start | bytes 589828
  31.5 10.1 %copy-start.15 = (bf16[3,128,256]{2,1,0:T(8,128)(2,1)}, bf16[3,128,256]{2,1,0:T(8,128)(2,1)S(1)}, u32[]{:S(2)}) copy-start(bf16[3,128,256]{2,1,0:T(8,128)(2,1)S(1)} %collective-permute-done.4.refs_1_) | copy-start | bytes 589828
  40.2 24.0 %copy-start.17 = (f32[8,8,512]{2,1,0:T(8,128)}, f32[8,8,512]{2,1,0:T(8,128)S(1)}, u32[]{:S(2)}) copy-start(f32[8,8,512]{2,1,0:T(8,128)S(1)} %stats_part.3.refs_7_.stats) | copy-start | bytes 393220
  40.2 1.4 %collective-permute-start.7 = (f32[8,8,512]{2,1,0:T(8,128)S(1)}, f32[8,8,512]{2,1,0:T(8,128)S(1)}, u32[]{:S(2)}, u32[]{:S(2)}) collective-permute-start(f32[8,8,512]{2,1,0:T(8,128)S(1)} %stats_part.3.refs_7_.stats), channel_id=1, source_target_pairs={{0,4},{4,0},{8,12},{12,8},{16,20},{20,16},{24,28},{28,24},{1,5},{5... | collective-permute-start | bytes 393224 | tf_op jit(solution)/shard_map/ppermute | solution.py:424
  41.6 18.7 %copy-start.19 = (f32[8,8,512]{2,1,0:T(8,128)}, f32[8,8,512]{2,1,0:T(8,128)S(1)}, u32[]{:S(2)}) copy-start(f32[8,8,512]{2,1,0:T(8,128)S(1)} %collective-permute-done.7.refs_8_.other) | copy-start | bytes 393220
  41.7 1.3 %copy-start.8 = (bf16[2048,256]{1,0:T(8,128)(2,1)S(1)}, bf16[2048,256]{1,0:T(8,128)(2,1)}, u32[]{:S(2)}) copy-start(bf16[2048,256]{1,0:T(8,128)(2,1)} %copy-done.7) | copy-start | bytes 3145732
  42.9 1.2 %copy-start.11 = (bf16[2048,256]{1,0:T(8,128)(2,1)S(1)}, bf16[2048,256]{1,0:T(8,128)(2,1)}, u32[]{:S(2)}) copy-start(bf16[2048,256]{1,0:T(8,128)(2,1)} %all-gather.2.cloned.1.call-done.refs_4_) | copy-start | bytes 3145732
  60.4 3.9 %copy-start.14 = (bf16[3,128,256]{2,1,0:T(8,128)(2,1)S(1)}, bf16[3,128,256]{2,1,0:T(8,128)(2,1)}, u32[]{:S(2)}) copy-start(bf16[3,128,256]{2,1,0:T(8,128)(2,1)} %copy-done.13) | copy-start | bytes 589828
  60.4 3.9 %copy-start.16 = (bf16[3,128,256]{2,1,0:T(8,128)(2,1)S(1)}, bf16[3,128,256]{2,1,0:T(8,128)(2,1)}, u32[]{:S(2)}) copy-start(bf16[3,128,256]{2,1,0:T(8,128)(2,1)} %copy-done.15) | copy-start | bytes 589828
  60.4 20.7 %all-to-all-start = ((bf16[4,160,1024]{2,1,0:T(8,128)(2,1)}), bf16[4,160,1024]{2,1,0:T(8,128)(2,1)S(1)}, u32[]{:S(2)}, u32[]{:S(2)}) async-start(bf16[4,160,1024]{2,1,0:T(8,128)(2,1)} %get-tuple-element.61), calls=%async_computation | async-start | bytes 2621440 | tf_op jit(solution)/shard_map/all_to_all | solution.py:442
  64.3 1.2 %copy-start.5 = (bf16[2048,256]{1,0:T(8,128)(2,1)S(1)}, bf16[2048,256]{1,0:T(8,128)(2,1)}, u32[]{:S(2)}) copy-start(bf16[2048,256]{1,0:T(8,128)(2,1)} %near.3) | copy-start | bytes 3145732
  65.5 1.2 %copy-start.9 = (bf16[2048,256]{1,0:T(8,128)(2,1)S(1)}, bf16[2048,256]{1,0:T(8,128)(2,1)}, u32[]{:S(2)}) copy-start(bf16[2048,256]{1,0:T(8,128)(2,1)} %copy-done.7) | copy-start | bytes 3145732
  66.7 1.2 %copy-start.12 = (bf16[2048,256]{1,0:T(8,128)(2,1)S(1)}, bf16[2048,256]{1,0:T(8,128)(2,1)}, u32[]{:S(2)}) copy-start(bf16[2048,256]{1,0:T(8,128)(2,1)} %all-gather.2.cloned.1.call-done.refs_4_) | copy-start | bytes 3145732
  67.9 0.9 copy-start.20
  81.1 8.9 %copy-start.2 = (bf16[512,256]{1,0:T(8,128)(2,1)S(1)}, bf16[512,256]{1,0:T(8,128)(2,1)}, u32[]{:S(2)}) copy-start(bf16[512,256]{1,0:T(8,128)(2,1)} %codes.1) | copy-start | bytes 786436
  81.1 17.0 %all-to-all-start.1 = ((bf16[4,160,512]{2,1,0:T(8,128)(2,1)}), bf16[4,160,512]{2,1,0:T(8,128)(2,1)S(1)}, u32[]{:S(2)}, u32[]{:S(2)}) async-start(bf16[4,160,512]{2,1,0:T(8,128)(2,1)} %get-tuple-element.72), calls=%async_computation.1 | async-start | bytes 1310720 | tf_op jit(solution)/shard_map/all_to_all | solution.py:442
  84.7 5.3 %copy-start.6 = (bf16[2048,256]{1,0:T(8,128)(2,1)S(1)}, bf16[2048,256]{1,0:T(8,128)(2,1)}, u32[]{:S(2)}) copy-start(bf16[2048,256]{1,0:T(8,128)(2,1)} %near.3) | copy-start | bytes 3145732
  84.7 5.3 %copy-start.18 = (f32[8,8,512]{2,1,0:T(8,128)S(1)}, f32[8,8,512]{2,1,0:T(8,128)}, u32[]{:S(2)}) copy-start(f32[8,8,512]{2,1,0:T(8,128)} %copy-done.17) | copy-start | bytes 393220
  84.7 5.2 %copy-start.21 = (f32[8,8,512]{2,1,0:T(8,128)S(1)}, f32[8,8,512]{2,1,0:T(8,128)}, u32[]{:S(2)}) copy-start(f32[8,8,512]{2,1,0:T(8,128)} %copy-done.19) | copy-start | bytes 393220
  84.7 5.2 %copy-start.23 = (f32[72,512]{1,0:T(8,128)S(1)}, f32[72,512]{1,0:T(8,128)}, u32[]{:S(2)}) copy-start(f32[72,512]{1,0:T(8,128)} %copy-done.22) | copy-start | bytes 442372
  84.7 5.2 %copy-start.25 = (bf16[80,512]{1,0:T(8,128)(2,1)S(1)}, bf16[80,512]{1,0:T(8,128)(2,1)}, u32[]{:S(2)}) copy-start(bf16[80,512]{1,0:T(8,128)(2,1)} %copy-done.24) | copy-start | bytes 245764
  84.7 5.2 %copy-start.27 = (bf16[80,512]{1,0:T(8,128)(2,1)S(1)}, bf16[80,512]{1,0:T(8,128)(2,1)}, u32[]{:S(2)}) copy-start(bf16[80,512]{1,0:T(8,128)(2,1)} %copy-done.26) | copy-start | bytes 245764
  84.7 5.2 %copy-start.29 = (bf16[80,512]{1,0:T(8,128)(2,1)S(1)}, bf16[80,512]{1,0:T(8,128)(2,1)}, u32[]{:S(2)}) copy-start(bf16[80,512]{1,0:T(8,128)(2,1)} %copy-done.28) | copy-start | bytes 245764
  86.4 11.6 %collective-permute-start.8 = (bf16[208,512]{1,0:T(8,128)(2,1)}, bf16[208,512]{1,0:T(8,128)(2,1)S(1)}, u32[]{:S(2)}, u32[]{:S(2)}) collective-permute-start(bf16[208,512]{1,0:T(8,128)(2,1)} %get-tuple-element.71), channel_id=1, source_target_pairs={{0,24},{4,28},{8,16},{12,20},{16,8},{20,12},{24,0},{28,4},{1,25},{... | collective-permute-start | bytes 638984 | tf_op jit(solution)/shard_map/ppermute | solution.py:424
  90.0 1.2 %copy-start.10 = (bf16[2048,256]{1,0:T(8,128)(2,1)S(1)}, bf16[2048,256]{1,0:T(8,128)(2,1)}, u32[]{:S(2)}) copy-start(bf16[2048,256]{1,0:T(8,128)(2,1)} %copy-done.7) | copy-start | bytes 3145732
  94.5 6.5 %collective-permute-start.9 = (bf16[160,512]{1,0:T(8,128)(2,1)S(1)}, bf16[160,512]{1,0:T(8,128)(2,1)S(1)}, u32[]{:S(2)}, u32[]{:S(2)}) collective-permute-start(bf16[160,512]{1,0:T(8,128)(2,1)S(1)} %get-tuple-element.76), channel_id=1, source_target_pairs={{0,1},{1,0},{2,3},{3,2},{4,5},{5,4},{6,7},{7,6},{8,9},{9,8},{10,11... | collective-permute-start | bytes 491528 | tf_op jit(solution)/shard_map/ppermute | solution.py:424
  96.5 8.6 %collective-permute-start.10 = (bf16[160,512]{1,0:T(8,128)(2,1)S(1)}, bf16[160,512]{1,0:T(8,128)(2,1)S(1)}, u32[]{:S(2)}, u32[]{:S(2)}) collective-permute-start(bf16[160,512]{1,0:T(8,128)(2,1)S(1)} %get-tuple-element.77), channel_id=1, source_target_pairs={{0,2},{1,3},{2,0},{3,1},{4,6},{5,7},{6,4},{7,5},{8,10},{9,11},{10,... | collective-permute-start | bytes 491528 | tf_op jit(solution)/shard_map/ppermute | solution.py:424
  97.9 7.2 %collective-permute-start.11 = (bf16[160,512]{1,0:T(8,128)(2,1)S(1)}, bf16[160,512]{1,0:T(8,128)(2,1)S(1)}, u32[]{:S(2)}, u32[]{:S(2)}) collective-permute-start(bf16[160,512]{1,0:T(8,128)(2,1)S(1)} %get-tuple-element.78), channel_id=1, source_target_pairs={{0,3},{1,2},{2,1},{3,0},{4,7},{5,6},{6,5},{7,4},{8,11},{9,10},{10,... | collective-permute-start | bytes 491528 | tf_op jit(solution)/shard_map/ppermute | solution.py:424
  98.0 10.0 %collective-permute-start.12 = (bf16[208,512]{1,0:T(8,128)(2,1)}, bf16[208,512]{1,0:T(8,128)(2,1)S(1)}, u32[]{:S(2)}, u32[]{:S(2)}) collective-permute-start(bf16[208,512]{1,0:T(8,128)(2,1)} %get-tuple-element.85), channel_id=1, source_target_pairs={{0,16},{4,20},{8,24},{12,28},{16,0},{20,4},{24,8},{28,12},{1,17},{... | collective-permute-start | bytes 638984 | tf_op jit(solution)/shard_map/ppermute | solution.py:424
  105.1 7.3 %collective-permute-start.13 = (bf16[208,512]{1,0:T(8,128)(2,1)S(1)}, bf16[208,512]{1,0:T(8,128)(2,1)S(1)}, u32[]{:S(2)}, u32[]{:S(2)}) collective-permute-start(bf16[208,512]{1,0:T(8,128)(2,1)S(1)} %join_spread.3), channel_id=1, source_target_pairs={{0,8},{4,12},{8,0},{12,4},{16,24},{20,28},{24,16},{28,20},{1,9},{5... | collective-permute-start | bytes 638984 | tf_op jit(solution)/shard_map/ppermute | solution.py:424
Sparse Core Ops, SparseCore 0:
  9.6 30.6 all-gather.1

commit v3 on v2

v3 whole, which is shorter than its diff:
```python
import functools
import math

import jax
import jax.numpy as jnp
from jax import lax
from jax.experimental import pallas as pl
from jax.experimental.pallas import tpu as pltpu
from jax.sharding import PartitionSpec as P

code_temp = 0.05
pred_temp = 0.1
code_scale = math.log2(math.e) / code_temp
pred_scale = math.log2(math.e) / pred_temp
log2 = math.log(2.0)
stat_rows = 8
sent_rows = 16
low = -1e30
chunk = 512
mebi = 1024 * 1024


def scores(embeds, protos):
    return lax.dot_general(
        embeds, protos, (((1,), (1,)), ((), ())), preferred_element_type=jnp.float32
    )


def bare(value):
    return value.astype(jnp.bfloat16)


def add(parts):
    return functools.reduce(jnp.add, parts)


def lane_fold(combine, value):
    parts = [value[:, i : i + 128] for i in range(0, value.shape[1], 128)]
    return functools.reduce(combine, parts)


def padded(rows, width):
    filler = jnp.zeros((stat_rows - len(rows), width), jnp.float32)
    return jnp.concatenate([*rows, filler], axis=0)


def split_stats(stats):
    terms = []
    for row in stats:
        for _ in range(3):
            term = bare(row)
            row = row - term.astype(jnp.float32)
            terms.append(term)
    filler = jnp.zeros((sent_rows - len(terms), stats[0].shape[1]), jnp.bfloat16)
    return jnp.concatenate([*terms, filler], axis=0)


def join_stats(terms, count):
    wide = terms.astype(jnp.float32)
    return [add([wide[3 * i + j : 3 * i + j + 1] for j in range(3)]) for i in range(count)]


def parted(value):
    share = value.shape[0] - stat_rows
    return value[:share, :], [value[share + i : share + i + 1, :] for i in range(2)]


def parted_sent(value):
    share = value.shape[0] - sent_rows
    return value[:share, :].astype(jnp.float32), join_stats(value[share:, :], 2)


def packed(part):
    pull, stats = part
    return jnp.concatenate([pull, padded(stats, pull.shape[1])], axis=0)


def join_preds(parts):
    peak = functools.reduce(jnp.maximum, [stats[0] for _, stats in parts])
    factors = [jnp.exp2(stats[0] - peak) for _, stats in parts]
    pull = add([part * factor for (part, _), factor in zip(parts, factors)])
    total = add([stats[1] * factor for (_, stats), factor in zip(parts, factors)])
    return pull, [peak, total]


def join_targets(parts):
    stats = [add([stats[i] for _, stats in parts]) for i in range(2)]
    return add([part for part, _ in parts]), stats


joins = {"pred": join_preds, "target": join_targets}


def send(info, place, pull, stats, outs, flipped):
    kept, *sent = outs
    share = pull.shape[1] // len(outs)
    high, tall = share + stat_rows, share + sent_rows
    flipped[...] = pull.T
    mine = pl.multiple_of(info[1] * share, share)
    kept[place * high : place * high + share, :] = flipped[pl.ds(mine, share), :]
    kept[place * high + share : (place + 1) * high, :] = padded(stats, pull.shape[0])
    terms = split_stats(stats)
    for s, out in enumerate(sent, 1):
        start = pl.multiple_of((info[1] ^ s) * share, share)
        out[place * tall : place * tall + share, :] = bare(flipped[pl.ds(start, share), :])
        out[place * tall + share : (place + 1) * tall, :] = terms


def whole(value):
    return pl.BlockSpec(value.shape, lambda *_: (0,) * len(value.shape))


def call(kernel, name, info, grid, ins, in_specs, outs, out_specs, scratch, flops, exps, room, passed=()):
    count, total = len(ins), len(ins) + len(outs)

    def without(*refs):
        return kernel(*refs[: 1 + total], *refs[1 + total + len(passed) :])

    outs = [*outs, *[jax.ShapeDtypeStruct(ins[i].shape, ins[i].dtype) for i in passed]]
    out_specs = [*out_specs, *[pl.BlockSpec(memory_space=pl.ANY)] * len(passed)]
    values = pl.pallas_call(
        without,
        grid_spec=pltpu.PrefetchScalarGridSpec(
            num_scalar_prefetch=1,
            grid=grid,
            in_specs=in_specs,
            out_specs=out_specs,
            scratch_shapes=scratch,
        ),
        out_shape=outs,
        input_output_aliases={1 + i: total - count + k for k, i in enumerate(passed)},
        compiler_params=pltpu.CompilerParams(vmem_limit_bytes=room * mebi),
        cost_estimate=pl.CostEstimate(flops=flops, bytes_accessed=flops // 128, transcendentals=exps),
        name=name,
    )(info, *ins)
    info, first = lax.optimization_barrier((info, values[0]))
    return info, first, *values[1:]


def placed_rows(info, quarters, block):
    part = quarters[0].shape[1]
    for s, quarter in enumerate(quarters):
        place = pl.multiple_of((info[1] ^ s) * part, part)
        block[pl.ds(place, part), :] = quarter[0]


def over_chunks(protos, width, step, unrolled=False):
    count = protos[0].shape[0] // width
    if unrolled:
        for i in range(count):
            for half, part in enumerate(protos):
                step(half * count + i, part[i * width : (i + 1) * width, :])
        return

    def both(i, carry):
        at = pl.ds(pl.multiple_of(i * width, width), width)
        for half, part in enumerate(protos):
            step(half * count + i, part[at, :])
        return carry

    lax.fori_loop(0, count, both, 0)


def stats_kernel(fresh, info, *refs):
    if fresh:
        *codes, near, across, stats, copied = refs
        copied[...] = near[...]
        stats[:, 0:1, :] = jnp.full((stats.shape[0], 1, stats.shape[2]), low, jnp.float32)
        stats[:, 1:, :] = jnp.zeros((stats.shape[0], stat_rows - 1, stats.shape[2]), jnp.float32)
    else:
        *codes, near, across, before, stats = refs
        stats[...] = before[...]
    for part in codes:
        rows = part[...].reshape(-1, part.shape[-1])

        def step(j, protos):
            raw = scores(rows, protos)
            old, total = stats[j, 0:1, :], stats[j, 1:2, :]
            new = jnp.maximum(old, jnp.max(raw, axis=0, keepdims=True))
            value = jnp.exp2((raw - new) * code_scale)
            stats[j, 1:2, :] = total * jnp.exp2((old - new) * code_scale) + jnp.sum(
                value, axis=0, keepdims=True
            )
            stats[j, 0:1, :] = new

        over_chunks((near, across), stats.shape[2], step, True)


def stats_part(info, codes, protos, before):
    count, dim = protos[0].shape
    width = min(chunk, count)
    rows = sum(math.prod(part.shape[:-1]) for part in codes)
    outs = [jax.ShapeDtypeStruct((2 * count // width, stat_rows, width), jnp.float32)]
    ins, passed = [*codes, *protos], [len(codes), len(codes) + 1]
    if before is None:
        outs.append(jax.ShapeDtypeStruct(protos[0].shape, protos[0].dtype))
        passed = passed[1:]
    else:
        ins.append(before)
    return call(
        functools.partial(stats_kernel, before is None), "stats_part", info, (1,), ins,
        [whole(value) for value in ins], outs, [whole(out) for out in outs], [],
        4 * rows * count * dim, 2 * rows * count, 6, passed,
    )


def offset_kernel(info, stats, other, out):
    count = stats.shape[0] // 2
    for j in range(2 * count):
        here, there = stats[j], other[(j + count) % (2 * count)]
        peak = jnp.maximum(here[0:1], there[0:1])
        mass = here[1:2] * jnp.exp2((here[0:1] - peak) * code_scale) + there[1:2] * jnp.exp2(
            (there[0:1] - peak) * code_scale
        )
        offset = peak * code_scale + jnp.log2(mass)
        out[j] = jnp.broadcast_to(offset, out.shape[1:])


def offset_part(info, stats, other):
    return call(
        offset_kernel, "offset_part", info, (1,), [stats, other], [whole(stats)] * 2, [stats],
        [whole(stats)], [], 1 << 20, 0, 5,
    )


def weighted(value, protos):
    return jnp.dot(bare(value), protos, preferred_element_type=jnp.float32)


def row_of(combine, value):
    return combine(value.T, axis=0, keepdims=True)


def pred_logits(preds, protos, raws, top, j):
    raw = scores(preds[...], protos)
    raws[j] = raw
    top[...] = jnp.maximum(top[...], lane_fold(jnp.maximum, raw))


def pred_pull(protos, raws, top, total, pull):
    width = raws.shape[2]
    stats = [row_of(jnp.max, top[...]) * pred_scale]
    peak = jnp.max(top[...], axis=1, keepdims=True)
    top[...] = jnp.broadcast_to(peak, top.shape)
    total[...] = jnp.zeros(total.shape, jnp.float32)
    pull[...] = jnp.zeros(pull.shape, jnp.float32)

    def step(j, protos):
        peak = jnp.concatenate([top[...]] * (width // 128), axis=1)
        value = jnp.exp2((raws[j] - peak) * pred_scale)
        total[...] += lane_fold(jnp.add, value)
        pull[...] += weighted(value, protos)

    over_chunks(protos, width, step)
    return pull[...], [*stats, row_of(jnp.sum, total[...])]


def target_step(codes, protos, offset, total, pull, j):
    value = jnp.exp2(scores(codes[...], protos) * code_scale - offset[j, 0:1, :])
    total[...] += lane_fold(jnp.add, value)
    pull[...] += weighted(value, protos)


def target_stats(preds, total, pull):
    cross = lane_fold(jnp.add, pull[...] * preds[...].astype(jnp.float32))
    return [row_of(jnp.sum, total[...]), row_of(jnp.sum, cross)]


def pred_kernel(info, preds, near, across, *refs):
    *outs, raws, top, total, pull, flipped = refs
    protos = near, across
    top[...] = jnp.full(top.shape, low, jnp.float32)
    over_chunks(protos, raws.shape[2], lambda j, part: pred_logits(preds, part, raws, top, j))
    send(info, 0, *pred_pull(protos, raws, top, total, pull), outs, flipped)


def target_kernel(info, codes, preds, near, across, offset, *refs):
    *refs, total, pull, flipped = refs
    earlier, outs = refs[: len(refs) // 2], refs[len(refs) // 2 :]
    total[...] = jnp.zeros(total.shape, jnp.float32)
    pull[...] = jnp.zeros(pull.shape, jnp.float32)
    over_chunks(
        (near, across),
        offset.shape[2],
        lambda j, part: target_step(codes, part, offset, total, pull, j),
        True,
    )
    send(info, 0, pull[...], target_stats(preds, total, pull), outs, flipped)
    for part, out in zip(earlier, outs):
        out[part.shape[0] :, :] = part[...]


def both_kernel(proto_count, info, *refs):
    *quarters, preds, near, across, offset = refs[: proto_count + 4]
    outs = refs[proto_count + 4 : -6]
    raws, top, total, pull, flipped, codes = refs[-6:]
    protos = near, across
    placed_rows(info, quarters, codes)
    top[...] = jnp.full(top.shape, low, jnp.float32)
    total[...] = jnp.zeros(total.shape, jnp.float32)
    pull[...] = jnp.zeros(pull.shape, jnp.float32)

    def step(j, part):
        pred_logits(preds, part, raws, top, j)
        target_step(codes, part, offset, total, pull, j)

    over_chunks(protos, offset.shape[2], step)
    send(info, 0, pull[...], target_stats(preds, total, pull), outs, flipped)
    send(info, 1, *pred_pull(protos, raws, top, total, pull), outs, flipped)


def rows_part(info, codes, preds, protos, offset, rows, proto_count, away, earlier):
    count, dim = protos[0].shape
    share = dim // proto_count
    width = min(chunk, count)
    shapes = [(2 * count // width, rows, width), (rows, 128), (rows, 128), (rows, dim), (dim, rows)]
    scratch = [pltpu.VMEM(shape, jnp.float32) for shape in shapes]
    if codes is None:
        kernel, ins, passed = pred_kernel, [preds, *protos], (1, 2)
        specs = [whole(value) for value in ins]
    elif not away:
        kernel, ins, passed = target_kernel, [codes, preds, *protos, offset, *earlier], ()
        specs, scratch = [whole(value) for value in ins], scratch[2:]
    else:
        kernel, ins = functools.partial(both_kernel, proto_count), [*codes, preds, *protos, offset]
        passed = tuple(len(codes) + i for i in range(3))
        quarter = pl.BlockSpec((1, *codes[0].shape[1:]), lambda i, info: (away - 1, 0, 0))
        block = pl.BlockSpec((rows, dim), lambda i, info: (info[0] ^ away, 0))
        specs = [quarter] * len(codes) + [block] + [whole(value) for value in ins[-3:]]
        scratch = [*scratch, pltpu.VMEM((rows, dim), jnp.bfloat16)]
    parts, work = 2 if codes is not None else 1, 2 if away else 1
    high, tall = parts * (share + stat_rows), parts * (share + sent_rows)
    outs = [jax.ShapeDtypeStruct((high, rows), jnp.float32)]
    outs += [jax.ShapeDtypeStruct((tall, rows), jnp.bfloat16)] * (proto_count - 1)
    return call(
        kernel, "rows_part", info, (1,), ins, specs, outs, [whole(out) for out in outs], scratch,
        work * 8 * rows * count * dim, work * 2 * rows * count,
        6 if kernel is target_kernel else 14, passed,
    )


names = ["target", "pred"]


def packed_far(target, pred):
    pull, stats = pred
    high = bare(pull)
    rest = bare(pull - high.astype(jnp.float32))
    return jnp.concatenate([bare(target[0]), high, rest, split_stats([*target[1], *stats])], axis=0)


def parted_far(value):
    share = (value.shape[0] - sent_rows) // 3
    target, high, rest = [
        value[i * share : (i + 1) * share, :].astype(jnp.float32) for i in range(3)
    ]
    stats = join_stats(value[3 * share :, :], 4)
    return {"target": (target, stats[:2]), "pred": (high + rest, stats[2:])}


def joined(parts, others=()):
    kept, *sent = parts
    high, tall = kept.shape[0] // len(names), sent[0].shape[0] // len(names)
    return [
        joins[name](
            [parted(kept[i * high : (i + 1) * high, :])]
            + [parted_sent(part[i * tall : (i + 1) * tall, :]) for part in sent]
            + [part[name] for part in others]
        )
        for i, name in enumerate(names)
    ]


def spread_kernel(info, *refs):
    *parts, out = refs
    out[...] = packed_far(*joined(parts))


def join_spread(info, parts):
    high, rows = parts[0].shape
    share = high // len(names) - stat_rows
    out = jax.ShapeDtypeStruct((3 * share + sent_rows, rows), jnp.bfloat16)
    return call(
        spread_kernel, "join_spread", info, (1,), parts, [whole(part) for part in parts], [out],
        [whole(out)], [], 1 << 20, 0, 5,
    )


def final_kernel(count, info, *refs):
    parts, far, (loss, pull) = refs[:count], refs[count:-2], refs[-2:]
    far = [parted_far(part[...]) for part in far]
    (target, (mass, cross)), (pred, (peak, total)) = joined(parts, far)
    pull[...] = target / mass - pred / total
    loss[...] = peak * log2 + jnp.log(total) - cross / mass / pred_temp


def finish(info, own, others):
    high, length = own[0].shape
    outs = [
        jax.ShapeDtypeStruct((1, length), jnp.float32),
        jax.ShapeDtypeStruct((high // len(names) - stat_rows, length), jnp.float32),
    ]
    ins = [*own, *others]
    return call(
        functools.partial(final_kernel, len(own)), "finish", info, (1,), ins,
        [whole(value) for value in ins], outs, [whole(out) for out in outs], [], 1 << 20, 0, 5,
    )[1:]


def swap(value, axis, bits):
    count = lax.axis_size(axis)
    return lax.ppermute(value, axis, [(i, i ^ bits) for i in range(count)])


def body(codes_view, pred_view, prototypes):
    rows = codes_view.shape[0]
    dp_count, proto_count = lax.axis_size("dp"), lax.axis_size("proto")
    z_count = dp_count // 2
    me, proto = lax.axis_index("dp"), lax.axis_index("proto")
    info = jnp.stack([me // 2, proto]).astype(jnp.int32)
    same_core = [[2 * z + core for z in range(z_count)] for core in range(2)]

    def sent(values):
        return [values[0]] + [swap(value, "proto", s) for s, value in enumerate(values[1:], 1)]

    protos = prototypes, swap(prototypes, "dp", 1)
    part = rows // proto_count
    piece = lax.dynamic_slice_in_dim(codes_view, proto * part, part, 0)
    quarters = [swap(piece, "dp", 2 * t) for t in range(1, z_count)]
    preds = lax.all_gather(pred_view, "dp", axis=0, tiled=True, axis_index_groups=same_core)

    info, stats, *protos = stats_part(info, [codes_view], protos, None)
    quarters, info = lax.optimization_barrier((quarters, info))
    quarters = jnp.stack(quarters)
    others = [swap(quarters, "proto", s) for s in range(1, proto_count)]
    info, *values = rows_part(info, None, pred_view, protos, None, rows, proto_count, 0, None)
    *earlier, near, across = values
    info, stats, *protos = stats_part(info, [quarters], (near, across), stats)
    info, stats, *protos = stats_part(info, others, protos, stats)
    codes = [quarters, *others]
    info, offset = offset_part(info, stats, swap(stats, "dp", 1))

    far, waiting = [], []
    for away in range(z_count - 1, 0, -1):
        info, *values = rows_part(
            info, codes, preds, protos, offset, rows, proto_count, away, None
        )
        *out, preds, near, across = values
        protos = near, across
        out = sent(out)
        for past, arrived in waiting:
            if far:
                far, arrived = lax.optimization_barrier((far, arrived))
            info, part = join_spread(info, arrived)
            far.append(swap(part, "dp", 2 * past))
        waiting = [(away, out)]
    info, *out = rows_part(
        info, codes_view, pred_view, protos, offset, rows, proto_count, 0, earlier
    )
    own = sent(out)
    ((past, arrived),) = waiting
    far, arrived = lax.optimization_barrier((far, arrived))
    info, part = join_spread(info, arrived)
    own, part = lax.optimization_barrier((own, part))
    loss, pull = finish(info, own, [*far, swap(part, "dp", 2 * past)])
    return (loss.reshape(rows), pull.T)


def solution(mesh):
    placed = (P("dp", None), P("dp", None), P(("proto", "dp"), None))
    return jax.shard_map(
        body, mesh=mesh, in_specs=placed, out_specs=(P("dp"), P("dp", "proto")), check_vma=False
    )
```

time: 121 us -> 108 us (0.89)
  waiting for transfers between devices: 21.6 us -> 12.3 us
  local copies, waits for them, and re-layouts: 11.4 us -> 2.7 us
  starting transfers between devices: 24.4 us -> 28.7 us
    ppermute x14 -> x23, starting transfers between devices: 16.9 us -> 28.6 us  [swap(): return lax.ppermute(value, axis, [(i, i ^ bits) for i in range(count)])]
    unnamed x60 -> x24, local copies, waits for them, and re-layouts: 10.6 us -> 2.69 us
    all_to_all x2 -> x0, starting transfers between devices: 7.46 us -> none  [far_rows(): return (info, kept, lax.all_to_all(out, 'proto', 0, 0))]
    ppermute x14 -> x23, waiting for transfers between devices: 17.9 us -> 11.5 us  [swap(): return lax.ppermute(value, axis, [(i, i ^ bits) for i in range(count)])]
    all_to_all x2 -> x0, waiting for transfers between devices: 3.47 us -> none  [far_rows(): return (info, kept, lax.all_to_all(out, 'proto', 0, 0))]
    pallas_call x9 -> x13, Pallas kernels: 48.9 us -> 49.4 us  [call(): pl.pallas_call(without, grid_spec=pltpu.PrefetchScalarGridSpec(num_scalar...]
  transfers between devices with their start and end apart: 17 -> 24, of which waited for: 9 -> 9; matrix products, arithmetic and copies ran while one was open for 1% -> 0% of each run, Pallas kernels for 26% -> 37%
where the time goes in v3:
time: 108 us; the launch traced here: 107 us
  Pallas kernels  49.4 us (46%)
  starting transfers between devices  28.7 us (27%)
  between operations  14.3 us (13%)
  waiting for transfers between devices  12.3 us (11%)
  local copies, waits for them, and re-layouts  2.7 us (2%)
    pallas_call x13, Pallas kernels, call(): pl.pallas_call(without, grid_spec=pltpu.PrefetchScalarGridSpec(num_scalar...  49.4 us
    ppermute x23, starting transfers between devices, swap(): return lax.ppermute(value, axis, [(i, i ^ bits) for i in range(count)])  28.6 us
    ppermute x23, waiting for transfers between devices, swap(): return lax.ppermute(value, axis, [(i, i ^ bits) for i in range(count)])  11.5 us
    unnamed x24, local copies, waits for them, and re-layouts  2.69 us
  transfers between devices with their start and end apart: 24, of which 9 were waited for; matrix products, arithmetic and copies ran while one was open for 0% of the time, Pallas kernels for 37%

profile of v3, /device:TPU:0, one launch (start us, length us, event | category | flops | bytes accessed | tf_op | source)
XLA Modules:
  0.0 107.5 jit_solution(16190530949774330821)
XLA Ops:
  7.2 0.5 collective-permute-start.3
  7.7 0.2 all-gather.2.cloned.1.call-update
  7.9 0.2 copy-done.1
  8.1 5.0 %collective-permute-start.2 = (bf16[128,256]{1,0:T(8,128)(2,1)S(1)}, bf16[128,256]{1,0:T(8,128)(2,1)S(1)}, u32[]{:S(2)}, u32[]{:S(2)}) collective-permute-start(bf16[128,256]{1,0:T(8,128)(2,1)S(1)} %constant_dynamic-slice_fusion), channel_id=1, source_target_pairs={{0,24},{4,28},{8,16},{12,20},{16,8},{20,12},{24,0},{28,4},{1,25},{... | collective-permute-start | bytes 196616 | tf_op jit(solution)/shard_map/ppermute | solution.py:412
  13.2 0.6 collective-permute-start
  13.8 0.1 pad_add_fusion.refs_0_
  13.9 1.2 %copy-done.2 = bf16[2048,256]{1,0:T(8,128)(2,1)S(1)} copy-done((bf16[2048,256]{1,0:T(8,128)(2,1)S(1)}, bf16[2048,256]{1,0:T(8,128)(2,1)}, u32[]{:S(2)}) %copy-start.2) | copy-done | bytes 1048600
  15.1 3.3 %stats_part.3 = (f32[8,8,512]{2,1,0:T(8,128)S(1)}, bf16[2048,256]{1,0:T(8,128)(2,1)S(1)}, bf16[2048,256]{1,0:T(8,128)(2,1)S(1)}) custom-call(s32[2]{0:T(128)S(1)} %pad_add_fusion.refs_0_, bf16[512,256]{1,0:T(8,128)(2,1)S(1)} %copy-done.1, bf16[2048,256]{1,0:T(8,128)(2,1)S(1)} %copy-done.2, ...), custom_call_target="tpu_custom_call", output_to_operand_aliasing={{2}: (3, {})} | custom-call | flops 1073741824 | bytes 8388608 | tf_op jit(solution)/shard_map/stats_part/pallas_call | solution.py:121
  18.5 0.3 collective-permute-done.1
  18.8 2.5 %collective-permute-start.6 = (bf16[3,128,256]{2,1,0:T(8,128)(2,1)S(1)}, bf16[3,128,256]{2,1,0:T(8,128)(2,1)S(1)}, u32[]{:S(2)}, u32[]{:S(2)}) collective-permute-start(bf16[3,128,256]{2,1,0:T(8,128)(2,1)S(1)} %pad_maximum_fusion.refs_1_), channel_id=1, source_target_pairs={{0,3},{1,2},{2,1},{3,0},{4,7},{5,6},{6,5},{7,4},{8,11},{9,10},{10,... | collective-permute-start | bytes 589832 | tf_op jit(solution)/shard_map/ppermute | solution.py:412
  21.3 0.5 collective-permute-start.5
  21.8 0.5 collective-permute-start.4
  22.4 5.1 %rows_part.5 = (f32[72,512]{1,0:T(8,128)S(1)}, bf16[80,512]{1,0:T(8,128)(2,1)S(1)}, bf16[80,512]{1,0:T(8,128)(2,1)S(1)}, bf16[80,512]{1,0:T(8,128)(2,1)S(1)}, bf...) custom-call(s32[2]{0:T(128)S(1)} %pad_add_fusion.refs_0_, ...), custom_call_target="tpu_custom_call", output_to_operand_aliasing={{4}: (2, {}), {5}: (3, {})} | custom-call | flops 2147483648 | bytes 16777216 | tf_op jit(solution)/shard_map/rows_part/pallas_call | solution.py:121
  27.5 2.7 %stats_part.4 = (f32[8,8,512]{2,1,0:T(8,128)S(1)}, bf16[2048,256]{1,0:T(8,128)(2,1)S(1)}, bf16[2048,256]{1,0:T(8,128)(2,1)S(1)}) custom-call(s32[2]{0:T(128)S(1)} %pad_add_fusion.refs_0_, bf16[3,128,256]{2,1,0:T(8,128)(2,1)S(1)} %pad_maximum_fusion.refs_1_, ...), custom_call_target="tpu_custom_call", output_to_operand_aliasing={{1}: (2, {}), {2}: (3, {})} | custom-call | flops 805306368 | bytes 6291456 | tf_op jit(solution)/shard_map/stats_part/pallas_call | solution.py:121
  30.3 0.2 collective-permute-done.5.refs_2_.refs_3_
  30.5 0.3 collective-permute-done.4.refs_1_.refs_2_
  30.7 6.8 %stats_part.5 = (f32[8,8,512]{2,1,0:T(8,128)S(1)}, bf16[2048,256]{1,0:T(8,128)(2,1)S(1)}, bf16[2048,256]{1,0:T(8,128)(2,1)S(1)}) custom-call(s32[2]{0:T(128)S(1)} %pad_add_fusion.refs_0_, bf16[3,128,256]{2,1,0:T(8,128)(2,1)S(1)} %collective-permute-done.4.refs_1_.refs_2_, ...), custom_call_target="tpu_custom_call", output_to_operand_aliasing={{1}: (4, {}), {2}: (5, {})} | custom-call | flops 2415919104 | bytes 18874368 | tf_op jit(solution)/shard_map/stats_part/pallas_call | solution.py:121
  37.6 1.3 %collective-permute-done.7.refs_2_ = f32[8,8,512]{2,1,0:T(8,128)S(1)} collective-permute-done((f32[8,8,512]{2,1,0:T(8,128)S(1)}, f32[8,8,512]{2,1,0:T(8,128)S(1)}, u32[]{:S(2)}, u32[]{:S(2)}) %collective-permute-start.7) | collective-permute-done | bytes 131104 | tf_op jit(solution)/shard_map/ppermute | solution.py:412
  39.0 0.6 offset_part.1.refs_8_.refs_5_
  39.6 0.7 all-gather.2.cloned.1.call-done.refs_5_
  40.2 1.2 %copy-done.3 = bf16[2048,256]{1,0:T(8,128)(2,1)S(1)} copy-done((bf16[2048,256]{1,0:T(8,128)(2,1)S(1)}, bf16[2048,256]{1,0:T(8,128)(2,1)}, u32[]{:S(2)}) %copy-start.3) | copy-done | bytes 1048600
  41.5 8.0 %rows_part.6 = (f32[144,512]{1,0:T(8,128)S(1)}, bf16[160,512]{1,0:T(8,128)(2,1)S(1)}, bf16[160,512]{1,0:T(8,128)(2,1)S(1)}, bf16[160,512]{1,0:T(8,128)(2,1)S(1)}...) custom-call(s32[2]{0:T(128)S(1)} %pad_add_fusion.refs_0_, ...), custom_call_target="tpu_custom_call", output_to_operand_aliasing={{4}: (5, {}), {5}: (6, {}), {6}: (7, {})} | custom-call | flops 4294967296 | bytes 33554432 | tf_op jit(solution)/shard_map/rows_part/pallas_call | solution.py:121
  49.4 1.5 %collective-permute-start.8 = (bf16[160,512]{1,0:T(8,128)(2,1)S(1)}, bf16[160,512]{1,0:T(8,128)(2,1)S(1)}, u32[]{:S(2)}, u32[]{:S(2)}) collective-permute-start(bf16[160,512]{1,0:T(8,128)(2,1)S(1)} %get-tuple-element.121), channel_id=1, source_target_pairs={{0,1},{1,0},{2,3},{3,2},{4,5},{5,4},{6,7},{7,6},{8,9},{9,8},{10,11... | collective-permute-start | bytes 491528 | tf_op jit(solution)/shard_map/ppermute | solution.py:412
  51.0 1.5 %collective-permute-start.9 = (bf16[160,512]{1,0:T(8,128)(2,1)S(1)}, bf16[160,512]{1,0:T(8,128)(2,1)S(1)}, u32[]{:S(2)}, u32[]{:S(2)}) collective-permute-start(bf16[160,512]{1,0:T(8,128)(2,1)S(1)} %get-tuple-element.122), channel_id=1, source_target_pairs={{0,2},{1,3},{2,0},{3,1},{4,6},{5,7},{6,4},{7,5},{8,10},{9,11},{10,... | collective-permute-start | bytes 491528 | tf_op jit(solution)/shard_map/ppermute | solution.py:412
  52.4 0.5 collective-permute-start.10
  53.0 8.2 %rows_part.7 = (f32[144,512]{1,0:T(8,128)S(1)}, bf16[160,512]{1,0:T(8,128)(2,1)S(1)}, bf16[160,512]{1,0:T(8,128)(2,1)S(1)}, bf16[160,512]{1,0:T(8,128)(2,1)S(1)}...) custom-call(s32[2]{0:T(128)S(1)} %pad_add_fusion.refs_0_, ...), custom_call_target="tpu_custom_call", output_to_operand_aliasing={{4}: (5, {}), {5}: (6, {}), {6}: (7, {})} | custom-call | flops 4294967296 | bytes 33554432 | tf_op jit(solution)/shard_map/rows_part/pallas_call | solution.py:121
  61.2 1.5 %collective-permute-start.12 = (bf16[160,512]{1,0:T(8,128)(2,1)S(1)}, bf16[160,512]{1,0:T(8,128)(2,1)S(1)}, u32[]{:S(2)}, u32[]{:S(2)}) collective-permute-start(bf16[160,512]{1,0:T(8,128)(2,1)S(1)} %get-tuple-element.132), channel_id=1, source_target_pairs={{0,1},{1,0},{2,3},{3,2},{4,5},{5,4},{6,7},{7,6},{8,9},{9,8},{10,11... | collective-permute-start | bytes 491528 | tf_op jit(solution)/shard_map/ppermute | solution.py:412
  62.7 1.5 %collective-permute-start.13 = (bf16[160,512]{1,0:T(8,128)(2,1)S(1)}, bf16[160,512]{1,0:T(8,128)(2,1)S(1)}, u32[]{:S(2)}, u32[]{:S(2)}) collective-permute-start(bf16[160,512]{1,0:T(8,128)(2,1)S(1)} %get-tuple-element.133), channel_id=1, source_target_pairs={{0,2},{1,3},{2,0},{3,1},{4,6},{5,7},{6,4},{7,5},{8,10},{9,11},{10,... | collective-permute-start | bytes 491528 | tf_op jit(solution)/shard_map/ppermute | solution.py:412
  64.2 0.5 collective-permute-start.14
  64.8 0.7 join_spread.3
  65.5 2.5 %collective-permute-start.11 = (bf16[208,512]{1,0:T(8,128)(2,1)S(1)}, bf16[208,512]{1,0:T(8,128)(2,1)S(1)}, u32[]{:S(2)}, u32[]{:S(2)}) collective-permute-start(bf16[208,512]{1,0:T(8,128)(2,1)S(1)} %join_spread.3), channel_id=1, source_target_pairs={{0,24},{4,28},{8,16},{12,20},{16,8},{20,12},{24,0},{28,4},{1,25},{... | collective-permute-start | bytes 638984 | tf_op jit(solution)/shard_map/ppermute | solution.py:412
  67.9 8.0 %rows_part.8 = (f32[144,512]{1,0:T(8,128)S(1)}, bf16[160,512]{1,0:T(8,128)(2,1)S(1)}, bf16[160,512]{1,0:T(8,128)(2,1)S(1)}, bf16[160,512]{1,0:T(8,128)(2,1)S(1)}...) custom-call(s32[2]{0:T(128)S(1)} %pad_add_fusion.refs_0_, ...), custom_call_target="tpu_custom_call", output_to_operand_aliasing={{4}: (5, {}), {5}: (6, {}), {6}: (7, {})} | custom-call | flops 4294967296 | bytes 33554432 | tf_op jit(solution)/shard_map/rows_part/pallas_call | solution.py:121
  75.9 1.6 %collective-permute-start.16 = (bf16[160,512]{1,0:T(8,128)(2,1)S(1)}, bf16[160,512]{1,0:T(8,128)(2,1)S(1)}, u32[]{:S(2)}, u32[]{:S(2)}) collective-permute-start(bf16[160,512]{1,0:T(8,128)(2,1)S(1)} %get-tuple-element.151), channel_id=1, source_target_pairs={{0,1},{1,0},{2,3},{3,2},{4,5},{5,4},{6,7},{7,6},{8,9},{9,8},{10,11... | collective-permute-start | bytes 491528 | tf_op jit(solution)/shard_map/ppermute | solution.py:412
  77.5 1.5 %collective-permute-start.17 = (bf16[160,512]{1,0:T(8,128)(2,1)S(1)}, bf16[160,512]{1,0:T(8,128)(2,1)S(1)}, u32[]{:S(2)}, u32[]{:S(2)}) collective-permute-start(bf16[160,512]{1,0:T(8,128)(2,1)S(1)} %get-tuple-element.152), channel_id=1, source_target_pairs={{0,2},{1,3},{2,0},{3,1},{4,6},{5,7},{6,4},{7,5},{8,10},{9,11},{10,... | collective-permute-start | bytes 491528 | tf_op jit(solution)/shard_map/ppermute | solution.py:412
  79.0 0.5 collective-permute-start.18
  79.6 0.7 join_spread.4
  80.3 0.6 collective-permute-start.15
  80.8 3.2 %rows_part.9 = (f32[144,512]{1,0:T(8,128)S(1)}, bf16[160,512]{1,0:T(8,128)(2,1)S(1)}, bf16[160,512]{1,0:T(8,128)(2,1)S(1)}, bf16[160,512]{1,0:T(8,128)(2,1)S(1)}) custom-call(s32[2]{0:T(128)S(1)} %pad_add_fusion.refs_0_, bf16[512,256]{1,0:T(8,128)(2,1)S(1)} %copy-done.1, bf16[512,256]{1,0:T(8,128)(2,1)S(1)} %copy-done, ...), custom_call_target="tpu_custom_call" | custom-call | flops 2147483648 | bytes 16777216 | tf_op jit(solution)/shard_map/rows_part/pallas_call | solution.py:121
  84.1 1.5 %collective-permute-start.19 = (bf16[160,512]{1,0:T(8,128)(2,1)S(1)}, bf16[160,512]{1,0:T(8,128)(2,1)S(1)}, u32[]{:S(2)}, u32[]{:S(2)}) collective-permute-start(bf16[160,512]{1,0:T(8,128)(2,1)S(1)} %get-tuple-element.160), channel_id=1, source_target_pairs={{0,1},{1,0},{2,3},{3,2},{4,5},{5,4},{6,7},{7,6},{8,9},{9,8},{10,11... | collective-permute-start | bytes 491528 | tf_op jit(solution)/shard_map/ppermute | solution.py:412
  85.6 1.5 %collective-permute-start.20 = (bf16[160,512]{1,0:T(8,128)(2,1)S(1)}, bf16[160,512]{1,0:T(8,128)(2,1)S(1)}, u32[]{:S(2)}, u32[]{:S(2)}) collective-permute-start(bf16[160,512]{1,0:T(8,128)(2,1)S(1)} %get-tuple-element.161), channel_id=1, source_target_pairs={{0,2},{1,3},{2,0},{3,1},{4,6},{5,7},{6,4},{7,5},{8,10},{9,11},{10,... | collective-permute-start | bytes 491528 | tf_op jit(solution)/shard_map/ppermute | solution.py:412
  87.1 0.5 collective-permute-start.21
  87.7 1.8 %collective-permute-done.15.refs_6_ = bf16[208,512]{1,0:T(8,128)(2,1)S(1)} collective-permute-done((bf16[208,512]{1,0:T(8,128)(2,1)S(1)}, bf16[208,512]{1,0:T(8,128)(2,1)S(1)}, u32[]{:S(2)}, u32[]{:S(2)}) %collective-permute-start.15) | collective-permute-done | bytes 213024 | tf_op jit(solution)/shard_map/ppermute | solution.py:412
  89.5 0.7 join_spread.5
  90.2 1.5 %collective-permute-done.20.refs_3_ = bf16[160,512]{1,0:T(8,128)(2,1)S(1)} collective-permute-done((bf16[160,512]{1,0:T(8,128)(2,1)S(1)}, bf16[160,512]{1,0:T(8,128)(2,1)S(1)}, u32[]{:S(2)}, u32[]{:S(2)}) %collective-permute-start.20) | collective-permute-done | bytes 163872 | tf_op jit(solution)/shard_map/ppermute | solution.py:412
  91.7 1.6 %collective-permute-done.21.refs_4_ = bf16[160,512]{1,0:T(8,128)(2,1)S(1)} collective-permute-done((bf16[160,512]{1,0:T(8,128)(2,1)S(1)}, bf16[160,512]{1,0:T(8,128)(2,1)S(1)}, u32[]{:S(2)}, u32[]{:S(2)}) %collective-permute-start.21) | collective-permute-done | bytes 163872 | tf_op jit(solution)/shard_map/ppermute | solution.py:412
  93.3 1.5 %collective-permute-start.22 = (bf16[208,512]{1,0:T(8,128)(2,1)S(1)}, bf16[208,512]{1,0:T(8,128)(2,1)S(1)}, u32[]{:S(2)}, u32[]{:S(2)}) collective-permute-start(bf16[208,512]{1,0:T(8,128)(2,1)S(1)} %join_spread.5), channel_id=1, source_target_pairs={{0,8},{4,12},{8,0},{12,4},{16,24},{20,28},{24,16},{28,20},{1,9},{5... | collective-permute-start | bytes 638984 | tf_op jit(solution)/shard_map/ppermute | solution.py:412
  94.8 4.4 %collective-permute-done.22.refs_7_ = bf16[208,512]{1,0:T(8,128)(2,1)S(1)} collective-permute-done((bf16[208,512]{1,0:T(8,128)(2,1)S(1)}, bf16[208,512]{1,0:T(8,128)(2,1)S(1)}, u32[]{:S(2)}, u32[]{:S(2)}) %collective-permute-start.22) | collective-permute-done | bytes 213024 | tf_op jit(solution)/shard_map/ppermute | solution.py:412
  99.2 1.5 %finish.1 = (f32[1,512]{1,0:T(1,128)}, f32[64,512]{1,0:T(8,128)}) custom-call(s32[2]{0:T(128)S(1)} %pad_add_fusion.refs_0_, f32[144,512]{1,0:T(8,128)S(1)} %get-tuple-element.164.refs_1_, bf16[160,512]{1,0:T(8,128)(2,1)S(1)} %collective-permute-done.19.refs_2_, bf16[160,512]{1,0:T(8,128)(2,1)S(1)} %collective-permute-done.20.refs_3_, ...), custom_call_target="tpu_custom_call" | custom-call | flops 1048576 | bytes 8192 | tf_op jit(solution)/shard_map/finish/pallas_call | solution.py:121
  (41 shorter events, 0.2 us)
Async XLA Ops:
  7.2 1.0 copy-start.1
  7.2 33.1 %all-gather.2.cloned.1.call-start = ((), (), s32[]{:S(2)}) async-start(), calls=%async_computation | async-start | bytes 1310720 | tf_op jit(solution)/shard_map/all_gather | solution.py:430
  7.2 6.7 %collective-permute-start.3 = (bf16[2048,256]{1,0:T(8,128)(2,1)}, bf16[2048,256]{1,0:T(8,128)(2,1)S(1)}, u32[]{:S(2)}, u32[]{:S(2)}) collective-permute-start(bf16[2048,256]{1,0:T(8,128)(2,1)} %refs_2_.2), channel_id=1, source_target_pairs={{0,4},{4,0},{8,12},{12,8},{16,20},{20,16},{24,28},{28,24},{1,5},{5... | collective-permute-start | bytes 3145736 | tf_op jit(solution)/shard_map/ppermute | solution.py:412
  8.1 10.3 %collective-permute-start.2 = (bf16[128,256]{1,0:T(8,128)(2,1)S(1)}, bf16[128,256]{1,0:T(8,128)(2,1)S(1)}, u32[]{:S(2)}, u32[]{:S(2)}) collective-permute-start(bf16[128,256]{1,0:T(8,128)(2,1)S(1)} %constant_dynamic-slice_fusion), channel_id=1, source_target_pairs={{0,24},{4,28},{8,16},{12,20},{16,8},{20,12},{24,0},{28,4},{1,25},{... | collective-permute-start | bytes 196616 | tf_op jit(solution)/shard_map/ppermute | solution.py:412
  13.2 5.6 %collective-permute-start.1 = (bf16[128,256]{1,0:T(8,128)(2,1)S(1)}, bf16[128,256]{1,0:T(8,128)(2,1)S(1)}, u32[]{:S(2)}, u32[]{:S(2)}) collective-permute-start(bf16[128,256]{1,0:T(8,128)(2,1)S(1)} %constant_dynamic-slice_fusion), channel_id=1, source_target_pairs={{0,16},{4,20},{8,24},{12,28},{16,0},{20,4},{24,8},{28,12},{1,17},{... | collective-permute-start | bytes 196616 | tf_op jit(solution)/shard_map/ppermute | solution.py:412
  13.2 5.6 %collective-permute-start = (bf16[128,256]{1,0:T(8,128)(2,1)S(1)}, bf16[128,256]{1,0:T(8,128)(2,1)S(1)}, u32[]{:S(2)}, u32[]{:S(2)}) collective-permute-start(bf16[128,256]{1,0:T(8,128)(2,1)S(1)} %constant_dynamic-slice_fusion), channel_id=1, source_target_pairs={{0,8},{4,12},{8,0},{12,4},{16,24},{20,28},{24,16},{28,20},{1,9},{5... | collective-permute-start | bytes 196616 | tf_op jit(solution)/shard_map/ppermute | solution.py:412
  13.9 1.2 %copy-start.2 = (bf16[2048,256]{1,0:T(8,128)(2,1)S(1)}, bf16[2048,256]{1,0:T(8,128)(2,1)}, u32[]{:S(2)}) copy-start(bf16[2048,256]{1,0:T(8,128)(2,1)} %refs_2_.2) | copy-start | bytes 3145732
  18.5 3.9 %copy-start = (bf16[512,256]{1,0:T(8,128)(2,1)S(1)}, bf16[512,256]{1,0:T(8,128)(2,1)}, u32[]{:S(2)}) copy-start(bf16[512,256]{1,0:T(8,128)(2,1)} %refs_2_.3) | copy-start | bytes 786436
  18.8 11.4 %collective-permute-start.6 = (bf16[3,128,256]{2,1,0:T(8,128)(2,1)S(1)}, bf16[3,128,256]{2,1,0:T(8,128)(2,1)S(1)}, u32[]{:S(2)}, u32[]{:S(2)}) collective-permute-start(bf16[3,128,256]{2,1,0:T(8,128)(2,1)S(1)} %pad_maximum_fusion.refs_1_), channel_id=1, source_target_pairs={{0,3},{1,2},{2,1},{3,0},{4,7},{5,6},{6,5},{7,4},{8,11},{9,10},{10,... | collective-permute-start | bytes 589832 | tf_op jit(solution)/shard_map/ppermute | solution.py:412
  21.3 9.1 %collective-permute-start.5 = (bf16[3,128,256]{2,1,0:T(8,128)(2,1)S(1)}, bf16[3,128,256]{2,1,0:T(8,128)(2,1)S(1)}, u32[]{:S(2)}, u32[]{:S(2)}) collective-permute-start(bf16[3,128,256]{2,1,0:T(8,128)(2,1)S(1)} %pad_maximum_fusion.refs_1_), channel_id=1, source_target_pairs={{0,2},{1,3},{2,0},{3,1},{4,6},{5,7},{6,4},{7,5},{8,10},{9,11},{10,... | collective-permute-start | bytes 589832 | tf_op jit(solution)/shard_map/ppermute | solution.py:412
  21.8 8.9 %collective-permute-start.4 = (bf16[3,128,256]{2,1,0:T(8,128)(2,1)S(1)}, bf16[3,128,256]{2,1,0:T(8,128)(2,1)S(1)}, u32[]{:S(2)}, u32[]{:S(2)}) collective-permute-start(bf16[3,128,256]{2,1,0:T(8,128)(2,1)S(1)} %pad_maximum_fusion.refs_1_), channel_id=1, source_target_pairs={{0,1},{1,0},{2,3},{3,2},{4,5},{5,4},{6,7},{7,6},{8,9},{9,8},{10,11... | collective-permute-start | bytes 589832 | tf_op jit(solution)/shard_map/ppermute | solution.py:412
  27.5 2.7 %copy-start.4 = (f32[72,512]{1,0:T(8,128)}, f32[72,512]{1,0:T(8,128)S(1)}, u32[]{:S(2)}) copy-start(f32[72,512]{1,0:T(8,128)S(1)} %get-tuple-element.142.refs_6_) | copy-start | bytes 442372
  27.5 2.7 %copy-start.6 = (bf16[80,512]{1,0:T(8,128)(2,1)}, bf16[80,512]{1,0:T(8,128)(2,1)S(1)}, u32[]{:S(2)}) copy-start(bf16[80,512]{1,0:T(8,128)(2,1)S(1)} %get-tuple-element.143.refs_7_) | copy-start | bytes 245764
  27.5 2.7 %copy-start.8 = (bf16[80,512]{1,0:T(8,128)(2,1)}, bf16[80,512]{1,0:T(8,128)(2,1)S(1)}, u32[]{:S(2)}) copy-start(bf16[80,512]{1,0:T(8,128)(2,1)S(1)} %get-tuple-element.144.refs_8_) | copy-start | bytes 245764
  27.5 2.7 %copy-start.10 = (bf16[80,512]{1,0:T(8,128)(2,1)}, bf16[80,512]{1,0:T(8,128)(2,1)S(1)}, u32[]{:S(2)}) copy-start(bf16[80,512]{1,0:T(8,128)(2,1)S(1)} %get-tuple-element.145.refs_9_) | copy-start | bytes 245764
  37.5 1.4 %collective-permute-start.7 = (f32[8,8,512]{2,1,0:T(8,128)S(1)}, f32[8,8,512]{2,1,0:T(8,128)S(1)}, u32[]{:S(2)}, u32[]{:S(2)}) collective-permute-start(f32[8,8,512]{2,1,0:T(8,128)S(1)} %get-tuple-element.108.refs_1_), channel_id=1, source_target_pairs={{0,4},{4,0},{8,12},{12,8},{16,20},{20,16},{24,28},{28,24},{1,5},{5... | collective-permute-start | bytes 393224 | tf_op jit(solution)/shard_map/ppermute | solution.py:412
  40.2 1.2 %copy-start.3 = (bf16[2048,256]{1,0:T(8,128)(2,1)S(1)}, bf16[2048,256]{1,0:T(8,128)(2,1)}, u32[]{:S(2)}) copy-start(bf16[2048,256]{1,0:T(8,128)(2,1)} %all-gather.2.cloned.1.call-done.refs_5_) | copy-start | bytes 3145732
  49.4 14.8 %collective-permute-start.8 = (bf16[160,512]{1,0:T(8,128)(2,1)S(1)}, bf16[160,512]{1,0:T(8,128)(2,1)S(1)}, u32[]{:S(2)}, u32[]{:S(2)}) collective-permute-start(bf16[160,512]{1,0:T(8,128)(2,1)S(1)} %get-tuple-element.121), channel_id=1, source_target_pairs={{0,1},{1,0},{2,3},{3,2},{4,5},{5,4},{6,7},{7,6},{8,9},{9,8},{10,11... | collective-permute-start | bytes 491528 | tf_op jit(solution)/shard_map/ppermute | solution.py:412
  51.0 13.8 %collective-permute-start.9 = (bf16[160,512]{1,0:T(8,128)(2,1)S(1)}, bf16[160,512]{1,0:T(8,128)(2,1)S(1)}, u32[]{:S(2)}, u32[]{:S(2)}) collective-permute-start(bf16[160,512]{1,0:T(8,128)(2,1)S(1)} %get-tuple-element.122), channel_id=1, source_target_pairs={{0,2},{1,3},{2,0},{3,1},{4,6},{5,7},{6,4},{7,5},{8,10},{9,11},{10,... | collective-permute-start | bytes 491528 | tf_op jit(solution)/shard_map/ppermute | solution.py:412
  52.4 12.3 %collective-permute-start.10 = (bf16[160,512]{1,0:T(8,128)(2,1)S(1)}, bf16[160,512]{1,0:T(8,128)(2,1)S(1)}, u32[]{:S(2)}, u32[]{:S(2)}) collective-permute-start(bf16[160,512]{1,0:T(8,128)(2,1)S(1)} %get-tuple-element.123), channel_id=1, source_target_pairs={{0,3},{1,2},{2,1},{3,0},{4,7},{5,6},{6,5},{7,4},{8,11},{9,10},{10,... | collective-permute-start | bytes 491528 | tf_op jit(solution)/shard_map/ppermute | solution.py:412
  61.2 16.3 %collective-permute-start.12 = (bf16[160,512]{1,0:T(8,128)(2,1)S(1)}, bf16[160,512]{1,0:T(8,128)(2,1)S(1)}, u32[]{:S(2)}, u32[]{:S(2)}) collective-permute-start(bf16[160,512]{1,0:T(8,128)(2,1)S(1)} %get-tuple-element.132), channel_id=1, source_target_pairs={{0,1},{1,0},{2,3},{3,2},{4,5},{5,4},{6,7},{7,6},{8,9},{9,8},{10,11... | collective-permute-start | bytes 491528 | tf_op jit(solution)/shard_map/ppermute | solution.py:412
  62.7 16.3 %collective-permute-start.13 = (bf16[160,512]{1,0:T(8,128)(2,1)S(1)}, bf16[160,512]{1,0:T(8,128)(2,1)S(1)}, u32[]{:S(2)}, u32[]{:S(2)}) collective-permute-start(bf16[160,512]{1,0:T(8,128)(2,1)S(1)} %get-tuple-element.133), channel_id=1, source_target_pairs={{0,2},{1,3},{2,0},{3,1},{4,6},{5,7},{6,4},{7,5},{8,10},{9,11},{10,... | collective-permute-start | bytes 491528 | tf_op jit(solution)/shard_map/ppermute | solution.py:412
  64.2 15.4 %collective-permute-start.14 = (bf16[160,512]{1,0:T(8,128)(2,1)S(1)}, bf16[160,512]{1,0:T(8,128)(2,1)S(1)}, u32[]{:S(2)}, u32[]{:S(2)}) collective-permute-start(bf16[160,512]{1,0:T(8,128)(2,1)S(1)} %get-tuple-element.134), channel_id=1, source_target_pairs={{0,3},{1,2},{2,1},{3,0},{4,7},{5,6},{6,5},{7,4},{8,11},{9,10},{10,... | collective-permute-start | bytes 491528 | tf_op jit(solution)/shard_map/ppermute | solution.py:412
  65.5 14.1 %collective-permute-start.11 = (bf16[208,512]{1,0:T(8,128)(2,1)S(1)}, bf16[208,512]{1,0:T(8,128)(2,1)S(1)}, u32[]{:S(2)}, u32[]{:S(2)}) collective-permute-start(bf16[208,512]{1,0:T(8,128)(2,1)S(1)} %join_spread.3), channel_id=1, source_target_pairs={{0,24},{4,28},{8,16},{12,20},{16,8},{20,12},{24,0},{28,4},{1,25},{... | collective-permute-start | bytes 638984 | tf_op jit(solution)/shard_map/ppermute | solution.py:412
  75.9 9.7 %collective-permute-start.16 = (bf16[160,512]{1,0:T(8,128)(2,1)S(1)}, bf16[160,512]{1,0:T(8,128)(2,1)S(1)}, u32[]{:S(2)}, u32[]{:S(2)}) collective-permute-start(bf16[160,512]{1,0:T(8,128)(2,1)S(1)} %get-tuple-element.151), channel_id=1, source_target_pairs={{0,1},{1,0},{2,3},{3,2},{4,5},{5,4},{6,7},{7,6},{8,9},{9,8},{10,11... | collective-permute-start | bytes 491528 | tf_op jit(solution)/shard_map/ppermute | solution.py:412
  77.5 9.6 %collective-permute-start.17 = (bf16[160,512]{1,0:T(8,128)(2,1)S(1)}, bf16[160,512]{1,0:T(8,128)(2,1)S(1)}, u32[]{:S(2)}, u32[]{:S(2)}) collective-permute-start(bf16[160,512]{1,0:T(8,128)(2,1)S(1)} %get-tuple-element.152), channel_id=1, source_target_pairs={{0,2},{1,3},{2,0},{3,1},{4,6},{5,7},{6,4},{7,5},{8,10},{9,11},{10,... | collective-permute-start | bytes 491528 | tf_op jit(solution)/shard_map/ppermute | solution.py:412
  79.0 1.8 %copy-start.5 = (f32[72,512]{1,0:T(8,128)S(1)}, f32[72,512]{1,0:T(8,128)}, u32[]{:S(2)}) copy-start(f32[72,512]{1,0:T(8,128)} %copy-done.4) | copy-start | bytes 442372
  79.0 1.8 %copy-start.7 = (bf16[80,512]{1,0:T(8,128)(2,1)S(1)}, bf16[80,512]{1,0:T(8,128)(2,1)}, u32[]{:S(2)}) copy-start(bf16[80,512]{1,0:T(8,128)(2,1)} %copy-done.6) | copy-start | bytes 245764
  79.0 1.8 %copy-start.9 = (bf16[80,512]{1,0:T(8,128)(2,1)S(1)}, bf16[80,512]{1,0:T(8,128)(2,1)}, u32[]{:S(2)}) copy-start(bf16[80,512]{1,0:T(8,128)(2,1)} %copy-done.8) | copy-start | bytes 245764
  79.0 1.8 %copy-start.11 = (bf16[80,512]{1,0:T(8,128)(2,1)S(1)}, bf16[80,512]{1,0:T(8,128)(2,1)}, u32[]{:S(2)}) copy-start(bf16[80,512]{1,0:T(8,128)(2,1)} %copy-done.10) | copy-start | bytes 245764
  79.0 8.6 %collective-permute-start.18 = (bf16[160,512]{1,0:T(8,128)(2,1)S(1)}, bf16[160,512]{1,0:T(8,128)(2,1)S(1)}, u32[]{:S(2)}, u32[]{:S(2)}) collective-permute-start(bf16[160,512]{1,0:T(8,128)(2,1)S(1)} %get-tuple-element.153), channel_id=1, source_target_pairs={{0,3},{1,2},{2,1},{3,0},{4,7},{5,6},{6,5},{7,4},{8,11},{9,10},{10,... | collective-permute-start | bytes 491528 | tf_op jit(solution)/shard_map/ppermute | solution.py:412
  80.3 9.2 %collective-permute-start.15 = (bf16[208,512]{1,0:T(8,128)(2,1)S(1)}, bf16[208,512]{1,0:T(8,128)(2,1)S(1)}, u32[]{:S(2)}, u32[]{:S(2)}) collective-permute-start(bf16[208,512]{1,0:T(8,128)(2,1)S(1)} %join_spread.4), channel_id=1, source_target_pairs={{0,16},{4,20},{8,24},{12,28},{16,0},{20,4},{24,8},{28,12},{1,17},{... | collective-permute-start | bytes 638984 | tf_op jit(solution)/shard_map/ppermute | solution.py:412
  84.1 6.1 %collective-permute-start.19 = (bf16[160,512]{1,0:T(8,128)(2,1)S(1)}, bf16[160,512]{1,0:T(8,128)(2,1)S(1)}, u32[]{:S(2)}, u32[]{:S(2)}) collective-permute-start(bf16[160,512]{1,0:T(8,128)(2,1)S(1)} %get-tuple-element.160), channel_id=1, source_target_pairs={{0,1},{1,0},{2,3},{3,2},{4,5},{5,4},{6,7},{7,6},{8,9},{9,8},{10,11... | collective-permute-start | bytes 491528 | tf_op jit(solution)/shard_map/ppermute | solution.py:412
  85.6 6.1 %collective-permute-start.20 = (bf16[160,512]{1,0:T(8,128)(2,1)S(1)}, bf16[160,512]{1,0:T(8,128)(2,1)S(1)}, u32[]{:S(2)}, u32[]{:S(2)}) collective-permute-start(bf16[160,512]{1,0:T(8,128)(2,1)S(1)} %get-tuple-element.161), channel_id=1, source_target_pairs={{0,2},{1,3},{2,0},{3,1},{4,6},{5,7},{6,4},{7,5},{8,10},{9,11},{10,... | collective-permute-start | bytes 491528 | tf_op jit(solution)/shard_map/ppermute | solution.py:412
  87.1 6.2 %collective-permute-start.21 = (bf16[160,512]{1,0:T(8,128)(2,1)S(1)}, bf16[160,512]{1,0:T(8,128)(2,1)S(1)}, u32[]{:S(2)}, u32[]{:S(2)}) collective-permute-start(bf16[160,512]{1,0:T(8,128)(2,1)S(1)} %get-tuple-element.162), channel_id=1, source_target_pairs={{0,3},{1,2},{2,1},{3,0},{4,7},{5,6},{6,5},{7,4},{8,11},{9,10},{10,... | collective-permute-start | bytes 491528 | tf_op jit(solution)/shard_map/ppermute | solution.py:412
  93.3 5.8 %collective-permute-start.22 = (bf16[208,512]{1,0:T(8,128)(2,1)S(1)}, bf16[208,512]{1,0:T(8,128)(2,1)S(1)}, u32[]{:S(2)}, u32[]{:S(2)}) collective-permute-start(bf16[208,512]{1,0:T(8,128)(2,1)S(1)} %join_spread.5), channel_id=1, source_target_pairs={{0,8},{4,12},{8,0},{12,4},{16,24},{20,28},{24,16},{28,20},{1,9},{5... | collective-permute-start | bytes 638984 | tf_op jit(solution)/shard_map/ppermute | solution.py:412
Sparse Core Ops, SparseCore 0:
  9.6 30.6 all-gather.1

commit v4 on v3

--- a/solution.py
+++ b/solution.py
@@ -291,11 +291,12 @@
 
 
 def both_kernel(proto_count, info, *refs):
-    *quarters, preds, near, across, offset = refs[: proto_count + 4]
-    outs = refs[proto_count + 4 : -6]
-    raws, top, total, pull, flipped, codes = refs[-6:]
+    near, across, offset = refs[2 * proto_count : 2 * proto_count + 3]
+    outs = refs[2 * proto_count + 3 : -7]
+    raws, top, total, pull, flipped, codes, preds = refs[-7:]
     protos = near, across
-    placed_rows(info, quarters, codes)
+    placed_rows(info, refs[:proto_count], codes)
+    placed_rows(info, refs[proto_count : 2 * proto_count], preds)
     top[...] = jnp.full(top.shape, low, jnp.float32)
     total[...] = jnp.zeros(total.shape, jnp.float32)
     pull[...] = jnp.zeros(pull.shape, jnp.float32)
@@ -322,12 +323,11 @@
         kernel, ins, passed = target_kernel, [codes, preds, *protos, offset, *earlier], ()
         specs, scratch = [whole(value) for value in ins], scratch[2:]
     else:
-        kernel, ins = functools.partial(both_kernel, proto_count), [*codes, preds, *protos, offset]
-        passed = tuple(len(codes) + i for i in range(3))
+        kernel, ins = functools.partial(both_kernel, proto_count), [*codes, *preds, *protos, offset]
+        passed = tuple(2 * proto_count + i for i in range(2))
         quarter = pl.BlockSpec((1, *codes[0].shape[1:]), lambda i, info: (away - 1, 0, 0))
-        block = pl.BlockSpec((rows, dim), lambda i, info: (info[0] ^ away, 0))
-        specs = [quarter] * len(codes) + [block] + [whole(value) for value in ins[-3:]]
-        scratch = [*scratch, pltpu.VMEM((rows, dim), jnp.bfloat16)]
+        specs = [quarter] * (2 * proto_count) + [whole(value) for value in ins[-3:]]
+        scratch = [*scratch] + [pltpu.VMEM((rows, dim), jnp.bfloat16)] * 2
     parts, work = 2 if codes is not None else 1, 2 if away else 1
     high, tall = parts * (share + stat_rows), parts * (share + sent_rows)
     outs = [jax.ShapeDtypeStruct((high, rows), jnp.float32)]
@@ -418,26 +418,33 @@
     z_count = dp_count // 2
     me, proto = lax.axis_index("dp"), lax.axis_index("proto")
     info = jnp.stack([me // 2, proto]).astype(jnp.int32)
-    same_core = [[2 * z + core for z in range(z_count)] for core in range(2)]
 
     def sent(values):
         return [values[0]] + [swap(value, "proto", s) for s, value in enumerate(values[1:], 1)]
 
     protos = prototypes, swap(prototypes, "dp", 1)
     part = rows // proto_count
-    piece = lax.dynamic_slice_in_dim(codes_view, proto * part, part, 0)
+    piece = jnp.concatenate(
+        [
+            lax.dynamic_slice_in_dim(view, proto * part, part, 0)
+            for view in (codes_view, pred_view)
+        ]
+    )
     quarters = [swap(piece, "dp", 2 * t) for t in range(1, z_count)]
-    preds = lax.all_gather(pred_view, "dp", axis=0, tiled=True, axis_index_groups=same_core)
+
+    def around(value):
+        return [value] + [swap(value, "proto", s) for s in range(1, proto_count)]
 
     info, stats, *protos = stats_part(info, [codes_view], protos, None)
-    quarters, info = lax.optimization_barrier((quarters, info))
-    quarters = jnp.stack(quarters)
-    others = [swap(quarters, "proto", s) for s in range(1, proto_count)]
     info, *values = rows_part(info, None, pred_view, protos, None, rows, proto_count, 0, None)
     *earlier, near, across = values
-    info, stats, *protos = stats_part(info, [quarters], (near, across), stats)
-    info, stats, *protos = stats_part(info, others, protos, stats)
-    codes = [quarters, *others]
+    quarters, info = lax.optimization_barrier((quarters, info))
+    codes = around(jnp.stack([value[:part] for value in quarters]))
+    preds = jnp.stack([value[part:] for value in quarters])
+    info, stats, *protos = stats_part(info, codes[:1], (near, across), stats)
+    preds, info = lax.optimization_barrier((preds, info))
+    preds = around(preds)
+    info, stats, *protos = stats_part(info, codes[1:], protos, stats)
     info, offset = offset_part(info, stats, swap(stats, "dp", 1))
 
     far, waiting = [], []
@@ -445,7 +452,7 @@
         info, *values = rows_part(
             info, codes, preds, protos, offset, rows, proto_count, away, None
         )
-        *out, preds, near, across = values
+        *out, near, across = values
         protos = near, across
         out = sent(out)
         for past, arrived in waiting:
@@ -461,7 +468,6 @@
     ((past, arrived),) = waiting
     far, arrived = lax.optimization_barrier((far, arrived))
     info, part = join_spread(info, arrived)
-    own, part = lax.optimization_barrier((own, part))
     loss, pull = finish(info, own, [*far, swap(part, "dp", 2 * past)])
     return (loss.reshape(rows), pull.T)
 

time: 108 us -> 101 us (0.935)
  between operations: 14.3 us -> 0.88 us
  starting transfers between devices: 28.7 us -> 33.2 us
  waiting for transfers between devices: 12.3 us -> 14.7 us
    ppermute x23 -> x26, starting transfers between devices: 28.6 us -> 33.2 us  [swap(): return lax.ppermute(value, axis, [(i, i ^ bits) for i in range(count)])]
    ppermute x23 -> x26, waiting for transfers between devices: 11.5 us -> 14.7 us  [swap(): return lax.ppermute(value, axis, [(i, i ^ bits) for i in range(count)])]
    unnamed x24 -> x6, local copies, waits for them, and re-layouts: 2.69 us -> 1.27 us
  transfers between devices with their start and end apart: 24 -> 26, of which waited for: 9 -> 8; matrix products, arithmetic and copies ran while one was open for 0% -> 1% of each run, Pallas kernels for 37% -> 38%
where the time goes in v4:
time: 101 us
  Pallas kernels  49.3 us (49%)
  starting transfers between devices  33.2 us (33%)
  waiting for transfers between devices  14.7 us (15%)
  local copies, waits for them, and re-layouts  2.23 us (2%)
    pallas_call x13, Pallas kernels, call(): pl.pallas_call(without, grid_spec=pltpu.PrefetchScalarGridSpec(num_scalar...  49.3 us
    ppermute x26, starting transfers between devices, swap(): return lax.ppermute(value, axis, [(i, i ^ bits) for i in range(count)])  33.2 us
    ppermute x26, waiting for transfers between devices, swap(): return lax.ppermute(value, axis, [(i, i ^ bits) for i in range(count)])  14.7 us
  transfers between devices with their start and end apart: 26, of which 8 were waited for; matrix products, arithmetic and copies ran while one was open for 1% of the time, Pallas kernels for 38%

profile of v4, /device:TPU:0, one launch (start us, length us, event | category | flops | bytes accessed | tf_op | source)
XLA Modules:
  0.0 100.5 jit_solution(15320380340193271565)
XLA Ops:
  0.6 0.5 collective-permute-start.3
  1.1 0.9 constant_dynamic-slice_fusion
  2.1 4.7 %collective-permute-start.2 = (bf16[256,256]{1,0:T(8,128)(2,1)S(1)}, bf16[256,256]{1,0:T(8,128)(2,1)S(1)}, u32[]{:S(2)}, u32[]{:S(2)}) collective-permute-start(bf16[256,256]{1,0:T(8,128)(2,1)S(1)} %pad_maximum_fusion.2), channel_id=1, source_target_pairs={{0,24},{4,28},{8,16},{12,20},{16,8},{20,12},{24,0},{28,4},{1,25},{... | collective-permute-start | bytes 393224 | tf_op jit(solution)/shard_map/ppermute | solution.py:412
  6.8 0.0 collective-permute-start.1
  6.8 0.6 collective-permute-start
  7.4 0.1 pad_add_fusion.refs_0_
  7.5 1.3 %copy-done.2 = bf16[2048,256]{1,0:T(8,128)(2,1)S(1)} copy-done((bf16[2048,256]{1,0:T(8,128)(2,1)S(1)}, bf16[2048,256]{1,0:T(8,128)(2,1)}, u32[]{:S(2)}) %copy-start.2) | copy-done | bytes 1048600
  8.8 3.3 %stats_part.3 = (f32[8,8,512]{2,1,0:T(8,128)S(1)}, bf16[2048,256]{1,0:T(8,128)(2,1)S(1)}, bf16[2048,256]{1,0:T(8,128)(2,1)S(1)}) custom-call(s32[2]{0:T(128)S(1)} %pad_add_fusion.refs_0_, bf16[512,256]{1,0:T(8,128)(2,1)S(1)} %copy-done, bf16[2048,256]{1,0:T(8,128)(2,1)S(1)} %copy-done.2, ...), custom_call_target="tpu_custom_call", output_to_operand_aliasing={{2}: (3, {})} | custom-call | flops 1073741824 | bytes 8388608 | tf_op jit(solution)/shard_map/stats_part/pallas_call | solution.py:121
  12.1 5.1 %rows_part.5 = (f32[72,512]{1,0:T(8,128)S(1)}, bf16[80,512]{1,0:T(8,128)(2,1)S(1)}, bf16[80,512]{1,0:T(8,128)(2,1)S(1)}, bf16[80,512]{1,0:T(8,128)(2,1)S(1)}, bf...) custom-call(s32[2]{0:T(128)S(1)} %pad_add_fusion.refs_0_, ...), custom_call_target="tpu_custom_call", output_to_operand_aliasing={{4}: (2, {}), {5}: (3, {})} | custom-call | flops 2147483648 | bytes 16777216 | tf_op jit(solution)/shard_map/rows_part/pallas_call | solution.py:121
  17.2 1.3 %collective-permute-done.1 = bf16[256,256]{1,0:T(8,128)(2,1)S(1)} collective-permute-done((bf16[256,256]{1,0:T(8,128)(2,1)S(1)}, bf16[256,256]{1,0:T(8,128)(2,1)S(1)}, u32[]{:S(2)}, u32[]{:S(2)}) %collective-permute-start.1) | collective-permute-done | bytes 131104 | tf_op jit(solution)/shard_map/ppermute | solution.py:412
  18.6 2.5 %collective-permute-start.6 = (bf16[3,128,256]{2,1,0:T(8,128)(2,1)S(1)}, bf16[3,128,256]{2,1,0:T(8,128)(2,1)S(1)}, u32[]{:S(2)}, u32[]{:S(2)}) collective-permute-start(bf16[3,128,256]{2,1,0:T(8,128)(2,1)S(1)} %pad_maximum_fusion.1.refs_1_), channel_id=1, source_target_pairs={{0,3},{1,2},{2,1},{3,0},{4,7},{5,6},{6,5},{7,4},{8,11},{9,10},{10,... | collective-permute-start | bytes 589832 | tf_op jit(solution)/shard_map/ppermute | solution.py:412
  21.1 0.5 collective-permute-start.5
  21.6 0.5 collective-permute-start.4
  22.2 2.7 %stats_part.4 = (f32[8,8,512]{2,1,0:T(8,128)S(1)}, bf16[2048,256]{1,0:T(8,128)(2,1)S(1)}, bf16[2048,256]{1,0:T(8,128)(2,1)S(1)}) custom-call(s32[2]{0:T(128)S(1)} %pad_add_fusion.refs_0_, bf16[3,128,256]{2,1,0:T(8,128)(2,1)S(1)} %pad_maximum_fusion.1.refs_1_, ...), custom_call_target="tpu_custom_call", output_to_operand_aliasing={{1}: (2, {}), {2}: (3, {})} | custom-call | flops 805306368 | bytes 6291456 | tf_op jit(solution)/shard_map/stats_part/pallas_call | solution.py:121
  24.9 2.5 %collective-permute-start.10 = (bf16[3,128,256]{2,1,0:T(8,128)(2,1)S(1)}, bf16[3,128,256]{2,1,0:T(8,128)(2,1)S(1)}, u32[]{:S(2)}, u32[]{:S(2)}) collective-permute-start(bf16[3,128,256]{2,1,0:T(8,128)(2,1)S(1)} %pad_maximum_fusion.refs_5_), channel_id=1, source_target_pairs={{0,3},{1,2},{2,1},{3,0},{4,7},{5,6},{6,5},{7,4},{8,11},{9,10},{10,... | collective-permute-start | bytes 589832 | tf_op jit(solution)/shard_map/ppermute | solution.py:412
  27.4 0.5 collective-permute-start.9
  27.9 1.0 %collective-permute-start.8 = (bf16[3,128,256]{2,1,0:T(8,128)(2,1)S(1)}, bf16[3,128,256]{2,1,0:T(8,128)(2,1)S(1)}, u32[]{:S(2)}, u32[]{:S(2)}) collective-permute-start(bf16[3,128,256]{2,1,0:T(8,128)(2,1)S(1)} %pad_maximum_fusion.refs_5_), channel_id=1, source_target_pairs={{0,1},{1,0},{2,3},{3,2},{4,5},{5,4},{6,7},{7,6},{8,9},{9,8},{10,11... | collective-permute-start | bytes 589832 | tf_op jit(solution)/shard_map/ppermute | solution.py:412
  28.9 2.8 %collective-permute-done.5.refs_2_.refs_3_ = bf16[3,128,256]{2,1,0:T(8,128)(2,1)S(1)} collective-permute-done((bf16[3,128,256]{2,1,0:T(8,128)(2,1)S(1)}, bf16[3,128,256]{2,1,0:T(8,128)(2,1)S(1)}, u32[]{:S(2)}, u32[]{:S(2)}) %collective-permute-start.5) | collective-permute-done | bytes 196640 | tf_op jit(solution)/shard_map/ppermute | solution.py:412
  31.7 6.7 %stats_part.5 = (f32[8,8,512]{2,1,0:T(8,128)S(1)}, bf16[2048,256]{1,0:T(8,128)(2,1)S(1)}, bf16[2048,256]{1,0:T(8,128)(2,1)S(1)}) custom-call(s32[2]{0:T(128)S(1)} %pad_add_fusion.refs_0_, bf16[3,128,256]{2,1,0:T(8,128)(2,1)S(1)} %collective-permute-done.4.refs_1_.refs_2_, ...), custom_call_target="tpu_custom_call", output_to_operand_aliasing={{1}: (4, {}), {2}: (5, {})} | custom-call | flops 2415919104 | bytes 18874368 | tf_op jit(solution)/shard_map/stats_part/pallas_call | solution.py:121
  38.3 0.1 collective-permute-start.7
  38.4 1.3 %collective-permute-done.7.refs_2_ = f32[8,8,512]{2,1,0:T(8,128)S(1)} collective-permute-done((f32[8,8,512]{2,1,0:T(8,128)S(1)}, f32[8,8,512]{2,1,0:T(8,128)S(1)}, u32[]{:S(2)}, u32[]{:S(2)}) %collective-permute-start.7) | collective-permute-done | bytes 131104 | tf_op jit(solution)/shard_map/ppermute | solution.py:412
  39.8 0.6 offset_part.1.refs_11_.refs_5_
  40.4 8.0 %rows_part.6 = (f32[144,512]{1,0:T(8,128)S(1)}, bf16[160,512]{1,0:T(8,128)(2,1)S(1)}, bf16[160,512]{1,0:T(8,128)(2,1)S(1)}, bf16[160,512]{1,0:T(8,128)(2,1)S(1)}...) custom-call(s32[2]{0:T(128)S(1)} %pad_add_fusion.refs_0_, ...), custom_call_target="tpu_custom_call", output_to_operand_aliasing={{4}: (9, {}), {5}: (10, {})} | custom-call | flops 4294967296 | bytes 33554432 | tf_op jit(solution)/shard_map/rows_part/pallas_call | solution.py:121
  48.4 1.6 %collective-permute-start.11 = (bf16[160,512]{1,0:T(8,128)(2,1)S(1)}, bf16[160,512]{1,0:T(8,128)(2,1)S(1)}, u32[]{:S(2)}, u32[]{:S(2)}) collective-permute-start(bf16[160,512]{1,0:T(8,128)(2,1)S(1)} %get-tuple-element.117), channel_id=1, source_target_pairs={{0,1},{1,0},{2,3},{3,2},{4,5},{5,4},{6,7},{7,6},{8,9},{9,8},{10,11... | collective-permute-start | bytes 491528 | tf_op jit(solution)/shard_map/ppermute | solution.py:412
  50.0 3.3 %collective-permute-start.12 = (bf16[160,512]{1,0:T(8,128)(2,1)S(1)}, bf16[160,512]{1,0:T(8,128)(2,1)S(1)}, u32[]{:S(2)}, u32[]{:S(2)}) collective-permute-start(bf16[160,512]{1,0:T(8,128)(2,1)S(1)} %get-tuple-element.118), channel_id=1, source_target_pairs={{0,2},{1,3},{2,0},{3,1},{4,6},{5,7},{6,4},{7,5},{8,10},{9,11},{10,... | collective-permute-start | bytes 491528 | tf_op jit(solution)/shard_map/ppermute | solution.py:412
  53.3 8.2 %rows_part.7 = (f32[144,512]{1,0:T(8,128)S(1)}, bf16[160,512]{1,0:T(8,128)(2,1)S(1)}, bf16[160,512]{1,0:T(8,128)(2,1)S(1)}, bf16[160,512]{1,0:T(8,128)(2,1)S(1)}...) custom-call(s32[2]{0:T(128)S(1)} %pad_add_fusion.refs_0_, ...), custom_call_target="tpu_custom_call", output_to_operand_aliasing={{4}: (9, {}), {5}: (10, {})} | custom-call | flops 4294967296 | bytes 33554432 | tf_op jit(solution)/shard_map/rows_part/pallas_call | solution.py:121
  61.5 1.5 %collective-permute-start.15 = (bf16[160,512]{1,0:T(8,128)(2,1)S(1)}, bf16[160,512]{1,0:T(8,128)(2,1)S(1)}, u32[]{:S(2)}, u32[]{:S(2)}) collective-permute-start(bf16[160,512]{1,0:T(8,128)(2,1)S(1)} %get-tuple-element.127), channel_id=1, source_target_pairs={{0,1},{1,0},{2,3},{3,2},{4,5},{5,4},{6,7},{7,6},{8,9},{9,8},{10,11... | collective-permute-start | bytes 491528 | tf_op jit(solution)/shard_map/ppermute | solution.py:412
  63.0 2.0 %collective-permute-start.16 = (bf16[160,512]{1,0:T(8,128)(2,1)S(1)}, bf16[160,512]{1,0:T(8,128)(2,1)S(1)}, u32[]{:S(2)}, u32[]{:S(2)}) collective-permute-start(bf16[160,512]{1,0:T(8,128)(2,1)S(1)} %get-tuple-element.128), channel_id=1, source_target_pairs={{0,2},{1,3},{2,0},{3,1},{4,6},{5,7},{6,4},{7,5},{8,10},{9,11},{10,... | collective-permute-start | bytes 491528 | tf_op jit(solution)/shard_map/ppermute | solution.py:412
  65.1 0.7 join_spread.3
  65.8 2.5 %collective-permute-start.14 = (bf16[208,512]{1,0:T(8,128)(2,1)S(1)}, bf16[208,512]{1,0:T(8,128)(2,1)S(1)}, u32[]{:S(2)}, u32[]{:S(2)}) collective-permute-start(bf16[208,512]{1,0:T(8,128)(2,1)S(1)} %join_spread.3), channel_id=1, source_target_pairs={{0,24},{4,28},{8,16},{12,20},{16,8},{20,12},{24,0},{28,4},{1,25},{... | collective-permute-start | bytes 638984 | tf_op jit(solution)/shard_map/ppermute | solution.py:412
  68.3 8.0 %rows_part.8 = (f32[144,512]{1,0:T(8,128)S(1)}, bf16[160,512]{1,0:T(8,128)(2,1)S(1)}, bf16[160,512]{1,0:T(8,128)(2,1)S(1)}, bf16[160,512]{1,0:T(8,128)(2,1)S(1)}...) custom-call(s32[2]{0:T(128)S(1)} %pad_add_fusion.refs_0_, ...), custom_call_target="tpu_custom_call", output_to_operand_aliasing={{4}: (9, {}), {5}: (10, {})} | custom-call | flops 4294967296 | bytes 33554432 | tf_op jit(solution)/shard_map/rows_part/pallas_call | solution.py:121
  76.4 0.7 join_spread.4
  77.1 0.1 collective-permute-start.18
  77.2 1.5 %collective-permute-start.19 = (bf16[160,512]{1,0:T(8,128)(2,1)S(1)}, bf16[160,512]{1,0:T(8,128)(2,1)S(1)}, u32[]{:S(2)}, u32[]{:S(2)}) collective-permute-start(bf16[160,512]{1,0:T(8,128)(2,1)S(1)} %get-tuple-element.146), channel_id=1, source_target_pairs={{0,1},{1,0},{2,3},{3,2},{4,5},{5,4},{6,7},{7,6},{8,9},{9,8},{10,11... | collective-permute-start | bytes 491528 | tf_op jit(solution)/shard_map/ppermute | solution.py:412
  78.7 2.0 %collective-permute-start.20 = (bf16[160,512]{1,0:T(8,128)(2,1)S(1)}, bf16[160,512]{1,0:T(8,128)(2,1)S(1)}, u32[]{:S(2)}, u32[]{:S(2)}) collective-permute-start(bf16[160,512]{1,0:T(8,128)(2,1)S(1)} %get-tuple-element.147), channel_id=1, source_target_pairs={{0,2},{1,3},{2,0},{3,1},{4,6},{5,7},{6,4},{7,5},{8,10},{9,11},{10,... | collective-permute-start | bytes 491528 | tf_op jit(solution)/shard_map/ppermute | solution.py:412
  80.7 0.0 collective-permute-start.21
  80.7 3.2 %rows_part.9 = (f32[144,512]{1,0:T(8,128)S(1)}, bf16[160,512]{1,0:T(8,128)(2,1)S(1)}, bf16[160,512]{1,0:T(8,128)(2,1)S(1)}, bf16[160,512]{1,0:T(8,128)(2,1)S(1)}) custom-call(s32[2]{0:T(128)S(1)} %pad_add_fusion.refs_0_, bf16[512,256]{1,0:T(8,128)(2,1)S(1)} %copy-done, bf16[512,256]{1,0:T(8,128)(2,1)S(1)} %copy-done.1, ...), custom_call_target="tpu_custom_call" | custom-call | flops 2147483648 | bytes 16777216 | tf_op jit(solution)/shard_map/rows_part/pallas_call | solution.py:121
  83.9 0.2 collective-permute-done.19.refs_2_
  84.1 3.1 %collective-permute-done.20.refs_3_ = bf16[160,512]{1,0:T(8,128)(2,1)S(1)} collective-permute-done((bf16[160,512]{1,0:T(8,128)(2,1)S(1)}, bf16[160,512]{1,0:T(8,128)(2,1)S(1)}, u32[]{:S(2)}, u32[]{:S(2)}) %collective-permute-start.20) | collective-permute-done | bytes 163872 | tf_op jit(solution)/shard_map/ppermute | solution.py:412
  87.3 0.7 join_spread.5
  88.0 1.7 %collective-permute-start.25 = (bf16[208,512]{1,0:T(8,128)(2,1)S(1)}, bf16[208,512]{1,0:T(8,128)(2,1)S(1)}, u32[]{:S(2)}, u32[]{:S(2)}) collective-permute-start(bf16[208,512]{1,0:T(8,128)(2,1)S(1)} %join_spread.5), channel_id=1, source_target_pairs={{0,8},{4,12},{8,0},{12,4},{16,24},{20,28},{24,16},{28,20},{1,9},{5... | collective-permute-start | bytes 638984 | tf_op jit(solution)/shard_map/ppermute | solution.py:412
  89.7 0.6 collective-permute-start.22
  90.3 0.7 collective-permute-start.23
  91.0 2.2 %collective-permute-start.24 = (bf16[160,512]{1,0:T(8,128)(2,1)S(1)}, bf16[160,512]{1,0:T(8,128)(2,1)S(1)}, u32[]{:S(2)}, u32[]{:S(2)}) collective-permute-start(bf16[160,512]{1,0:T(8,128)(2,1)S(1)} %get-tuple-element.157), channel_id=1, source_target_pairs={{0,3},{1,2},{2,1},{3,0},{4,7},{5,6},{6,5},{7,4},{8,11},{9,10},{10,... | collective-permute-start | bytes 491528 | tf_op jit(solution)/shard_map/ppermute | solution.py:412
  93.1 3.1 %collective-permute-done.22.refs_2_ = bf16[160,512]{1,0:T(8,128)(2,1)S(1)} collective-permute-done((bf16[160,512]{1,0:T(8,128)(2,1)S(1)}, bf16[160,512]{1,0:T(8,128)(2,1)S(1)}, u32[]{:S(2)}, u32[]{:S(2)}) %collective-permute-start.22) | collective-permute-done | bytes 163872 | tf_op jit(solution)/shard_map/ppermute | solution.py:412
  96.3 1.5 %collective-permute-done.23.refs_3_ = bf16[160,512]{1,0:T(8,128)(2,1)S(1)} collective-permute-done((bf16[160,512]{1,0:T(8,128)(2,1)S(1)}, bf16[160,512]{1,0:T(8,128)(2,1)S(1)}, u32[]{:S(2)}, u32[]{:S(2)}) %collective-permute-start.23) | collective-permute-done | bytes 163872 | tf_op jit(solution)/shard_map/ppermute | solution.py:412
  97.7 1.4 %collective-permute-done.24.refs_4_ = bf16[160,512]{1,0:T(8,128)(2,1)S(1)} collective-permute-done((bf16[160,512]{1,0:T(8,128)(2,1)S(1)}, bf16[160,512]{1,0:T(8,128)(2,1)S(1)}, u32[]{:S(2)}, u32[]{:S(2)}) %collective-permute-start.24) | collective-permute-done | bytes 163872 | tf_op jit(solution)/shard_map/ppermute | solution.py:412
  99.1 1.5 %finish.1 = (f32[1,512]{1,0:T(1,128)}, f32[64,512]{1,0:T(8,128)}) custom-call(s32[2]{0:T(128)S(1)} %pad_add_fusion.refs_0_, f32[144,512]{1,0:T(8,128)S(1)} %get-tuple-element.154.refs_1_, bf16[160,512]{1,0:T(8,128)(2,1)S(1)} %collective-permute-done.22.refs_2_, bf16[160,512]{1,0:T(8,128)(2,1)S(1)} %collective-permute-done.23.refs_3_, ...), custom_call_target="tpu_custom_call" | custom-call | flops 1048576 | bytes 8192 | tf_op jit(solution)/shard_map/finish/pallas_call | solution.py:121
  (31 shorter events, 0.2 us)
Async XLA Ops:
  0.6 6.9 %collective-permute-start.3 = (bf16[2048,256]{1,0:T(8,128)(2,1)}, bf16[2048,256]{1,0:T(8,128)(2,1)S(1)}, u32[]{:S(2)}, u32[]{:S(2)}) collective-permute-start(bf16[2048,256]{1,0:T(8,128)(2,1)} %refs_2_.2), channel_id=1, source_target_pairs={{0,4},{4,0},{8,12},{12,8},{16,20},{20,16},{24,28},{28,24},{1,5},{5... | collective-permute-start | bytes 3145736 | tf_op jit(solution)/shard_map/ppermute | solution.py:412
  1.1 6.4 %copy-start = (bf16[512,256]{1,0:T(8,128)(2,1)S(1)}, bf16[512,256]{1,0:T(8,128)(2,1)}, u32[]{:S(2)}) copy-start(bf16[512,256]{1,0:T(8,128)(2,1)} %refs_1_.5) | copy-start | bytes 786436
  2.1 15.1 %collective-permute-start.2 = (bf16[256,256]{1,0:T(8,128)(2,1)S(1)}, bf16[256,256]{1,0:T(8,128)(2,1)S(1)}, u32[]{:S(2)}, u32[]{:S(2)}) collective-permute-start(bf16[256,256]{1,0:T(8,128)(2,1)S(1)} %pad_maximum_fusion.2), channel_id=1, source_target_pairs={{0,24},{4,28},{8,16},{12,20},{16,8},{20,12},{24,0},{28,4},{1,25},{... | collective-permute-start | bytes 393224 | tf_op jit(solution)/shard_map/ppermute | solution.py:412
  6.8 11.7 %collective-permute-start.1 = (bf16[256,256]{1,0:T(8,128)(2,1)S(1)}, bf16[256,256]{1,0:T(8,128)(2,1)S(1)}, u32[]{:S(2)}, u32[]{:S(2)}) collective-permute-start(bf16[256,256]{1,0:T(8,128)(2,1)S(1)} %pad_maximum_fusion.2), channel_id=1, source_target_pairs={{0,16},{4,20},{8,24},{12,28},{16,0},{20,4},{24,8},{28,12},{1,17},{... | collective-permute-start | bytes 393224 | tf_op jit(solution)/shard_map/ppermute | solution.py:412
  6.8 11.7 %collective-permute-start = (bf16[256,256]{1,0:T(8,128)(2,1)S(1)}, bf16[256,256]{1,0:T(8,128)(2,1)S(1)}, u32[]{:S(2)}, u32[]{:S(2)}) collective-permute-start(bf16[256,256]{1,0:T(8,128)(2,1)S(1)} %pad_maximum_fusion.2), channel_id=1, source_target_pairs={{0,8},{4,12},{8,0},{12,4},{16,24},{20,28},{24,16},{28,20},{1,9},{5... | collective-permute-start | bytes 393224 | tf_op jit(solution)/shard_map/ppermute | solution.py:412
  7.5 4.6 %copy-start.1 = (bf16[512,256]{1,0:T(8,128)(2,1)S(1)}, bf16[512,256]{1,0:T(8,128)(2,1)}, u32[]{:S(2)}) copy-start(bf16[512,256]{1,0:T(8,128)(2,1)} %refs_2_.3) | copy-start | bytes 786436
  7.5 1.3 %copy-start.2 = (bf16[2048,256]{1,0:T(8,128)(2,1)S(1)}, bf16[2048,256]{1,0:T(8,128)(2,1)}, u32[]{:S(2)}) copy-start(bf16[2048,256]{1,0:T(8,128)(2,1)} %refs_2_.2) | copy-start | bytes 3145732
  18.6 9.3 %collective-permute-start.6 = (bf16[3,128,256]{2,1,0:T(8,128)(2,1)S(1)}, bf16[3,128,256]{2,1,0:T(8,128)(2,1)S(1)}, u32[]{:S(2)}, u32[]{:S(2)}) collective-permute-start(bf16[3,128,256]{2,1,0:T(8,128)(2,1)S(1)} %pad_maximum_fusion.1.refs_1_), channel_id=1, source_target_pairs={{0,3},{1,2},{2,1},{3,0},{4,7},{5,6},{6,5},{7,4},{8,11},{9,10},{10,... | collective-permute-start | bytes 589832 | tf_op jit(solution)/shard_map/ppermute | solution.py:412
  21.1 10.6 %collective-permute-start.5 = (bf16[3,128,256]{2,1,0:T(8,128)(2,1)S(1)}, bf16[3,128,256]{2,1,0:T(8,128)(2,1)S(1)}, u32[]{:S(2)}, u32[]{:S(2)}) collective-permute-start(bf16[3,128,256]{2,1,0:T(8,128)(2,1)S(1)} %pad_maximum_fusion.1.refs_1_), channel_id=1, source_target_pairs={{0,2},{1,3},{2,0},{3,1},{4,6},{5,7},{6,4},{7,5},{8,10},{9,11},{10,... | collective-permute-start | bytes 589832 | tf_op jit(solution)/shard_map/ppermute | solution.py:412
  21.6 10.1 %collective-permute-start.4 = (bf16[3,128,256]{2,1,0:T(8,128)(2,1)S(1)}, bf16[3,128,256]{2,1,0:T(8,128)(2,1)S(1)}, u32[]{:S(2)}, u32[]{:S(2)}) collective-permute-start(bf16[3,128,256]{2,1,0:T(8,128)(2,1)S(1)} %pad_maximum_fusion.1.refs_1_), channel_id=1, source_target_pairs={{0,1},{1,0},{2,3},{3,2},{4,5},{5,4},{6,7},{7,6},{8,9},{9,8},{10,11... | collective-permute-start | bytes 589832 | tf_op jit(solution)/shard_map/ppermute | solution.py:412
  24.9 15.5 %collective-permute-start.10 = (bf16[3,128,256]{2,1,0:T(8,128)(2,1)S(1)}, bf16[3,128,256]{2,1,0:T(8,128)(2,1)S(1)}, u32[]{:S(2)}, u32[]{:S(2)}) collective-permute-start(bf16[3,128,256]{2,1,0:T(8,128)(2,1)S(1)} %pad_maximum_fusion.refs_5_), channel_id=1, source_target_pairs={{0,3},{1,2},{2,1},{3,0},{4,7},{5,6},{6,5},{7,4},{8,11},{9,10},{10,... | collective-permute-start | bytes 589832 | tf_op jit(solution)/shard_map/ppermute | solution.py:412
  27.4 13.0 %collective-permute-start.9 = (bf16[3,128,256]{2,1,0:T(8,128)(2,1)S(1)}, bf16[3,128,256]{2,1,0:T(8,128)(2,1)S(1)}, u32[]{:S(2)}, u32[]{:S(2)}) collective-permute-start(bf16[3,128,256]{2,1,0:T(8,128)(2,1)S(1)} %pad_maximum_fusion.refs_5_), channel_id=1, source_target_pairs={{0,2},{1,3},{2,0},{3,1},{4,6},{5,7},{6,4},{7,5},{8,10},{9,11},{10,... | collective-permute-start | bytes 589832 | tf_op jit(solution)/shard_map/ppermute | solution.py:412
  27.9 12.5 %collective-permute-start.8 = (bf16[3,128,256]{2,1,0:T(8,128)(2,1)S(1)}, bf16[3,128,256]{2,1,0:T(8,128)(2,1)S(1)}, u32[]{:S(2)}, u32[]{:S(2)}) collective-permute-start(bf16[3,128,256]{2,1,0:T(8,128)(2,1)S(1)} %pad_maximum_fusion.refs_5_), channel_id=1, source_target_pairs={{0,1},{1,0},{2,3},{3,2},{4,5},{5,4},{6,7},{7,6},{8,9},{9,8},{10,11... | collective-permute-start | bytes 589832 | tf_op jit(solution)/shard_map/ppermute | solution.py:412
  38.3 1.4 %collective-permute-start.7 = (f32[8,8,512]{2,1,0:T(8,128)S(1)}, f32[8,8,512]{2,1,0:T(8,128)S(1)}, u32[]{:S(2)}, u32[]{:S(2)}) collective-permute-start(f32[8,8,512]{2,1,0:T(8,128)S(1)} %get-tuple-element.104.refs_1_), channel_id=1, source_target_pairs={{0,4},{4,0},{8,12},{12,8},{16,20},{20,16},{24,28},{28,24},{1,5},{5... | collective-permute-start | bytes 393224 | tf_op jit(solution)/shard_map/ppermute | solution.py:412
  48.4 16.6 %collective-permute-start.11 = (bf16[160,512]{1,0:T(8,128)(2,1)S(1)}, bf16[160,512]{1,0:T(8,128)(2,1)S(1)}, u32[]{:S(2)}, u32[]{:S(2)}) collective-permute-start(bf16[160,512]{1,0:T(8,128)(2,1)S(1)} %get-tuple-element.117), channel_id=1, source_target_pairs={{0,1},{1,0},{2,3},{3,2},{4,5},{5,4},{6,7},{7,6},{8,9},{9,8},{10,11... | collective-permute-start | bytes 491528 | tf_op jit(solution)/shard_map/ppermute | solution.py:412
  50.0 15.1 %collective-permute-start.12 = (bf16[160,512]{1,0:T(8,128)(2,1)S(1)}, bf16[160,512]{1,0:T(8,128)(2,1)S(1)}, u32[]{:S(2)}, u32[]{:S(2)}) collective-permute-start(bf16[160,512]{1,0:T(8,128)(2,1)S(1)} %get-tuple-element.118), channel_id=1, source_target_pairs={{0,2},{1,3},{2,0},{3,1},{4,6},{5,7},{6,4},{7,5},{8,10},{9,11},{10,... | collective-permute-start | bytes 491528 | tf_op jit(solution)/shard_map/ppermute | solution.py:412
  53.3 11.8 %collective-permute-start.13 = (bf16[160,512]{1,0:T(8,128)(2,1)S(1)}, bf16[160,512]{1,0:T(8,128)(2,1)S(1)}, u32[]{:S(2)}, u32[]{:S(2)}) collective-permute-start(bf16[160,512]{1,0:T(8,128)(2,1)S(1)} %get-tuple-element.119), channel_id=1, source_target_pairs={{0,3},{1,2},{2,1},{3,0},{4,7},{5,6},{6,5},{7,4},{8,11},{9,10},{10,... | collective-permute-start | bytes 491528 | tf_op jit(solution)/shard_map/ppermute | solution.py:412
  61.5 14.8 %collective-permute-start.15 = (bf16[160,512]{1,0:T(8,128)(2,1)S(1)}, bf16[160,512]{1,0:T(8,128)(2,1)S(1)}, u32[]{:S(2)}, u32[]{:S(2)}) collective-permute-start(bf16[160,512]{1,0:T(8,128)(2,1)S(1)} %get-tuple-element.127), channel_id=1, source_target_pairs={{0,1},{1,0},{2,3},{3,2},{4,5},{5,4},{6,7},{7,6},{8,9},{9,8},{10,11... | collective-permute-start | bytes 491528 | tf_op jit(solution)/shard_map/ppermute | solution.py:412
  63.0 13.3 %collective-permute-start.16 = (bf16[160,512]{1,0:T(8,128)(2,1)S(1)}, bf16[160,512]{1,0:T(8,128)(2,1)S(1)}, u32[]{:S(2)}, u32[]{:S(2)}) collective-permute-start(bf16[160,512]{1,0:T(8,128)(2,1)S(1)} %get-tuple-element.128), channel_id=1, source_target_pairs={{0,2},{1,3},{2,0},{3,1},{4,6},{5,7},{6,4},{7,5},{8,10},{9,11},{10,... | collective-permute-start | bytes 491528 | tf_op jit(solution)/shard_map/ppermute | solution.py:412
  65.1 11.3 %collective-permute-start.17 = (bf16[160,512]{1,0:T(8,128)(2,1)S(1)}, bf16[160,512]{1,0:T(8,128)(2,1)S(1)}, u32[]{:S(2)}, u32[]{:S(2)}) collective-permute-start(bf16[160,512]{1,0:T(8,128)(2,1)S(1)} %get-tuple-element.129), channel_id=1, source_target_pairs={{0,3},{1,2},{2,1},{3,0},{4,7},{5,6},{6,5},{7,4},{8,11},{9,10},{10,... | collective-permute-start | bytes 491528 | tf_op jit(solution)/shard_map/ppermute | solution.py:412
  65.8 10.6 %collective-permute-start.14 = (bf16[208,512]{1,0:T(8,128)(2,1)S(1)}, bf16[208,512]{1,0:T(8,128)(2,1)S(1)}, u32[]{:S(2)}, u32[]{:S(2)}) collective-permute-start(bf16[208,512]{1,0:T(8,128)(2,1)S(1)} %join_spread.3), channel_id=1, source_target_pairs={{0,24},{4,28},{8,16},{12,20},{16,8},{20,12},{24,0},{28,4},{1,25},{... | collective-permute-start | bytes 638984 | tf_op jit(solution)/shard_map/ppermute | solution.py:412
  77.1 10.2 %collective-permute-start.18 = (bf16[208,512]{1,0:T(8,128)(2,1)S(1)}, bf16[208,512]{1,0:T(8,128)(2,1)S(1)}, u32[]{:S(2)}, u32[]{:S(2)}) collective-permute-start(bf16[208,512]{1,0:T(8,128)(2,1)S(1)} %join_spread.4), channel_id=1, source_target_pairs={{0,16},{4,20},{8,24},{12,28},{16,0},{20,4},{24,8},{28,12},{1,17},{... | collective-permute-start | bytes 638984 | tf_op jit(solution)/shard_map/ppermute | solution.py:412
  77.2 7.0 %collective-permute-start.19 = (bf16[160,512]{1,0:T(8,128)(2,1)S(1)}, bf16[160,512]{1,0:T(8,128)(2,1)S(1)}, u32[]{:S(2)}, u32[]{:S(2)}) collective-permute-start(bf16[160,512]{1,0:T(8,128)(2,1)S(1)} %get-tuple-element.146), channel_id=1, source_target_pairs={{0,1},{1,0},{2,3},{3,2},{4,5},{5,4},{6,7},{7,6},{8,9},{9,8},{10,11... | collective-permute-start | bytes 491528 | tf_op jit(solution)/shard_map/ppermute | solution.py:412
  78.7 8.6 %collective-permute-start.20 = (bf16[160,512]{1,0:T(8,128)(2,1)S(1)}, bf16[160,512]{1,0:T(8,128)(2,1)S(1)}, u32[]{:S(2)}, u32[]{:S(2)}) collective-permute-start(bf16[160,512]{1,0:T(8,128)(2,1)S(1)} %get-tuple-element.147), channel_id=1, source_target_pairs={{0,2},{1,3},{2,0},{3,1},{4,6},{5,7},{6,4},{7,5},{8,10},{9,11},{10,... | collective-permute-start | bytes 491528 | tf_op jit(solution)/shard_map/ppermute | solution.py:412
  80.7 6.6 %collective-permute-start.21 = (bf16[160,512]{1,0:T(8,128)(2,1)S(1)}, bf16[160,512]{1,0:T(8,128)(2,1)S(1)}, u32[]{:S(2)}, u32[]{:S(2)}) collective-permute-start(bf16[160,512]{1,0:T(8,128)(2,1)S(1)} %get-tuple-element.148), channel_id=1, source_target_pairs={{0,3},{1,2},{2,1},{3,0},{4,7},{5,6},{6,5},{7,4},{8,11},{9,10},{10,... | collective-permute-start | bytes 491528 | tf_op jit(solution)/shard_map/ppermute | solution.py:412
  88.0 11.1 %collective-permute-start.25 = (bf16[208,512]{1,0:T(8,128)(2,1)S(1)}, bf16[208,512]{1,0:T(8,128)(2,1)S(1)}, u32[]{:S(2)}, u32[]{:S(2)}) collective-permute-start(bf16[208,512]{1,0:T(8,128)(2,1)S(1)} %join_spread.5), channel_id=1, source_target_pairs={{0,8},{4,12},{8,0},{12,4},{16,24},{20,28},{24,16},{28,20},{1,9},{5... | collective-permute-start | bytes 638984 | tf_op jit(solution)/shard_map/ppermute | solution.py:412
  89.7 6.6 %collective-permute-start.22 = (bf16[160,512]{1,0:T(8,128)(2,1)S(1)}, bf16[160,512]{1,0:T(8,128)(2,1)S(1)}, u32[]{:S(2)}, u32[]{:S(2)}) collective-permute-start(bf16[160,512]{1,0:T(8,128)(2,1)S(1)} %get-tuple-element.155), channel_id=1, source_target_pairs={{0,1},{1,0},{2,3},{3,2},{4,5},{5,4},{6,7},{7,6},{8,9},{9,8},{10,11... | collective-permute-start | bytes 491528 | tf_op jit(solution)/shard_map/ppermute | solution.py:412
  90.3 7.5 %collective-permute-start.23 = (bf16[160,512]{1,0:T(8,128)(2,1)S(1)}, bf16[160,512]{1,0:T(8,128)(2,1)S(1)}, u32[]{:S(2)}, u32[]{:S(2)}) collective-permute-start(bf16[160,512]{1,0:T(8,128)(2,1)S(1)} %get-tuple-element.156), channel_id=1, source_target_pairs={{0,2},{1,3},{2,0},{3,1},{4,6},{5,7},{6,4},{7,5},{8,10},{9,11},{10,... | collective-permute-start | bytes 491528 | tf_op jit(solution)/shard_map/ppermute | solution.py:412
  91.0 8.1 %collective-permute-start.24 = (bf16[160,512]{1,0:T(8,128)(2,1)S(1)}, bf16[160,512]{1,0:T(8,128)(2,1)S(1)}, u32[]{:S(2)}, u32[]{:S(2)}) collective-permute-start(bf16[160,512]{1,0:T(8,128)(2,1)S(1)} %get-tuple-element.157), channel_id=1, source_target_pairs={{0,3},{1,2},{2,1},{3,0},{4,7},{5,6},{6,5},{7,4},{8,11},{9,10},{10,... | collective-permute-start | bytes 491528 | tf_op jit(solution)/shard_map/ppermute | solution.py:412

commit v5 on v4

--- a/solution.py
+++ b/solution.py
@@ -13,6 +13,7 @@
 code_scale = math.log2(math.e) / code_temp
 pred_scale = math.log2(math.e) / pred_temp
 log2 = math.log(2.0)
+too_large = 2.0**100
 stat_rows = 8
 sent_rows = 16
 low = -1e30
@@ -161,29 +162,50 @@
     lax.fori_loop(0, count, both, 0)
 
 
+def column_sums(raw, peak):
+    return jnp.sum(jnp.exp2((raw - peak) * code_scale), axis=0, keepdims=True)
+
+
 def stats_kernel(fresh, info, *refs):
     if fresh:
         *codes, near, across, stats, copied = refs
         copied[...] = near[...]
-        stats[:, 0:1, :] = jnp.full((stats.shape[0], 1, stats.shape[2]), low, jnp.float32)
-        stats[:, 1:, :] = jnp.zeros((stats.shape[0], stat_rows - 1, stats.shape[2]), jnp.float32)
     else:
         *codes, near, across, before, stats = refs
         stats[...] = before[...]
-    for part in codes:
-        rows = part[...].reshape(-1, part.shape[-1])
-
-        def step(j, protos):
-            raw = scores(rows, protos)
-            old, total = stats[j, 0:1, :], stats[j, 1:2, :]
-            new = jnp.maximum(old, jnp.max(raw, axis=0, keepdims=True))
-            value = jnp.exp2((raw - new) * code_scale)
-            stats[j, 1:2, :] = total * jnp.exp2((old - new) * code_scale) + jnp.sum(
-                value, axis=0, keepdims=True
-            )
-            stats[j, 0:1, :] = new
-
-        over_chunks((near, across), stats.shape[2], step, True)
+    protos, width = (near, across), stats.shape[2]
+
+    def first(j, part):
+        raw = scores(codes[0][...], part)
+        peak = jnp.max(raw, axis=0, keepdims=True)
+        stats[j, 0:1, :] = peak
+        stats[j, 1:2, :] = column_sums(raw, peak)
+
+    def kept_peak(rows, j, part):
+        stats[j, 1:2, :] += column_sums(scores(rows, part), stats[j, 0:1, :])
+
+    def new_peak(rows, j, part):
+        raw = scores(rows, part)
+        old, total = stats[j, 0:1, :], stats[j, 1:2, :]
+        peak = jnp.maximum(old, jnp.max(raw, axis=0, keepdims=True))
+        stats[j, 0:1, :] = peak
+        stats[j, 1:2, :] = total * jnp.exp2((old - peak) * code_scale) + column_sums(raw, peak)
+
+    def all_rows(add_rows, unrolled):
+        for part in codes:
+            rows = part[...].reshape(-1, part.shape[-1])
+            over_chunks(protos, width, functools.partial(add_rows, rows), unrolled)
+
+    if fresh:
+        over_chunks(protos, width, first, True)
+        return
+    all_rows(kept_peak, True)
+    worst = jnp.max(stats[:, 1:2, :])
+
+    @pl.when(jnp.logical_not(worst < too_large))
+    def _():
+        stats[...] = before[...]
+        all_rows(new_peak, False)
 
 
 def stats_part(info, codes, protos, before):
@@ -237,7 +259,7 @@
     top[...] = jnp.maximum(top[...], lane_fold(jnp.maximum, raw))
 
 
-def pred_pull(protos, raws, top, total, pull):
+def pred_pull(protos, raws, top, total, pull, beside=None):
     width = raws.shape[2]
     stats = [row_of(jnp.max, top[...]) * pred_scale]
     peak = jnp.max(top[...], axis=1, keepdims=True)
@@ -250,15 +272,21 @@
         value = jnp.exp2((raws[j] - peak) * pred_scale)
         total[...] += lane_fold(jnp.add, value)
         pull[...] += weighted(value, protos)
+        if beside is not None:
+            beside(j, protos)
 
     over_chunks(protos, width, step)
     return pull[...], [*stats, row_of(jnp.sum, total[...])]
 
 
-def target_step(codes, protos, offset, total, pull, j):
+def target_values(codes, protos, offset, total, j):
     value = jnp.exp2(scores(codes[...], protos) * code_scale - offset[j, 0:1, :])
     total[...] += lane_fold(jnp.add, value)
-    pull[...] += weighted(value, protos)
+    return value
+
+
+def target_step(codes, protos, offset, total, pull, j):
+    pull[...] += weighted(target_values(codes, protos, offset, total, j), protos)
 
 
 def target_stats(preds, total, pull):
@@ -292,8 +320,8 @@
 
 def both_kernel(proto_count, info, *refs):
     near, across, offset = refs[2 * proto_count : 2 * proto_count + 3]
-    outs = refs[2 * proto_count + 3 : -7]
-    raws, top, total, pull, flipped, codes, preds = refs[-7:]
+    outs = refs[2 * proto_count + 3 : -10]
+    raws, top, total, pull, flipped, codes, preds, held, pull_pred, total_pred = refs[-10:]
     protos = near, across
     placed_rows(info, refs[:proto_count], codes)
     placed_rows(info, refs[proto_count : 2 * proto_count], preds)
@@ -303,11 +331,15 @@
 
     def step(j, part):
         pred_logits(preds, part, raws, top, j)
-        target_step(codes, part, offset, total, pull, j)
+        held[j] = bare(target_values(codes, part, offset, total, j))
+
+    def beside(j, part):
+        pull[...] += jnp.dot(held[j], part, preferred_element_type=jnp.float32)
 
     over_chunks(protos, offset.shape[2], step)
+    done = pred_pull(protos, raws, top, total_pred, pull_pred, beside)
     send(info, 0, pull[...], target_stats(preds, total, pull), outs, flipped)
-    send(info, 1, *pred_pull(protos, raws, top, total, pull), outs, flipped)
+    send(info, 1, *done, outs, flipped)
 
 
 def rows_part(info, codes, preds, protos, offset, rows, proto_count, away, earlier):
@@ -328,6 +360,8 @@
         quarter = pl.BlockSpec((1, *codes[0].shape[1:]), lambda i, info: (away - 1, 0, 0))
         specs = [quarter] * (2 * proto_count) + [whole(value) for value in ins[-3:]]
         scratch = [*scratch] + [pltpu.VMEM((rows, dim), jnp.bfloat16)] * 2
+        scratch += [pltpu.VMEM(shapes[0], jnp.bfloat16)]
+        scratch += [pltpu.VMEM(shape, jnp.float32) for shape in ((rows, dim), (rows, 128))]
     parts, work = 2 if codes is not None else 1, 2 if away else 1
     high, tall = parts * (share + stat_rows), parts * (share + sent_rows)
     outs = [jax.ShapeDtypeStruct((high, rows), jnp.float32)]
@@ -335,7 +369,7 @@
     return call(
         kernel, "rows_part", info, (1,), ins, specs, outs, [whole(out) for out in outs], scratch,
         work * 8 * rows * count * dim, work * 2 * rows * count,
-        6 if kernel is target_kernel else 14, passed,
+        6 if kernel is target_kernel else 20, passed,
     )
 
 

time: 101 us -> 103 us (1.020)
  Pallas kernels: 49.3 us -> 53.7 us
  waiting for transfers between devices: 14.7 us -> 13.2 us
    pallas_call x13, Pallas kernels: 49.3 us -> 53.7 us  [call(): pl.pallas_call(without, grid_spec=pltpu.PrefetchScalarGridSpec(num_scalar...]
    ppermute x26, waiting for transfers between devices: 14.7 us -> 13.2 us  [swap(): return lax.ppermute(value, axis, [(i, i ^ bits) for i in range(count)])]
  transfers between devices with their start and end apart: 26 -> 26, of which waited for: 8 -> 8; matrix products, arithmetic and copies ran while one was open for 1% -> 1% of each run, Pallas kernels for 38% -> 42%
where the time goes in v5:
time: 103 us
  Pallas kernels  53.7 us (52%)
  starting transfers between devices  32.9 us (32%)
  waiting for transfers between devices  13.2 us (13%)
  local copies, waits for them, and re-layouts  2.23 us (2%)
    pallas_call x13, Pallas kernels, call(): pl.pallas_call(without, grid_spec=pltpu.PrefetchScalarGridSpec(num_scalar...  53.7 us
    ppermute x26, starting transfers between devices, swap(): return lax.ppermute(value, axis, [(i, i ^ bits) for i in range(count)])  32.9 us
    ppermute x26, waiting for transfers between devices, swap(): return lax.ppermute(value, axis, [(i, i ^ bits) for i in range(count)])  13.2 us
  transfers between devices with their start and end apart: 26, of which 8 were waited for; matrix products, arithmetic and copies ran while one was open for 1% of the time, Pallas kernels for 42%

profile of v5, /device:TPU:0, one launch (start us, length us, event | category | flops | bytes accessed | tf_op | source)
XLA Modules:
  0.0 103.0 jit_solution(2808375468149131609)
XLA Ops:
  0.6 0.5 collective-permute-start.3
  1.1 0.9 constant_dynamic-slice_fusion
  2.1 4.7 %collective-permute-start.2 = (bf16[256,256]{1,0:T(8,128)(2,1)S(1)}, bf16[256,256]{1,0:T(8,128)(2,1)S(1)}, u32[]{:S(2)}, u32[]{:S(2)}) collective-permute-start(bf16[256,256]{1,0:T(8,128)(2,1)S(1)} %pad_maximum_fusion.2), channel_id=1, source_target_pairs={{0,24},{4,28},{8,16},{12,20},{16,8},{20,12},{24,0},{28,4},{1,25},{... | collective-permute-start | bytes 393224 | tf_op jit(solution)/shard_map/ppermute | solution.py:446
  6.8 0.6 collective-permute-start
  7.4 0.1 pad_add_fusion.refs_0_
  7.5 1.3 %copy-done.2 = bf16[2048,256]{1,0:T(8,128)(2,1)S(1)} copy-done((bf16[2048,256]{1,0:T(8,128)(2,1)S(1)}, bf16[2048,256]{1,0:T(8,128)(2,1)}, u32[]{:S(2)}) %copy-start.2) | copy-done | bytes 1048600
  8.8 3.1 %stats_part.3 = (f32[8,8,512]{2,1,0:T(8,128)S(1)}, bf16[2048,256]{1,0:T(8,128)(2,1)S(1)}, bf16[2048,256]{1,0:T(8,128)(2,1)S(1)}) custom-call(s32[2]{0:T(128)S(1)} %pad_add_fusion.refs_0_, bf16[512,256]{1,0:T(8,128)(2,1)S(1)} %copy-done, bf16[2048,256]{1,0:T(8,128)(2,1)S(1)} %copy-done.2, ...), custom_call_target="tpu_custom_call", output_to_operand_aliasing={{2}: (3, {})} | custom-call | flops 1073741824 | bytes 8388608 | tf_op jit(solution)/shard_map/stats_part/pallas_call | solution.py:122
  11.9 4.9 %rows_part.5 = (f32[72,512]{1,0:T(8,128)S(1)}, bf16[80,512]{1,0:T(8,128)(2,1)S(1)}, bf16[80,512]{1,0:T(8,128)(2,1)S(1)}, bf16[80,512]{1,0:T(8,128)(2,1)S(1)}, bf...) custom-call(s32[2]{0:T(128)S(1)} %pad_add_fusion.refs_0_, ...), custom_call_target="tpu_custom_call", output_to_operand_aliasing={{4}: (2, {}), {5}: (3, {})} | custom-call | flops 2147483648 | bytes 16777216 | tf_op jit(solution)/shard_map/rows_part/pallas_call | solution.py:122
  16.8 1.7 %collective-permute-done.1 = bf16[256,256]{1,0:T(8,128)(2,1)S(1)} collective-permute-done((bf16[256,256]{1,0:T(8,128)(2,1)S(1)}, bf16[256,256]{1,0:T(8,128)(2,1)S(1)}, u32[]{:S(2)}, u32[]{:S(2)}) %collective-permute-start.1) | collective-permute-done | bytes 131104 | tf_op jit(solution)/shard_map/ppermute | solution.py:446
  18.6 2.5 %collective-permute-start.6 = (bf16[3,128,256]{2,1,0:T(8,128)(2,1)S(1)}, bf16[3,128,256]{2,1,0:T(8,128)(2,1)S(1)}, u32[]{:S(2)}, u32[]{:S(2)}) collective-permute-start(bf16[3,128,256]{2,1,0:T(8,128)(2,1)S(1)} %pad_maximum_fusion.1.refs_1_), channel_id=1, source_target_pairs={{0,3},{1,2},{2,1},{3,0},{4,7},{5,6},{6,5},{7,4},{8,11},{9,10},{10,... | collective-permute-start | bytes 589832 | tf_op jit(solution)/shard_map/ppermute | solution.py:446
  21.1 0.5 collective-permute-start.5
  21.6 0.5 collective-permute-start.4
  22.2 4.3 %stats_part.4 = (f32[8,8,512]{2,1,0:T(8,128)S(1)}, bf16[2048,256]{1,0:T(8,128)(2,1)S(1)}, bf16[2048,256]{1,0:T(8,128)(2,1)S(1)}) custom-call(s32[2]{0:T(128)S(1)} %pad_add_fusion.refs_0_, bf16[3,128,256]{2,1,0:T(8,128)(2,1)S(1)} %pad_maximum_fusion.1.refs_1_, ...), custom_call_target="tpu_custom_call", output_to_operand_aliasing={{1}: (2, {}), {2}: (3, {})} | custom-call | flops 805306368 | bytes 6291456 | tf_op jit(solution)/shard_map/stats_part/pallas_call | solution.py:122
  26.5 2.5 %collective-permute-start.10 = (bf16[3,128,256]{2,1,0:T(8,128)(2,1)S(1)}, bf16[3,128,256]{2,1,0:T(8,128)(2,1)S(1)}, u32[]{:S(2)}, u32[]{:S(2)}) collective-permute-start(bf16[3,128,256]{2,1,0:T(8,128)(2,1)S(1)} %pad_maximum_fusion.refs_5_), channel_id=1, source_target_pairs={{0,3},{1,2},{2,1},{3,0},{4,7},{5,6},{6,5},{7,4},{8,11},{9,10},{10,... | collective-permute-start | bytes 589832 | tf_op jit(solution)/shard_map/ppermute | solution.py:446
  29.0 0.5 collective-permute-start.9
  29.6 0.5 collective-permute-start.8
  30.1 1.6 %collective-permute-done.5.refs_2_.refs_3_ = bf16[3,128,256]{2,1,0:T(8,128)(2,1)S(1)} collective-permute-done((bf16[3,128,256]{2,1,0:T(8,128)(2,1)S(1)}, bf16[3,128,256]{2,1,0:T(8,128)(2,1)S(1)}, u32[]{:S(2)}, u32[]{:S(2)}) %collective-permute-start.5) | collective-permute-done | bytes 196640 | tf_op jit(solution)/shard_map/ppermute | solution.py:446
  31.7 11.5 %stats_part.5 = (f32[8,8,512]{2,1,0:T(8,128)S(1)}, bf16[2048,256]{1,0:T(8,128)(2,1)S(1)}, bf16[2048,256]{1,0:T(8,128)(2,1)S(1)}) custom-call(s32[2]{0:T(128)S(1)} %pad_add_fusion.refs_0_, bf16[3,128,256]{2,1,0:T(8,128)(2,1)S(1)} %collective-permute-done.4.refs_1_.refs_2_, ...), custom_call_target="tpu_custom_call", output_to_operand_aliasing={{1}: (4, {}), {2}: (5, {})} | custom-call | flops 2415919104 | bytes 18874368 | tf_op jit(solution)/shard_map/stats_part/pallas_call | solution.py:122
  43.2 0.1 collective-permute-start.7
  43.3 1.3 %collective-permute-done.7.refs_2_ = f32[8,8,512]{2,1,0:T(8,128)S(1)} collective-permute-done((f32[8,8,512]{2,1,0:T(8,128)S(1)}, f32[8,8,512]{2,1,0:T(8,128)S(1)}, u32[]{:S(2)}, u32[]{:S(2)}) %collective-permute-start.7) | collective-permute-done | bytes 131104 | tf_op jit(solution)/shard_map/ppermute | solution.py:446
  44.7 0.6 offset_part.1.refs_11_.refs_5_
  45.3 7.5 %rows_part.6 = (f32[144,512]{1,0:T(8,128)S(1)}, bf16[160,512]{1,0:T(8,128)(2,1)S(1)}, bf16[160,512]{1,0:T(8,128)(2,1)S(1)}, bf16[160,512]{1,0:T(8,128)(2,1)S(1)}...) custom-call(s32[2]{0:T(128)S(1)} %pad_add_fusion.refs_0_, ...), custom_call_target="tpu_custom_call", output_to_operand_aliasing={{4}: (9, {}), {5}: (10, {})} | custom-call | flops 4294967296 | bytes 33554432 | tf_op jit(solution)/shard_map/rows_part/pallas_call | solution.py:122
  52.8 1.6 %collective-permute-start.11 = (bf16[160,512]{1,0:T(8,128)(2,1)S(1)}, bf16[160,512]{1,0:T(8,128)(2,1)S(1)}, u32[]{:S(2)}, u32[]{:S(2)}) collective-permute-start(bf16[160,512]{1,0:T(8,128)(2,1)S(1)} %get-tuple-element.117), channel_id=1, source_target_pairs={{0,1},{1,0},{2,3},{3,2},{4,5},{5,4},{6,7},{7,6},{8,9},{9,8},{10,11... | collective-permute-start | bytes 491528 | tf_op jit(solution)/shard_map/ppermute | solution.py:446
  54.3 3.3 %collective-permute-start.12 = (bf16[160,512]{1,0:T(8,128)(2,1)S(1)}, bf16[160,512]{1,0:T(8,128)(2,1)S(1)}, u32[]{:S(2)}, u32[]{:S(2)}) collective-permute-start(bf16[160,512]{1,0:T(8,128)(2,1)S(1)} %get-tuple-element.118), channel_id=1, source_target_pairs={{0,2},{1,3},{2,0},{3,1},{4,6},{5,7},{6,4},{7,5},{8,10},{9,11},{10,... | collective-permute-start | bytes 491528 | tf_op jit(solution)/shard_map/ppermute | solution.py:446
  57.6 7.5 %rows_part.7 = (f32[144,512]{1,0:T(8,128)S(1)}, bf16[160,512]{1,0:T(8,128)(2,1)S(1)}, bf16[160,512]{1,0:T(8,128)(2,1)S(1)}, bf16[160,512]{1,0:T(8,128)(2,1)S(1)}...) custom-call(s32[2]{0:T(128)S(1)} %pad_add_fusion.refs_0_, ...), custom_call_target="tpu_custom_call", output_to_operand_aliasing={{4}: (9, {}), {5}: (10, {})} | custom-call | flops 4294967296 | bytes 33554432 | tf_op jit(solution)/shard_map/rows_part/pallas_call | solution.py:122
  65.1 1.5 %collective-permute-start.15 = (bf16[160,512]{1,0:T(8,128)(2,1)S(1)}, bf16[160,512]{1,0:T(8,128)(2,1)S(1)}, u32[]{:S(2)}, u32[]{:S(2)}) collective-permute-start(bf16[160,512]{1,0:T(8,128)(2,1)S(1)} %get-tuple-element.127), channel_id=1, source_target_pairs={{0,1},{1,0},{2,3},{3,2},{4,5},{5,4},{6,7},{7,6},{8,9},{9,8},{10,11... | collective-permute-start | bytes 491528 | tf_op jit(solution)/shard_map/ppermute | solution.py:446
  66.6 2.0 %collective-permute-start.16 = (bf16[160,512]{1,0:T(8,128)(2,1)S(1)}, bf16[160,512]{1,0:T(8,128)(2,1)S(1)}, u32[]{:S(2)}, u32[]{:S(2)}) collective-permute-start(bf16[160,512]{1,0:T(8,128)(2,1)S(1)} %get-tuple-element.128), channel_id=1, source_target_pairs={{0,2},{1,3},{2,0},{3,1},{4,6},{5,7},{6,4},{7,5},{8,10},{9,11},{10,... | collective-permute-start | bytes 491528 | tf_op jit(solution)/shard_map/ppermute | solution.py:446
  68.7 0.0 collective-permute-start.17
  68.7 0.7 join_spread.3
  69.4 2.5 %collective-permute-start.14 = (bf16[208,512]{1,0:T(8,128)(2,1)S(1)}, bf16[208,512]{1,0:T(8,128)(2,1)S(1)}, u32[]{:S(2)}, u32[]{:S(2)}) collective-permute-start(bf16[208,512]{1,0:T(8,128)(2,1)S(1)} %join_spread.3), channel_id=1, source_target_pairs={{0,24},{4,28},{8,16},{12,20},{16,8},{20,12},{24,0},{28,4},{1,25},{... | collective-permute-start | bytes 638984 | tf_op jit(solution)/shard_map/ppermute | solution.py:446
  71.9 7.5 %rows_part.8 = (f32[144,512]{1,0:T(8,128)S(1)}, bf16[160,512]{1,0:T(8,128)(2,1)S(1)}, bf16[160,512]{1,0:T(8,128)(2,1)S(1)}, bf16[160,512]{1,0:T(8,128)(2,1)S(1)}...) custom-call(s32[2]{0:T(128)S(1)} %pad_add_fusion.refs_0_, ...), custom_call_target="tpu_custom_call", output_to_operand_aliasing={{4}: (9, {}), {5}: (10, {})} | custom-call | flops 4294967296 | bytes 33554432 | tf_op jit(solution)/shard_map/rows_part/pallas_call | solution.py:122
  79.4 0.7 join_spread.4
  80.1 0.3 collective-permute-start.18
  80.4 1.5 %collective-permute-start.19 = (bf16[160,512]{1,0:T(8,128)(2,1)S(1)}, bf16[160,512]{1,0:T(8,128)(2,1)S(1)}, u32[]{:S(2)}, u32[]{:S(2)}) collective-permute-start(bf16[160,512]{1,0:T(8,128)(2,1)S(1)} %get-tuple-element.146), channel_id=1, source_target_pairs={{0,1},{1,0},{2,3},{3,2},{4,5},{5,4},{6,7},{7,6},{8,9},{9,8},{10,11... | collective-permute-start | bytes 491528 | tf_op jit(solution)/shard_map/ppermute | solution.py:446
  81.9 1.9 %collective-permute-start.20 = (bf16[160,512]{1,0:T(8,128)(2,1)S(1)}, bf16[160,512]{1,0:T(8,128)(2,1)S(1)}, u32[]{:S(2)}, u32[]{:S(2)}) collective-permute-start(bf16[160,512]{1,0:T(8,128)(2,1)S(1)} %get-tuple-element.147), channel_id=1, source_target_pairs={{0,2},{1,3},{2,0},{3,1},{4,6},{5,7},{6,4},{7,5},{8,10},{9,11},{10,... | collective-permute-start | bytes 491528 | tf_op jit(solution)/shard_map/ppermute | solution.py:446
  83.8 0.2 collective-permute-start.21
  83.9 3.2 %rows_part.9 = (f32[144,512]{1,0:T(8,128)S(1)}, bf16[160,512]{1,0:T(8,128)(2,1)S(1)}, bf16[160,512]{1,0:T(8,128)(2,1)S(1)}, bf16[160,512]{1,0:T(8,128)(2,1)S(1)}) custom-call(s32[2]{0:T(128)S(1)} %pad_add_fusion.refs_0_, bf16[512,256]{1,0:T(8,128)(2,1)S(1)} %copy-done, bf16[512,256]{1,0:T(8,128)(2,1)S(1)} %copy-done.1, ...), custom_call_target="tpu_custom_call" | custom-call | flops 2147483648 | bytes 16777216 | tf_op jit(solution)/shard_map/rows_part/pallas_call | solution.py:122
  87.2 0.1 collective-permute-done.19.refs_2_
  87.2 3.2 %collective-permute-done.20.refs_3_ = bf16[160,512]{1,0:T(8,128)(2,1)S(1)} collective-permute-done((bf16[160,512]{1,0:T(8,128)(2,1)S(1)}, bf16[160,512]{1,0:T(8,128)(2,1)S(1)}, u32[]{:S(2)}, u32[]{:S(2)}) %collective-permute-start.20) | collective-permute-done | bytes 163872 | tf_op jit(solution)/shard_map/ppermute | solution.py:446
  90.4 0.7 join_spread.5
  91.1 1.6 %collective-permute-start.25 = (bf16[208,512]{1,0:T(8,128)(2,1)S(1)}, bf16[208,512]{1,0:T(8,128)(2,1)S(1)}, u32[]{:S(2)}, u32[]{:S(2)}) collective-permute-start(bf16[208,512]{1,0:T(8,128)(2,1)S(1)} %join_spread.5), channel_id=1, source_target_pairs={{0,8},{4,12},{8,0},{12,4},{16,24},{20,28},{24,16},{28,20},{1,9},{5... | collective-permute-start | bytes 638984 | tf_op jit(solution)/shard_map/ppermute | solution.py:446
  92.7 0.6 collective-permute-start.22
  93.3 0.7 collective-permute-start.23
  94.0 2.2 %collective-permute-start.24 = (bf16[160,512]{1,0:T(8,128)(2,1)S(1)}, bf16[160,512]{1,0:T(8,128)(2,1)S(1)}, u32[]{:S(2)}, u32[]{:S(2)}) collective-permute-start(bf16[160,512]{1,0:T(8,128)(2,1)S(1)} %get-tuple-element.157), channel_id=1, source_target_pairs={{0,3},{1,2},{2,1},{3,0},{4,7},{5,6},{6,5},{7,4},{8,11},{9,10},{10,... | collective-permute-start | bytes 491528 | tf_op jit(solution)/shard_map/ppermute | solution.py:446
  96.2 2.4 %collective-permute-done.22.refs_2_ = bf16[160,512]{1,0:T(8,128)(2,1)S(1)} collective-permute-done((bf16[160,512]{1,0:T(8,128)(2,1)S(1)}, bf16[160,512]{1,0:T(8,128)(2,1)S(1)}, u32[]{:S(2)}, u32[]{:S(2)}) %collective-permute-start.22) | collective-permute-done | bytes 163872 | tf_op jit(solution)/shard_map/ppermute | solution.py:446
  98.6 1.5 %collective-permute-done.23.refs_3_ = bf16[160,512]{1,0:T(8,128)(2,1)S(1)} collective-permute-done((bf16[160,512]{1,0:T(8,128)(2,1)S(1)}, bf16[160,512]{1,0:T(8,128)(2,1)S(1)}, u32[]{:S(2)}, u32[]{:S(2)}) %collective-permute-start.23) | collective-permute-done | bytes 163872 | tf_op jit(solution)/shard_map/ppermute | solution.py:446
  100.1 1.4 %collective-permute-done.24.refs_4_ = bf16[160,512]{1,0:T(8,128)(2,1)S(1)} collective-permute-done((bf16[160,512]{1,0:T(8,128)(2,1)S(1)}, bf16[160,512]{1,0:T(8,128)(2,1)S(1)}, u32[]{:S(2)}, u32[]{:S(2)}) %collective-permute-start.24) | collective-permute-done | bytes 163872 | tf_op jit(solution)/shard_map/ppermute | solution.py:446
  101.5 1.5 %finish.1 = (f32[1,512]{1,0:T(1,128)}, f32[64,512]{1,0:T(8,128)}) custom-call(s32[2]{0:T(128)S(1)} %pad_add_fusion.refs_0_, f32[144,512]{1,0:T(8,128)S(1)} %get-tuple-element.154.refs_1_, bf16[160,512]{1,0:T(8,128)(2,1)S(1)} %collective-permute-done.22.refs_2_, bf16[160,512]{1,0:T(8,128)(2,1)S(1)} %collective-permute-done.23.refs_3_, ...), custom_call_target="tpu_custom_call" | custom-call | flops 1048576 | bytes 8192 | tf_op jit(solution)/shard_map/finish/pallas_call | solution.py:122
  (31 shorter events, 0.2 us)
Async XLA Ops:
  0.6 6.9 %collective-permute-start.3 = (bf16[2048,256]{1,0:T(8,128)(2,1)}, bf16[2048,256]{1,0:T(8,128)(2,1)S(1)}, u32[]{:S(2)}, u32[]{:S(2)}) collective-permute-start(bf16[2048,256]{1,0:T(8,128)(2,1)} %refs_2_.2), channel_id=1, source_target_pairs={{0,4},{4,0},{8,12},{12,8},{16,20},{20,16},{24,28},{28,24},{1,5},{5... | collective-permute-start | bytes 3145736 | tf_op jit(solution)/shard_map/ppermute | solution.py:446
  1.1 6.4 %copy-start = (bf16[512,256]{1,0:T(8,128)(2,1)S(1)}, bf16[512,256]{1,0:T(8,128)(2,1)}, u32[]{:S(2)}) copy-start(bf16[512,256]{1,0:T(8,128)(2,1)} %refs_1_.5) | copy-start | bytes 786436
  2.1 14.7 %collective-permute-start.2 = (bf16[256,256]{1,0:T(8,128)(2,1)S(1)}, bf16[256,256]{1,0:T(8,128)(2,1)S(1)}, u32[]{:S(2)}, u32[]{:S(2)}) collective-permute-start(bf16[256,256]{1,0:T(8,128)(2,1)S(1)} %pad_maximum_fusion.2), channel_id=1, source_target_pairs={{0,24},{4,28},{8,16},{12,20},{16,8},{20,12},{24,0},{28,4},{1,25},{... | collective-permute-start | bytes 393224 | tf_op jit(solution)/shard_map/ppermute | solution.py:446
  6.8 11.7 %collective-permute-start.1 = (bf16[256,256]{1,0:T(8,128)(2,1)S(1)}, bf16[256,256]{1,0:T(8,128)(2,1)S(1)}, u32[]{:S(2)}, u32[]{:S(2)}) collective-permute-start(bf16[256,256]{1,0:T(8,128)(2,1)S(1)} %pad_maximum_fusion.2), channel_id=1, source_target_pairs={{0,16},{4,20},{8,24},{12,28},{16,0},{20,4},{24,8},{28,12},{1,17},{... | collective-permute-start | bytes 393224 | tf_op jit(solution)/shard_map/ppermute | solution.py:446
  6.8 11.7 %collective-permute-start = (bf16[256,256]{1,0:T(8,128)(2,1)S(1)}, bf16[256,256]{1,0:T(8,128)(2,1)S(1)}, u32[]{:S(2)}, u32[]{:S(2)}) collective-permute-start(bf16[256,256]{1,0:T(8,128)(2,1)S(1)} %pad_maximum_fusion.2), channel_id=1, source_target_pairs={{0,8},{4,12},{8,0},{12,4},{16,24},{20,28},{24,16},{28,20},{1,9},{5... | collective-permute-start | bytes 393224 | tf_op jit(solution)/shard_map/ppermute | solution.py:446
  7.5 4.4 %copy-start.1 = (bf16[512,256]{1,0:T(8,128)(2,1)S(1)}, bf16[512,256]{1,0:T(8,128)(2,1)}, u32[]{:S(2)}) copy-start(bf16[512,256]{1,0:T(8,128)(2,1)} %refs_2_.3) | copy-start | bytes 786436
  7.5 1.3 %copy-start.2 = (bf16[2048,256]{1,0:T(8,128)(2,1)S(1)}, bf16[2048,256]{1,0:T(8,128)(2,1)}, u32[]{:S(2)}) copy-start(bf16[2048,256]{1,0:T(8,128)(2,1)} %refs_2_.2) | copy-start | bytes 3145732
  18.6 11.0 %collective-permute-start.6 = (bf16[3,128,256]{2,1,0:T(8,128)(2,1)S(1)}, bf16[3,128,256]{2,1,0:T(8,128)(2,1)S(1)}, u32[]{:S(2)}, u32[]{:S(2)}) collective-permute-start(bf16[3,128,256]{2,1,0:T(8,128)(2,1)S(1)} %pad_maximum_fusion.1.refs_1_), channel_id=1, source_target_pairs={{0,3},{1,2},{2,1},{3,0},{4,7},{5,6},{6,5},{7,4},{8,11},{9,10},{10,... | collective-permute-start | bytes 589832 | tf_op jit(solution)/shard_map/ppermute | solution.py:446
  21.1 10.6 %collective-permute-start.5 = (bf16[3,128,256]{2,1,0:T(8,128)(2,1)S(1)}, bf16[3,128,256]{2,1,0:T(8,128)(2,1)S(1)}, u32[]{:S(2)}, u32[]{:S(2)}) collective-permute-start(bf16[3,128,256]{2,1,0:T(8,128)(2,1)S(1)} %pad_maximum_fusion.1.refs_1_), channel_id=1, source_target_pairs={{0,2},{1,3},{2,0},{3,1},{4,6},{5,7},{6,4},{7,5},{8,10},{9,11},{10,... | collective-permute-start | bytes 589832 | tf_op jit(solution)/shard_map/ppermute | solution.py:446
  21.6 10.1 %collective-permute-start.4 = (bf16[3,128,256]{2,1,0:T(8,128)(2,1)S(1)}, bf16[3,128,256]{2,1,0:T(8,128)(2,1)S(1)}, u32[]{:S(2)}, u32[]{:S(2)}) collective-permute-start(bf16[3,128,256]{2,1,0:T(8,128)(2,1)S(1)} %pad_maximum_fusion.1.refs_1_), channel_id=1, source_target_pairs={{0,1},{1,0},{2,3},{3,2},{4,5},{5,4},{6,7},{7,6},{8,9},{9,8},{10,11... | collective-permute-start | bytes 589832 | tf_op jit(solution)/shard_map/ppermute | solution.py:446
  26.5 18.7 %collective-permute-start.10 = (bf16[3,128,256]{2,1,0:T(8,128)(2,1)S(1)}, bf16[3,128,256]{2,1,0:T(8,128)(2,1)S(1)}, u32[]{:S(2)}, u32[]{:S(2)}) collective-permute-start(bf16[3,128,256]{2,1,0:T(8,128)(2,1)S(1)} %pad_maximum_fusion.refs_5_), channel_id=1, source_target_pairs={{0,3},{1,2},{2,1},{3,0},{4,7},{5,6},{6,5},{7,4},{8,11},{9,10},{10,... | collective-permute-start | bytes 589832 | tf_op jit(solution)/shard_map/ppermute | solution.py:446
  29.0 16.2 %collective-permute-start.9 = (bf16[3,128,256]{2,1,0:T(8,128)(2,1)S(1)}, bf16[3,128,256]{2,1,0:T(8,128)(2,1)S(1)}, u32[]{:S(2)}, u32[]{:S(2)}) collective-permute-start(bf16[3,128,256]{2,1,0:T(8,128)(2,1)S(1)} %pad_maximum_fusion.refs_5_), channel_id=1, source_target_pairs={{0,2},{1,3},{2,0},{3,1},{4,6},{5,7},{6,4},{7,5},{8,10},{9,11},{10,... | collective-permute-start | bytes 589832 | tf_op jit(solution)/shard_map/ppermute | solution.py:446
  29.6 15.7 %collective-permute-start.8 = (bf16[3,128,256]{2,1,0:T(8,128)(2,1)S(1)}, bf16[3,128,256]{2,1,0:T(8,128)(2,1)S(1)}, u32[]{:S(2)}, u32[]{:S(2)}) collective-permute-start(bf16[3,128,256]{2,1,0:T(8,128)(2,1)S(1)} %pad_maximum_fusion.refs_5_), channel_id=1, source_target_pairs={{0,1},{1,0},{2,3},{3,2},{4,5},{5,4},{6,7},{7,6},{8,9},{9,8},{10,11... | collective-permute-start | bytes 589832 | tf_op jit(solution)/shard_map/ppermute | solution.py:446
  43.2 1.4 %collective-permute-start.7 = (f32[8,8,512]{2,1,0:T(8,128)S(1)}, f32[8,8,512]{2,1,0:T(8,128)S(1)}, u32[]{:S(2)}, u32[]{:S(2)}) collective-permute-start(f32[8,8,512]{2,1,0:T(8,128)S(1)} %get-tuple-element.104.refs_1_), channel_id=1, source_target_pairs={{0,4},{4,0},{8,12},{12,8},{16,20},{20,16},{24,28},{28,24},{1,5},{5... | collective-permute-start | bytes 393224 | tf_op jit(solution)/shard_map/ppermute | solution.py:446
  52.8 15.9 %collective-permute-start.11 = (bf16[160,512]{1,0:T(8,128)(2,1)S(1)}, bf16[160,512]{1,0:T(8,128)(2,1)S(1)}, u32[]{:S(2)}, u32[]{:S(2)}) collective-permute-start(bf16[160,512]{1,0:T(8,128)(2,1)S(1)} %get-tuple-element.117), channel_id=1, source_target_pairs={{0,1},{1,0},{2,3},{3,2},{4,5},{5,4},{6,7},{7,6},{8,9},{9,8},{10,11... | collective-permute-start | bytes 491528 | tf_op jit(solution)/shard_map/ppermute | solution.py:446
  54.3 14.3 %collective-permute-start.12 = (bf16[160,512]{1,0:T(8,128)(2,1)S(1)}, bf16[160,512]{1,0:T(8,128)(2,1)S(1)}, u32[]{:S(2)}, u32[]{:S(2)}) collective-permute-start(bf16[160,512]{1,0:T(8,128)(2,1)S(1)} %get-tuple-element.118), channel_id=1, source_target_pairs={{0,2},{1,3},{2,0},{3,1},{4,6},{5,7},{6,4},{7,5},{8,10},{9,11},{10,... | collective-permute-start | bytes 491528 | tf_op jit(solution)/shard_map/ppermute | solution.py:446
  57.6 11.0 %collective-permute-start.13 = (bf16[160,512]{1,0:T(8,128)(2,1)S(1)}, bf16[160,512]{1,0:T(8,128)(2,1)S(1)}, u32[]{:S(2)}, u32[]{:S(2)}) collective-permute-start(bf16[160,512]{1,0:T(8,128)(2,1)S(1)} %get-tuple-element.119), channel_id=1, source_target_pairs={{0,3},{1,2},{2,1},{3,0},{4,7},{5,6},{6,5},{7,4},{8,11},{9,10},{10,... | collective-permute-start | bytes 491528 | tf_op jit(solution)/shard_map/ppermute | solution.py:446
  65.1 14.3 %collective-permute-start.15 = (bf16[160,512]{1,0:T(8,128)(2,1)S(1)}, bf16[160,512]{1,0:T(8,128)(2,1)S(1)}, u32[]{:S(2)}, u32[]{:S(2)}) collective-permute-start(bf16[160,512]{1,0:T(8,128)(2,1)S(1)} %get-tuple-element.127), channel_id=1, source_target_pairs={{0,1},{1,0},{2,3},{3,2},{4,5},{5,4},{6,7},{7,6},{8,9},{9,8},{10,11... | collective-permute-start | bytes 491528 | tf_op jit(solution)/shard_map/ppermute | solution.py:446
  66.6 12.8 %collective-permute-start.16 = (bf16[160,512]{1,0:T(8,128)(2,1)S(1)}, bf16[160,512]{1,0:T(8,128)(2,1)S(1)}, u32[]{:S(2)}, u32[]{:S(2)}) collective-permute-start(bf16[160,512]{1,0:T(8,128)(2,1)S(1)} %get-tuple-element.128), channel_id=1, source_target_pairs={{0,2},{1,3},{2,0},{3,1},{4,6},{5,7},{6,4},{7,5},{8,10},{9,11},{10,... | collective-permute-start | bytes 491528 | tf_op jit(solution)/shard_map/ppermute | solution.py:446
  68.7 10.8 %collective-permute-start.17 = (bf16[160,512]{1,0:T(8,128)(2,1)S(1)}, bf16[160,512]{1,0:T(8,128)(2,1)S(1)}, u32[]{:S(2)}, u32[]{:S(2)}) collective-permute-start(bf16[160,512]{1,0:T(8,128)(2,1)S(1)} %get-tuple-element.129), channel_id=1, source_target_pairs={{0,3},{1,2},{2,1},{3,0},{4,7},{5,6},{6,5},{7,4},{8,11},{9,10},{10,... | collective-permute-start | bytes 491528 | tf_op jit(solution)/shard_map/ppermute | solution.py:446
  69.4 10.0 %collective-permute-start.14 = (bf16[208,512]{1,0:T(8,128)(2,1)S(1)}, bf16[208,512]{1,0:T(8,128)(2,1)S(1)}, u32[]{:S(2)}, u32[]{:S(2)}) collective-permute-start(bf16[208,512]{1,0:T(8,128)(2,1)S(1)} %join_spread.3), channel_id=1, source_target_pairs={{0,24},{4,28},{8,16},{12,20},{16,8},{20,12},{24,0},{28,4},{1,25},{... | collective-permute-start | bytes 638984 | tf_op jit(solution)/shard_map/ppermute | solution.py:446
  80.1 10.3 %collective-permute-start.18 = (bf16[208,512]{1,0:T(8,128)(2,1)S(1)}, bf16[208,512]{1,0:T(8,128)(2,1)S(1)}, u32[]{:S(2)}, u32[]{:S(2)}) collective-permute-start(bf16[208,512]{1,0:T(8,128)(2,1)S(1)} %join_spread.4), channel_id=1, source_target_pairs={{0,16},{4,20},{8,24},{12,28},{16,0},{20,4},{24,8},{28,12},{1,17},{... | collective-permute-start | bytes 638984 | tf_op jit(solution)/shard_map/ppermute | solution.py:446
  80.4 6.8 %collective-permute-start.19 = (bf16[160,512]{1,0:T(8,128)(2,1)S(1)}, bf16[160,512]{1,0:T(8,128)(2,1)S(1)}, u32[]{:S(2)}, u32[]{:S(2)}) collective-permute-start(bf16[160,512]{1,0:T(8,128)(2,1)S(1)} %get-tuple-element.146), channel_id=1, source_target_pairs={{0,1},{1,0},{2,3},{3,2},{4,5},{5,4},{6,7},{7,6},{8,9},{9,8},{10,11... | collective-permute-start | bytes 491528 | tf_op jit(solution)/shard_map/ppermute | solution.py:446
  81.9 8.5 %collective-permute-start.20 = (bf16[160,512]{1,0:T(8,128)(2,1)S(1)}, bf16[160,512]{1,0:T(8,128)(2,1)S(1)}, u32[]{:S(2)}, u32[]{:S(2)}) collective-permute-start(bf16[160,512]{1,0:T(8,128)(2,1)S(1)} %get-tuple-element.147), channel_id=1, source_target_pairs={{0,2},{1,3},{2,0},{3,1},{4,6},{5,7},{6,4},{7,5},{8,10},{9,11},{10,... | collective-permute-start | bytes 491528 | tf_op jit(solution)/shard_map/ppermute | solution.py:446
  83.8 6.6 %collective-permute-start.21 = (bf16[160,512]{1,0:T(8,128)(2,1)S(1)}, bf16[160,512]{1,0:T(8,128)(2,1)S(1)}, u32[]{:S(2)}, u32[]{:S(2)}) collective-permute-start(bf16[160,512]{1,0:T(8,128)(2,1)S(1)} %get-tuple-element.148), channel_id=1, source_target_pairs={{0,3},{1,2},{2,1},{3,0},{4,7},{5,6},{6,5},{7,4},{8,11},{9,10},{10,... | collective-permute-start | bytes 491528 | tf_op jit(solution)/shard_map/ppermute | solution.py:446
  91.1 10.4 %collective-permute-start.25 = (bf16[208,512]{1,0:T(8,128)(2,1)S(1)}, bf16[208,512]{1,0:T(8,128)(2,1)S(1)}, u32[]{:S(2)}, u32[]{:S(2)}) collective-permute-start(bf16[208,512]{1,0:T(8,128)(2,1)S(1)} %join_spread.5), channel_id=1, source_target_pairs={{0,8},{4,12},{8,0},{12,4},{16,24},{20,28},{24,16},{28,20},{1,9},{5... | collective-permute-start | bytes 638984 | tf_op jit(solution)/shard_map/ppermute | solution.py:446
  92.7 5.9 %collective-permute-start.22 = (bf16[160,512]{1,0:T(8,128)(2,1)S(1)}, bf16[160,512]{1,0:T(8,128)(2,1)S(1)}, u32[]{:S(2)}, u32[]{:S(2)}) collective-permute-start(bf16[160,512]{1,0:T(8,128)(2,1)S(1)} %get-tuple-element.155), channel_id=1, source_target_pairs={{0,1},{1,0},{2,3},{3,2},{4,5},{5,4},{6,7},{7,6},{8,9},{9,8},{10,11... | collective-permute-start | bytes 491528 | tf_op jit(solution)/shard_map/ppermute | solution.py:446
  93.3 6.8 %collective-permute-start.23 = (bf16[160,512]{1,0:T(8,128)(2,1)S(1)}, bf16[160,512]{1,0:T(8,128)(2,1)S(1)}, u32[]{:S(2)}, u32[]{:S(2)}) collective-permute-start(bf16[160,512]{1,0:T(8,128)(2,1)S(1)} %get-tuple-element.156), channel_id=1, source_target_pairs={{0,2},{1,3},{2,0},{3,1},{4,6},{5,7},{6,4},{7,5},{8,10},{9,11},{10,... | collective-permute-start | bytes 491528 | tf_op jit(solution)/shard_map/ppermute | solution.py:446
  94.0 7.4 %collective-permute-start.24 = (bf16[160,512]{1,0:T(8,128)(2,1)S(1)}, bf16[160,512]{1,0:T(8,128)(2,1)S(1)}, u32[]{:S(2)}, u32[]{:S(2)}) collective-permute-start(bf16[160,512]{1,0:T(8,128)(2,1)S(1)} %get-tuple-element.157), channel_id=1, source_target_pairs={{0,3},{1,2},{2,1},{3,0},{4,7},{5,6},{6,5},{7,4},{8,11},{9,10},{10,... | collective-permute-start | bytes 491528 | tf_op jit(solution)/shard_map/ppermute | solution.py:446

commit v6 on v5

--- a/solution.py
+++ b/solution.py
@@ -342,32 +342,33 @@
     send(info, 1, *done, outs, flipped)
 
 
-def rows_part(info, codes, preds, protos, offset, rows, proto_count, away, earlier):
+def rows_part(info, codes, preds, protos, offset, rows, proto_count, aways, earlier):
     count, dim = protos[0].shape
     share = dim // proto_count
-    width = min(chunk, count)
+    width, blocks = min(chunk, count), max(len(aways), 1)
     shapes = [(2 * count // width, rows, width), (rows, 128), (rows, 128), (rows, dim), (dim, rows)]
     scratch = [pltpu.VMEM(shape, jnp.float32) for shape in shapes]
     if codes is None:
         kernel, ins, passed = pred_kernel, [preds, *protos], (1, 2)
         specs = [whole(value) for value in ins]
-    elif not away:
+    elif not aways:
         kernel, ins, passed = target_kernel, [codes, preds, *protos, offset, *earlier], ()
         specs, scratch = [whole(value) for value in ins], scratch[2:]
     else:
         kernel, ins = functools.partial(both_kernel, proto_count), [*codes, *preds, *protos, offset]
         passed = tuple(2 * proto_count + i for i in range(2))
-        quarter = pl.BlockSpec((1, *codes[0].shape[1:]), lambda i, info: (away - 1, 0, 0))
+        quarter = pl.BlockSpec((1, *codes[0].shape[1:]), lambda i, info: (aways[0] - 1 - i, 0, 0))
         specs = [quarter] * (2 * proto_count) + [whole(value) for value in ins[-3:]]
         scratch = [*scratch] + [pltpu.VMEM((rows, dim), jnp.bfloat16)] * 2
         scratch += [pltpu.VMEM(shapes[0], jnp.bfloat16)]
         scratch += [pltpu.VMEM(shape, jnp.float32) for shape in ((rows, dim), (rows, 128))]
-    parts, work = 2 if codes is not None else 1, 2 if away else 1
+    parts, work = 2 if codes is not None else 1, 2 * blocks if aways else 1
     high, tall = parts * (share + stat_rows), parts * (share + sent_rows)
-    outs = [jax.ShapeDtypeStruct((high, rows), jnp.float32)]
-    outs += [jax.ShapeDtypeStruct((tall, rows), jnp.bfloat16)] * (proto_count - 1)
+    outs = [jax.ShapeDtypeStruct((high, blocks * rows), jnp.float32)]
+    outs += [jax.ShapeDtypeStruct((tall, blocks * rows), jnp.bfloat16)] * (proto_count - 1)
     return call(
-        kernel, "rows_part", info, (1,), ins, specs, outs, [whole(out) for out in outs], scratch,
+        kernel, "rows_part", info, (blocks,), ins, specs, outs,
+        [pl.BlockSpec((out.shape[0], rows), lambda i, info: (0, i)) for out in outs], scratch,
         work * 8 * rows * count * dim, work * 2 * rows * count,
         6 if kernel is target_kernel else 20, passed,
     )
@@ -392,38 +393,43 @@
     return {"target": (target, stats[:2]), "pred": (high + rest, stats[2:])}
 
 
-def joined(parts, others=()):
+def joined(parts, at=slice(None), others=()):
     kept, *sent = parts
     high, tall = kept.shape[0] // len(names), sent[0].shape[0] // len(names)
     return [
         joins[name](
-            [parted(kept[i * high : (i + 1) * high, :])]
-            + [parted_sent(part[i * tall : (i + 1) * tall, :]) for part in sent]
+            [parted(kept[i * high : (i + 1) * high, at])]
+            + [parted_sent(part[i * tall : (i + 1) * tall, at]) for part in sent]
             + [part[name] for part in others]
         )
         for i, name in enumerate(names)
     ]
 
 
-def spread_kernel(info, *refs):
-    *parts, out = refs
-    out[...] = packed_far(*joined(parts))
-
-
-def join_spread(info, parts):
-    high, rows = parts[0].shape
+def spread_kernel(count, info, *refs):
+    parts, outs = refs[:count], refs[count:]
+    rows = outs[0].shape[1]
+    for block, out in enumerate(outs):
+        out[...] = packed_far(*joined(parts, slice(block * rows, (block + 1) * rows)))
+
+
+def join_spread(info, parts, rows):
+    high, length = parts[0].shape
     share = high // len(names) - stat_rows
-    out = jax.ShapeDtypeStruct((3 * share + sent_rows, rows), jnp.bfloat16)
+    outs = [
+        jax.ShapeDtypeStruct((3 * share + sent_rows, rows), jnp.bfloat16)
+        for _ in range(length // rows)
+    ]
     return call(
-        spread_kernel, "join_spread", info, (1,), parts, [whole(part) for part in parts], [out],
-        [whole(out)], [], 1 << 20, 0, 5,
+        functools.partial(spread_kernel, len(parts)), "join_spread", info, (1,), parts,
+        [whole(part) for part in parts], outs, [whole(out) for out in outs], [], 1 << 20, 0, 5,
     )
 
 
 def final_kernel(count, info, *refs):
     parts, far, (loss, pull) = refs[:count], refs[count:-2], refs[-2:]
     far = [parted_far(part[...]) for part in far]
-    (target, (mass, cross)), (pred, (peak, total)) = joined(parts, far)
+    (target, (mass, cross)), (pred, (peak, total)) = joined(parts, others=far)
     pull[...] = target / mass - pred / total
     loss[...] = peak * log2 + jnp.log(total) - cross / mass / pred_temp
 
@@ -470,7 +476,7 @@
         return [value] + [swap(value, "proto", s) for s in range(1, proto_count)]
 
     info, stats, *protos = stats_part(info, [codes_view], protos, None)
-    info, *values = rows_part(info, None, pred_view, protos, None, rows, proto_count, 0, None)
+    info, *values = rows_part(info, None, pred_view, protos, None, rows, proto_count, (), None)
     *earlier, near, across = values
     quarters, info = lax.optimization_barrier((quarters, info))
     codes = around(jnp.stack([value[:part] for value in quarters]))
@@ -481,28 +487,24 @@
     info, stats, *protos = stats_part(info, codes[1:], protos, stats)
     info, offset = offset_part(info, stats, swap(stats, "dp", 1))
 
-    far, waiting = [], []
-    for away in range(z_count - 1, 0, -1):
-        info, *values = rows_part(
-            info, codes, preds, protos, offset, rows, proto_count, away, None
+    def far_rows(info, protos, aways):
+        info, *out, near, across = rows_part(
+            info, codes, preds, protos, offset, rows, proto_count, aways, None
         )
-        *out, near, across = values
-        protos = near, across
-        out = sent(out)
-        for past, arrived in waiting:
-            if far:
-                far, arrived = lax.optimization_barrier((far, arrived))
-            info, part = join_spread(info, arrived)
-            far.append(swap(part, "dp", 2 * past))
-        waiting = [(away, out)]
+        return info, sent(out), (near, across)
+
+    aways = range(z_count - 1, 1, -1)
+    info, far, protos = far_rows(info, protos, aways)
+    info, late, protos = far_rows(info, protos, range(1, 0, -1))
+    info, *far = join_spread(info, far, rows)
+    far = [swap(part, "dp", 2 * away) for away, part in zip(aways, far)]
     info, *out = rows_part(
-        info, codes_view, pred_view, protos, offset, rows, proto_count, 0, earlier
+        info, codes_view, pred_view, protos, offset, rows, proto_count, (), earlier
     )
     own = sent(out)
-    ((past, arrived),) = waiting
-    far, arrived = lax.optimization_barrier((far, arrived))
-    info, part = join_spread(info, arrived)
-    loss, pull = finish(info, own, [*far, swap(part, "dp", 2 * past)])
+    far, late = lax.optimization_barrier((far, late))
+    info, part = join_spread(info, late, rows)
+    loss, pull = finish(info, own, [*far, swap(part, "dp", 2)])
     return (loss.reshape(rows), pull.T)
 
 

time: 103 us -> 112 us (1.087)
  waiting for transfers between devices: 13.2 us -> 28 us
  starting transfers between devices: 32.9 us -> 27.5 us
    ppermute x26 -> x23, waiting for transfers between devices: 13.2 us -> 28 us  [swap(): return lax.ppermute(value, axis, [(i, i ^ bits) for i in range(count)])]
    ppermute x26 -> x23, starting transfers between devices: 32.9 us -> 27.5 us  [swap(): return lax.ppermute(value, axis, [(i, i ^ bits) for i in range(count)])]
    pallas_call x13 -> x11, Pallas kernels: 53.7 us -> 52.8 us  [call(): pl.pallas_call(without, grid_spec=pltpu.PrefetchScalarGridSpec(num_scalar...]
  transfers between devices with their start and end apart: 26 -> 23, of which waited for: 8 -> 8; matrix products, arithmetic and copies ran while one was open for 1% -> 1% of each run, Pallas kernels for 42% -> 32%
where the time goes in v6:
time: 112 us
  Pallas kernels  52.8 us (47%)
  waiting for transfers between devices  28 us (25%)
  starting transfers between devices  27.5 us (25%)
  local copies, waits for them, and re-layouts  2.23 us (2%)
    pallas_call x11, Pallas kernels, call(): pl.pallas_call(without, grid_spec=pltpu.PrefetchScalarGridSpec(num_scalar...  52.8 us
    ppermute x23, waiting for transfers between devices, swap(): return lax.ppermute(value, axis, [(i, i ^ bits) for i in range(count)])  28 us
    ppermute x23, starting transfers between devices, swap(): return lax.ppermute(value, axis, [(i, i ^ bits) for i in range(count)])  27.5 us
  transfers between devices with their start and end apart: 23, of which 8 were waited for; matrix products, arithmetic and copies ran while one was open for 1% of the time, Pallas kernels for 32%

profile of v6, /device:TPU:0, one launch (start us, length us, event | category | flops | bytes accessed | tf_op | source)
XLA Modules:
  0.0 111.6 jit_solution(17939790941860996922)
XLA Ops:
  0.6 0.5 collective-permute-start.3
  1.1 0.9 constant_dynamic-slice_fusion
  2.1 4.7 %collective-permute-start.2 = (bf16[256,256]{1,0:T(8,128)(2,1)S(1)}, bf16[256,256]{1,0:T(8,128)(2,1)S(1)}, u32[]{:S(2)}, u32[]{:S(2)}) collective-permute-start(bf16[256,256]{1,0:T(8,128)(2,1)S(1)} %pad_maximum_fusion.2), channel_id=1, source_target_pairs={{0,24},{4,28},{8,16},{12,20},{16,8},{20,12},{24,0},{28,4},{1,25},{... | collective-permute-start | bytes 393224 | tf_op jit(solution)/shard_map/ppermute | solution.py:452
  6.8 0.6 collective-permute-start
  7.4 0.1 pad_add_fusion.refs_0_
  7.5 0.0 collective-permute-done.3.refs_3_
  7.5 1.3 %copy-done.2 = bf16[2048,256]{1,0:T(8,128)(2,1)S(1)} copy-done((bf16[2048,256]{1,0:T(8,128)(2,1)S(1)}, bf16[2048,256]{1,0:T(8,128)(2,1)}, u32[]{:S(2)}) %copy-start.2) | copy-done | bytes 1048600
  8.8 3.1 %stats_part.3 = (f32[8,8,512]{2,1,0:T(8,128)S(1)}, bf16[2048,256]{1,0:T(8,128)(2,1)S(1)}, bf16[2048,256]{1,0:T(8,128)(2,1)S(1)}) custom-call(s32[2]{0:T(128)S(1)} %pad_add_fusion.refs_0_, bf16[512,256]{1,0:T(8,128)(2,1)S(1)} %copy-done, bf16[2048,256]{1,0:T(8,128)(2,1)S(1)} %copy-done.2, ...), custom_call_target="tpu_custom_call", output_to_operand_aliasing={{2}: (3, {})} | custom-call | flops 1073741824 | bytes 8388608 | tf_op jit(solution)/shard_map/stats_part/pallas_call | solution.py:122
  11.9 4.9 %rows_part.4 = (f32[72,512]{1,0:T(8,128)S(1)}, bf16[80,512]{1,0:T(8,128)(2,1)S(1)}, bf16[80,512]{1,0:T(8,128)(2,1)S(1)}, bf16[80,512]{1,0:T(8,128)(2,1)S(1)}, bf...) custom-call(s32[2]{0:T(128)S(1)} %pad_add_fusion.refs_0_, ...), custom_call_target="tpu_custom_call", output_to_operand_aliasing={{4}: (2, {}), {5}: (3, {})} | custom-call | flops 2147483648 | bytes 16777216 | tf_op jit(solution)/shard_map/rows_part/pallas_call | solution.py:122
  16.8 0.0 collective-permute-done.2
  16.8 1.7 %collective-permute-done.1 = bf16[256,256]{1,0:T(8,128)(2,1)S(1)} collective-permute-done((bf16[256,256]{1,0:T(8,128)(2,1)S(1)}, bf16[256,256]{1,0:T(8,128)(2,1)S(1)}, u32[]{:S(2)}, u32[]{:S(2)}) %collective-permute-start.1) | collective-permute-done | bytes 131104 | tf_op jit(solution)/shard_map/ppermute | solution.py:452
  18.6 2.5 %collective-permute-start.6 = (bf16[3,128,256]{2,1,0:T(8,128)(2,1)S(1)}, bf16[3,128,256]{2,1,0:T(8,128)(2,1)S(1)}, u32[]{:S(2)}, u32[]{:S(2)}) collective-permute-start(bf16[3,128,256]{2,1,0:T(8,128)(2,1)S(1)} %pad_maximum_fusion.1.refs_1_), channel_id=1, source_target_pairs={{0,3},{1,2},{2,1},{3,0},{4,7},{5,6},{6,5},{7,4},{8,11},{9,10},{10,... | collective-permute-start | bytes 589832 | tf_op jit(solution)/shard_map/ppermute | solution.py:452
  21.1 0.5 collective-permute-start.5
  21.6 0.5 collective-permute-start.4
  22.2 4.3 %stats_part.4 = (f32[8,8,512]{2,1,0:T(8,128)S(1)}, bf16[2048,256]{1,0:T(8,128)(2,1)S(1)}, bf16[2048,256]{1,0:T(8,128)(2,1)S(1)}) custom-call(s32[2]{0:T(128)S(1)} %pad_add_fusion.refs_0_, bf16[3,128,256]{2,1,0:T(8,128)(2,1)S(1)} %pad_maximum_fusion.1.refs_1_, ...), custom_call_target="tpu_custom_call", output_to_operand_aliasing={{1}: (2, {}), {2}: (3, {})} | custom-call | flops 805306368 | bytes 6291456 | tf_op jit(solution)/shard_map/stats_part/pallas_call | solution.py:122
  26.5 2.5 %collective-permute-start.10 = (bf16[3,128,256]{2,1,0:T(8,128)(2,1)S(1)}, bf16[3,128,256]{2,1,0:T(8,128)(2,1)S(1)}, u32[]{:S(2)}, u32[]{:S(2)}) collective-permute-start(bf16[3,128,256]{2,1,0:T(8,128)(2,1)S(1)} %pad_maximum_fusion.refs_5_), channel_id=1, source_target_pairs={{0,3},{1,2},{2,1},{3,0},{4,7},{5,6},{6,5},{7,4},{8,11},{9,10},{10,... | collective-permute-start | bytes 589832 | tf_op jit(solution)/shard_map/ppermute | solution.py:452
  29.0 0.5 collective-permute-start.9
  29.6 0.0 collective-permute-done.6.refs_3_.refs_4_
  29.6 0.5 collective-permute-start.8
  30.1 1.6 %collective-permute-done.5.refs_2_.refs_3_ = bf16[3,128,256]{2,1,0:T(8,128)(2,1)S(1)} collective-permute-done((bf16[3,128,256]{2,1,0:T(8,128)(2,1)S(1)}, bf16[3,128,256]{2,1,0:T(8,128)(2,1)S(1)}, u32[]{:S(2)}, u32[]{:S(2)}) %collective-permute-start.5) | collective-permute-done | bytes 196640 | tf_op jit(solution)/shard_map/ppermute | solution.py:452
  31.7 11.6 %stats_part.5 = (f32[8,8,512]{2,1,0:T(8,128)S(1)}, bf16[2048,256]{1,0:T(8,128)(2,1)S(1)}, bf16[2048,256]{1,0:T(8,128)(2,1)S(1)}) custom-call(s32[2]{0:T(128)S(1)} %pad_add_fusion.refs_0_, bf16[3,128,256]{2,1,0:T(8,128)(2,1)S(1)} %collective-permute-done.4.refs_1_.refs_2_, ...), custom_call_target="tpu_custom_call", output_to_operand_aliasing={{1}: (4, {}), {2}: (5, {})} | custom-call | flops 2415919104 | bytes 18874368 | tf_op jit(solution)/shard_map/stats_part/pallas_call | solution.py:122
  43.3 0.1 collective-permute-start.7
  43.4 1.3 %collective-permute-done.7.refs_2_ = f32[8,8,512]{2,1,0:T(8,128)S(1)} collective-permute-done((f32[8,8,512]{2,1,0:T(8,128)S(1)}, f32[8,8,512]{2,1,0:T(8,128)S(1)}, u32[]{:S(2)}, u32[]{:S(2)}) %collective-permute-start.7) | collective-permute-done | bytes 131104 | tf_op jit(solution)/shard_map/ppermute | solution.py:452
  44.7 0.6 offset_part.1.refs_11_.refs_5_
  45.3 0.0 collective-permute-done.9.refs_7_
  45.4 0.0 collective-permute-done.8.refs_6_
  45.4 14.6 %rows_part.5 = (f32[144,1024]{1,0:T(8,128)S(1)}, bf16[160,1024]{1,0:T(8,128)(2,1)S(1)}, bf16[160,1024]{1,0:T(8,128)(2,1)S(1)}, bf16[160,1024]{1,0:T(8,128)(2,1)S...) custom-call(s32[2]{0:T(128)S(1)} %pad_add_fusion.refs_0_, ...), custom_call_target="tpu_custom_call", output_to_operand_aliasing={{4}: (9, {}), {5}: (10, {})} | custom-call | flops 8589934592 | bytes 67108864 | tf_op jit(solution)/shard_map/rows_part/pallas_call | solution.py:122
  59.9 1.6 %collective-permute-start.11 = (bf16[160,1024]{1,0:T(8,128)(2,1)S(1)}, bf16[160,1024]{1,0:T(8,128)(2,1)S(1)}, u32[]{:S(2)}, u32[]{:S(2)}) collective-permute-start(bf16[160,1024]{1,0:T(8,128)(2,1)S(1)} %get-tuple-element.104), channel_id=1, source_target_pairs={{0,1},{1,0},{2,3},{3,2},{4,5},{5,4},{6,7},{7,6},{8,9},{9,8},{10,11... | collective-permute-start | bytes 983048 | tf_op jit(solution)/shard_map/ppermute | solution.py:452
  61.5 3.3 %collective-permute-start.12 = (bf16[160,1024]{1,0:T(8,128)(2,1)S(1)}, bf16[160,1024]{1,0:T(8,128)(2,1)S(1)}, u32[]{:S(2)}, u32[]{:S(2)}) collective-permute-start(bf16[160,1024]{1,0:T(8,128)(2,1)S(1)} %get-tuple-element.105), channel_id=1, source_target_pairs={{0,2},{1,3},{2,0},{3,1},{4,6},{5,7},{6,4},{7,5},{8,10},{9,11},{10,... | collective-permute-start | bytes 983048 | tf_op jit(solution)/shard_map/ppermute | solution.py:452
  64.8 0.0 collective-permute-start.13
  64.8 7.5 %rows_part.6 = (f32[144,512]{1,0:T(8,128)S(1)}, bf16[160,512]{1,0:T(8,128)(2,1)S(1)}, bf16[160,512]{1,0:T(8,128)(2,1)S(1)}, bf16[160,512]{1,0:T(8,128)(2,1)S(1)}...) custom-call(s32[2]{0:T(128)S(1)} %pad_add_fusion.refs_0_, ...), custom_call_target="tpu_custom_call", output_to_operand_aliasing={{4}: (9, {}), {5}: (10, {})} | custom-call | flops 4294967296 | bytes 33554432 | tf_op jit(solution)/shard_map/rows_part/pallas_call | solution.py:122
  72.3 7.3 %collective-permute-done.12.refs_3_ = bf16[160,1024]{1,0:T(8,128)(2,1)S(1)} collective-permute-done((bf16[160,1024]{1,0:T(8,128)(2,1)S(1)}, bf16[160,1024]{1,0:T(8,128)(2,1)S(1)}, u32[]{:S(2)}, u32[]{:S(2)}) %collective-permute-start.12) | collective-permute-done | bytes 327712 | tf_op jit(solution)/shard_map/ppermute | solution.py:452
  79.5 0.8 join_spread.2
  80.4 2.5 %collective-permute-start.14 = (bf16[208,512]{1,0:T(8,128)(2,1)S(1)}, bf16[208,512]{1,0:T(8,128)(2,1)S(1)}, u32[]{:S(2)}, u32[]{:S(2)}) collective-permute-start(bf16[208,512]{1,0:T(8,128)(2,1)S(1)} %get-tuple-element.117), channel_id=1, source_target_pairs={{0,24},{4,28},{8,16},{12,20},{16,8},{20,12},{24,0},{28,4},{1,25},{... | collective-permute-start | bytes 638984 | tf_op jit(solution)/shard_map/ppermute | solution.py:452
  82.9 1.5 %collective-permute-start.16 = (bf16[160,512]{1,0:T(8,128)(2,1)S(1)}, bf16[160,512]{1,0:T(8,128)(2,1)S(1)}, u32[]{:S(2)}, u32[]{:S(2)}) collective-permute-start(bf16[160,512]{1,0:T(8,128)(2,1)S(1)} %get-tuple-element.120), channel_id=1, source_target_pairs={{0,1},{1,0},{2,3},{3,2},{4,5},{5,4},{6,7},{7,6},{8,9},{9,8},{10,11... | collective-permute-start | bytes 491528 | tf_op jit(solution)/shard_map/ppermute | solution.py:452
  84.4 0.6 collective-permute-start.17
  85.0 1.4 %collective-permute-start.18 = (bf16[160,512]{1,0:T(8,128)(2,1)S(1)}, bf16[160,512]{1,0:T(8,128)(2,1)S(1)}, u32[]{:S(2)}, u32[]{:S(2)}) collective-permute-start(bf16[160,512]{1,0:T(8,128)(2,1)S(1)} %get-tuple-element.122), channel_id=1, source_target_pairs={{0,3},{1,2},{2,1},{3,0},{4,7},{5,6},{6,5},{7,4},{8,11},{9,10},{10,... | collective-permute-start | bytes 491528 | tf_op jit(solution)/shard_map/ppermute | solution.py:452
  86.4 3.2 %rows_part.7 = (f32[144,512]{1,0:T(8,128)S(1)}, bf16[160,512]{1,0:T(8,128)(2,1)S(1)}, bf16[160,512]{1,0:T(8,128)(2,1)S(1)}, bf16[160,512]{1,0:T(8,128)(2,1)S(1)}) custom-call(s32[2]{0:T(128)S(1)} %pad_add_fusion.refs_0_, bf16[512,256]{1,0:T(8,128)(2,1)S(1)} %copy-done, bf16[512,256]{1,0:T(8,128)(2,1)S(1)} %copy-done.1, ...), custom_call_target="tpu_custom_call" | custom-call | flops 2147483648 | bytes 16777216 | tf_op jit(solution)/shard_map/rows_part/pallas_call | solution.py:122
  89.7 3.1 %collective-permute-done.17.refs_3_ = bf16[160,512]{1,0:T(8,128)(2,1)S(1)} collective-permute-done((bf16[160,512]{1,0:T(8,128)(2,1)S(1)}, bf16[160,512]{1,0:T(8,128)(2,1)S(1)}, u32[]{:S(2)}, u32[]{:S(2)}) %collective-permute-start.17) | collective-permute-done | bytes 163872 | tf_op jit(solution)/shard_map/ppermute | solution.py:452
  92.8 7.4 %collective-permute-done.15.refs_6_ = bf16[208,512]{1,0:T(8,128)(2,1)S(1)} collective-permute-done((bf16[208,512]{1,0:T(8,128)(2,1)S(1)}, bf16[208,512]{1,0:T(8,128)(2,1)S(1)}, u32[]{:S(2)}, u32[]{:S(2)}) %collective-permute-start.15) | collective-permute-done | bytes 213024 | tf_op jit(solution)/shard_map/ppermute | solution.py:452
  100.2 0.7 join_spread.3
  100.9 0.1 collective-permute-start.22
  100.9 1.4 %collective-permute-start.19 = (bf16[160,512]{1,0:T(8,128)(2,1)S(1)}, bf16[160,512]{1,0:T(8,128)(2,1)S(1)}, u32[]{:S(2)}, u32[]{:S(2)}) collective-permute-start(bf16[160,512]{1,0:T(8,128)(2,1)S(1)} %get-tuple-element.129), channel_id=1, source_target_pairs={{0,1},{1,0},{2,3},{3,2},{4,5},{5,4},{6,7},{7,6},{8,9},{9,8},{10,11... | collective-permute-start | bytes 491528 | tf_op jit(solution)/shard_map/ppermute | solution.py:452
  102.4 0.6 collective-permute-start.20
  103.0 1.5 %collective-permute-start.21 = (bf16[160,512]{1,0:T(8,128)(2,1)S(1)}, bf16[160,512]{1,0:T(8,128)(2,1)S(1)}, u32[]{:S(2)}, u32[]{:S(2)}) collective-permute-start(bf16[160,512]{1,0:T(8,128)(2,1)S(1)} %get-tuple-element.131), channel_id=1, source_target_pairs={{0,3},{1,2},{2,1},{3,0},{4,7},{5,6},{6,5},{7,4},{8,11},{9,10},{10,... | collective-permute-start | bytes 491528 | tf_op jit(solution)/shard_map/ppermute | solution.py:452
  104.5 3.3 %collective-permute-done.19.refs_2_ = bf16[160,512]{1,0:T(8,128)(2,1)S(1)} collective-permute-done((bf16[160,512]{1,0:T(8,128)(2,1)S(1)}, bf16[160,512]{1,0:T(8,128)(2,1)S(1)}, u32[]{:S(2)}, u32[]{:S(2)}) %collective-permute-start.19) | collective-permute-done | bytes 163872 | tf_op jit(solution)/shard_map/ppermute | solution.py:452
  107.8 2.3 %collective-permute-done.20.refs_3_ = bf16[160,512]{1,0:T(8,128)(2,1)S(1)} collective-permute-done((bf16[160,512]{1,0:T(8,128)(2,1)S(1)}, bf16[160,512]{1,0:T(8,128)(2,1)S(1)}, u32[]{:S(2)}, u32[]{:S(2)}) %collective-permute-start.20) | collective-permute-done | bytes 163872 | tf_op jit(solution)/shard_map/ppermute | solution.py:452
  110.1 1.5 %finish.1 = (f32[1,512]{1,0:T(1,128)}, f32[64,512]{1,0:T(8,128)}) custom-call(s32[2]{0:T(128)S(1)} %pad_add_fusion.refs_0_, f32[144,512]{1,0:T(8,128)S(1)} %get-tuple-element.128.refs_1_, bf16[160,512]{1,0:T(8,128)(2,1)S(1)} %collective-permute-done.19.refs_2_, bf16[160,512]{1,0:T(8,128)(2,1)S(1)} %collective-permute-done.20.refs_3_, ...), custom_call_target="tpu_custom_call" | custom-call | flops 1048576 | bytes 8192 | tf_op jit(solution)/shard_map/finish/pallas_call | solution.py:122
  (23 shorter events, 0.1 us)
Async XLA Ops:
  0.6 6.9 %collective-permute-start.3 = (bf16[2048,256]{1,0:T(8,128)(2,1)}, bf16[2048,256]{1,0:T(8,128)(2,1)S(1)}, u32[]{:S(2)}, u32[]{:S(2)}) collective-permute-start(bf16[2048,256]{1,0:T(8,128)(2,1)} %refs_2_.2), channel_id=1, source_target_pairs={{0,4},{4,0},{8,12},{12,8},{16,20},{20,16},{24,28},{28,24},{1,5},{5... | collective-permute-start | bytes 3145736 | tf_op jit(solution)/shard_map/ppermute | solution.py:452
  1.1 6.4 %copy-start = (bf16[512,256]{1,0:T(8,128)(2,1)S(1)}, bf16[512,256]{1,0:T(8,128)(2,1)}, u32[]{:S(2)}) copy-start(bf16[512,256]{1,0:T(8,128)(2,1)} %refs_1_.5) | copy-start | bytes 786436
  2.1 14.7 %collective-permute-start.2 = (bf16[256,256]{1,0:T(8,128)(2,1)S(1)}, bf16[256,256]{1,0:T(8,128)(2,1)S(1)}, u32[]{:S(2)}, u32[]{:S(2)}) collective-permute-start(bf16[256,256]{1,0:T(8,128)(2,1)S(1)} %pad_maximum_fusion.2), channel_id=1, source_target_pairs={{0,24},{4,28},{8,16},{12,20},{16,8},{20,12},{24,0},{28,4},{1,25},{... | collective-permute-start | bytes 393224 | tf_op jit(solution)/shard_map/ppermute | solution.py:452
  6.8 11.7 %collective-permute-start.1 = (bf16[256,256]{1,0:T(8,128)(2,1)S(1)}, bf16[256,256]{1,0:T(8,128)(2,1)S(1)}, u32[]{:S(2)}, u32[]{:S(2)}) collective-permute-start(bf16[256,256]{1,0:T(8,128)(2,1)S(1)} %pad_maximum_fusion.2), channel_id=1, source_target_pairs={{0,16},{4,20},{8,24},{12,28},{16,0},{20,4},{24,8},{28,12},{1,17},{... | collective-permute-start | bytes 393224 | tf_op jit(solution)/shard_map/ppermute | solution.py:452
  6.8 11.7 %collective-permute-start = (bf16[256,256]{1,0:T(8,128)(2,1)S(1)}, bf16[256,256]{1,0:T(8,128)(2,1)S(1)}, u32[]{:S(2)}, u32[]{:S(2)}) collective-permute-start(bf16[256,256]{1,0:T(8,128)(2,1)S(1)} %pad_maximum_fusion.2), channel_id=1, source_target_pairs={{0,8},{4,12},{8,0},{12,4},{16,24},{20,28},{24,16},{28,20},{1,9},{5... | collective-permute-start | bytes 393224 | tf_op jit(solution)/shard_map/ppermute | solution.py:452
  7.5 4.4 %copy-start.1 = (bf16[512,256]{1,0:T(8,128)(2,1)S(1)}, bf16[512,256]{1,0:T(8,128)(2,1)}, u32[]{:S(2)}) copy-start(bf16[512,256]{1,0:T(8,128)(2,1)} %refs_2_.3) | copy-start | bytes 786436
  7.5 1.3 %copy-start.2 = (bf16[2048,256]{1,0:T(8,128)(2,1)S(1)}, bf16[2048,256]{1,0:T(8,128)(2,1)}, u32[]{:S(2)}) copy-start(bf16[2048,256]{1,0:T(8,128)(2,1)} %refs_2_.2) | copy-start | bytes 3145732
  18.6 11.0 %collective-permute-start.6 = (bf16[3,128,256]{2,1,0:T(8,128)(2,1)S(1)}, bf16[3,128,256]{2,1,0:T(8,128)(2,1)S(1)}, u32[]{:S(2)}, u32[]{:S(2)}) collective-permute-start(bf16[3,128,256]{2,1,0:T(8,128)(2,1)S(1)} %pad_maximum_fusion.1.refs_1_), channel_id=1, source_target_pairs={{0,3},{1,2},{2,1},{3,0},{4,7},{5,6},{6,5},{7,4},{8,11},{9,10},{10,... | collective-permute-start | bytes 589832 | tf_op jit(solution)/shard_map/ppermute | solution.py:452
  21.1 10.6 %collective-permute-start.5 = (bf16[3,128,256]{2,1,0:T(8,128)(2,1)S(1)}, bf16[3,128,256]{2,1,0:T(8,128)(2,1)S(1)}, u32[]{:S(2)}, u32[]{:S(2)}) collective-permute-start(bf16[3,128,256]{2,1,0:T(8,128)(2,1)S(1)} %pad_maximum_fusion.1.refs_1_), channel_id=1, source_target_pairs={{0,2},{1,3},{2,0},{3,1},{4,6},{5,7},{6,4},{7,5},{8,10},{9,11},{10,... | collective-permute-start | bytes 589832 | tf_op jit(solution)/shard_map/ppermute | solution.py:452
  21.6 10.1 %collective-permute-start.4 = (bf16[3,128,256]{2,1,0:T(8,128)(2,1)S(1)}, bf16[3,128,256]{2,1,0:T(8,128)(2,1)S(1)}, u32[]{:S(2)}, u32[]{:S(2)}) collective-permute-start(bf16[3,128,256]{2,1,0:T(8,128)(2,1)S(1)} %pad_maximum_fusion.1.refs_1_), channel_id=1, source_target_pairs={{0,1},{1,0},{2,3},{3,2},{4,5},{5,4},{6,7},{7,6},{8,9},{9,8},{10,11... | collective-permute-start | bytes 589832 | tf_op jit(solution)/shard_map/ppermute | solution.py:452
  26.5 18.8 %collective-permute-start.10 = (bf16[3,128,256]{2,1,0:T(8,128)(2,1)S(1)}, bf16[3,128,256]{2,1,0:T(8,128)(2,1)S(1)}, u32[]{:S(2)}, u32[]{:S(2)}) collective-permute-start(bf16[3,128,256]{2,1,0:T(8,128)(2,1)S(1)} %pad_maximum_fusion.refs_5_), channel_id=1, source_target_pairs={{0,3},{1,2},{2,1},{3,0},{4,7},{5,6},{6,5},{7,4},{8,11},{9,10},{10,... | collective-permute-start | bytes 589832 | tf_op jit(solution)/shard_map/ppermute | solution.py:452
  29.0 16.3 %collective-permute-start.9 = (bf16[3,128,256]{2,1,0:T(8,128)(2,1)S(1)}, bf16[3,128,256]{2,1,0:T(8,128)(2,1)S(1)}, u32[]{:S(2)}, u32[]{:S(2)}) collective-permute-start(bf16[3,128,256]{2,1,0:T(8,128)(2,1)S(1)} %pad_maximum_fusion.refs_5_), channel_id=1, source_target_pairs={{0,2},{1,3},{2,0},{3,1},{4,6},{5,7},{6,4},{7,5},{8,10},{9,11},{10,... | collective-permute-start | bytes 589832 | tf_op jit(solution)/shard_map/ppermute | solution.py:452
  29.6 15.8 %collective-permute-start.8 = (bf16[3,128,256]{2,1,0:T(8,128)(2,1)S(1)}, bf16[3,128,256]{2,1,0:T(8,128)(2,1)S(1)}, u32[]{:S(2)}, u32[]{:S(2)}) collective-permute-start(bf16[3,128,256]{2,1,0:T(8,128)(2,1)S(1)} %pad_maximum_fusion.refs_5_), channel_id=1, source_target_pairs={{0,1},{1,0},{2,3},{3,2},{4,5},{5,4},{6,7},{7,6},{8,9},{9,8},{10,11... | collective-permute-start | bytes 589832 | tf_op jit(solution)/shard_map/ppermute | solution.py:452
  43.3 1.4 %collective-permute-start.7 = (f32[8,8,512]{2,1,0:T(8,128)S(1)}, f32[8,8,512]{2,1,0:T(8,128)S(1)}, u32[]{:S(2)}, u32[]{:S(2)}) collective-permute-start(f32[8,8,512]{2,1,0:T(8,128)S(1)} %get-tuple-element.91.refs_1_), channel_id=1, source_target_pairs={{0,4},{4,0},{8,12},{12,8},{16,20},{20,16},{24,28},{28,24},{1,5},{5... | collective-permute-start | bytes 393224 | tf_op jit(solution)/shard_map/ppermute | solution.py:452
  59.9 12.3 %collective-permute-start.11 = (bf16[160,1024]{1,0:T(8,128)(2,1)S(1)}, bf16[160,1024]{1,0:T(8,128)(2,1)S(1)}, u32[]{:S(2)}, u32[]{:S(2)}) collective-permute-start(bf16[160,1024]{1,0:T(8,128)(2,1)S(1)} %get-tuple-element.104), channel_id=1, source_target_pairs={{0,1},{1,0},{2,3},{3,2},{4,5},{5,4},{6,7},{7,6},{8,9},{9,8},{10,11... | collective-permute-start | bytes 983048 | tf_op jit(solution)/shard_map/ppermute | solution.py:452
  61.5 18.0 %collective-permute-start.12 = (bf16[160,1024]{1,0:T(8,128)(2,1)S(1)}, bf16[160,1024]{1,0:T(8,128)(2,1)S(1)}, u32[]{:S(2)}, u32[]{:S(2)}) collective-permute-start(bf16[160,1024]{1,0:T(8,128)(2,1)S(1)} %get-tuple-element.105), channel_id=1, source_target_pairs={{0,2},{1,3},{2,0},{3,1},{4,6},{5,7},{6,4},{7,5},{8,10},{9,11},{10,... | collective-permute-start | bytes 983048 | tf_op jit(solution)/shard_map/ppermute | solution.py:452
  64.8 14.8 %collective-permute-start.13 = (bf16[160,1024]{1,0:T(8,128)(2,1)S(1)}, bf16[160,1024]{1,0:T(8,128)(2,1)S(1)}, u32[]{:S(2)}, u32[]{:S(2)}) collective-permute-start(bf16[160,1024]{1,0:T(8,128)(2,1)S(1)} %get-tuple-element.106), channel_id=1, source_target_pairs={{0,3},{1,2},{2,1},{3,0},{4,7},{5,6},{6,5},{7,4},{8,11},{9,10},{10,... | collective-permute-start | bytes 983048 | tf_op jit(solution)/shard_map/ppermute | solution.py:452
  80.4 12.4 %collective-permute-start.14 = (bf16[208,512]{1,0:T(8,128)(2,1)S(1)}, bf16[208,512]{1,0:T(8,128)(2,1)S(1)}, u32[]{:S(2)}, u32[]{:S(2)}) collective-permute-start(bf16[208,512]{1,0:T(8,128)(2,1)S(1)} %get-tuple-element.117), channel_id=1, source_target_pairs={{0,24},{4,28},{8,16},{12,20},{16,8},{20,12},{24,0},{28,4},{1,25},{... | collective-permute-start | bytes 638984 | tf_op jit(solution)/shard_map/ppermute | solution.py:452
  82.9 17.2 %collective-permute-start.15 = (bf16[208,512]{1,0:T(8,128)(2,1)S(1)}, bf16[208,512]{1,0:T(8,128)(2,1)S(1)}, u32[]{:S(2)}, u32[]{:S(2)}) collective-permute-start(bf16[208,512]{1,0:T(8,128)(2,1)S(1)} %get-tuple-element.118), channel_id=1, source_target_pairs={{0,16},{4,20},{8,24},{12,28},{16,0},{20,4},{24,8},{28,12},{1,17},{... | collective-permute-start | bytes 638984 | tf_op jit(solution)/shard_map/ppermute | solution.py:452
  82.9 6.7 %collective-permute-start.16 = (bf16[160,512]{1,0:T(8,128)(2,1)S(1)}, bf16[160,512]{1,0:T(8,128)(2,1)S(1)}, u32[]{:S(2)}, u32[]{:S(2)}) collective-permute-start(bf16[160,512]{1,0:T(8,128)(2,1)S(1)} %get-tuple-element.120), channel_id=1, source_target_pairs={{0,1},{1,0},{2,3},{3,2},{4,5},{5,4},{6,7},{7,6},{8,9},{9,8},{10,11... | collective-permute-start | bytes 491528 | tf_op jit(solution)/shard_map/ppermute | solution.py:452
  84.4 8.4 %collective-permute-start.17 = (bf16[160,512]{1,0:T(8,128)(2,1)S(1)}, bf16[160,512]{1,0:T(8,128)(2,1)S(1)}, u32[]{:S(2)}, u32[]{:S(2)}) collective-permute-start(bf16[160,512]{1,0:T(8,128)(2,1)S(1)} %get-tuple-element.121), channel_id=1, source_target_pairs={{0,2},{1,3},{2,0},{3,1},{4,6},{5,7},{6,4},{7,5},{8,10},{9,11},{10,... | collective-permute-start | bytes 491528 | tf_op jit(solution)/shard_map/ppermute | solution.py:452
  85.0 7.7 %collective-permute-start.18 = (bf16[160,512]{1,0:T(8,128)(2,1)S(1)}, bf16[160,512]{1,0:T(8,128)(2,1)S(1)}, u32[]{:S(2)}, u32[]{:S(2)}) collective-permute-start(bf16[160,512]{1,0:T(8,128)(2,1)S(1)} %get-tuple-element.122), channel_id=1, source_target_pairs={{0,3},{1,2},{2,1},{3,0},{4,7},{5,6},{6,5},{7,4},{8,11},{9,10},{10,... | collective-permute-start | bytes 491528 | tf_op jit(solution)/shard_map/ppermute | solution.py:452
  100.9 9.3 %collective-permute-start.22 = (bf16[208,512]{1,0:T(8,128)(2,1)S(1)}, bf16[208,512]{1,0:T(8,128)(2,1)S(1)}, u32[]{:S(2)}, u32[]{:S(2)}) collective-permute-start(bf16[208,512]{1,0:T(8,128)(2,1)S(1)} %join_spread.3), channel_id=1, source_target_pairs={{0,8},{4,12},{8,0},{12,4},{16,24},{20,28},{24,16},{28,20},{1,9},{5... | collective-permute-start | bytes 638984 | tf_op jit(solution)/shard_map/ppermute | solution.py:452
  100.9 6.8 %collective-permute-start.19 = (bf16[160,512]{1,0:T(8,128)(2,1)S(1)}, bf16[160,512]{1,0:T(8,128)(2,1)S(1)}, u32[]{:S(2)}, u32[]{:S(2)}) collective-permute-start(bf16[160,512]{1,0:T(8,128)(2,1)S(1)} %get-tuple-element.129), channel_id=1, source_target_pairs={{0,1},{1,0},{2,3},{3,2},{4,5},{5,4},{6,7},{7,6},{8,9},{9,8},{10,11... | collective-permute-start | bytes 491528 | tf_op jit(solution)/shard_map/ppermute | solution.py:452
  102.4 7.7 %collective-permute-start.20 = (bf16[160,512]{1,0:T(8,128)(2,1)S(1)}, bf16[160,512]{1,0:T(8,128)(2,1)S(1)}, u32[]{:S(2)}, u32[]{:S(2)}) collective-permute-start(bf16[160,512]{1,0:T(8,128)(2,1)S(1)} %get-tuple-element.130), channel_id=1, source_target_pairs={{0,2},{1,3},{2,0},{3,1},{4,6},{5,7},{6,4},{7,5},{8,10},{9,11},{10,... | collective-permute-start | bytes 491528 | tf_op jit(solution)/shard_map/ppermute | solution.py:452
  103.0 7.1 %collective-permute-start.21 = (bf16[160,512]{1,0:T(8,128)(2,1)S(1)}, bf16[160,512]{1,0:T(8,128)(2,1)S(1)}, u32[]{:S(2)}, u32[]{:S(2)}) collective-permute-start(bf16[160,512]{1,0:T(8,128)(2,1)S(1)} %get-tuple-element.131), channel_id=1, source_target_pairs={{0,3},{1,2},{2,1},{3,0},{4,7},{5,6},{6,5},{7,4},{8,11},{9,10},{10,... | collective-permute-start | bytes 491528 | tf_op jit(solution)/shard_map/ppermute | solution.py:452

commit v7 on v5

--- a/solution.py
+++ b/solution.py
@@ -17,7 +17,7 @@
 stat_rows = 8
 sent_rows = 16
 low = -1e30
-chunk = 512
+chunk = 1024
 mebi = 1024 * 1024
 
 
@@ -222,7 +222,7 @@
     return call(
         functools.partial(stats_kernel, before is None), "stats_part", info, (1,), ins,
         [whole(value) for value in ins], outs, [whole(out) for out in outs], [],
-        4 * rows * count * dim, 2 * rows * count, 6, passed,
+        4 * rows * count * dim, 2 * rows * count, 12, passed,
     )
 
 
@@ -369,7 +369,7 @@
     return call(
         kernel, "rows_part", info, (1,), ins, specs, outs, [whole(out) for out in outs], scratch,
         work * 8 * rows * count * dim, work * 2 * rows * count,
-        6 if kernel is target_kernel else 20, passed,
+        12 if kernel is target_kernel else 26, passed,
     )
 
 
@@ -502,6 +502,7 @@
     ((past, arrived),) = waiting
     far, arrived = lax.optimization_barrier((far, arrived))
     info, part = join_spread(info, arrived)
+    own[1], part = lax.optimization_barrier((own[1], part))
     loss, pull = finish(info, own, [*far, swap(part, "dp", 2 * past)])
     return (loss.reshape(rows), pull.T)
 

time: 103 us -> 101 us (0.981)
  Pallas kernels: 53.7 us -> 49.5 us
  waiting for transfers between devices: 13.2 us -> 15.4 us
    pallas_call x13, Pallas kernels: 53.7 us -> 49.5 us  [call(): pl.pallas_call(without, grid_spec=pltpu.PrefetchScalarGridSpec(num_scalar...]
    ppermute x26, waiting for transfers between devices: 13.2 us -> 15.4 us  [swap(): return lax.ppermute(value, axis, [(i, i ^ bits) for i in range(count)])]
  transfers between devices with their start and end apart: 26 -> 26, of which waited for: 8 -> 7; matrix products, arithmetic and copies ran while one was open for 1% -> 1% of each run, Pallas kernels for 42% -> 41%
where the time goes in v7:
time: 101 us
  Pallas kernels  49.5 us (49%)
  starting transfers between devices  33 us (33%)
  waiting for transfers between devices  15.4 us (15%)
  local copies, waits for them, and re-layouts  2.23 us (2%)
    pallas_call x13, Pallas kernels, call(): pl.pallas_call(without, grid_spec=pltpu.PrefetchScalarGridSpec(num_scalar...  49.5 us
    ppermute x26, starting transfers between devices, swap(): return lax.ppermute(value, axis, [(i, i ^ bits) for i in range(count)])  33 us
    ppermute x26, waiting for transfers between devices, swap(): return lax.ppermute(value, axis, [(i, i ^ bits) for i in range(count)])  15.4 us
  transfers between devices with their start and end apart: 26, of which 7 were waited for; matrix products, arithmetic and copies ran while one was open for 1% of the time, Pallas kernels for 41%

profile of v7, /device:TPU:0, one launch (start us, length us, event | category | flops | bytes accessed | tf_op | source)
XLA Modules:
  0.0 101.1 jit_solution(968110143273640228)
XLA Ops:
  0.6 0.5 collective-permute-start.3
  1.1 0.9 constant_dynamic-slice_fusion
  2.1 4.7 %collective-permute-start.2 = (bf16[256,256]{1,0:T(8,128)(2,1)S(1)}, bf16[256,256]{1,0:T(8,128)(2,1)S(1)}, u32[]{:S(2)}, u32[]{:S(2)}) collective-permute-start(bf16[256,256]{1,0:T(8,128)(2,1)S(1)} %pad_maximum_fusion.2), channel_id=1, source_target_pairs={{0,24},{4,28},{8,16},{12,20},{16,8},{20,12},{24,0},{28,4},{1,25},{... | collective-permute-start | bytes 393224 | tf_op jit(solution)/shard_map/ppermute | solution.py:446
  6.8 0.6 collective-permute-start
  7.4 0.1 pad_add_fusion.refs_0_
  7.5 0.0 collective-permute-done.3.refs_3_
  7.5 1.3 %copy-done.2 = bf16[2048,256]{1,0:T(8,128)(2,1)S(1)} copy-done((bf16[2048,256]{1,0:T(8,128)(2,1)S(1)}, bf16[2048,256]{1,0:T(8,128)(2,1)}, u32[]{:S(2)}) %copy-start.2) | copy-done | bytes 1048600
  8.8 3.0 %stats_part.3 = (f32[4,8,1024]{2,1,0:T(8,128)S(1)}, bf16[2048,256]{1,0:T(8,128)(2,1)S(1)}, bf16[2048,256]{1,0:T(8,128)(2,1)S(1)}) custom-call(s32[2]{0:T(128)S(1)} %pad_add_fusion.refs_0_, bf16[512,256]{1,0:T(8,128)(2,1)S(1)} %copy-done, bf16[2048,256]{1,0:T(8,128)(2,1)S(1)} %copy-done.2, ...), custom_call_target="tpu_custom_call", output_to_operand_aliasing={{2}: (3, {})} | custom-call | flops 1073741824 | bytes 8388608 | tf_op jit(solution)/shard_map/stats_part/pallas_call | solution.py:122
  11.8 4.2 %rows_part.5 = (f32[72,512]{1,0:T(8,128)S(1)}, bf16[80,512]{1,0:T(8,128)(2,1)S(1)}, bf16[80,512]{1,0:T(8,128)(2,1)S(1)}, bf16[80,512]{1,0:T(8,128)(2,1)S(1)}, bf...) custom-call(s32[2]{0:T(128)S(1)} %pad_add_fusion.refs_0_, ...), custom_call_target="tpu_custom_call", output_to_operand_aliasing={{4}: (2, {}), {5}: (3, {})} | custom-call | flops 2147483648 | bytes 16777216 | tf_op jit(solution)/shard_map/rows_part/pallas_call | solution.py:122
  16.0 2.5 %collective-permute-done.1 = bf16[256,256]{1,0:T(8,128)(2,1)S(1)} collective-permute-done((bf16[256,256]{1,0:T(8,128)(2,1)S(1)}, bf16[256,256]{1,0:T(8,128)(2,1)S(1)}, u32[]{:S(2)}, u32[]{:S(2)}) %collective-permute-start.1) | collective-permute-done | bytes 131104 | tf_op jit(solution)/shard_map/ppermute | solution.py:446
  18.6 2.5 %collective-permute-start.6 = (bf16[3,128,256]{2,1,0:T(8,128)(2,1)S(1)}, bf16[3,128,256]{2,1,0:T(8,128)(2,1)S(1)}, u32[]{:S(2)}, u32[]{:S(2)}) collective-permute-start(bf16[3,128,256]{2,1,0:T(8,128)(2,1)S(1)} %pad_maximum_fusion.1.refs_1_), channel_id=1, source_target_pairs={{0,3},{1,2},{2,1},{3,0},{4,7},{5,6},{6,5},{7,4},{8,11},{9,10},{10,... | collective-permute-start | bytes 589832 | tf_op jit(solution)/shard_map/ppermute | solution.py:446
  21.1 0.5 collective-permute-start.5
  21.6 0.5 collective-permute-start.4
  22.2 4.0 %stats_part.4 = (f32[4,8,1024]{2,1,0:T(8,128)S(1)}, bf16[2048,256]{1,0:T(8,128)(2,1)S(1)}, bf16[2048,256]{1,0:T(8,128)(2,1)S(1)}) custom-call(s32[2]{0:T(128)S(1)} %pad_add_fusion.refs_0_, bf16[3,128,256]{2,1,0:T(8,128)(2,1)S(1)} %pad_maximum_fusion.1.refs_1_, ...), custom_call_target="tpu_custom_call", output_to_operand_aliasing={{1}: (2, {}), {2}: (3, {})} | custom-call | flops 805306368 | bytes 6291456 | tf_op jit(solution)/shard_map/stats_part/pallas_call | solution.py:122
  26.2 2.5 %collective-permute-start.10 = (bf16[3,128,256]{2,1,0:T(8,128)(2,1)S(1)}, bf16[3,128,256]{2,1,0:T(8,128)(2,1)S(1)}, u32[]{:S(2)}, u32[]{:S(2)}) collective-permute-start(bf16[3,128,256]{2,1,0:T(8,128)(2,1)S(1)} %pad_maximum_fusion.refs_5_), channel_id=1, source_target_pairs={{0,3},{1,2},{2,1},{3,0},{4,7},{5,6},{6,5},{7,4},{8,11},{9,10},{10,... | collective-permute-start | bytes 589832 | tf_op jit(solution)/shard_map/ppermute | solution.py:446
  28.7 0.5 collective-permute-start.9
  29.2 0.0 collective-permute-done.6.refs_3_.refs_4_
  29.2 0.5 collective-permute-start.8
  29.8 1.9 %collective-permute-done.5.refs_2_.refs_3_ = bf16[3,128,256]{2,1,0:T(8,128)(2,1)S(1)} collective-permute-done((bf16[3,128,256]{2,1,0:T(8,128)(2,1)S(1)}, bf16[3,128,256]{2,1,0:T(8,128)(2,1)S(1)}, u32[]{:S(2)}, u32[]{:S(2)}) %collective-permute-start.5) | collective-permute-done | bytes 196640 | tf_op jit(solution)/shard_map/ppermute | solution.py:446
  31.7 10.6 %stats_part.5 = (f32[4,8,1024]{2,1,0:T(8,128)S(1)}, bf16[2048,256]{1,0:T(8,128)(2,1)S(1)}, bf16[2048,256]{1,0:T(8,128)(2,1)S(1)}) custom-call(s32[2]{0:T(128)S(1)} %pad_add_fusion.refs_0_, bf16[3,128,256]{2,1,0:T(8,128)(2,1)S(1)} %collective-permute-done.4.refs_1_.refs_2_, ...), custom_call_target="tpu_custom_call", output_to_operand_aliasing={{1}: (4, {}), {2}: (5, {})} | custom-call | flops 2415919104 | bytes 18874368 | tf_op jit(solution)/shard_map/stats_part/pallas_call | solution.py:122
  42.3 0.1 collective-permute-start.7
  42.4 1.3 %collective-permute-done.7.refs_2_ = f32[4,8,1024]{2,1,0:T(8,128)S(1)} collective-permute-done((f32[4,8,1024]{2,1,0:T(8,128)S(1)}, f32[4,8,1024]{2,1,0:T(8,128)S(1)}, u32[]{:S(2)}, u32[]{:S(2)}) %collective-permute-start.7) | collective-permute-done | bytes 131104 | tf_op jit(solution)/shard_map/ppermute | solution.py:446
  43.7 0.6 offset_part.1.refs_11_.refs_5_
  44.4 6.7 %rows_part.6 = (f32[144,512]{1,0:T(8,128)S(1)}, bf16[160,512]{1,0:T(8,128)(2,1)S(1)}, bf16[160,512]{1,0:T(8,128)(2,1)S(1)}, bf16[160,512]{1,0:T(8,128)(2,1)S(1)}...) custom-call(s32[2]{0:T(128)S(1)} %pad_add_fusion.refs_0_, ...), custom_call_target="tpu_custom_call", output_to_operand_aliasing={{4}: (9, {}), {5}: (10, {})} | custom-call | flops 4294967296 | bytes 33554432 | tf_op jit(solution)/shard_map/rows_part/pallas_call | solution.py:122
  51.1 1.6 %collective-permute-start.11 = (bf16[160,512]{1,0:T(8,128)(2,1)S(1)}, bf16[160,512]{1,0:T(8,128)(2,1)S(1)}, u32[]{:S(2)}, u32[]{:S(2)}) collective-permute-start(bf16[160,512]{1,0:T(8,128)(2,1)S(1)} %get-tuple-element.119), channel_id=1, source_target_pairs={{0,1},{1,0},{2,3},{3,2},{4,5},{5,4},{6,7},{7,6},{8,9},{9,8},{10,11... | collective-permute-start | bytes 491528 | tf_op jit(solution)/shard_map/ppermute | solution.py:446
  52.6 3.3 %collective-permute-start.12 = (bf16[160,512]{1,0:T(8,128)(2,1)S(1)}, bf16[160,512]{1,0:T(8,128)(2,1)S(1)}, u32[]{:S(2)}, u32[]{:S(2)}) collective-permute-start(bf16[160,512]{1,0:T(8,128)(2,1)S(1)} %get-tuple-element.120), channel_id=1, source_target_pairs={{0,2},{1,3},{2,0},{3,1},{4,6},{5,7},{6,4},{7,5},{8,10},{9,11},{10,... | collective-permute-start | bytes 491528 | tf_op jit(solution)/shard_map/ppermute | solution.py:446
  55.9 6.7 %rows_part.7 = (f32[144,512]{1,0:T(8,128)S(1)}, bf16[160,512]{1,0:T(8,128)(2,1)S(1)}, bf16[160,512]{1,0:T(8,128)(2,1)S(1)}, bf16[160,512]{1,0:T(8,128)(2,1)S(1)}...) custom-call(s32[2]{0:T(128)S(1)} %pad_add_fusion.refs_0_, ...), custom_call_target="tpu_custom_call", output_to_operand_aliasing={{4}: (9, {}), {5}: (10, {})} | custom-call | flops 4294967296 | bytes 33554432 | tf_op jit(solution)/shard_map/rows_part/pallas_call | solution.py:122
  62.6 1.5 %collective-permute-start.15 = (bf16[160,512]{1,0:T(8,128)(2,1)S(1)}, bf16[160,512]{1,0:T(8,128)(2,1)S(1)}, u32[]{:S(2)}, u32[]{:S(2)}) collective-permute-start(bf16[160,512]{1,0:T(8,128)(2,1)S(1)} %get-tuple-element.129), channel_id=1, source_target_pairs={{0,1},{1,0},{2,3},{3,2},{4,5},{5,4},{6,7},{7,6},{8,9},{9,8},{10,11... | collective-permute-start | bytes 491528 | tf_op jit(solution)/shard_map/ppermute | solution.py:446
  64.1 2.0 %collective-permute-start.16 = (bf16[160,512]{1,0:T(8,128)(2,1)S(1)}, bf16[160,512]{1,0:T(8,128)(2,1)S(1)}, u32[]{:S(2)}, u32[]{:S(2)}) collective-permute-start(bf16[160,512]{1,0:T(8,128)(2,1)S(1)} %get-tuple-element.130), channel_id=1, source_target_pairs={{0,2},{1,3},{2,0},{3,1},{4,6},{5,7},{6,4},{7,5},{8,10},{9,11},{10,... | collective-permute-start | bytes 491528 | tf_op jit(solution)/shard_map/ppermute | solution.py:446
  66.2 0.7 join_spread.3
  66.9 2.5 %collective-permute-start.14 = (bf16[208,512]{1,0:T(8,128)(2,1)S(1)}, bf16[208,512]{1,0:T(8,128)(2,1)S(1)}, u32[]{:S(2)}, u32[]{:S(2)}) collective-permute-start(bf16[208,512]{1,0:T(8,128)(2,1)S(1)} %join_spread.3), channel_id=1, source_target_pairs={{0,24},{4,28},{8,16},{12,20},{16,8},{20,12},{24,0},{28,4},{1,25},{... | collective-permute-start | bytes 638984 | tf_op jit(solution)/shard_map/ppermute | solution.py:446
  69.4 6.9 %rows_part.8 = (f32[144,512]{1,0:T(8,128)S(1)}, bf16[160,512]{1,0:T(8,128)(2,1)S(1)}, bf16[160,512]{1,0:T(8,128)(2,1)S(1)}, bf16[160,512]{1,0:T(8,128)(2,1)S(1)}...) custom-call(s32[2]{0:T(128)S(1)} %pad_add_fusion.refs_0_, ...), custom_call_target="tpu_custom_call", output_to_operand_aliasing={{4}: (9, {}), {5}: (10, {})} | custom-call | flops 4294967296 | bytes 33554432 | tf_op jit(solution)/shard_map/rows_part/pallas_call | solution.py:122
  76.3 1.5 %collective-permute-start.19 = (bf16[160,512]{1,0:T(8,128)(2,1)S(1)}, bf16[160,512]{1,0:T(8,128)(2,1)S(1)}, u32[]{:S(2)}, u32[]{:S(2)}) collective-permute-start(bf16[160,512]{1,0:T(8,128)(2,1)S(1)} %get-tuple-element.148), channel_id=1, source_target_pairs={{0,1},{1,0},{2,3},{3,2},{4,5},{5,4},{6,7},{7,6},{8,9},{9,8},{10,11... | collective-permute-start | bytes 491528 | tf_op jit(solution)/shard_map/ppermute | solution.py:446
  77.9 2.0 %collective-permute-start.20 = (bf16[160,512]{1,0:T(8,128)(2,1)S(1)}, bf16[160,512]{1,0:T(8,128)(2,1)S(1)}, u32[]{:S(2)}, u32[]{:S(2)}) collective-permute-start(bf16[160,512]{1,0:T(8,128)(2,1)S(1)} %get-tuple-element.149), channel_id=1, source_target_pairs={{0,2},{1,3},{2,0},{3,1},{4,6},{5,7},{6,4},{7,5},{8,10},{9,11},{10,... | collective-permute-start | bytes 491528 | tf_op jit(solution)/shard_map/ppermute | solution.py:446
  79.9 0.0 collective-permute-start.21
  79.9 0.7 join_spread.4
  80.6 0.1 collective-permute-start.18
  80.7 3.2 %rows_part.9 = (f32[144,512]{1,0:T(8,128)S(1)}, bf16[160,512]{1,0:T(8,128)(2,1)S(1)}, bf16[160,512]{1,0:T(8,128)(2,1)S(1)}, bf16[160,512]{1,0:T(8,128)(2,1)S(1)}) custom-call(s32[2]{0:T(128)S(1)} %pad_add_fusion.refs_0_, bf16[512,256]{1,0:T(8,128)(2,1)S(1)} %copy-done, bf16[512,256]{1,0:T(8,128)(2,1)S(1)} %copy-done.1, ...), custom_call_target="tpu_custom_call" | custom-call | flops 2147483648 | bytes 16777216 | tf_op jit(solution)/shard_map/rows_part/pallas_call | solution.py:122
  83.9 1.6 %collective-permute-start.22 = (bf16[160,512]{1,0:T(8,128)(2,1)S(1)}, bf16[160,512]{1,0:T(8,128)(2,1)S(1)}, u32[]{:S(2)}, u32[]{:S(2)}) collective-permute-start(bf16[160,512]{1,0:T(8,128)(2,1)S(1)} %get-tuple-element.157), channel_id=1, source_target_pairs={{0,1},{1,0},{2,3},{3,2},{4,5},{5,4},{6,7},{7,6},{8,9},{9,8},{10,11... | collective-permute-start | bytes 491528 | tf_op jit(solution)/shard_map/ppermute | solution.py:446
  85.5 0.3 collective-permute-done.20.refs_3_
  85.8 1.3 %collective-permute-done.21.refs_4_ = bf16[160,512]{1,0:T(8,128)(2,1)S(1)} collective-permute-done((bf16[160,512]{1,0:T(8,128)(2,1)S(1)}, bf16[160,512]{1,0:T(8,128)(2,1)S(1)}, u32[]{:S(2)}, u32[]{:S(2)}) %collective-permute-start.21) | collective-permute-done | bytes 163872 | tf_op jit(solution)/shard_map/ppermute | solution.py:446
  87.1 2.5 %collective-permute-done.18.refs_6_ = bf16[208,512]{1,0:T(8,128)(2,1)S(1)} collective-permute-done((bf16[208,512]{1,0:T(8,128)(2,1)S(1)}, bf16[208,512]{1,0:T(8,128)(2,1)S(1)}, u32[]{:S(2)}, u32[]{:S(2)}) %collective-permute-start.18) | collective-permute-done | bytes 213024 | tf_op jit(solution)/shard_map/ppermute | solution.py:446
  89.6 0.7 join_spread.5
  90.3 0.9 collective-permute-start.25
  91.2 1.5 %collective-permute-start.23 = (bf16[160,512]{1,0:T(8,128)(2,1)S(1)}, bf16[160,512]{1,0:T(8,128)(2,1)S(1)}, u32[]{:S(2)}, u32[]{:S(2)}) collective-permute-start(bf16[160,512]{1,0:T(8,128)(2,1)S(1)} %get-tuple-element.160), channel_id=1, source_target_pairs={{0,2},{1,3},{2,0},{3,1},{4,6},{5,7},{6,4},{7,5},{8,10},{9,11},{10,... | collective-permute-start | bytes 491528 | tf_op jit(solution)/shard_map/ppermute | solution.py:446
  92.7 1.4 %collective-permute-start.24 = (bf16[160,512]{1,0:T(8,128)(2,1)S(1)}, bf16[160,512]{1,0:T(8,128)(2,1)S(1)}, u32[]{:S(2)}, u32[]{:S(2)}) collective-permute-start(bf16[160,512]{1,0:T(8,128)(2,1)S(1)} %get-tuple-element.161), channel_id=1, source_target_pairs={{0,3},{1,2},{2,1},{3,0},{4,7},{5,6},{6,5},{7,4},{8,11},{9,10},{10,... | collective-permute-start | bytes 491528 | tf_op jit(solution)/shard_map/ppermute | solution.py:446
  94.2 5.5 %collective-permute-done.23.refs_3_ = bf16[160,512]{1,0:T(8,128)(2,1)S(1)} collective-permute-done((bf16[160,512]{1,0:T(8,128)(2,1)S(1)}, bf16[160,512]{1,0:T(8,128)(2,1)S(1)}, u32[]{:S(2)}, u32[]{:S(2)}) %collective-permute-start.23) | collective-permute-done | bytes 163872 | tf_op jit(solution)/shard_map/ppermute | solution.py:446
  99.7 1.5 %finish.1 = (f32[1,512]{1,0:T(1,128)}, f32[64,512]{1,0:T(8,128)}) custom-call(s32[2]{0:T(128)S(1)} %pad_add_fusion.refs_0_, f32[144,512]{1,0:T(8,128)S(1)} %get-tuple-element.156.refs_1_, bf16[160,512]{1,0:T(8,128)(2,1)S(1)} %collective-permute-done.22.refs_2_, bf16[160,512]{1,0:T(8,128)(2,1)S(1)} %collective-permute-done.23.refs_3_, ...), custom_call_target="tpu_custom_call" | custom-call | flops 1048576 | bytes 8192 | tf_op jit(solution)/shard_map/finish/pallas_call | solution.py:122
  (31 shorter events, 0.2 us)
Async XLA Ops:
  0.6 6.9 %collective-permute-start.3 = (bf16[2048,256]{1,0:T(8,128)(2,1)}, bf16[2048,256]{1,0:T(8,128)(2,1)S(1)}, u32[]{:S(2)}, u32[]{:S(2)}) collective-permute-start(bf16[2048,256]{1,0:T(8,128)(2,1)} %refs_2_.2), channel_id=1, source_target_pairs={{0,4},{4,0},{8,12},{12,8},{16,20},{20,16},{24,28},{28,24},{1,5},{5... | collective-permute-start | bytes 3145736 | tf_op jit(solution)/shard_map/ppermute | solution.py:446
  1.1 6.4 %copy-start = (bf16[512,256]{1,0:T(8,128)(2,1)S(1)}, bf16[512,256]{1,0:T(8,128)(2,1)}, u32[]{:S(2)}) copy-start(bf16[512,256]{1,0:T(8,128)(2,1)} %refs_1_.5) | copy-start | bytes 786436
  2.1 13.9 %collective-permute-start.2 = (bf16[256,256]{1,0:T(8,128)(2,1)S(1)}, bf16[256,256]{1,0:T(8,128)(2,1)S(1)}, u32[]{:S(2)}, u32[]{:S(2)}) collective-permute-start(bf16[256,256]{1,0:T(8,128)(2,1)S(1)} %pad_maximum_fusion.2), channel_id=1, source_target_pairs={{0,24},{4,28},{8,16},{12,20},{16,8},{20,12},{24,0},{28,4},{1,25},{... | collective-permute-start | bytes 393224 | tf_op jit(solution)/shard_map/ppermute | solution.py:446
  6.8 11.7 %collective-permute-start.1 = (bf16[256,256]{1,0:T(8,128)(2,1)S(1)}, bf16[256,256]{1,0:T(8,128)(2,1)S(1)}, u32[]{:S(2)}, u32[]{:S(2)}) collective-permute-start(bf16[256,256]{1,0:T(8,128)(2,1)S(1)} %pad_maximum_fusion.2), channel_id=1, source_target_pairs={{0,16},{4,20},{8,24},{12,28},{16,0},{20,4},{24,8},{28,12},{1,17},{... | collective-permute-start | bytes 393224 | tf_op jit(solution)/shard_map/ppermute | solution.py:446
  6.8 11.7 %collective-permute-start = (bf16[256,256]{1,0:T(8,128)(2,1)S(1)}, bf16[256,256]{1,0:T(8,128)(2,1)S(1)}, u32[]{:S(2)}, u32[]{:S(2)}) collective-permute-start(bf16[256,256]{1,0:T(8,128)(2,1)S(1)} %pad_maximum_fusion.2), channel_id=1, source_target_pairs={{0,8},{4,12},{8,0},{12,4},{16,24},{20,28},{24,16},{28,20},{1,9},{5... | collective-permute-start | bytes 393224 | tf_op jit(solution)/shard_map/ppermute | solution.py:446
  7.5 4.3 %copy-start.1 = (bf16[512,256]{1,0:T(8,128)(2,1)S(1)}, bf16[512,256]{1,0:T(8,128)(2,1)}, u32[]{:S(2)}) copy-start(bf16[512,256]{1,0:T(8,128)(2,1)} %refs_2_.3) | copy-start | bytes 786436
  7.5 1.3 %copy-start.2 = (bf16[2048,256]{1,0:T(8,128)(2,1)S(1)}, bf16[2048,256]{1,0:T(8,128)(2,1)}, u32[]{:S(2)}) copy-start(bf16[2048,256]{1,0:T(8,128)(2,1)} %refs_2_.2) | copy-start | bytes 3145732
  18.6 10.6 %collective-permute-start.6 = (bf16[3,128,256]{2,1,0:T(8,128)(2,1)S(1)}, bf16[3,128,256]{2,1,0:T(8,128)(2,1)S(1)}, u32[]{:S(2)}, u32[]{:S(2)}) collective-permute-start(bf16[3,128,256]{2,1,0:T(8,128)(2,1)S(1)} %pad_maximum_fusion.1.refs_1_), channel_id=1, source_target_pairs={{0,3},{1,2},{2,1},{3,0},{4,7},{5,6},{6,5},{7,4},{8,11},{9,10},{10,... | collective-permute-start | bytes 589832 | tf_op jit(solution)/shard_map/ppermute | solution.py:446
  21.1 10.6 %collective-permute-start.5 = (bf16[3,128,256]{2,1,0:T(8,128)(2,1)S(1)}, bf16[3,128,256]{2,1,0:T(8,128)(2,1)S(1)}, u32[]{:S(2)}, u32[]{:S(2)}) collective-permute-start(bf16[3,128,256]{2,1,0:T(8,128)(2,1)S(1)} %pad_maximum_fusion.1.refs_1_), channel_id=1, source_target_pairs={{0,2},{1,3},{2,0},{3,1},{4,6},{5,7},{6,4},{7,5},{8,10},{9,11},{10,... | collective-permute-start | bytes 589832 | tf_op jit(solution)/shard_map/ppermute | solution.py:446
  21.6 10.1 %collective-permute-start.4 = (bf16[3,128,256]{2,1,0:T(8,128)(2,1)S(1)}, bf16[3,128,256]{2,1,0:T(8,128)(2,1)S(1)}, u32[]{:S(2)}, u32[]{:S(2)}) collective-permute-start(bf16[3,128,256]{2,1,0:T(8,128)(2,1)S(1)} %pad_maximum_fusion.1.refs_1_), channel_id=1, source_target_pairs={{0,1},{1,0},{2,3},{3,2},{4,5},{5,4},{6,7},{7,6},{8,9},{9,8},{10,11... | collective-permute-start | bytes 589832 | tf_op jit(solution)/shard_map/ppermute | solution.py:446
  26.2 18.1 %collective-permute-start.10 = (bf16[3,128,256]{2,1,0:T(8,128)(2,1)S(1)}, bf16[3,128,256]{2,1,0:T(8,128)(2,1)S(1)}, u32[]{:S(2)}, u32[]{:S(2)}) collective-permute-start(bf16[3,128,256]{2,1,0:T(8,128)(2,1)S(1)} %pad_maximum_fusion.refs_5_), channel_id=1, source_target_pairs={{0,3},{1,2},{2,1},{3,0},{4,7},{5,6},{6,5},{7,4},{8,11},{9,10},{10,... | collective-permute-start | bytes 589832 | tf_op jit(solution)/shard_map/ppermute | solution.py:446
  28.7 15.6 %collective-permute-start.9 = (bf16[3,128,256]{2,1,0:T(8,128)(2,1)S(1)}, bf16[3,128,256]{2,1,0:T(8,128)(2,1)S(1)}, u32[]{:S(2)}, u32[]{:S(2)}) collective-permute-start(bf16[3,128,256]{2,1,0:T(8,128)(2,1)S(1)} %pad_maximum_fusion.refs_5_), channel_id=1, source_target_pairs={{0,2},{1,3},{2,0},{3,1},{4,6},{5,7},{6,4},{7,5},{8,10},{9,11},{10,... | collective-permute-start | bytes 589832 | tf_op jit(solution)/shard_map/ppermute | solution.py:446
  29.2 15.1 %collective-permute-start.8 = (bf16[3,128,256]{2,1,0:T(8,128)(2,1)S(1)}, bf16[3,128,256]{2,1,0:T(8,128)(2,1)S(1)}, u32[]{:S(2)}, u32[]{:S(2)}) collective-permute-start(bf16[3,128,256]{2,1,0:T(8,128)(2,1)S(1)} %pad_maximum_fusion.refs_5_), channel_id=1, source_target_pairs={{0,1},{1,0},{2,3},{3,2},{4,5},{5,4},{6,7},{7,6},{8,9},{9,8},{10,11... | collective-permute-start | bytes 589832 | tf_op jit(solution)/shard_map/ppermute | solution.py:446
  42.3 1.4 %collective-permute-start.7 = (f32[4,8,1024]{2,1,0:T(8,128)S(1)}, f32[4,8,1024]{2,1,0:T(8,128)S(1)}, u32[]{:S(2)}, u32[]{:S(2)}) collective-permute-start(f32[4,8,1024]{2,1,0:T(8,128)S(1)} %get-tuple-element.106.refs_1_), channel_id=1, source_target_pairs={{0,4},{4,0},{8,12},{12,8},{16,20},{20,16},{24,28},{28,24},{1,5},{5... | collective-permute-start | bytes 393224 | tf_op jit(solution)/shard_map/ppermute | solution.py:446
  51.1 15.1 %collective-permute-start.11 = (bf16[160,512]{1,0:T(8,128)(2,1)S(1)}, bf16[160,512]{1,0:T(8,128)(2,1)S(1)}, u32[]{:S(2)}, u32[]{:S(2)}) collective-permute-start(bf16[160,512]{1,0:T(8,128)(2,1)S(1)} %get-tuple-element.119), channel_id=1, source_target_pairs={{0,1},{1,0},{2,3},{3,2},{4,5},{5,4},{6,7},{7,6},{8,9},{9,8},{10,11... | collective-permute-start | bytes 491528 | tf_op jit(solution)/shard_map/ppermute | solution.py:446
  52.6 13.5 %collective-permute-start.12 = (bf16[160,512]{1,0:T(8,128)(2,1)S(1)}, bf16[160,512]{1,0:T(8,128)(2,1)S(1)}, u32[]{:S(2)}, u32[]{:S(2)}) collective-permute-start(bf16[160,512]{1,0:T(8,128)(2,1)S(1)} %get-tuple-element.120), channel_id=1, source_target_pairs={{0,2},{1,3},{2,0},{3,1},{4,6},{5,7},{6,4},{7,5},{8,10},{9,11},{10,... | collective-permute-start | bytes 491528 | tf_op jit(solution)/shard_map/ppermute | solution.py:446
  55.9 10.3 %collective-permute-start.13 = (bf16[160,512]{1,0:T(8,128)(2,1)S(1)}, bf16[160,512]{1,0:T(8,128)(2,1)S(1)}, u32[]{:S(2)}, u32[]{:S(2)}) collective-permute-start(bf16[160,512]{1,0:T(8,128)(2,1)S(1)} %get-tuple-element.121), channel_id=1, source_target_pairs={{0,3},{1,2},{2,1},{3,0},{4,7},{5,6},{6,5},{7,4},{8,11},{9,10},{10,... | collective-permute-start | bytes 491528 | tf_op jit(solution)/shard_map/ppermute | solution.py:446
  62.6 15.2 %collective-permute-start.15 = (bf16[160,512]{1,0:T(8,128)(2,1)S(1)}, bf16[160,512]{1,0:T(8,128)(2,1)S(1)}, u32[]{:S(2)}, u32[]{:S(2)}) collective-permute-start(bf16[160,512]{1,0:T(8,128)(2,1)S(1)} %get-tuple-element.129), channel_id=1, source_target_pairs={{0,1},{1,0},{2,3},{3,2},{4,5},{5,4},{6,7},{7,6},{8,9},{9,8},{10,11... | collective-permute-start | bytes 491528 | tf_op jit(solution)/shard_map/ppermute | solution.py:446
  64.1 15.7 %collective-permute-start.16 = (bf16[160,512]{1,0:T(8,128)(2,1)S(1)}, bf16[160,512]{1,0:T(8,128)(2,1)S(1)}, u32[]{:S(2)}, u32[]{:S(2)}) collective-permute-start(bf16[160,512]{1,0:T(8,128)(2,1)S(1)} %get-tuple-element.130), channel_id=1, source_target_pairs={{0,2},{1,3},{2,0},{3,1},{4,6},{5,7},{6,4},{7,5},{8,10},{9,11},{10,... | collective-permute-start | bytes 491528 | tf_op jit(solution)/shard_map/ppermute | solution.py:446
  66.2 13.7 %collective-permute-start.17 = (bf16[160,512]{1,0:T(8,128)(2,1)S(1)}, bf16[160,512]{1,0:T(8,128)(2,1)S(1)}, u32[]{:S(2)}, u32[]{:S(2)}) collective-permute-start(bf16[160,512]{1,0:T(8,128)(2,1)S(1)} %get-tuple-element.131), channel_id=1, source_target_pairs={{0,3},{1,2},{2,1},{3,0},{4,7},{5,6},{6,5},{7,4},{8,11},{9,10},{10,... | collective-permute-start | bytes 491528 | tf_op jit(solution)/shard_map/ppermute | solution.py:446
  66.9 13.0 %collective-permute-start.14 = (bf16[208,512]{1,0:T(8,128)(2,1)S(1)}, bf16[208,512]{1,0:T(8,128)(2,1)S(1)}, u32[]{:S(2)}, u32[]{:S(2)}) collective-permute-start(bf16[208,512]{1,0:T(8,128)(2,1)S(1)} %join_spread.3), channel_id=1, source_target_pairs={{0,24},{4,28},{8,16},{12,20},{16,8},{20,12},{24,0},{28,4},{1,25},{... | collective-permute-start | bytes 638984 | tf_op jit(solution)/shard_map/ppermute | solution.py:446
  76.3 9.2 %collective-permute-start.19 = (bf16[160,512]{1,0:T(8,128)(2,1)S(1)}, bf16[160,512]{1,0:T(8,128)(2,1)S(1)}, u32[]{:S(2)}, u32[]{:S(2)}) collective-permute-start(bf16[160,512]{1,0:T(8,128)(2,1)S(1)} %get-tuple-element.148), channel_id=1, source_target_pairs={{0,1},{1,0},{2,3},{3,2},{4,5},{5,4},{6,7},{7,6},{8,9},{9,8},{10,11... | collective-permute-start | bytes 491528 | tf_op jit(solution)/shard_map/ppermute | solution.py:446
  77.9 8.0 %collective-permute-start.20 = (bf16[160,512]{1,0:T(8,128)(2,1)S(1)}, bf16[160,512]{1,0:T(8,128)(2,1)S(1)}, u32[]{:S(2)}, u32[]{:S(2)}) collective-permute-start(bf16[160,512]{1,0:T(8,128)(2,1)S(1)} %get-tuple-element.149), channel_id=1, source_target_pairs={{0,2},{1,3},{2,0},{3,1},{4,6},{5,7},{6,4},{7,5},{8,10},{9,11},{10,... | collective-permute-start | bytes 491528 | tf_op jit(solution)/shard_map/ppermute | solution.py:446
  79.9 7.3 %collective-permute-start.21 = (bf16[160,512]{1,0:T(8,128)(2,1)S(1)}, bf16[160,512]{1,0:T(8,128)(2,1)S(1)}, u32[]{:S(2)}, u32[]{:S(2)}) collective-permute-start(bf16[160,512]{1,0:T(8,128)(2,1)S(1)} %get-tuple-element.150), channel_id=1, source_target_pairs={{0,3},{1,2},{2,1},{3,0},{4,7},{5,6},{6,5},{7,4},{8,11},{9,10},{10,... | collective-permute-start | bytes 491528 | tf_op jit(solution)/shard_map/ppermute | solution.py:446
  80.6 9.0 %collective-permute-start.18 = (bf16[208,512]{1,0:T(8,128)(2,1)S(1)}, bf16[208,512]{1,0:T(8,128)(2,1)S(1)}, u32[]{:S(2)}, u32[]{:S(2)}) collective-permute-start(bf16[208,512]{1,0:T(8,128)(2,1)S(1)} %join_spread.4), channel_id=1, source_target_pairs={{0,16},{4,20},{8,24},{12,28},{16,0},{20,4},{24,8},{28,12},{1,17},{... | collective-permute-start | bytes 638984 | tf_op jit(solution)/shard_map/ppermute | solution.py:446
  83.9 6.4 %collective-permute-start.22 = (bf16[160,512]{1,0:T(8,128)(2,1)S(1)}, bf16[160,512]{1,0:T(8,128)(2,1)S(1)}, u32[]{:S(2)}, u32[]{:S(2)}) collective-permute-start(bf16[160,512]{1,0:T(8,128)(2,1)S(1)} %get-tuple-element.157), channel_id=1, source_target_pairs={{0,1},{1,0},{2,3},{3,2},{4,5},{5,4},{6,7},{7,6},{8,9},{9,8},{10,11... | collective-permute-start | bytes 491528 | tf_op jit(solution)/shard_map/ppermute | solution.py:446
  90.3 9.3 %collective-permute-start.25 = (bf16[208,512]{1,0:T(8,128)(2,1)S(1)}, bf16[208,512]{1,0:T(8,128)(2,1)S(1)}, u32[]{:S(2)}, u32[]{:S(2)}) collective-permute-start(bf16[208,512]{1,0:T(8,128)(2,1)S(1)} %join_spread.5), channel_id=1, source_target_pairs={{0,8},{4,12},{8,0},{12,4},{16,24},{20,28},{24,16},{28,20},{1,9},{5... | collective-permute-start | bytes 638984 | tf_op jit(solution)/shard_map/ppermute | solution.py:446
  91.2 8.4 %collective-permute-start.23 = (bf16[160,512]{1,0:T(8,128)(2,1)S(1)}, bf16[160,512]{1,0:T(8,128)(2,1)S(1)}, u32[]{:S(2)}, u32[]{:S(2)}) collective-permute-start(bf16[160,512]{1,0:T(8,128)(2,1)S(1)} %get-tuple-element.160), channel_id=1, source_target_pairs={{0,2},{1,3},{2,0},{3,1},{4,6},{5,7},{6,4},{7,5},{8,10},{9,11},{10,... | collective-permute-start | bytes 491528 | tf_op jit(solution)/shard_map/ppermute | solution.py:446
  92.7 6.9 %collective-permute-start.24 = (bf16[160,512]{1,0:T(8,128)(2,1)S(1)}, bf16[160,512]{1,0:T(8,128)(2,1)S(1)}, u32[]{:S(2)}, u32[]{:S(2)}) collective-permute-start(bf16[160,512]{1,0:T(8,128)(2,1)S(1)} %get-tuple-element.161), channel_id=1, source_target_pairs={{0,3},{1,2},{2,1},{3,0},{4,7},{5,6},{6,5},{7,4},{8,11},{9,10},{10,... | collective-permute-start | bytes 491528 | tf_op jit(solution)/shard_map/ppermute | solution.py:446

commit v8 on v7

--- a/solution.py
+++ b/solution.py
@@ -502,7 +502,6 @@
     ((past, arrived),) = waiting
     far, arrived = lax.optimization_barrier((far, arrived))
     info, part = join_spread(info, arrived)
-    own[1], part = lax.optimization_barrier((own[1], part))
     loss, pull = finish(info, own, [*far, swap(part, "dp", 2 * past)])
     return (loss.reshape(rows), pull.T)
 

time: 101 us -> 99.5 us (0.985)
  waiting for transfers between devices: 15.4 us -> 13.4 us
    ppermute x26, waiting for transfers between devices: 15.4 us -> 13.4 us  [swap(): return lax.ppermute(value, axis, [(i, i ^ bits) for i in range(count)])]
  transfers between devices with their start and end apart: 26 -> 26, of which waited for: 7 -> 7; matrix products, arithmetic and copies ran while one was open for 1% -> 1% of each run, Pallas kernels for 41% -> 40%
where the time goes in v8:
time: 99.5 us; the launch traced here: 99.4 us
  Pallas kernels  49.5 us (50%)
  starting transfers between devices  33.2 us (33%)
  waiting for transfers between devices  13.4 us (13%)
  local copies, waits for them, and re-layouts  2.23 us (2%)
    pallas_call x13, Pallas kernels, call(): pl.pallas_call(without, grid_spec=pltpu.PrefetchScalarGridSpec(num_scalar...  49.5 us
    ppermute x26, starting transfers between devices, swap(): return lax.ppermute(value, axis, [(i, i ^ bits) for i in range(count)])  33.2 us
    ppermute x26, waiting for transfers between devices, swap(): return lax.ppermute(value, axis, [(i, i ^ bits) for i in range(count)])  13.4 us
  transfers between devices with their start and end apart: 26, of which 7 were waited for; matrix products, arithmetic and copies ran while one was open for 1% of the time, Pallas kernels for 40%

profile of v8, /device:TPU:0, one launch (start us, length us, event | category | flops | bytes accessed | tf_op | source)
XLA Modules:
  0.0 99.4 jit_solution(7006174576069211331)
XLA Ops:
  0.6 0.5 collective-permute-start.3
  1.1 0.9 constant_dynamic-slice_fusion
  2.1 4.7 %collective-permute-start.2 = (bf16[256,256]{1,0:T(8,128)(2,1)S(1)}, bf16[256,256]{1,0:T(8,128)(2,1)S(1)}, u32[]{:S(2)}, u32[]{:S(2)}) collective-permute-start(bf16[256,256]{1,0:T(8,128)(2,1)S(1)} %pad_maximum_fusion.2), channel_id=1, source_target_pairs={{0,24},{4,28},{8,16},{12,20},{16,8},{20,12},{24,0},{28,4},{1,25},{... | collective-permute-start | bytes 393224 | tf_op jit(solution)/shard_map/ppermute | solution.py:446
  6.8 0.0 collective-permute-start.1
  6.8 0.6 collective-permute-start
  7.4 0.1 pad_add_fusion.refs_0_
  7.5 1.3 %copy-done.2 = bf16[2048,256]{1,0:T(8,128)(2,1)S(1)} copy-done((bf16[2048,256]{1,0:T(8,128)(2,1)S(1)}, bf16[2048,256]{1,0:T(8,128)(2,1)}, u32[]{:S(2)}) %copy-start.2) | copy-done | bytes 1048600
  8.8 3.0 %stats_part.3 = (f32[4,8,1024]{2,1,0:T(8,128)S(1)}, bf16[2048,256]{1,0:T(8,128)(2,1)S(1)}, bf16[2048,256]{1,0:T(8,128)(2,1)S(1)}) custom-call(s32[2]{0:T(128)S(1)} %pad_add_fusion.refs_0_, bf16[512,256]{1,0:T(8,128)(2,1)S(1)} %copy-done, bf16[2048,256]{1,0:T(8,128)(2,1)S(1)} %copy-done.2, ...), custom_call_target="tpu_custom_call", output_to_operand_aliasing={{2}: (3, {})} | custom-call | flops 1073741824 | bytes 8388608 | tf_op jit(solution)/shard_map/stats_part/pallas_call | solution.py:122
  11.8 4.2 %rows_part.5 = (f32[72,512]{1,0:T(8,128)S(1)}, bf16[80,512]{1,0:T(8,128)(2,1)S(1)}, bf16[80,512]{1,0:T(8,128)(2,1)S(1)}, bf16[80,512]{1,0:T(8,128)(2,1)S(1)}, bf...) custom-call(s32[2]{0:T(128)S(1)} %pad_add_fusion.refs_0_, ...), custom_call_target="tpu_custom_call", output_to_operand_aliasing={{4}: (2, {}), {5}: (3, {})} | custom-call | flops 2147483648 | bytes 16777216 | tf_op jit(solution)/shard_map/rows_part/pallas_call | solution.py:122
  16.0 0.0 collective-permute-done.2
  16.0 2.5 %collective-permute-done.1 = bf16[256,256]{1,0:T(8,128)(2,1)S(1)} collective-permute-done((bf16[256,256]{1,0:T(8,128)(2,1)S(1)}, bf16[256,256]{1,0:T(8,128)(2,1)S(1)}, u32[]{:S(2)}, u32[]{:S(2)}) %collective-permute-start.1) | collective-permute-done | bytes 131104 | tf_op jit(solution)/shard_map/ppermute | solution.py:446
  18.6 2.5 %collective-permute-start.6 = (bf16[3,128,256]{2,1,0:T(8,128)(2,1)S(1)}, bf16[3,128,256]{2,1,0:T(8,128)(2,1)S(1)}, u32[]{:S(2)}, u32[]{:S(2)}) collective-permute-start(bf16[3,128,256]{2,1,0:T(8,128)(2,1)S(1)} %pad_maximum_fusion.1.refs_1_), channel_id=1, source_target_pairs={{0,3},{1,2},{2,1},{3,0},{4,7},{5,6},{6,5},{7,4},{8,11},{9,10},{10,... | collective-permute-start | bytes 589832 | tf_op jit(solution)/shard_map/ppermute | solution.py:446
  21.1 0.5 collective-permute-start.5
  21.6 0.5 collective-permute-start.4
  22.2 4.0 %stats_part.4 = (f32[4,8,1024]{2,1,0:T(8,128)S(1)}, bf16[2048,256]{1,0:T(8,128)(2,1)S(1)}, bf16[2048,256]{1,0:T(8,128)(2,1)S(1)}) custom-call(s32[2]{0:T(128)S(1)} %pad_add_fusion.refs_0_, bf16[3,128,256]{2,1,0:T(8,128)(2,1)S(1)} %pad_maximum_fusion.1.refs_1_, ...), custom_call_target="tpu_custom_call", output_to_operand_aliasing={{1}: (2, {}), {2}: (3, {})} | custom-call | flops 805306368 | bytes 6291456 | tf_op jit(solution)/shard_map/stats_part/pallas_call | solution.py:122
  26.2 2.5 %collective-permute-start.10 = (bf16[3,128,256]{2,1,0:T(8,128)(2,1)S(1)}, bf16[3,128,256]{2,1,0:T(8,128)(2,1)S(1)}, u32[]{:S(2)}, u32[]{:S(2)}) collective-permute-start(bf16[3,128,256]{2,1,0:T(8,128)(2,1)S(1)} %pad_maximum_fusion.refs_5_), channel_id=1, source_target_pairs={{0,3},{1,2},{2,1},{3,0},{4,7},{5,6},{6,5},{7,4},{8,11},{9,10},{10,... | collective-permute-start | bytes 589832 | tf_op jit(solution)/shard_map/ppermute | solution.py:446
  28.7 0.5 collective-permute-start.9
  29.2 0.5 collective-permute-start.8
  29.8 1.9 %collective-permute-done.5.refs_2_.refs_3_ = bf16[3,128,256]{2,1,0:T(8,128)(2,1)S(1)} collective-permute-done((bf16[3,128,256]{2,1,0:T(8,128)(2,1)S(1)}, bf16[3,128,256]{2,1,0:T(8,128)(2,1)S(1)}, u32[]{:S(2)}, u32[]{:S(2)}) %collective-permute-start.5) | collective-permute-done | bytes 196640 | tf_op jit(solution)/shard_map/ppermute | solution.py:446
  31.7 10.6 %stats_part.5 = (f32[4,8,1024]{2,1,0:T(8,128)S(1)}, bf16[2048,256]{1,0:T(8,128)(2,1)S(1)}, bf16[2048,256]{1,0:T(8,128)(2,1)S(1)}) custom-call(s32[2]{0:T(128)S(1)} %pad_add_fusion.refs_0_, bf16[3,128,256]{2,1,0:T(8,128)(2,1)S(1)} %collective-permute-done.4.refs_1_.refs_2_, ...), custom_call_target="tpu_custom_call", output_to_operand_aliasing={{1}: (4, {}), {2}: (5, {})} | custom-call | flops 2415919104 | bytes 18874368 | tf_op jit(solution)/shard_map/stats_part/pallas_call | solution.py:122
  42.3 0.1 collective-permute-start.7
  42.4 1.3 %collective-permute-done.7.refs_2_ = f32[4,8,1024]{2,1,0:T(8,128)S(1)} collective-permute-done((f32[4,8,1024]{2,1,0:T(8,128)S(1)}, f32[4,8,1024]{2,1,0:T(8,128)S(1)}, u32[]{:S(2)}, u32[]{:S(2)}) %collective-permute-start.7) | collective-permute-done | bytes 131104 | tf_op jit(solution)/shard_map/ppermute | solution.py:446
  43.7 0.6 offset_part.1.refs_11_.refs_5_
  44.4 6.7 %rows_part.6 = (f32[144,512]{1,0:T(8,128)S(1)}, bf16[160,512]{1,0:T(8,128)(2,1)S(1)}, bf16[160,512]{1,0:T(8,128)(2,1)S(1)}, bf16[160,512]{1,0:T(8,128)(2,1)S(1)}...) custom-call(s32[2]{0:T(128)S(1)} %pad_add_fusion.refs_0_, ...), custom_call_target="tpu_custom_call", output_to_operand_aliasing={{4}: (9, {}), {5}: (10, {})} | custom-call | flops 4294967296 | bytes 33554432 | tf_op jit(solution)/shard_map/rows_part/pallas_call | solution.py:122
  51.1 1.6 %collective-permute-start.11 = (bf16[160,512]{1,0:T(8,128)(2,1)S(1)}, bf16[160,512]{1,0:T(8,128)(2,1)S(1)}, u32[]{:S(2)}, u32[]{:S(2)}) collective-permute-start(bf16[160,512]{1,0:T(8,128)(2,1)S(1)} %get-tuple-element.117), channel_id=1, source_target_pairs={{0,1},{1,0},{2,3},{3,2},{4,5},{5,4},{6,7},{7,6},{8,9},{9,8},{10,11... | collective-permute-start | bytes 491528 | tf_op jit(solution)/shard_map/ppermute | solution.py:446
  52.6 3.3 %collective-permute-start.12 = (bf16[160,512]{1,0:T(8,128)(2,1)S(1)}, bf16[160,512]{1,0:T(8,128)(2,1)S(1)}, u32[]{:S(2)}, u32[]{:S(2)}) collective-permute-start(bf16[160,512]{1,0:T(8,128)(2,1)S(1)} %get-tuple-element.118), channel_id=1, source_target_pairs={{0,2},{1,3},{2,0},{3,1},{4,6},{5,7},{6,4},{7,5},{8,10},{9,11},{10,... | collective-permute-start | bytes 491528 | tf_op jit(solution)/shard_map/ppermute | solution.py:446
  55.9 6.7 %rows_part.7 = (f32[144,512]{1,0:T(8,128)S(1)}, bf16[160,512]{1,0:T(8,128)(2,1)S(1)}, bf16[160,512]{1,0:T(8,128)(2,1)S(1)}, bf16[160,512]{1,0:T(8,128)(2,1)S(1)}...) custom-call(s32[2]{0:T(128)S(1)} %pad_add_fusion.refs_0_, ...), custom_call_target="tpu_custom_call", output_to_operand_aliasing={{4}: (9, {}), {5}: (10, {})} | custom-call | flops 4294967296 | bytes 33554432 | tf_op jit(solution)/shard_map/rows_part/pallas_call | solution.py:122
  62.6 1.5 %collective-permute-start.15 = (bf16[160,512]{1,0:T(8,128)(2,1)S(1)}, bf16[160,512]{1,0:T(8,128)(2,1)S(1)}, u32[]{:S(2)}, u32[]{:S(2)}) collective-permute-start(bf16[160,512]{1,0:T(8,128)(2,1)S(1)} %get-tuple-element.127), channel_id=1, source_target_pairs={{0,1},{1,0},{2,3},{3,2},{4,5},{5,4},{6,7},{7,6},{8,9},{9,8},{10,11... | collective-permute-start | bytes 491528 | tf_op jit(solution)/shard_map/ppermute | solution.py:446
  64.1 2.0 %collective-permute-start.16 = (bf16[160,512]{1,0:T(8,128)(2,1)S(1)}, bf16[160,512]{1,0:T(8,128)(2,1)S(1)}, u32[]{:S(2)}, u32[]{:S(2)}) collective-permute-start(bf16[160,512]{1,0:T(8,128)(2,1)S(1)} %get-tuple-element.128), channel_id=1, source_target_pairs={{0,2},{1,3},{2,0},{3,1},{4,6},{5,7},{6,4},{7,5},{8,10},{9,11},{10,... | collective-permute-start | bytes 491528 | tf_op jit(solution)/shard_map/ppermute | solution.py:446
  66.2 0.7 join_spread.3
  66.9 2.5 %collective-permute-start.14 = (bf16[208,512]{1,0:T(8,128)(2,1)S(1)}, bf16[208,512]{1,0:T(8,128)(2,1)S(1)}, u32[]{:S(2)}, u32[]{:S(2)}) collective-permute-start(bf16[208,512]{1,0:T(8,128)(2,1)S(1)} %join_spread.3), channel_id=1, source_target_pairs={{0,24},{4,28},{8,16},{12,20},{16,8},{20,12},{24,0},{28,4},{1,25},{... | collective-permute-start | bytes 638984 | tf_op jit(solution)/shard_map/ppermute | solution.py:446
  69.4 6.9 %rows_part.8 = (f32[144,512]{1,0:T(8,128)S(1)}, bf16[160,512]{1,0:T(8,128)(2,1)S(1)}, bf16[160,512]{1,0:T(8,128)(2,1)S(1)}, bf16[160,512]{1,0:T(8,128)(2,1)S(1)}...) custom-call(s32[2]{0:T(128)S(1)} %pad_add_fusion.refs_0_, ...), custom_call_target="tpu_custom_call", output_to_operand_aliasing={{4}: (9, {}), {5}: (10, {})} | custom-call | flops 4294967296 | bytes 33554432 | tf_op jit(solution)/shard_map/rows_part/pallas_call | solution.py:122
  76.4 0.7 join_spread.4
  77.1 0.7 collective-permute-start.18
  77.8 1.5 %collective-permute-start.19 = (bf16[160,512]{1,0:T(8,128)(2,1)S(1)}, bf16[160,512]{1,0:T(8,128)(2,1)S(1)}, u32[]{:S(2)}, u32[]{:S(2)}) collective-permute-start(bf16[160,512]{1,0:T(8,128)(2,1)S(1)} %get-tuple-element.146), channel_id=1, source_target_pairs={{0,1},{1,0},{2,3},{3,2},{4,5},{5,4},{6,7},{7,6},{8,9},{9,8},{10,11... | collective-permute-start | bytes 491528 | tf_op jit(solution)/shard_map/ppermute | solution.py:446
  79.2 1.7 %collective-permute-start.20 = (bf16[160,512]{1,0:T(8,128)(2,1)S(1)}, bf16[160,512]{1,0:T(8,128)(2,1)S(1)}, u32[]{:S(2)}, u32[]{:S(2)}) collective-permute-start(bf16[160,512]{1,0:T(8,128)(2,1)S(1)} %get-tuple-element.147), channel_id=1, source_target_pairs={{0,2},{1,3},{2,0},{3,1},{4,6},{5,7},{6,4},{7,5},{8,10},{9,11},{10,... | collective-permute-start | bytes 491528 | tf_op jit(solution)/shard_map/ppermute | solution.py:446
  81.0 0.3 collective-permute-start.21
  81.3 3.2 %rows_part.9 = (f32[144,512]{1,0:T(8,128)S(1)}, bf16[160,512]{1,0:T(8,128)(2,1)S(1)}, bf16[160,512]{1,0:T(8,128)(2,1)S(1)}, bf16[160,512]{1,0:T(8,128)(2,1)S(1)}) custom-call(s32[2]{0:T(128)S(1)} %pad_add_fusion.refs_0_, bf16[512,256]{1,0:T(8,128)(2,1)S(1)} %copy-done, bf16[512,256]{1,0:T(8,128)(2,1)S(1)} %copy-done.1, ...), custom_call_target="tpu_custom_call" | custom-call | flops 2147483648 | bytes 16777216 | tf_op jit(solution)/shard_map/rows_part/pallas_call | solution.py:122
  84.5 2.9 %collective-permute-done.20.refs_3_ = bf16[160,512]{1,0:T(8,128)(2,1)S(1)} collective-permute-done((bf16[160,512]{1,0:T(8,128)(2,1)S(1)}, bf16[160,512]{1,0:T(8,128)(2,1)S(1)}, u32[]{:S(2)}, u32[]{:S(2)}) %collective-permute-start.20) | collective-permute-done | bytes 163872 | tf_op jit(solution)/shard_map/ppermute | solution.py:446
  87.4 0.7 join_spread.5
  88.1 1.6 %collective-permute-start.25 = (bf16[208,512]{1,0:T(8,128)(2,1)S(1)}, bf16[208,512]{1,0:T(8,128)(2,1)S(1)}, u32[]{:S(2)}, u32[]{:S(2)}) collective-permute-start(bf16[208,512]{1,0:T(8,128)(2,1)S(1)} %join_spread.5), channel_id=1, source_target_pairs={{0,8},{4,12},{8,0},{12,4},{16,24},{20,28},{24,16},{28,20},{1,9},{5... | collective-permute-start | bytes 638984 | tf_op jit(solution)/shard_map/ppermute | solution.py:446
  89.7 0.6 collective-permute-start.22
  90.3 0.7 collective-permute-start.23
  91.0 2.2 %collective-permute-start.24 = (bf16[160,512]{1,0:T(8,128)(2,1)S(1)}, bf16[160,512]{1,0:T(8,128)(2,1)S(1)}, u32[]{:S(2)}, u32[]{:S(2)}) collective-permute-start(bf16[160,512]{1,0:T(8,128)(2,1)S(1)} %get-tuple-element.157), channel_id=1, source_target_pairs={{0,3},{1,2},{2,1},{3,0},{4,7},{5,6},{6,5},{7,4},{8,11},{9,10},{10,... | collective-permute-start | bytes 491528 | tf_op jit(solution)/shard_map/ppermute | solution.py:446
  93.1 2.1 %collective-permute-done.22.refs_2_ = bf16[160,512]{1,0:T(8,128)(2,1)S(1)} collective-permute-done((bf16[160,512]{1,0:T(8,128)(2,1)S(1)}, bf16[160,512]{1,0:T(8,128)(2,1)S(1)}, u32[]{:S(2)}, u32[]{:S(2)}) %collective-permute-start.22) | collective-permute-done | bytes 163872 | tf_op jit(solution)/shard_map/ppermute | solution.py:446
  95.3 1.3 %collective-permute-done.23.refs_3_ = bf16[160,512]{1,0:T(8,128)(2,1)S(1)} collective-permute-done((bf16[160,512]{1,0:T(8,128)(2,1)S(1)}, bf16[160,512]{1,0:T(8,128)(2,1)S(1)}, u32[]{:S(2)}, u32[]{:S(2)}) %collective-permute-start.23) | collective-permute-done | bytes 163872 | tf_op jit(solution)/shard_map/ppermute | solution.py:446
  96.6 1.3 %collective-permute-done.24.refs_4_ = bf16[160,512]{1,0:T(8,128)(2,1)S(1)} collective-permute-done((bf16[160,512]{1,0:T(8,128)(2,1)S(1)}, bf16[160,512]{1,0:T(8,128)(2,1)S(1)}, u32[]{:S(2)}, u32[]{:S(2)}) %collective-permute-start.24) | collective-permute-done | bytes 163872 | tf_op jit(solution)/shard_map/ppermute | solution.py:446
  97.9 1.5 %finish.1 = (f32[1,512]{1,0:T(1,128)}, f32[64,512]{1,0:T(8,128)}) custom-call(s32[2]{0:T(128)S(1)} %pad_add_fusion.refs_0_, f32[144,512]{1,0:T(8,128)S(1)} %get-tuple-element.154.refs_1_, bf16[160,512]{1,0:T(8,128)(2,1)S(1)} %collective-permute-done.22.refs_2_, bf16[160,512]{1,0:T(8,128)(2,1)S(1)} %collective-permute-done.23.refs_3_, ...), custom_call_target="tpu_custom_call" | custom-call | flops 1048576 | bytes 8192 | tf_op jit(solution)/shard_map/finish/pallas_call | solution.py:122
  (31 shorter events, 0.2 us)
Async XLA Ops:
  0.6 6.9 %collective-permute-start.3 = (bf16[2048,256]{1,0:T(8,128)(2,1)}, bf16[2048,256]{1,0:T(8,128)(2,1)S(1)}, u32[]{:S(2)}, u32[]{:S(2)}) collective-permute-start(bf16[2048,256]{1,0:T(8,128)(2,1)} %refs_2_.2), channel_id=1, source_target_pairs={{0,4},{4,0},{8,12},{12,8},{16,20},{20,16},{24,28},{28,24},{1,5},{5... | collective-permute-start | bytes 3145736 | tf_op jit(solution)/shard_map/ppermute | solution.py:446
  1.1 6.4 %copy-start = (bf16[512,256]{1,0:T(8,128)(2,1)S(1)}, bf16[512,256]{1,0:T(8,128)(2,1)}, u32[]{:S(2)}) copy-start(bf16[512,256]{1,0:T(8,128)(2,1)} %refs_1_.5) | copy-start | bytes 786436
  2.1 13.9 %collective-permute-start.2 = (bf16[256,256]{1,0:T(8,128)(2,1)S(1)}, bf16[256,256]{1,0:T(8,128)(2,1)S(1)}, u32[]{:S(2)}, u32[]{:S(2)}) collective-permute-start(bf16[256,256]{1,0:T(8,128)(2,1)S(1)} %pad_maximum_fusion.2), channel_id=1, source_target_pairs={{0,24},{4,28},{8,16},{12,20},{16,8},{20,12},{24,0},{28,4},{1,25},{... | collective-permute-start | bytes 393224 | tf_op jit(solution)/shard_map/ppermute | solution.py:446
  6.8 11.7 %collective-permute-start.1 = (bf16[256,256]{1,0:T(8,128)(2,1)S(1)}, bf16[256,256]{1,0:T(8,128)(2,1)S(1)}, u32[]{:S(2)}, u32[]{:S(2)}) collective-permute-start(bf16[256,256]{1,0:T(8,128)(2,1)S(1)} %pad_maximum_fusion.2), channel_id=1, source_target_pairs={{0,16},{4,20},{8,24},{12,28},{16,0},{20,4},{24,8},{28,12},{1,17},{... | collective-permute-start | bytes 393224 | tf_op jit(solution)/shard_map/ppermute | solution.py:446
  6.8 11.7 %collective-permute-start = (bf16[256,256]{1,0:T(8,128)(2,1)S(1)}, bf16[256,256]{1,0:T(8,128)(2,1)S(1)}, u32[]{:S(2)}, u32[]{:S(2)}) collective-permute-start(bf16[256,256]{1,0:T(8,128)(2,1)S(1)} %pad_maximum_fusion.2), channel_id=1, source_target_pairs={{0,8},{4,12},{8,0},{12,4},{16,24},{20,28},{24,16},{28,20},{1,9},{5... | collective-permute-start | bytes 393224 | tf_op jit(solution)/shard_map/ppermute | solution.py:446
  7.5 4.3 %copy-start.1 = (bf16[512,256]{1,0:T(8,128)(2,1)S(1)}, bf16[512,256]{1,0:T(8,128)(2,1)}, u32[]{:S(2)}) copy-start(bf16[512,256]{1,0:T(8,128)(2,1)} %refs_2_.3) | copy-start | bytes 786436
  7.5 1.3 %copy-start.2 = (bf16[2048,256]{1,0:T(8,128)(2,1)S(1)}, bf16[2048,256]{1,0:T(8,128)(2,1)}, u32[]{:S(2)}) copy-start(bf16[2048,256]{1,0:T(8,128)(2,1)} %refs_2_.2) | copy-start | bytes 3145732
  18.6 10.6 %collective-permute-start.6 = (bf16[3,128,256]{2,1,0:T(8,128)(2,1)S(1)}, bf16[3,128,256]{2,1,0:T(8,128)(2,1)S(1)}, u32[]{:S(2)}, u32[]{:S(2)}) collective-permute-start(bf16[3,128,256]{2,1,0:T(8,128)(2,1)S(1)} %pad_maximum_fusion.1.refs_1_), channel_id=1, source_target_pairs={{0,3},{1,2},{2,1},{3,0},{4,7},{5,6},{6,5},{7,4},{8,11},{9,10},{10,... | collective-permute-start | bytes 589832 | tf_op jit(solution)/shard_map/ppermute | solution.py:446
  21.1 10.6 %collective-permute-start.5 = (bf16[3,128,256]{2,1,0:T(8,128)(2,1)S(1)}, bf16[3,128,256]{2,1,0:T(8,128)(2,1)S(1)}, u32[]{:S(2)}, u32[]{:S(2)}) collective-permute-start(bf16[3,128,256]{2,1,0:T(8,128)(2,1)S(1)} %pad_maximum_fusion.1.refs_1_), channel_id=1, source_target_pairs={{0,2},{1,3},{2,0},{3,1},{4,6},{5,7},{6,4},{7,5},{8,10},{9,11},{10,... | collective-permute-start | bytes 589832 | tf_op jit(solution)/shard_map/ppermute | solution.py:446
  21.6 10.1 %collective-permute-start.4 = (bf16[3,128,256]{2,1,0:T(8,128)(2,1)S(1)}, bf16[3,128,256]{2,1,0:T(8,128)(2,1)S(1)}, u32[]{:S(2)}, u32[]{:S(2)}) collective-permute-start(bf16[3,128,256]{2,1,0:T(8,128)(2,1)S(1)} %pad_maximum_fusion.1.refs_1_), channel_id=1, source_target_pairs={{0,1},{1,0},{2,3},{3,2},{4,5},{5,4},{6,7},{7,6},{8,9},{9,8},{10,11... | collective-permute-start | bytes 589832 | tf_op jit(solution)/shard_map/ppermute | solution.py:446
  26.2 18.1 %collective-permute-start.10 = (bf16[3,128,256]{2,1,0:T(8,128)(2,1)S(1)}, bf16[3,128,256]{2,1,0:T(8,128)(2,1)S(1)}, u32[]{:S(2)}, u32[]{:S(2)}) collective-permute-start(bf16[3,128,256]{2,1,0:T(8,128)(2,1)S(1)} %pad_maximum_fusion.refs_5_), channel_id=1, source_target_pairs={{0,3},{1,2},{2,1},{3,0},{4,7},{5,6},{6,5},{7,4},{8,11},{9,10},{10,... | collective-permute-start | bytes 589832 | tf_op jit(solution)/shard_map/ppermute | solution.py:446
  28.7 15.6 %collective-permute-start.9 = (bf16[3,128,256]{2,1,0:T(8,128)(2,1)S(1)}, bf16[3,128,256]{2,1,0:T(8,128)(2,1)S(1)}, u32[]{:S(2)}, u32[]{:S(2)}) collective-permute-start(bf16[3,128,256]{2,1,0:T(8,128)(2,1)S(1)} %pad_maximum_fusion.refs_5_), channel_id=1, source_target_pairs={{0,2},{1,3},{2,0},{3,1},{4,6},{5,7},{6,4},{7,5},{8,10},{9,11},{10,... | collective-permute-start | bytes 589832 | tf_op jit(solution)/shard_map/ppermute | solution.py:446
  29.2 15.1 %collective-permute-start.8 = (bf16[3,128,256]{2,1,0:T(8,128)(2,1)S(1)}, bf16[3,128,256]{2,1,0:T(8,128)(2,1)S(1)}, u32[]{:S(2)}, u32[]{:S(2)}) collective-permute-start(bf16[3,128,256]{2,1,0:T(8,128)(2,1)S(1)} %pad_maximum_fusion.refs_5_), channel_id=1, source_target_pairs={{0,1},{1,0},{2,3},{3,2},{4,5},{5,4},{6,7},{7,6},{8,9},{9,8},{10,11... | collective-permute-start | bytes 589832 | tf_op jit(solution)/shard_map/ppermute | solution.py:446
  42.3 1.4 %collective-permute-start.7 = (f32[4,8,1024]{2,1,0:T(8,128)S(1)}, f32[4,8,1024]{2,1,0:T(8,128)S(1)}, u32[]{:S(2)}, u32[]{:S(2)}) collective-permute-start(f32[4,8,1024]{2,1,0:T(8,128)S(1)} %get-tuple-element.104.refs_1_), channel_id=1, source_target_pairs={{0,4},{4,0},{8,12},{12,8},{16,20},{20,16},{24,28},{28,24},{1,5},{5... | collective-permute-start | bytes 393224 | tf_op jit(solution)/shard_map/ppermute | solution.py:446
  51.1 15.1 %collective-permute-start.11 = (bf16[160,512]{1,0:T(8,128)(2,1)S(1)}, bf16[160,512]{1,0:T(8,128)(2,1)S(1)}, u32[]{:S(2)}, u32[]{:S(2)}) collective-permute-start(bf16[160,512]{1,0:T(8,128)(2,1)S(1)} %get-tuple-element.117), channel_id=1, source_target_pairs={{0,1},{1,0},{2,3},{3,2},{4,5},{5,4},{6,7},{7,6},{8,9},{9,8},{10,11... | collective-permute-start | bytes 491528 | tf_op jit(solution)/shard_map/ppermute | solution.py:446
  52.6 13.5 %collective-permute-start.12 = (bf16[160,512]{1,0:T(8,128)(2,1)S(1)}, bf16[160,512]{1,0:T(8,128)(2,1)S(1)}, u32[]{:S(2)}, u32[]{:S(2)}) collective-permute-start(bf16[160,512]{1,0:T(8,128)(2,1)S(1)} %get-tuple-element.118), channel_id=1, source_target_pairs={{0,2},{1,3},{2,0},{3,1},{4,6},{5,7},{6,4},{7,5},{8,10},{9,11},{10,... | collective-permute-start | bytes 491528 | tf_op jit(solution)/shard_map/ppermute | solution.py:446
  55.9 10.3 %collective-permute-start.13 = (bf16[160,512]{1,0:T(8,128)(2,1)S(1)}, bf16[160,512]{1,0:T(8,128)(2,1)S(1)}, u32[]{:S(2)}, u32[]{:S(2)}) collective-permute-start(bf16[160,512]{1,0:T(8,128)(2,1)S(1)} %get-tuple-element.119), channel_id=1, source_target_pairs={{0,3},{1,2},{2,1},{3,0},{4,7},{5,6},{6,5},{7,4},{8,11},{9,10},{10,... | collective-permute-start | bytes 491528 | tf_op jit(solution)/shard_map/ppermute | solution.py:446
  62.6 13.7 %collective-permute-start.15 = (bf16[160,512]{1,0:T(8,128)(2,1)S(1)}, bf16[160,512]{1,0:T(8,128)(2,1)S(1)}, u32[]{:S(2)}, u32[]{:S(2)}) collective-permute-start(bf16[160,512]{1,0:T(8,128)(2,1)S(1)} %get-tuple-element.127), channel_id=1, source_target_pairs={{0,1},{1,0},{2,3},{3,2},{4,5},{5,4},{6,7},{7,6},{8,9},{9,8},{10,11... | collective-permute-start | bytes 491528 | tf_op jit(solution)/shard_map/ppermute | solution.py:446
  64.1 12.2 %collective-permute-start.16 = (bf16[160,512]{1,0:T(8,128)(2,1)S(1)}, bf16[160,512]{1,0:T(8,128)(2,1)S(1)}, u32[]{:S(2)}, u32[]{:S(2)}) collective-permute-start(bf16[160,512]{1,0:T(8,128)(2,1)S(1)} %get-tuple-element.128), channel_id=1, source_target_pairs={{0,2},{1,3},{2,0},{3,1},{4,6},{5,7},{6,4},{7,5},{8,10},{9,11},{10,... | collective-permute-start | bytes 491528 | tf_op jit(solution)/shard_map/ppermute | solution.py:446
  66.2 10.2 %collective-permute-start.17 = (bf16[160,512]{1,0:T(8,128)(2,1)S(1)}, bf16[160,512]{1,0:T(8,128)(2,1)S(1)}, u32[]{:S(2)}, u32[]{:S(2)}) collective-permute-start(bf16[160,512]{1,0:T(8,128)(2,1)S(1)} %get-tuple-element.129), channel_id=1, source_target_pairs={{0,3},{1,2},{2,1},{3,0},{4,7},{5,6},{6,5},{7,4},{8,11},{9,10},{10,... | collective-permute-start | bytes 491528 | tf_op jit(solution)/shard_map/ppermute | solution.py:446
  66.9 9.5 %collective-permute-start.14 = (bf16[208,512]{1,0:T(8,128)(2,1)S(1)}, bf16[208,512]{1,0:T(8,128)(2,1)S(1)}, u32[]{:S(2)}, u32[]{:S(2)}) collective-permute-start(bf16[208,512]{1,0:T(8,128)(2,1)S(1)} %join_spread.3), channel_id=1, source_target_pairs={{0,24},{4,28},{8,16},{12,20},{16,8},{20,12},{24,0},{28,4},{1,25},{... | collective-permute-start | bytes 638984 | tf_op jit(solution)/shard_map/ppermute | solution.py:446
  77.1 10.3 %collective-permute-start.18 = (bf16[208,512]{1,0:T(8,128)(2,1)S(1)}, bf16[208,512]{1,0:T(8,128)(2,1)S(1)}, u32[]{:S(2)}, u32[]{:S(2)}) collective-permute-start(bf16[208,512]{1,0:T(8,128)(2,1)S(1)} %join_spread.4), channel_id=1, source_target_pairs={{0,16},{4,20},{8,24},{12,28},{16,0},{20,4},{24,8},{28,12},{1,17},{... | collective-permute-start | bytes 638984 | tf_op jit(solution)/shard_map/ppermute | solution.py:446
  77.8 6.7 %collective-permute-start.19 = (bf16[160,512]{1,0:T(8,128)(2,1)S(1)}, bf16[160,512]{1,0:T(8,128)(2,1)S(1)}, u32[]{:S(2)}, u32[]{:S(2)}) collective-permute-start(bf16[160,512]{1,0:T(8,128)(2,1)S(1)} %get-tuple-element.146), channel_id=1, source_target_pairs={{0,1},{1,0},{2,3},{3,2},{4,5},{5,4},{6,7},{7,6},{8,9},{9,8},{10,11... | collective-permute-start | bytes 491528 | tf_op jit(solution)/shard_map/ppermute | solution.py:446
  79.2 8.1 %collective-permute-start.20 = (bf16[160,512]{1,0:T(8,128)(2,1)S(1)}, bf16[160,512]{1,0:T(8,128)(2,1)S(1)}, u32[]{:S(2)}, u32[]{:S(2)}) collective-permute-start(bf16[160,512]{1,0:T(8,128)(2,1)S(1)} %get-tuple-element.147), channel_id=1, source_target_pairs={{0,2},{1,3},{2,0},{3,1},{4,6},{5,7},{6,4},{7,5},{8,10},{9,11},{10,... | collective-permute-start | bytes 491528 | tf_op jit(solution)/shard_map/ppermute | solution.py:446
  81.0 6.4 %collective-permute-start.21 = (bf16[160,512]{1,0:T(8,128)(2,1)S(1)}, bf16[160,512]{1,0:T(8,128)(2,1)S(1)}, u32[]{:S(2)}, u32[]{:S(2)}) collective-permute-start(bf16[160,512]{1,0:T(8,128)(2,1)S(1)} %get-tuple-element.148), channel_id=1, source_target_pairs={{0,3},{1,2},{2,1},{3,0},{4,7},{5,6},{6,5},{7,4},{8,11},{9,10},{10,... | collective-permute-start | bytes 491528 | tf_op jit(solution)/shard_map/ppermute | solution.py:446
  88.1 9.8 %collective-permute-start.25 = (bf16[208,512]{1,0:T(8,128)(2,1)S(1)}, bf16[208,512]{1,0:T(8,128)(2,1)S(1)}, u32[]{:S(2)}, u32[]{:S(2)}) collective-permute-start(bf16[208,512]{1,0:T(8,128)(2,1)S(1)} %join_spread.5), channel_id=1, source_target_pairs={{0,8},{4,12},{8,0},{12,4},{16,24},{20,28},{24,16},{28,20},{1,9},{5... | collective-permute-start | bytes 638984 | tf_op jit(solution)/shard_map/ppermute | solution.py:446
  89.7 5.6 %collective-permute-start.22 = (bf16[160,512]{1,0:T(8,128)(2,1)S(1)}, bf16[160,512]{1,0:T(8,128)(2,1)S(1)}, u32[]{:S(2)}, u32[]{:S(2)}) collective-permute-start(bf16[160,512]{1,0:T(8,128)(2,1)S(1)} %get-tuple-element.155), channel_id=1, source_target_pairs={{0,1},{1,0},{2,3},{3,2},{4,5},{5,4},{6,7},{7,6},{8,9},{9,8},{10,11... | collective-permute-start | bytes 491528 | tf_op jit(solution)/shard_map/ppermute | solution.py:446
  90.3 6.3 %collective-permute-start.23 = (bf16[160,512]{1,0:T(8,128)(2,1)S(1)}, bf16[160,512]{1,0:T(8,128)(2,1)S(1)}, u32[]{:S(2)}, u32[]{:S(2)}) collective-permute-start(bf16[160,512]{1,0:T(8,128)(2,1)S(1)} %get-tuple-element.156), channel_id=1, source_target_pairs={{0,2},{1,3},{2,0},{3,1},{4,6},{5,7},{6,4},{7,5},{8,10},{9,11},{10,... | collective-permute-start | bytes 491528 | tf_op jit(solution)/shard_map/ppermute | solution.py:446
  91.0 6.9 %collective-permute-start.24 = (bf16[160,512]{1,0:T(8,128)(2,1)S(1)}, bf16[160,512]{1,0:T(8,128)(2,1)S(1)}, u32[]{:S(2)}, u32[]{:S(2)}) collective-permute-start(bf16[160,512]{1,0:T(8,128)(2,1)S(1)} %get-tuple-element.157), channel_id=1, source_target_pairs={{0,3},{1,2},{2,1},{3,0},{4,7},{5,6},{6,5},{7,4},{8,11},{9,10},{10,... | collective-permute-start | bytes 491528 | tf_op jit(solution)/shard_map/ppermute | solution.py:446

commit v9 on v8

--- a/solution.py
+++ b/solution.py
@@ -500,7 +500,7 @@
     )
     own = sent(out)
     ((past, arrived),) = waiting
-    far, arrived = lax.optimization_barrier((far, arrived))
+    far[:-1], arrived = lax.optimization_barrier((far[:-1], arrived))
     info, part = join_spread(info, arrived)
     loss, pull = finish(info, own, [*far, swap(part, "dp", 2 * past)])
     return (loss.reshape(rows), pull.T)

time: 99.5 us -> 99.8 us (level)
  transfers between devices with their start and end apart: 26 -> 26, of which waited for: 7 -> 8; matrix products, arithmetic and copies ran while one was open for 1% -> 1% of each run, Pallas kernels for 40% -> 41%
where the time goes in v9:
time: 99.8 us; the launch traced here: 99.6 us
  Pallas kernels  49.5 us (50%)
  starting transfers between devices  33 us (33%)
  waiting for transfers between devices  13.9 us (14%)
  local copies, waits for them, and re-layouts  2.23 us (2%)
    pallas_call x13, Pallas kernels, call(): pl.pallas_call(without, grid_spec=pltpu.PrefetchScalarGridSpec(num_scalar...  49.5 us
    ppermute x26, starting transfers between devices, swap(): return lax.ppermute(value, axis, [(i, i ^ bits) for i in range(count)])  33 us
    ppermute x26, waiting for transfers between devices, swap(): return lax.ppermute(value, axis, [(i, i ^ bits) for i in range(count)])  13.9 us
  transfers between devices with their start and end apart: 26, of which 8 were waited for; matrix products, arithmetic and copies ran while one was open for 1% of the time, Pallas kernels for 41%

profile of v9, /device:TPU:0, one launch (start us, length us, event | category | flops | bytes accessed | tf_op | source)
XLA Modules:
  0.0 99.6 jit_solution(11957725392874660921)
XLA Ops:
  0.6 0.5 collective-permute-start.3
  1.1 0.9 constant_dynamic-slice_fusion
  2.1 4.7 %collective-permute-start.2 = (bf16[256,256]{1,0:T(8,128)(2,1)S(1)}, bf16[256,256]{1,0:T(8,128)(2,1)S(1)}, u32[]{:S(2)}, u32[]{:S(2)}) collective-permute-start(bf16[256,256]{1,0:T(8,128)(2,1)S(1)} %pad_maximum_fusion.2), channel_id=1, source_target_pairs={{0,24},{4,28},{8,16},{12,20},{16,8},{20,12},{24,0},{28,4},{1,25},{... | collective-permute-start | bytes 393224 | tf_op jit(solution)/shard_map/ppermute | solution.py:446
  6.8 0.6 collective-permute-start
  7.4 0.1 pad_add_fusion.refs_0_
  7.5 0.0 collective-permute-done.3.refs_3_
  7.5 1.3 %copy-done.2 = bf16[2048,256]{1,0:T(8,128)(2,1)S(1)} copy-done((bf16[2048,256]{1,0:T(8,128)(2,1)S(1)}, bf16[2048,256]{1,0:T(8,128)(2,1)}, u32[]{:S(2)}) %copy-start.2) | copy-done | bytes 1048600
  8.8 3.0 %stats_part.3 = (f32[4,8,1024]{2,1,0:T(8,128)S(1)}, bf16[2048,256]{1,0:T(8,128)(2,1)S(1)}, bf16[2048,256]{1,0:T(8,128)(2,1)S(1)}) custom-call(s32[2]{0:T(128)S(1)} %pad_add_fusion.refs_0_, bf16[512,256]{1,0:T(8,128)(2,1)S(1)} %copy-done, bf16[2048,256]{1,0:T(8,128)(2,1)S(1)} %copy-done.2, ...), custom_call_target="tpu_custom_call", output_to_operand_aliasing={{2}: (3, {})} | custom-call | flops 1073741824 | bytes 8388608 | tf_op jit(solution)/shard_map/stats_part/pallas_call | solution.py:122
  11.8 4.2 %rows_part.5 = (f32[72,512]{1,0:T(8,128)S(1)}, bf16[80,512]{1,0:T(8,128)(2,1)S(1)}, bf16[80,512]{1,0:T(8,128)(2,1)S(1)}, bf16[80,512]{1,0:T(8,128)(2,1)S(1)}, bf...) custom-call(s32[2]{0:T(128)S(1)} %pad_add_fusion.refs_0_, ...), custom_call_target="tpu_custom_call", output_to_operand_aliasing={{4}: (2, {}), {5}: (3, {})} | custom-call | flops 2147483648 | bytes 16777216 | tf_op jit(solution)/shard_map/rows_part/pallas_call | solution.py:122
  16.0 2.5 %collective-permute-done.1 = bf16[256,256]{1,0:T(8,128)(2,1)S(1)} collective-permute-done((bf16[256,256]{1,0:T(8,128)(2,1)S(1)}, bf16[256,256]{1,0:T(8,128)(2,1)S(1)}, u32[]{:S(2)}, u32[]{:S(2)}) %collective-permute-start.1) | collective-permute-done | bytes 131104 | tf_op jit(solution)/shard_map/ppermute | solution.py:446
  18.6 2.5 %collective-permute-start.6 = (bf16[3,128,256]{2,1,0:T(8,128)(2,1)S(1)}, bf16[3,128,256]{2,1,0:T(8,128)(2,1)S(1)}, u32[]{:S(2)}, u32[]{:S(2)}) collective-permute-start(bf16[3,128,256]{2,1,0:T(8,128)(2,1)S(1)} %pad_maximum_fusion.1.refs_1_), channel_id=1, source_target_pairs={{0,3},{1,2},{2,1},{3,0},{4,7},{5,6},{6,5},{7,4},{8,11},{9,10},{10,... | collective-permute-start | bytes 589832 | tf_op jit(solution)/shard_map/ppermute | solution.py:446
  21.1 0.5 collective-permute-start.5
  21.6 0.5 collective-permute-start.4
  22.2 4.0 %stats_part.4 = (f32[4,8,1024]{2,1,0:T(8,128)S(1)}, bf16[2048,256]{1,0:T(8,128)(2,1)S(1)}, bf16[2048,256]{1,0:T(8,128)(2,1)S(1)}) custom-call(s32[2]{0:T(128)S(1)} %pad_add_fusion.refs_0_, bf16[3,128,256]{2,1,0:T(8,128)(2,1)S(1)} %pad_maximum_fusion.1.refs_1_, ...), custom_call_target="tpu_custom_call", output_to_operand_aliasing={{1}: (2, {}), {2}: (3, {})} | custom-call | flops 805306368 | bytes 6291456 | tf_op jit(solution)/shard_map/stats_part/pallas_call | solution.py:122
  26.2 2.5 %collective-permute-start.10 = (bf16[3,128,256]{2,1,0:T(8,128)(2,1)S(1)}, bf16[3,128,256]{2,1,0:T(8,128)(2,1)S(1)}, u32[]{:S(2)}, u32[]{:S(2)}) collective-permute-start(bf16[3,128,256]{2,1,0:T(8,128)(2,1)S(1)} %pad_maximum_fusion.refs_5_), channel_id=1, source_target_pairs={{0,3},{1,2},{2,1},{3,0},{4,7},{5,6},{6,5},{7,4},{8,11},{9,10},{10,... | collective-permute-start | bytes 589832 | tf_op jit(solution)/shard_map/ppermute | solution.py:446
  28.7 0.5 collective-permute-start.9
  29.2 0.5 collective-permute-start.8
  29.8 1.9 %collective-permute-done.5.refs_2_.refs_3_ = bf16[3,128,256]{2,1,0:T(8,128)(2,1)S(1)} collective-permute-done((bf16[3,128,256]{2,1,0:T(8,128)(2,1)S(1)}, bf16[3,128,256]{2,1,0:T(8,128)(2,1)S(1)}, u32[]{:S(2)}, u32[]{:S(2)}) %collective-permute-start.5) | collective-permute-done | bytes 196640 | tf_op jit(solution)/shard_map/ppermute | solution.py:446
  31.7 10.6 %stats_part.5 = (f32[4,8,1024]{2,1,0:T(8,128)S(1)}, bf16[2048,256]{1,0:T(8,128)(2,1)S(1)}, bf16[2048,256]{1,0:T(8,128)(2,1)S(1)}) custom-call(s32[2]{0:T(128)S(1)} %pad_add_fusion.refs_0_, bf16[3,128,256]{2,1,0:T(8,128)(2,1)S(1)} %collective-permute-done.4.refs_1_.refs_2_, ...), custom_call_target="tpu_custom_call", output_to_operand_aliasing={{1}: (4, {}), {2}: (5, {})} | custom-call | flops 2415919104 | bytes 18874368 | tf_op jit(solution)/shard_map/stats_part/pallas_call | solution.py:122
  42.3 0.1 collective-permute-start.7
  42.4 1.3 %collective-permute-done.7.refs_2_ = f32[4,8,1024]{2,1,0:T(8,128)S(1)} collective-permute-done((f32[4,8,1024]{2,1,0:T(8,128)S(1)}, f32[4,8,1024]{2,1,0:T(8,128)S(1)}, u32[]{:S(2)}, u32[]{:S(2)}) %collective-permute-start.7) | collective-permute-done | bytes 131104 | tf_op jit(solution)/shard_map/ppermute | solution.py:446
  43.7 0.6 offset_part.1.refs_11_.refs_5_
  44.4 6.7 %rows_part.6 = (f32[144,512]{1,0:T(8,128)S(1)}, bf16[160,512]{1,0:T(8,128)(2,1)S(1)}, bf16[160,512]{1,0:T(8,128)(2,1)S(1)}, bf16[160,512]{1,0:T(8,128)(2,1)S(1)}...) custom-call(s32[2]{0:T(128)S(1)} %pad_add_fusion.refs_0_, ...), custom_call_target="tpu_custom_call", output_to_operand_aliasing={{4}: (9, {}), {5}: (10, {})} | custom-call | flops 4294967296 | bytes 33554432 | tf_op jit(solution)/shard_map/rows_part/pallas_call | solution.py:122
  51.1 1.6 %collective-permute-start.11 = (bf16[160,512]{1,0:T(8,128)(2,1)S(1)}, bf16[160,512]{1,0:T(8,128)(2,1)S(1)}, u32[]{:S(2)}, u32[]{:S(2)}) collective-permute-start(bf16[160,512]{1,0:T(8,128)(2,1)S(1)} %get-tuple-element.116), channel_id=1, source_target_pairs={{0,1},{1,0},{2,3},{3,2},{4,5},{5,4},{6,7},{7,6},{8,9},{9,8},{10,11... | collective-permute-start | bytes 491528 | tf_op jit(solution)/shard_map/ppermute | solution.py:446
  52.6 3.3 %collective-permute-start.12 = (bf16[160,512]{1,0:T(8,128)(2,1)S(1)}, bf16[160,512]{1,0:T(8,128)(2,1)S(1)}, u32[]{:S(2)}, u32[]{:S(2)}) collective-permute-start(bf16[160,512]{1,0:T(8,128)(2,1)S(1)} %get-tuple-element.117), channel_id=1, source_target_pairs={{0,2},{1,3},{2,0},{3,1},{4,6},{5,7},{6,4},{7,5},{8,10},{9,11},{10,... | collective-permute-start | bytes 491528 | tf_op jit(solution)/shard_map/ppermute | solution.py:446
  55.9 6.7 %rows_part.7 = (f32[144,512]{1,0:T(8,128)S(1)}, bf16[160,512]{1,0:T(8,128)(2,1)S(1)}, bf16[160,512]{1,0:T(8,128)(2,1)S(1)}, bf16[160,512]{1,0:T(8,128)(2,1)S(1)}...) custom-call(s32[2]{0:T(128)S(1)} %pad_add_fusion.refs_0_, ...), custom_call_target="tpu_custom_call", output_to_operand_aliasing={{4}: (9, {}), {5}: (10, {})} | custom-call | flops 4294967296 | bytes 33554432 | tf_op jit(solution)/shard_map/rows_part/pallas_call | solution.py:122
  62.6 1.5 %collective-permute-start.15 = (bf16[160,512]{1,0:T(8,128)(2,1)S(1)}, bf16[160,512]{1,0:T(8,128)(2,1)S(1)}, u32[]{:S(2)}, u32[]{:S(2)}) collective-permute-start(bf16[160,512]{1,0:T(8,128)(2,1)S(1)} %get-tuple-element.126), channel_id=1, source_target_pairs={{0,1},{1,0},{2,3},{3,2},{4,5},{5,4},{6,7},{7,6},{8,9},{9,8},{10,11... | collective-permute-start | bytes 491528 | tf_op jit(solution)/shard_map/ppermute | solution.py:446
  64.1 2.0 %collective-permute-start.16 = (bf16[160,512]{1,0:T(8,128)(2,1)S(1)}, bf16[160,512]{1,0:T(8,128)(2,1)S(1)}, u32[]{:S(2)}, u32[]{:S(2)}) collective-permute-start(bf16[160,512]{1,0:T(8,128)(2,1)S(1)} %get-tuple-element.127), channel_id=1, source_target_pairs={{0,2},{1,3},{2,0},{3,1},{4,6},{5,7},{6,4},{7,5},{8,10},{9,11},{10,... | collective-permute-start | bytes 491528 | tf_op jit(solution)/shard_map/ppermute | solution.py:446
  66.2 0.7 join_spread.3
  66.9 2.5 %collective-permute-start.14 = (bf16[208,512]{1,0:T(8,128)(2,1)S(1)}, bf16[208,512]{1,0:T(8,128)(2,1)S(1)}, u32[]{:S(2)}, u32[]{:S(2)}) collective-permute-start(bf16[208,512]{1,0:T(8,128)(2,1)S(1)} %join_spread.3), channel_id=1, source_target_pairs={{0,24},{4,28},{8,16},{12,20},{16,8},{20,12},{24,0},{28,4},{1,25},{... | collective-permute-start | bytes 638984 | tf_op jit(solution)/shard_map/ppermute | solution.py:446
  69.4 6.9 %rows_part.8 = (f32[144,512]{1,0:T(8,128)S(1)}, bf16[160,512]{1,0:T(8,128)(2,1)S(1)}, bf16[160,512]{1,0:T(8,128)(2,1)S(1)}, bf16[160,512]{1,0:T(8,128)(2,1)S(1)}...) custom-call(s32[2]{0:T(128)S(1)} %pad_add_fusion.refs_0_, ...), custom_call_target="tpu_custom_call", output_to_operand_aliasing={{4}: (9, {}), {5}: (10, {})} | custom-call | flops 4294967296 | bytes 33554432 | tf_op jit(solution)/shard_map/rows_part/pallas_call | solution.py:122
  76.3 1.5 %collective-permute-start.18 = (bf16[160,512]{1,0:T(8,128)(2,1)S(1)}, bf16[160,512]{1,0:T(8,128)(2,1)S(1)}, u32[]{:S(2)}, u32[]{:S(2)}) collective-permute-start(bf16[160,512]{1,0:T(8,128)(2,1)S(1)} %get-tuple-element.144), channel_id=1, source_target_pairs={{0,1},{1,0},{2,3},{3,2},{4,5},{5,4},{6,7},{7,6},{8,9},{9,8},{10,11... | collective-permute-start | bytes 491528 | tf_op jit(solution)/shard_map/ppermute | solution.py:446
  77.9 2.0 %collective-permute-start.19 = (bf16[160,512]{1,0:T(8,128)(2,1)S(1)}, bf16[160,512]{1,0:T(8,128)(2,1)S(1)}, u32[]{:S(2)}, u32[]{:S(2)}) collective-permute-start(bf16[160,512]{1,0:T(8,128)(2,1)S(1)} %get-tuple-element.145), channel_id=1, source_target_pairs={{0,2},{1,3},{2,0},{3,1},{4,6},{5,7},{6,4},{7,5},{8,10},{9,11},{10,... | collective-permute-start | bytes 491528 | tf_op jit(solution)/shard_map/ppermute | solution.py:446
  79.9 0.0 collective-permute-start.20
  79.9 0.7 join_spread.4
  80.6 3.2 %rows_part.9 = (f32[144,512]{1,0:T(8,128)S(1)}, bf16[160,512]{1,0:T(8,128)(2,1)S(1)}, bf16[160,512]{1,0:T(8,128)(2,1)S(1)}, bf16[160,512]{1,0:T(8,128)(2,1)S(1)}) custom-call(s32[2]{0:T(128)S(1)} %pad_add_fusion.refs_0_, bf16[512,256]{1,0:T(8,128)(2,1)S(1)} %copy-done, bf16[512,256]{1,0:T(8,128)(2,1)S(1)} %copy-done.1, ...), custom_call_target="tpu_custom_call" | custom-call | flops 2147483648 | bytes 16777216 | tf_op jit(solution)/shard_map/rows_part/pallas_call | solution.py:122
  83.9 2.6 %collective-permute-done.19.refs_3_ = bf16[160,512]{1,0:T(8,128)(2,1)S(1)} collective-permute-done((bf16[160,512]{1,0:T(8,128)(2,1)S(1)}, bf16[160,512]{1,0:T(8,128)(2,1)S(1)}, u32[]{:S(2)}, u32[]{:S(2)}) %collective-permute-start.19) | collective-permute-done | bytes 163872 | tf_op jit(solution)/shard_map/ppermute | solution.py:446
  86.5 0.7 join_spread.5
  87.2 0.1 collective-permute-start.25
  87.3 1.9 %collective-permute-start.24 = (bf16[208,512]{1,0:T(8,128)(2,1)S(1)}, bf16[208,512]{1,0:T(8,128)(2,1)S(1)}, u32[]{:S(2)}, u32[]{:S(2)}) collective-permute-start(bf16[208,512]{1,0:T(8,128)(2,1)S(1)} %join_spread.4), channel_id=1, source_target_pairs={{0,16},{4,20},{8,24},{12,28},{16,0},{20,4},{24,8},{28,12},{1,17},{... | collective-permute-start | bytes 638984 | tf_op jit(solution)/shard_map/ppermute | solution.py:446
  89.2 0.6 collective-permute-start.21
  89.8 0.7 collective-permute-start.22
  90.5 2.2 %collective-permute-start.23 = (bf16[160,512]{1,0:T(8,128)(2,1)S(1)}, bf16[160,512]{1,0:T(8,128)(2,1)S(1)}, u32[]{:S(2)}, u32[]{:S(2)}) collective-permute-start(bf16[160,512]{1,0:T(8,128)(2,1)S(1)} %get-tuple-element.155), channel_id=1, source_target_pairs={{0,3},{1,2},{2,1},{3,0},{4,7},{5,6},{6,5},{7,4},{8,11},{9,10},{10,... | collective-permute-start | bytes 491528 | tf_op jit(solution)/shard_map/ppermute | solution.py:446
  92.7 1.9 %collective-permute-done.21.refs_2_ = bf16[160,512]{1,0:T(8,128)(2,1)S(1)} collective-permute-done((bf16[160,512]{1,0:T(8,128)(2,1)S(1)}, bf16[160,512]{1,0:T(8,128)(2,1)S(1)}, u32[]{:S(2)}, u32[]{:S(2)}) %collective-permute-start.21) | collective-permute-done | bytes 163872 | tf_op jit(solution)/shard_map/ppermute | solution.py:446
  94.6 0.5 collective-permute-done.22.refs_3_
  95.1 1.7 %collective-permute-done.23.refs_4_ = bf16[160,512]{1,0:T(8,128)(2,1)S(1)} collective-permute-done((bf16[160,512]{1,0:T(8,128)(2,1)S(1)}, bf16[160,512]{1,0:T(8,128)(2,1)S(1)}, u32[]{:S(2)}, u32[]{:S(2)}) %collective-permute-start.23) | collective-permute-done | bytes 163872 | tf_op jit(solution)/shard_map/ppermute | solution.py:446
  96.9 1.3 %collective-permute-done.24.refs_6_ = bf16[208,512]{1,0:T(8,128)(2,1)S(1)} collective-permute-done((bf16[208,512]{1,0:T(8,128)(2,1)S(1)}, bf16[208,512]{1,0:T(8,128)(2,1)S(1)}, u32[]{:S(2)}, u32[]{:S(2)}) %collective-permute-start.24) | collective-permute-done | bytes 213024 | tf_op jit(solution)/shard_map/ppermute | solution.py:446
  98.1 1.5 %finish.1 = (f32[1,512]{1,0:T(1,128)}, f32[64,512]{1,0:T(8,128)}) custom-call(s32[2]{0:T(128)S(1)} %pad_add_fusion.refs_0_, f32[144,512]{1,0:T(8,128)S(1)} %get-tuple-element.152.refs_1_, bf16[160,512]{1,0:T(8,128)(2,1)S(1)} %collective-permute-done.21.refs_2_, bf16[160,512]{1,0:T(8,128)(2,1)S(1)} %collective-permute-done.22.refs_3_, ...), custom_call_target="tpu_custom_call" | custom-call | flops 1048576 | bytes 8192 | tf_op jit(solution)/shard_map/finish/pallas_call | solution.py:122
  (31 shorter events, 0.2 us)
Async XLA Ops:
  0.6 6.9 %collective-permute-start.3 = (bf16[2048,256]{1,0:T(8,128)(2,1)}, bf16[2048,256]{1,0:T(8,128)(2,1)S(1)}, u32[]{:S(2)}, u32[]{:S(2)}) collective-permute-start(bf16[2048,256]{1,0:T(8,128)(2,1)} %refs_2_.2), channel_id=1, source_target_pairs={{0,4},{4,0},{8,12},{12,8},{16,20},{20,16},{24,28},{28,24},{1,5},{5... | collective-permute-start | bytes 3145736 | tf_op jit(solution)/shard_map/ppermute | solution.py:446
  1.1 6.4 %copy-start = (bf16[512,256]{1,0:T(8,128)(2,1)S(1)}, bf16[512,256]{1,0:T(8,128)(2,1)}, u32[]{:S(2)}) copy-start(bf16[512,256]{1,0:T(8,128)(2,1)} %refs_1_.5) | copy-start | bytes 786436
  2.1 13.9 %collective-permute-start.2 = (bf16[256,256]{1,0:T(8,128)(2,1)S(1)}, bf16[256,256]{1,0:T(8,128)(2,1)S(1)}, u32[]{:S(2)}, u32[]{:S(2)}) collective-permute-start(bf16[256,256]{1,0:T(8,128)(2,1)S(1)} %pad_maximum_fusion.2), channel_id=1, source_target_pairs={{0,24},{4,28},{8,16},{12,20},{16,8},{20,12},{24,0},{28,4},{1,25},{... | collective-permute-start | bytes 393224 | tf_op jit(solution)/shard_map/ppermute | solution.py:446
  6.8 11.7 %collective-permute-start.1 = (bf16[256,256]{1,0:T(8,128)(2,1)S(1)}, bf16[256,256]{1,0:T(8,128)(2,1)S(1)}, u32[]{:S(2)}, u32[]{:S(2)}) collective-permute-start(bf16[256,256]{1,0:T(8,128)(2,1)S(1)} %pad_maximum_fusion.2), channel_id=1, source_target_pairs={{0,16},{4,20},{8,24},{12,28},{16,0},{20,4},{24,8},{28,12},{1,17},{... | collective-permute-start | bytes 393224 | tf_op jit(solution)/shard_map/ppermute | solution.py:446
  6.8 11.7 %collective-permute-start = (bf16[256,256]{1,0:T(8,128)(2,1)S(1)}, bf16[256,256]{1,0:T(8,128)(2,1)S(1)}, u32[]{:S(2)}, u32[]{:S(2)}) collective-permute-start(bf16[256,256]{1,0:T(8,128)(2,1)S(1)} %pad_maximum_fusion.2), channel_id=1, source_target_pairs={{0,8},{4,12},{8,0},{12,4},{16,24},{20,28},{24,16},{28,20},{1,9},{5... | collective-permute-start | bytes 393224 | tf_op jit(solution)/shard_map/ppermute | solution.py:446
  7.5 4.3 %copy-start.1 = (bf16[512,256]{1,0:T(8,128)(2,1)S(1)}, bf16[512,256]{1,0:T(8,128)(2,1)}, u32[]{:S(2)}) copy-start(bf16[512,256]{1,0:T(8,128)(2,1)} %refs_2_.3) | copy-start | bytes 786436
  7.5 1.3 %copy-start.2 = (bf16[2048,256]{1,0:T(8,128)(2,1)S(1)}, bf16[2048,256]{1,0:T(8,128)(2,1)}, u32[]{:S(2)}) copy-start(bf16[2048,256]{1,0:T(8,128)(2,1)} %refs_2_.2) | copy-start | bytes 3145732
  18.6 10.6 %collective-permute-start.6 = (bf16[3,128,256]{2,1,0:T(8,128)(2,1)S(1)}, bf16[3,128,256]{2,1,0:T(8,128)(2,1)S(1)}, u32[]{:S(2)}, u32[]{:S(2)}) collective-permute-start(bf16[3,128,256]{2,1,0:T(8,128)(2,1)S(1)} %pad_maximum_fusion.1.refs_1_), channel_id=1, source_target_pairs={{0,3},{1,2},{2,1},{3,0},{4,7},{5,6},{6,5},{7,4},{8,11},{9,10},{10,... | collective-permute-start | bytes 589832 | tf_op jit(solution)/shard_map/ppermute | solution.py:446
  21.1 10.6 %collective-permute-start.5 = (bf16[3,128,256]{2,1,0:T(8,128)(2,1)S(1)}, bf16[3,128,256]{2,1,0:T(8,128)(2,1)S(1)}, u32[]{:S(2)}, u32[]{:S(2)}) collective-permute-start(bf16[3,128,256]{2,1,0:T(8,128)(2,1)S(1)} %pad_maximum_fusion.1.refs_1_), channel_id=1, source_target_pairs={{0,2},{1,3},{2,0},{3,1},{4,6},{5,7},{6,4},{7,5},{8,10},{9,11},{10,... | collective-permute-start | bytes 589832 | tf_op jit(solution)/shard_map/ppermute | solution.py:446
  21.6 10.1 %collective-permute-start.4 = (bf16[3,128,256]{2,1,0:T(8,128)(2,1)S(1)}, bf16[3,128,256]{2,1,0:T(8,128)(2,1)S(1)}, u32[]{:S(2)}, u32[]{:S(2)}) collective-permute-start(bf16[3,128,256]{2,1,0:T(8,128)(2,1)S(1)} %pad_maximum_fusion.1.refs_1_), channel_id=1, source_target_pairs={{0,1},{1,0},{2,3},{3,2},{4,5},{5,4},{6,7},{7,6},{8,9},{9,8},{10,11... | collective-permute-start | bytes 589832 | tf_op jit(solution)/shard_map/ppermute | solution.py:446
  26.2 18.1 %collective-permute-start.10 = (bf16[3,128,256]{2,1,0:T(8,128)(2,1)S(1)}, bf16[3,128,256]{2,1,0:T(8,128)(2,1)S(1)}, u32[]{:S(2)}, u32[]{:S(2)}) collective-permute-start(bf16[3,128,256]{2,1,0:T(8,128)(2,1)S(1)} %pad_maximum_fusion.refs_5_), channel_id=1, source_target_pairs={{0,3},{1,2},{2,1},{3,0},{4,7},{5,6},{6,5},{7,4},{8,11},{9,10},{10,... | collective-permute-start | bytes 589832 | tf_op jit(solution)/shard_map/ppermute | solution.py:446
  28.7 15.6 %collective-permute-start.9 = (bf16[3,128,256]{2,1,0:T(8,128)(2,1)S(1)}, bf16[3,128,256]{2,1,0:T(8,128)(2,1)S(1)}, u32[]{:S(2)}, u32[]{:S(2)}) collective-permute-start(bf16[3,128,256]{2,1,0:T(8,128)(2,1)S(1)} %pad_maximum_fusion.refs_5_), channel_id=1, source_target_pairs={{0,2},{1,3},{2,0},{3,1},{4,6},{5,7},{6,4},{7,5},{8,10},{9,11},{10,... | collective-permute-start | bytes 589832 | tf_op jit(solution)/shard_map/ppermute | solution.py:446
  29.2 15.1 %collective-permute-start.8 = (bf16[3,128,256]{2,1,0:T(8,128)(2,1)S(1)}, bf16[3,128,256]{2,1,0:T(8,128)(2,1)S(1)}, u32[]{:S(2)}, u32[]{:S(2)}) collective-permute-start(bf16[3,128,256]{2,1,0:T(8,128)(2,1)S(1)} %pad_maximum_fusion.refs_5_), channel_id=1, source_target_pairs={{0,1},{1,0},{2,3},{3,2},{4,5},{5,4},{6,7},{7,6},{8,9},{9,8},{10,11... | collective-permute-start | bytes 589832 | tf_op jit(solution)/shard_map/ppermute | solution.py:446
  42.3 1.4 %collective-permute-start.7 = (f32[4,8,1024]{2,1,0:T(8,128)S(1)}, f32[4,8,1024]{2,1,0:T(8,128)S(1)}, u32[]{:S(2)}, u32[]{:S(2)}) collective-permute-start(f32[4,8,1024]{2,1,0:T(8,128)S(1)} %get-tuple-element.103.refs_1_), channel_id=1, source_target_pairs={{0,4},{4,0},{8,12},{12,8},{16,20},{20,16},{24,28},{28,24},{1,5},{5... | collective-permute-start | bytes 393224 | tf_op jit(solution)/shard_map/ppermute | solution.py:446
  51.1 15.1 %collective-permute-start.11 = (bf16[160,512]{1,0:T(8,128)(2,1)S(1)}, bf16[160,512]{1,0:T(8,128)(2,1)S(1)}, u32[]{:S(2)}, u32[]{:S(2)}) collective-permute-start(bf16[160,512]{1,0:T(8,128)(2,1)S(1)} %get-tuple-element.116), channel_id=1, source_target_pairs={{0,1},{1,0},{2,3},{3,2},{4,5},{5,4},{6,7},{7,6},{8,9},{9,8},{10,11... | collective-permute-start | bytes 491528 | tf_op jit(solution)/shard_map/ppermute | solution.py:446
  52.6 13.5 %collective-permute-start.12 = (bf16[160,512]{1,0:T(8,128)(2,1)S(1)}, bf16[160,512]{1,0:T(8,128)(2,1)S(1)}, u32[]{:S(2)}, u32[]{:S(2)}) collective-permute-start(bf16[160,512]{1,0:T(8,128)(2,1)S(1)} %get-tuple-element.117), channel_id=1, source_target_pairs={{0,2},{1,3},{2,0},{3,1},{4,6},{5,7},{6,4},{7,5},{8,10},{9,11},{10,... | collective-permute-start | bytes 491528 | tf_op jit(solution)/shard_map/ppermute | solution.py:446
  55.9 10.3 %collective-permute-start.13 = (bf16[160,512]{1,0:T(8,128)(2,1)S(1)}, bf16[160,512]{1,0:T(8,128)(2,1)S(1)}, u32[]{:S(2)}, u32[]{:S(2)}) collective-permute-start(bf16[160,512]{1,0:T(8,128)(2,1)S(1)} %get-tuple-element.118), channel_id=1, source_target_pairs={{0,3},{1,2},{2,1},{3,0},{4,7},{5,6},{6,5},{7,4},{8,11},{9,10},{10,... | collective-permute-start | bytes 491528 | tf_op jit(solution)/shard_map/ppermute | solution.py:446
  62.6 15.2 %collective-permute-start.15 = (bf16[160,512]{1,0:T(8,128)(2,1)S(1)}, bf16[160,512]{1,0:T(8,128)(2,1)S(1)}, u32[]{:S(2)}, u32[]{:S(2)}) collective-permute-start(bf16[160,512]{1,0:T(8,128)(2,1)S(1)} %get-tuple-element.126), channel_id=1, source_target_pairs={{0,1},{1,0},{2,3},{3,2},{4,5},{5,4},{6,7},{7,6},{8,9},{9,8},{10,11... | collective-permute-start | bytes 491528 | tf_op jit(solution)/shard_map/ppermute | solution.py:446
  64.1 15.7 %collective-permute-start.16 = (bf16[160,512]{1,0:T(8,128)(2,1)S(1)}, bf16[160,512]{1,0:T(8,128)(2,1)S(1)}, u32[]{:S(2)}, u32[]{:S(2)}) collective-permute-start(bf16[160,512]{1,0:T(8,128)(2,1)S(1)} %get-tuple-element.127), channel_id=1, source_target_pairs={{0,2},{1,3},{2,0},{3,1},{4,6},{5,7},{6,4},{7,5},{8,10},{9,11},{10,... | collective-permute-start | bytes 491528 | tf_op jit(solution)/shard_map/ppermute | solution.py:446
  66.2 13.7 %collective-permute-start.17 = (bf16[160,512]{1,0:T(8,128)(2,1)S(1)}, bf16[160,512]{1,0:T(8,128)(2,1)S(1)}, u32[]{:S(2)}, u32[]{:S(2)}) collective-permute-start(bf16[160,512]{1,0:T(8,128)(2,1)S(1)} %get-tuple-element.128), channel_id=1, source_target_pairs={{0,3},{1,2},{2,1},{3,0},{4,7},{5,6},{6,5},{7,4},{8,11},{9,10},{10,... | collective-permute-start | bytes 491528 | tf_op jit(solution)/shard_map/ppermute | solution.py:446
  66.9 13.0 %collective-permute-start.14 = (bf16[208,512]{1,0:T(8,128)(2,1)S(1)}, bf16[208,512]{1,0:T(8,128)(2,1)S(1)}, u32[]{:S(2)}, u32[]{:S(2)}) collective-permute-start(bf16[208,512]{1,0:T(8,128)(2,1)S(1)} %join_spread.3), channel_id=1, source_target_pairs={{0,24},{4,28},{8,16},{12,20},{16,8},{20,12},{24,0},{28,4},{1,25},{... | collective-permute-start | bytes 638984 | tf_op jit(solution)/shard_map/ppermute | solution.py:446
  76.3 7.5 %collective-permute-start.18 = (bf16[160,512]{1,0:T(8,128)(2,1)S(1)}, bf16[160,512]{1,0:T(8,128)(2,1)S(1)}, u32[]{:S(2)}, u32[]{:S(2)}) collective-permute-start(bf16[160,512]{1,0:T(8,128)(2,1)S(1)} %get-tuple-element.144), channel_id=1, source_target_pairs={{0,1},{1,0},{2,3},{3,2},{4,5},{5,4},{6,7},{7,6},{8,9},{9,8},{10,11... | collective-permute-start | bytes 491528 | tf_op jit(solution)/shard_map/ppermute | solution.py:446
  77.9 8.6 %collective-permute-start.19 = (bf16[160,512]{1,0:T(8,128)(2,1)S(1)}, bf16[160,512]{1,0:T(8,128)(2,1)S(1)}, u32[]{:S(2)}, u32[]{:S(2)}) collective-permute-start(bf16[160,512]{1,0:T(8,128)(2,1)S(1)} %get-tuple-element.145), channel_id=1, source_target_pairs={{0,2},{1,3},{2,0},{3,1},{4,6},{5,7},{6,4},{7,5},{8,10},{9,11},{10,... | collective-permute-start | bytes 491528 | tf_op jit(solution)/shard_map/ppermute | solution.py:446
  79.9 6.6 %collective-permute-start.20 = (bf16[160,512]{1,0:T(8,128)(2,1)S(1)}, bf16[160,512]{1,0:T(8,128)(2,1)S(1)}, u32[]{:S(2)}, u32[]{:S(2)}) collective-permute-start(bf16[160,512]{1,0:T(8,128)(2,1)S(1)} %get-tuple-element.146), channel_id=1, source_target_pairs={{0,3},{1,2},{2,1},{3,0},{4,7},{5,6},{6,5},{7,4},{8,11},{9,10},{10,... | collective-permute-start | bytes 491528 | tf_op jit(solution)/shard_map/ppermute | solution.py:446
  87.2 9.7 %collective-permute-start.25 = (bf16[208,512]{1,0:T(8,128)(2,1)S(1)}, bf16[208,512]{1,0:T(8,128)(2,1)S(1)}, u32[]{:S(2)}, u32[]{:S(2)}) collective-permute-start(bf16[208,512]{1,0:T(8,128)(2,1)S(1)} %join_spread.5), channel_id=1, source_target_pairs={{0,8},{4,12},{8,0},{12,4},{16,24},{20,28},{24,16},{28,20},{1,9},{5... | collective-permute-start | bytes 638984 | tf_op jit(solution)/shard_map/ppermute | solution.py:446
  87.3 10.9 %collective-permute-start.24 = (bf16[208,512]{1,0:T(8,128)(2,1)S(1)}, bf16[208,512]{1,0:T(8,128)(2,1)S(1)}, u32[]{:S(2)}, u32[]{:S(2)}) collective-permute-start(bf16[208,512]{1,0:T(8,128)(2,1)S(1)} %join_spread.4), channel_id=1, source_target_pairs={{0,16},{4,20},{8,24},{12,28},{16,0},{20,4},{24,8},{28,12},{1,17},{... | collective-permute-start | bytes 638984 | tf_op jit(solution)/shard_map/ppermute | solution.py:446
  89.2 5.4 %collective-permute-start.21 = (bf16[160,512]{1,0:T(8,128)(2,1)S(1)}, bf16[160,512]{1,0:T(8,128)(2,1)S(1)}, u32[]{:S(2)}, u32[]{:S(2)}) collective-permute-start(bf16[160,512]{1,0:T(8,128)(2,1)S(1)} %get-tuple-element.153), channel_id=1, source_target_pairs={{0,1},{1,0},{2,3},{3,2},{4,5},{5,4},{6,7},{7,6},{8,9},{9,8},{10,11... | collective-permute-start | bytes 491528 | tf_op jit(solution)/shard_map/ppermute | solution.py:446
  89.8 5.3 %collective-permute-start.22 = (bf16[160,512]{1,0:T(8,128)(2,1)S(1)}, bf16[160,512]{1,0:T(8,128)(2,1)S(1)}, u32[]{:S(2)}, u32[]{:S(2)}) collective-permute-start(bf16[160,512]{1,0:T(8,128)(2,1)S(1)} %get-tuple-element.154), channel_id=1, source_target_pairs={{0,2},{1,3},{2,0},{3,1},{4,6},{5,7},{6,4},{7,5},{8,10},{9,11},{10,... | collective-permute-start | bytes 491528 | tf_op jit(solution)/shard_map/ppermute | solution.py:446
  90.5 6.4 %collective-permute-start.23 = (bf16[160,512]{1,0:T(8,128)(2,1)S(1)}, bf16[160,512]{1,0:T(8,128)(2,1)S(1)}, u32[]{:S(2)}, u32[]{:S(2)}) collective-permute-start(bf16[160,512]{1,0:T(8,128)(2,1)S(1)} %get-tuple-element.155), channel_id=1, source_target_pairs={{0,3},{1,2},{2,1},{3,0},{4,7},{5,6},{6,5},{7,4},{8,11},{9,10},{10,... | collective-permute-start | bytes 491528 | tf_op jit(solution)/shard_map/ppermute | solution.py:446
